TPU v7x, 32 devices: a whole 2x2x4 slice. The times are simulated.
32 devices in a mesh: dp: 8 (over z, x), head: 4 (over y, core).
Axes of the slice: x: 2, y: 2, z: 4, core: 2. Of those that a mesh axis runs over, the one named last changes fastest.
Arguments:
- cell_ids: int32 [1024, 64], P('dp'), may hold values from 0 to 31
- cell_mask: int32 [1024, 64], P('dp'), may hold values from 0 to 1
- labels: int32 [1024, 64], P('dp', 'head'), may hold values from 0 to 31
- abd_weights: float32 [4096, 8, 6144], P('dp', 'head'), may hold values from -4 to 4
- abd_first: float32 [4096, 8, 6144], P('dp', 'head'), may hold values from -8.6617505e-07 to 8.6617505e-07
- abd_second: float32 [4096, 8, 6144], P('dp', 'head'), may hold values from 4.95908e-16 to 1.983632e-15
- abd_gains: float32 [2, 4096], replicated, may hold values from 0.45 to 1.65
- abd_gains_first: float32 [2, 4096], replicated, may hold values from -1.9073486e-06 to 1.9073486e-06
- abd_gains_second: float32 [2, 4096], replicated, may hold values from 7.934528e-15 to 3.173811e-14
- aba_weights: float32 [64, 768], replicated, may hold values from -4 to 4
- aba_first: float32 [64, 768], replicated, may hold values from -4.7683716e-07 to 4.7683716e-07
- aba_second: float32 [64, 768], replicated, may hold values from 4.95908e-16 to 1.983632e-15
- aba_gains: float32 [2, 64], replicated, may hold values from 0.5 to 1.5
- aba_gains_first: float32 [2, 64], replicated, may hold values from -1.9073486e-06 to 1.9073486e-06
- aba_gains_second: float32 [2, 64], replicated, may hold values from 7.934528e-15 to 3.173811e-14
- embed_table: float32 [64, 33, 64], replicated, may hold values from -6 to 6
- embed_first: float32 [64, 33, 64], replicated, may hold values from -4.7683716e-07 to 4.7683716e-07
- embed_second: float32 [64, 33, 64], replicated, may hold values from 4.95908e-16 to 1.983632e-15
- output_table: float32 [64, 64, 32], P('head'), may hold values from -0.75 to 0.75
- output_first: float32 [64, 64, 32], P('head'), may hold values from -5.281555e-07 to 5.281555e-07
- output_second: float32 [64, 64, 32], P('head'), may hold values from 4.95908e-16 to 1.983632e-15
Outputs:
- loss_sum: float32 [], replicated
- weight_total: float32 [], replicated
- grad_norm: float32 [], replicated
- abd_new: float32 [4096, 8, 6144], P('dp', 'head')
- abd_first_new: float32 [4096, 8, 6144], P('dp', 'head')
- abd_second_new: float32 [4096, 8, 6144], P('dp', 'head')
- abd_gains_new: float32 [2, 4096], replicated
- abd_gains_first_new: float32 [2, 4096], replicated
- abd_gains_second_new: float32 [2, 4096], replicated
- aba_new: float32 [64, 768], replicated
- aba_first_new: float32 [64, 768], replicated
- aba_second_new: float32 [64, 768], replicated
- aba_gains_new: float32 [2, 64], replicated
- aba_gains_first_new: float32 [2, 64], replicated
- aba_gains_second_new: float32 [2, 64], replicated
- embed_new: float32 [64, 33, 64], replicated
- embed_first_new: float32 [64, 33, 64], replicated
- embed_second_new: float32 [64, 33, 64], replicated
- output_new: float32 [64, 64, 32], P('head')
- output_first_new: float32 [64, 64, 32], P('head')
- output_second_new: float32 [64, 64, 32], P('head')
All inputs are finite; a program needn't handle non-finite values.
Results may differ from a plain program's by a relative error of at most 0.017.
Values may be sent and summed in bfloat16 or wider, within the bound.
No kernel may reach another device: no remote copies, remote signals or barrier semaphores. Data moves between devices by JAX's collectives and lax.ppermute only.
A program may use at most 640 MiB of HBM per device.

v0:
```python
import jax
import jax.numpy as jnp
from jax import lax
from jax.sharding import PartitionSpec as P

H = 8
AH = 8
STEP = 10
HD = 512
FF = 16384


EPS_NORM = 1e-05
CLIP_LIMIT = 0.01
LEARN_RATE = 0.3
BETA_FIRST = 0.9
BETA_SECOND = 0.999
ADAM_EPSILON = 1e-08
WEIGHT_DECAY = 0.01


def layer_norm(values, gain_row):
    center = jnp.mean(values, axis=-1, keepdims=True)
    centred = values - center
    spread = jnp.mean(centred * centred, axis=-1, keepdims=True)
    return centred * lax.rsqrt(spread + EPS_NORM) * gain_row


def gelu_apply(values):
    return 0.5 * values * (1.0 + lax.erf(values * 0.7071067811865476))


def norm_back(values, gain_row, upstream):
    unused_value, pull_back = jax.vjp(layer_norm, values, gain_row)
    return pull_back(upstream)


def gelu_back(values, upstream):
    unused_value, pull_back = jax.vjp(gelu_apply, values)
    return pull_back(upstream)[0]


def attend_keys(queries, key_rows, value_rows, factor):
    scores = (
        jnp.einsum("...qd,...kd->...qk", queries, key_rows, preferred_element_type=jnp.float32)
        * factor
    )
    highest = jnp.max(scores, axis=-1, keepdims=True)
    weights = jnp.exp(scores - highest)
    totals = jnp.sum(weights, axis=-1, keepdims=True)
    result = jnp.einsum(
        "...qk,...kd->...qd",
        (weights / totals).astype(jnp.bfloat16),
        value_rows,
        preferred_element_type=jnp.float32,
    )
    return (result, highest + jnp.log(totals))


def attend_back(queries, key_rows, value_rows, log_total, result_grad, factor):
    scores = (
        jnp.einsum("...qd,...kd->...qk", queries, key_rows, preferred_element_type=jnp.float32)
        * factor
    )
    softmax_probs = jnp.exp(scores - log_total)
    prob_grad = jnp.einsum(
        "...qd,...kd->...qk", result_grad, value_rows, preferred_element_type=jnp.float32
    )
    score_grad = softmax_probs * (
        prob_grad - jnp.sum(softmax_probs * prob_grad, axis=-1, keepdims=True)
    )
    score_grad = score_grad.astype(jnp.bfloat16)
    query_grad = (
        jnp.einsum("...qk,...kd->...qd", score_grad, key_rows, preferred_element_type=jnp.float32)
        * factor
    )
    key_grad = (
        jnp.einsum("...qk,...qd->...kd", score_grad, queries, preferred_element_type=jnp.float32)
        * factor
    )
    value_grad = jnp.einsum(
        "...qk,...qd->...kd",
        softmax_probs.astype(jnp.bfloat16),
        result_grad,
        preferred_element_type=jnp.float32,
    )
    return (query_grad, key_grad, value_grad)


def head_total(values):
    return lax.psum(values, "head")


def abd_forward(inputs, weights, gain_rows):
    up_end = 4 * HD + FF // H
    normed = layer_norm(inputs, gain_rows[0]).astype(jnp.bfloat16)
    triple = jnp.einsum(
        "td,dhc->htc", normed, weights[:, :, : 3 * HD], preferred_element_type=jnp.float32
    ).astype(jnp.bfloat16)
    queries = triple[..., :HD]
    key_all, value_all = (
        lax.all_gather(triple[..., HD : 2 * HD], "dp", axis=1, tiled=True),
        lax.all_gather(triple[..., 2 * HD :], "dp", axis=1, tiled=True),
    )
    attended, log_total = attend_keys(queries, key_all, value_all, HD ** (-0.5))
    attended = attended.astype(jnp.bfloat16)
    middle = inputs + head_total(
        jnp.einsum(
            "htj,dhj->td",
            attended,
            weights[:, :, 3 * HD : 4 * HD],
            preferred_element_type=jnp.float32,
        )
    )
    second = layer_norm(middle, gain_rows[1]).astype(jnp.bfloat16)
    before = jnp.einsum(
        "td,dhu->htu", second, weights[:, :, 4 * HD : up_end], preferred_element_type=jnp.float32
    )
    hidden = gelu_apply(before).astype(jnp.bfloat16)
    after = middle + head_total(
        jnp.einsum(
            "htu,dhu->td", hidden, weights[:, :, up_end:], preferred_element_type=jnp.float32
        )
    )
    return (
        after,
        (
            inputs,
            normed,
            queries,
            key_all,
            value_all,
            log_total,
            attended,
            middle,
            second,
            before,
            hidden,
        ),
    )


def abd_backward(upstream, stored, weights, gain_rows):
    (
        inputs,
        normed,
        queries,
        key_all,
        value_all,
        log_total,
        attended,
        middle,
        second,
        before,
        hidden,
    ) = stored
    up_end = 4 * HD + FF // H
    down_grad = upstream.astype(jnp.bfloat16)
    hidden_grad = jnp.einsum(
        "td,dhu->htu", down_grad, weights[:, :, up_end:], preferred_element_type=jnp.float32
    )
    before_grad = gelu_back(before, hidden_grad).astype(jnp.bfloat16)
    second_grad = head_total(
        jnp.einsum(
            "htu,dhu->td",
            before_grad,
            weights[:, :, 4 * HD : up_end],
            preferred_element_type=jnp.float32,
        )
    )
    middle_part, gain_two = norm_back(middle, gain_rows[1], second_grad)
    middle_grad = upstream + middle_part
    branch_grad = middle_grad.astype(jnp.bfloat16)
    attended_grad = jnp.einsum(
        "td,dhj->htj",
        branch_grad,
        weights[:, :, 3 * HD : 4 * HD],
        preferred_element_type=jnp.float32,
    ).astype(jnp.bfloat16)
    query_grad, key_grad, value_grad = attend_back(
        queries, key_all, value_all, log_total, attended_grad, HD ** (-0.5)
    )
    key_own, value_own = (
        lax.psum_scatter(
            key_grad.astype(jnp.bfloat16), "dp", scatter_dimension=1, tiled=True
        ).astype(jnp.float32),
        lax.psum_scatter(
            value_grad.astype(jnp.bfloat16), "dp", scatter_dimension=1, tiled=True
        ).astype(jnp.float32),
    )
    triple_grad = jnp.concatenate(
        [
            query_grad.astype(jnp.bfloat16),
            key_own.astype(jnp.bfloat16),
            value_own.astype(jnp.bfloat16),
        ],
        axis=-1,
    )
    normed_grad = head_total(
        jnp.einsum(
            "htc,dhc->td", triple_grad, weights[:, :, : 3 * HD], preferred_element_type=jnp.float32
        )
    )
    input_part, gain_one = norm_back(inputs, gain_rows[0], normed_grad)
    input_grad = middle_grad + input_part
    pieces = [source for source in (normed, branch_grad, second, down_grad)]
    weight_grad = lax.psum_scatter(
        jnp.concatenate(
            [
                jnp.einsum(
                    "tc,htk->chk", pieces[0], triple_grad, preferred_element_type=jnp.float32
                ),
                jnp.einsum("tc,htj->chj", pieces[1], attended, preferred_element_type=jnp.float32),
                jnp.einsum(
                    "tc,htu->chu", pieces[2], before_grad, preferred_element_type=jnp.float32
                ),
                jnp.einsum("tc,htu->chu", pieces[3], hidden, preferred_element_type=jnp.float32),
            ],
            axis=-1,
        ).astype(jnp.bfloat16),
        "dp",
        scatter_dimension=0,
        tiled=True,
    ).astype(jnp.float32)
    return (input_grad, weight_grad, jnp.stack([gain_one, gain_two]))


def aba_forward(row_block, weights, gain_rows):
    embed_width = weights.shape[0]
    row_count = row_block.shape[0]
    attr_count = row_block.shape[1] // embed_width
    size_each = embed_width // AH
    inputs = row_block.reshape(row_count, attr_count, embed_width)
    normed = layer_norm(inputs, gain_rows[0]).astype(jnp.bfloat16)
    projection = weights[:, : 3 * embed_width].reshape(embed_width, 3, AH, size_each)
    triple = jnp.einsum(
        "rfe,eshd->srhfd", normed, projection, preferred_element_type=jnp.float32
    ).astype(jnp.bfloat16)
    attended, log_total = attend_keys(triple[0], triple[1], triple[2], size_each ** (-0.5))
    attended = attended.astype(jnp.bfloat16)
    out_proj = weights[:, 3 * embed_width : 4 * embed_width].reshape(embed_width, AH, size_each)
    middle = inputs + jnp.einsum(
        "rhfd,ohd->rfo", attended, out_proj, preferred_element_type=jnp.float32
    )
    second = layer_norm(middle, gain_rows[1]).astype(jnp.bfloat16)
    before = jnp.einsum(
        "rfe,eu->rfu",
        second,
        weights[:, 4 * embed_width : 8 * embed_width],
        preferred_element_type=jnp.float32,
    )
    hidden = gelu_apply(before).astype(jnp.bfloat16)
    after = middle + jnp.einsum(
        "rfu,ou->rfo", hidden, weights[:, 8 * embed_width :], preferred_element_type=jnp.float32
    )
    return (
        after.reshape(row_count, attr_count * embed_width),
        (inputs, normed, triple, log_total, attended, middle, second, before, hidden),
    )


def aba_backward(upstream, stored, weights, gain_rows):
    inputs, normed, triple, log_total, attended, middle, second, before, hidden = stored
    row_count, attr_count, embed_width = inputs.shape
    size_each = embed_width // AH
    upstream = upstream.reshape(row_count, attr_count, embed_width)
    down_grad = upstream.astype(jnp.bfloat16)
    hidden_grad = jnp.einsum(
        "rfo,ou->rfu", down_grad, weights[:, 8 * embed_width :], preferred_element_type=jnp.float32
    )
    before_grad = gelu_back(before, hidden_grad).astype(jnp.bfloat16)
    second_grad = jnp.einsum(
        "rfu,eu->rfe",
        before_grad,
        weights[:, 4 * embed_width : 8 * embed_width],
        preferred_element_type=jnp.float32,
    )
    middle_part, gain_two = norm_back(middle, gain_rows[1], second_grad)
    middle_grad = upstream + middle_part
    branch_grad = middle_grad.astype(jnp.bfloat16)
    out_proj = weights[:, 3 * embed_width : 4 * embed_width].reshape(embed_width, AH, size_each)
    attended_grad = jnp.einsum(
        "rfo,ohd->rhfd", branch_grad, out_proj, preferred_element_type=jnp.float32
    ).astype(jnp.bfloat16)
    query_grad, key_grad, value_grad = attend_back(
        triple[0], triple[1], triple[2], log_total, attended_grad, size_each ** (-0.5)
    )
    triple_grad = jnp.stack([query_grad, key_grad, value_grad]).astype(jnp.bfloat16)
    projection = weights[:, : 3 * embed_width].reshape(embed_width, 3, AH, size_each)
    normed_grad = jnp.einsum(
        "srhfd,eshd->rfe", triple_grad, projection, preferred_element_type=jnp.float32
    )
    input_part, gain_one = norm_back(inputs, gain_rows[0], normed_grad)
    input_grad = middle_grad + input_part
    weight_grad = jnp.concatenate(
        [
            jnp.einsum(
                "rfe,srhfd->eshd", normed, triple_grad, preferred_element_type=jnp.float32
            ).reshape(embed_width, 3 * embed_width),
            jnp.einsum(
                "rfo,rhfd->ohd", branch_grad, attended, preferred_element_type=jnp.float32
            ).reshape(embed_width, embed_width),
            jnp.einsum("rfe,rfu->eu", second, before_grad, preferred_element_type=jnp.float32),
            jnp.einsum("rfo,rfu->ou", down_grad, hidden, preferred_element_type=jnp.float32),
        ],
        axis=1,
    )
    return (
        input_grad.reshape(row_count, attr_count * embed_width),
        weight_grad,
        jnp.stack([gain_one, gain_two]),
    )


def moments_of(weight, gradient, first, second, clip_factor, decay):
    scaled = gradient * clip_factor
    first_new = BETA_FIRST * first + (1.0 - BETA_FIRST) * scaled
    second_new = BETA_SECOND * second + (1.0 - BETA_SECOND) * scaled * scaled
    update = (
        first_new
        / (1.0 - BETA_FIRST**STEP)
        / (jnp.sqrt(second_new / (1.0 - BETA_SECOND**STEP)) + ADAM_EPSILON)
        + decay * weight
    )
    return (first_new, second_new, update)


def apply_trust(weight, update, weight_sq, update_sq):
    trust_ratio = jnp.sqrt(weight_sq) / (jnp.sqrt(update_sq) + 1e-06)
    return weight - LEARN_RATE * trust_ratio * update


def local_step(weight, gradient, first, second, clip_factor, decay):
    first_new, second_new, update = moments_of(weight, gradient, first, second, clip_factor, decay)
    return (
        apply_trust(weight, update, jnp.sum(weight * weight), jnp.sum(update * update)),
        first_new,
        second_new,
    )


def per_device(
    cell_ids,
    cell_mask,
    labels,
    abd_weights,
    abd_first,
    abd_second,
    abd_gains,
    abd_gains_first,
    abd_gains_second,
    aba_weights,
    aba_first,
    aba_second,
    aba_gains,
    aba_gains_first,
    aba_gains_second,
    embed_table,
    embed_first,
    embed_second,
    output_table,
    output_first,
    output_second,
):
    tokens, attr_count = cell_ids.shape
    embed_width = embed_table.shape[2]
    classes = output_table.shape[2]
    model_width = attr_count * embed_width
    head_count = lax.axis_size("head")
    head_index = lax.axis_index("head")
    local_attrs = attr_count // head_count
    attr_start = head_index * local_attrs
    local_rows = tokens // head_count
    first_device = (lax.axis_index("dp") == 0).astype(jnp.float32)
    picked = jnp.where(cell_mask == 1, classes, cell_ids)
    picked_hot = (
        picked[:, :, None] == jnp.arange(classes + 1, dtype=jnp.int32)[None, None, :]
    ).astype(jnp.float32)
    embedded = jnp.einsum(
        "tfk,fke->tfe", picked_hot, embed_table, precision=lax.Precision.HIGHEST
    ).reshape(tokens, model_width)
    mask_own = lax.dynamic_slice_in_dim(cell_mask, attr_start, local_attrs, 1).astype(jnp.float32)
    label_hot = (labels[:, :, None] == jnp.arange(classes, dtype=jnp.int32)[None, None, :]).astype(
        jnp.float32
    )
    counts_own = jnp.einsum("tf,tfc->fc", mask_own, label_hot, precision=lax.Precision.HIGHEST)
    counts_pad = lax.dynamic_update_slice(
        jnp.zeros((attr_count, classes), jnp.float32), counts_own, (attr_start, 0)
    )
    counts = lax.psum(counts_pad, ("dp", "head"))
    class_weight = lax.rsqrt(1.0 + counts)
    weight_total = jnp.sum(counts * class_weight)
    weight_own = lax.dynamic_slice_in_dim(class_weight, attr_start, local_attrs, 0)
    abd_full = lax.all_gather(abd_weights.astype(jnp.bfloat16), "dp", axis=0, tiled=True)
    after_abd, abd_stored = abd_forward(embedded, abd_full, abd_gains)
    own_rows = lax.dynamic_slice_in_dim(after_abd, head_index * local_rows, local_rows, 0)
    aba_low = aba_weights.astype(jnp.bfloat16)
    after_aba, aba_stored = aba_forward(own_rows, aba_low, aba_gains)
    columns = lax.all_to_all(
        after_aba.astype(jnp.bfloat16), "head", split_axis=1, concat_axis=0, tiled=True
    ).astype(after_aba.dtype)
    final_low = columns.reshape(tokens, local_attrs, embed_width).astype(jnp.bfloat16)
    output_low = output_table.astype(jnp.bfloat16)
    logits = jnp.einsum("tfe,fec->tfc", final_low, output_low, preferred_element_type=jnp.float32)
    highest = jnp.max(logits, axis=-1, keepdims=True)
    shifted = jnp.exp(logits - highest)
    totals = jnp.sum(shifted, axis=-1, keepdims=True)
    log_total = (highest + jnp.log(totals))[:, :, 0]
    cell_weight = mask_own * jnp.sum(label_hot * weight_own[None], axis=-1)
    loss_local = jnp.sum(cell_weight * (log_total - jnp.sum(label_hot * logits, axis=-1)))
    logit_grad = ((cell_weight / weight_total)[:, :, None] * (shifted / totals - label_hot)).astype(
        jnp.bfloat16
    )
    final_grad = jnp.einsum(
        "tfc,fec->tfe", logit_grad, output_low, preferred_element_type=jnp.float32
    ).reshape(tokens, local_attrs * embed_width)
    output_grad = jnp.einsum(
        "tfe,tfc->fec", final_low, logit_grad, preferred_element_type=jnp.float32
    )
    back_rows = lax.all_to_all(
        final_grad.astype(jnp.bfloat16), "head", split_axis=0, concat_axis=1, tiled=True
    ).astype(final_grad.dtype)
    rows_grad, aba_grad, aba_gains_grad = aba_backward(back_rows, aba_stored, aba_low, aba_gains)
    after_grad = lax.all_gather(rows_grad.astype(jnp.bfloat16), "head", axis=0, tiled=True).astype(
        rows_grad.dtype
    )
    back_weights = lax.all_gather(abd_weights.astype(jnp.bfloat16), "dp", axis=0, tiled=True)
    embedded_grad, abd_grad, abd_gains_grad = abd_backward(
        after_grad, abd_stored, back_weights, abd_gains
    )
    own_columns = (jnp.arange(model_width) // (model_width // head_count) == head_index).astype(
        jnp.float32
    )
    abd_gains_grad = abd_gains_grad * own_columns[None, :]
    embedded_own = lax.dynamic_slice_in_dim(
        embedded_grad.reshape(tokens, attr_count, embed_width), attr_start, local_attrs, 1
    )
    picked_own = lax.dynamic_slice_in_dim(picked_hot, attr_start, local_attrs, 1)
    embed_own = jnp.einsum(
        "tfk,tfe->fke", picked_own, embedded_own, precision=lax.Precision.HIGHEST
    )
    embed_pad = lax.dynamic_update_slice(
        jnp.zeros(embed_table.shape, jnp.float32), embed_own, (attr_start, 0, 0)
    )
    output_pad = lax.dynamic_update_slice(
        jnp.zeros((attr_count, embed_width, classes), jnp.float32), output_grad, (attr_start, 0, 0)
    )
    abd_gains_grad, aba_grad, aba_gains_grad, embed_grad, output_full = lax.psum(
        (abd_gains_grad, aba_grad, aba_gains_grad, embed_pad, output_pad), ("dp", "head")
    )
    output_grad = lax.dynamic_slice_in_dim(output_full, attr_start, local_attrs, 0)
    abd_weight_sq = jnp.sum(abd_weights * abd_weights)
    output_weight_sq = first_device * jnp.sum(output_table * output_table)
    squares = [
        jnp.sum(abd_grad * abd_grad),
        first_device * jnp.sum(output_grad * output_grad),
        loss_local,
    ]
    summed = lax.psum(jnp.stack(squares), ("dp", "head"))
    replicated_sq = (
        jnp.sum(abd_gains_grad * abd_gains_grad)
        + jnp.sum(aba_grad * aba_grad)
        + jnp.sum(aba_gains_grad * aba_gains_grad)
        + jnp.sum(embed_grad * embed_grad)
    )
    grad_norm = jnp.sqrt(summed[0] + summed[1] + replicated_sq)
    loss_sum = summed[2]
    clip_factor = jnp.minimum(1.0, CLIP_LIMIT / (grad_norm + 1e-06))
    abd_first_new, abd_second_new, abd_update = moments_of(
        abd_weights, abd_grad, abd_first, abd_second, clip_factor, WEIGHT_DECAY
    )
    output_first_new, output_second_new, output_update = moments_of(
        output_table, output_grad, output_first, output_second, clip_factor, WEIGHT_DECAY
    )
    update_sq = [
        jnp.sum(abd_update * abd_update),
        first_device * jnp.sum(output_update * output_update),
    ]
    update_sq = update_sq + [abd_weight_sq, output_weight_sq]
    trust_sums = lax.psum(jnp.stack(update_sq), ("dp", "head"))
    weight_sums = trust_sums[2:4]
    abd_new = apply_trust(abd_weights, abd_update, weight_sums[0], trust_sums[0])
    output_new = apply_trust(output_table, output_update, weight_sums[1], trust_sums[1])
    gain_triple = local_step(
        abd_gains, abd_gains_grad, abd_gains_first, abd_gains_second, clip_factor, 0.0
    )
    aba_triple = local_step(aba_weights, aba_grad, aba_first, aba_second, clip_factor, WEIGHT_DECAY)
    aba_gain_triple = local_step(
        aba_gains, aba_gains_grad, aba_gains_first, aba_gains_second, clip_factor, 0.0
    )
    embed_triple = local_step(
        embed_table, embed_grad, embed_first, embed_second, clip_factor, WEIGHT_DECAY
    )
    return (
        loss_sum,
        weight_total,
        grad_norm,
        abd_new,
        abd_first_new,
        abd_second_new,
        gain_triple[0],
        gain_triple[1],
        gain_triple[2],
        aba_triple[0],
        aba_triple[1],
        aba_triple[2],
        aba_gain_triple[0],
        aba_gain_triple[1],
        aba_gain_triple[2],
        embed_triple[0],
        embed_triple[1],
        embed_triple[2],
        output_new,
        output_first_new,
        output_second_new,
    )


def solution(mesh):
    in_specs = (
        P("dp", None),
        P("dp", None),
        P("dp", "head"),
        P("dp", "head", None),
        P("dp", "head", None),
        P("dp", "head", None),
        P(),
        P(),
        P(),
        P(),
        P(),
        P(),
        P(),
        P(),
        P(),
        P(),
        P(),
        P(),
        P("head", None, None),
        P("head", None, None),
        P("head", None, None),
    )
    out_specs = (
        P(),
        P(),
        P(),
        P("dp", "head", None),
        P("dp", "head", None),
        P("dp", "head", None),
        P(),
        P(),
        P(),
        P(),
        P(),
        P(),
        P(),
        P(),
        P(),
        P(),
        P(),
        P(),
        P("head", None, None),
        P("head", None, None),
        P("head", None, None),
    )
    return jax.shard_map(
        per_device, mesh=mesh, in_specs=in_specs, out_specs=out_specs, check_vma=False
    )
```

profile of v0, /device:TPU:0, one launch (start us, length us, event | category | flops | bytes accessed | tf_op | source)
XLA Modules:
  0.0 4626.6 jit_solution(7331027865321534527)
XLA Ops:
  7.2 24.1 copy.212
  32.6 3.6 fusion.161
  38.2 3.0 fusion.46
  41.8 1888.5 %all-gather.5.cloned.1.call-done = bf16[4096,2,6144]{2,0,1:T(8,128)(2,1)} async-done(((bf16[512,2,6144]{2,0,1:T(8,128)(2,1)}), bf16[4096,2,6144]{2,0,1:T(8,128)(2,1)}) %all-gather.5.cloned.1.call-update) | async-done | bytes 100663312 | tf_op jit(solution)/shard_map/all_gather | solution.py:394
  1930.3 10.2 fusion.42
  1943.1 48.6 %all-gather.7.cloned.1.call-done = bf16[2,1024,512]{2,1,0:T(8,128)(2,1)} async-done(((bf16[2,128,512]{2,1,0:T(8,128)(2,1)}), bf16[2,1024,512]{2,1,0:T(8,128)(2,1)}) %all-gather.7.cloned.1.call-update) | async-done | bytes 2097168 | tf_op jit(solution)/shard_map/all_gather | solution.py:102
  1991.7 2.6 fusion.162
  1994.6 47.6 %all-gather.9.cloned.1.call-done = bf16[2,1024,512]{2,1,0:T(8,128)(2,1)} async-done(((bf16[2,128,512]{2,1,0:T(8,128)(2,1)}), bf16[2,1024,512]{2,1,0:T(8,128)(2,1)}) %all-gather.9.cloned.1.call-update) | async-done | bytes 2097168 | tf_op jit(solution)/shard_map/all_gather | solution.py:103
  2045.1 7.5 fusion.22
  2053.1 49.6 %all-reduce.8.cloned.1.call-done = f32[128,4096]{1,0:T(8,128)} async-done(((f32[128,4096]{1,0:T(8,128)}), f32[128,4096]{1,0:T(8,128)}) %all-reduce.8.cloned.1.call-update) | async-done | bytes 2097168 | tf_op jit(solution)/shard_map/psum | solution.py:91
  2106.4 13.6 fusion.7
  2121.4 16.7 fusion.31
  2140.4 40.9 psum.84
  2181.2 9.6 all-reduce.10.cloned.1.call-done
  2200.4 2.4 mul.793
  2209.8 2.4 fusion.16
  2225.8 4.2 all-to-all-start
  2232.0 4.1 all-to-all-done
  2238.3 2.1 copy.145
  2246.8 2.2 copy.146
  2251.1 4.0 all-to-all-start.1
  2255.3 6.0 all-to-all-done.1
  2265.6 3.0 add_convert_fusion.1
  2269.6 2.2 multiply_reduce_fusion.12
  2273.4 3.1 fusion.63
  2276.5 2.6 multiply_reduce_fusion.2
  2279.1 2.9 multiply_convert_fusion
  2282.0 2.3 fusion.61
  2291.1 2.2 convert_element_type.195
  2293.4 16.8 all-gather.11.cloned.1.call-done
  2310.2 15.3 add_convert_fusion
  2325.5 17.3 fusion.28
  2343.5 50.9 %all-reduce.12.cloned.1.call-done = f32[128,4096]{1,0:T(8,128)} async-done(((f32[128,4096]{1,0:T(8,128)}), f32[128,4096]{1,0:T(8,128)}) %all-reduce.12.cloned.1.call-update) | async-done | bytes 2097168 | tf_op jit(solution)/shard_map/psum | solution.py:91
  2394.4 3.1 multiply_reduce_fusion.5
  2399.8 5.0 fusion.72
  2405.6 2.2 convolution_convert_fusion.4
  2420.3 3.2 multiply_convert_fusion.1
  2423.8 15.7 convolution_convert_fusion
  2439.5 14.1 convolution_convert_fusion.1
  2453.5 2.2 fusion.70
  2455.7 5.8 convolution_convert_fusion.3
  2461.5 14.2 reduce-scatter.6.cloned.1.call-done
  2475.7 70.6 %reduce-scatter.4.cloned.1.call-done = bf16[2,128,512]{2,1,0:T(8,128)(2,1)} async-done(((bf16[2,1024,512]{2,1,0:T(8,128)(2,1)}), bf16[2,128,512]{2,1,0:T(8,128)(2,1)}) %reduce-scatter.4.cloned.1.call-update) | async-done | bytes 262160 | tf_op jit(solution)/shard_map/reduce_scatter | solution.py:184
  2546.4 13.9 fusion.25
  2561.9 13.5 convolution_convert_fusion.2
  2575.4 35.6 all-reduce.14.cloned.1.call-done
  2611.0 2.4 multiply_reduce_fusion.4
  2620.6 67.7 %pad_maximum_fusion = bf16[4096,2,6144]{0,2,1:T(8,128)(2,1)} fusion(bf16[4096,2,2048]{0,2,1:T(8,128)(2,1)} %convolution_convert_fusion, bf16[4096,2,2048]{0,2,1:T(8,128)(2,1)} %convolution_convert_fusion.1, bf16[4096,2,512]{0,2,1:T(8,128)(2,1)} %convolution_convert_fusion.3, bf16[4096,2,1536]{0,2,1:T(8,128)(2,1)} %convolution_convert_fusion.2), kind=kLoop, calls=%fused_computation | loop fusion | flops 402653184 | bytes 201326592 | tf_op jit(solution)/shard_map/concatenate | solution.py:208
  2688.3 36.9 copy.172
  2725.2 36.9 copy.169
  2762.1 37.1 copy.170
  2799.3 27.9 multiply_reduce_fusion
  2831.7 1465.7 %reduce-scatter.8.cloned.1.call-done = bf16[512,2,6144]{0,2,1:T(8,128)(2,1)} async-done(((bf16[4096,2,6144]{0,2,1:T(8,128)(2,1)}), bf16[512,2,6144]{0,2,1:T(8,128)(2,1)}) %reduce-scatter.8.cloned.1.call-update) | async-done | bytes 12582928 | tf_op jit(solution)/shard_map/reduce_scatter | solution.py:207
  4297.4 11.6 fusion.10
  4311.0 39.7 all-reduce
  4356.6 2.6 multiply_reduce_fusion.20
  4360.4 45.6 multiply_reduce_fusion.1
  4407.4 40.0 psum.95
  4449.4 37.3 copy.174
  4486.7 37.3 copy.175
  4524.0 33.7 multiply_subtract_fusion
  4557.8 37.4 copy.173
  4603.6 4.1 multiply_reduce_fusion.9
  4614.5 2.8 multiply_subtract_fusion.1
  (421 shorter events, 116.7 us)
Async XLA Ops:
  7.2 1923.1 %all-gather.5.cloned.1.call-start = ((), (), s32[]{:S(2)}) async-start(), calls=%async_computation.5 | async-start | bytes 113246208 | tf_op jit(solution)/shard_map/all_gather | solution.py:394
  31.3 1960.3 %all-gather.7.cloned.1.call-start = ((), (), s32[]{:S(2)}) async-start(), calls=%async_computation.6 | async-start | bytes 2359296 | tf_op jit(solution)/shard_map/all_gather | solution.py:102
  38.2 2064.6 %copy-start.1 = (f32[128,4096]{1,0:T(8,128)}, f32[128,4096]{1,0:T(8,128)S(1)}, u32[]{:S(2)}) copy-start(f32[128,4096]{1,0:T(8,128)S(1)} %copy.131) | copy-start | bytes 6291460
  38.2 1902.3 %copy-start.101 = (f32[128]{0:T(128)}, f32[128]{0:T(128)S(1)}, u32[]{:S(2)}) copy-start(f32[128]{0:T(128)S(1)} %broadcast_multiply_fusion.3) | copy-start | bytes 1540
  41.8 1898.8 %copy-start.113 = (f32[128]{0:T(128)}, f32[128]{0:T(128)S(1)}, u32[]{:S(2)}) copy-start(f32[128]{0:T(128)S(1)} %fusion.132) | copy-start | bytes 1540
  41.8 1898.8 %copy-start.66 = (f32[1,4096]{1,0:T(1,128)}, f32[1,4096]{1,0:T(1,128)S(1)}, u32[]{:S(2)}) copy-start(f32[1,4096]{1,0:T(1,128)S(1)} %get-tuple-element.138) | copy-start | bytes 49156
  41.8 2064.6 %copy-start.68 = (f32[1,4096]{1,0:T(1,128)}, f32[1,4096]{1,0:T(1,128)S(1)}, u32[]{:S(2)}) copy-start(f32[1,4096]{1,0:T(1,128)S(1)} %get-tuple-element.137) | copy-start | bytes 49156
  1942.3 100.0 %all-gather.9.cloned.1.call-start = ((), (), s32[]{:S(2)}) async-start(), calls=%async_computation.7 | async-start | bytes 2359296 | tf_op jit(solution)/shard_map/all_gather | solution.py:103
  1943.0 159.7 %all-reduce.8.cloned.1.call-start = ((), (), s32[]{:S(2)}) async-start(), calls=%async_computation.8 | async-start | bytes 4194304 | tf_op jit(solution)/shard_map/psum | solution.py:91
  1994.3 50.1 %copy-start.5 = (f32[2,128,1024]{2,1,0:T(8,128)}, f32[2,128,1024]{2,1,0:T(8,128)S(1)}, u32[]{:S(2)}) copy-start(f32[2,128,1024]{2,1,0:T(8,128)S(1)} %get-tuple-element.154) | copy-start | bytes 3145732
  1994.3 50.1 %copy-start.109 = (f32[2,128]{1,0:T(2,128)}, f32[2,128]{1,0:T(2,128)S(1)}, u32[]{:S(2)}) copy-start(f32[2,128]{1,0:T(2,128)S(1)} %get-tuple-element.153) | copy-start | bytes 3076
  1994.6 49.8 %copy-start.125 = (f32[2,128]{1,0:T(2,128)}, f32[2,128]{1,0:T(2,128)S(1)}, u32[]{:S(2)}) copy-start(f32[2,128]{1,0:T(2,128)S(1)} %fusion.87) | copy-start | bytes 3076
  2052.7 138.2 %all-reduce.10.cloned.1.call-start = ((), (), s32[]{:S(2)}) async-start(), calls=%async_computation.9 | async-start | bytes 4194304 | tf_op jit(solution)/shard_map/psum | solution.py:91
  2104.7 15.3 copy-start.103
  2106.4 13.6 copy-start.135
  2106.4 13.6 copy-start.115
  2121.4 16.7 copy-start.46
  2138.1 52.8 %copy-start.4 = (f32[128,4096]{1,0:T(8,128)S(1)}, f32[128,4096]{1,0:T(8,128)}, u32[]{:S(2)}) copy-start(f32[128,4096]{1,0:T(8,128)} %copy-done.3) | copy-start | bytes 6291460
  2138.1 79.4 %copy-start.57 = (bf16[64,768]{1,0:T(8,128)(2,1)}, bf16[64,768]{1,0:T(8,128)(2,1)S(1)}, u32[]{:S(2)}) copy-start(bf16[64,768]{1,0:T(8,128)(2,1)S(1)} %convert_element_type.172) | copy-start | bytes 294916
  2138.8 68.7 %copy-start.82 = (bf16[64,192]{0,1:T(8,128)(2,1)}, bf16[64,192]{0,1:T(8,128)(2,1)S(1)}, u32[]{:S(2)}) copy-start(bf16[64,192]{0,1:T(8,128)(2,1)S(1)} %copy.137) | copy-start | bytes 73732
  2140.0 74.9 %copy-start.88 = (bf16[64,64]{0,1:T(8,128)(2,1)}, bf16[64,64]{0,1:T(8,128)(2,1)S(1)}, u32[]{:S(2)}) copy-start(bf16[64,64]{0,1:T(8,128)(2,1)S(1)} %copy.139) | copy-start | bytes 24580
  2195.7 7.1 copy-start.8
  2219.9 20.5 copy-start.37
  2225.8 10.3 all-to-all-start
  2246.8 8.4 copy-start.59
  2251.1 10.1 all-to-all-start.1
  2255.2 55.0 %all-gather.11.cloned.1.call-start = ((), (), s32[]{:S(2)}) async-start(), calls=%async_computation.10 | async-start | bytes 1310720 | tf_op jit(solution)/shard_map/all_gather | solution.py:424
  2265.6 7.7 slice-start
  2293.3 101.1 %all-reduce.12.cloned.1.call-start = ((), (), s32[]{:S(2)}) async-start(), calls=%async_computation.11 | async-start | bytes 4194304 | tf_op jit(solution)/shard_map/psum | solution.py:91
  2342.8 51.6 %copy-start.69 = (f32[1,4096]{1,0:T(1,128)S(1)}, f32[1,4096]{1,0:T(1,128)}, u32[]{:S(2)}) copy-start(f32[1,4096]{1,0:T(1,128)} %copy-done.68) | copy-start | bytes 49156
  2342.8 51.6 %copy-start.104 = (f32[128]{0:T(128)S(1)}, f32[128]{0:T(128)}, u32[]{:S(2)}) copy-start(f32[128]{0:T(128)} %copy-done.103) | copy-start | bytes 1540
  2342.9 51.6 %copy-start.116 = (f32[128]{0:T(128)S(1)}, f32[128]{0:T(128)}, u32[]{:S(2)}) copy-start(f32[128]{0:T(128)} %copy-done.115) | copy-start | bytes 1540
  2342.9 132.8 %reduce-scatter.6.cloned.1.call-start = ((), (), s32[]{:S(2)}) async-start(), calls=%async_computation.13 | async-start | bytes 2359296 | tf_op jit(solution)/shard_map/reduce_scatter | solution.py:187
  2343.5 61.3 %copy-start.99 = (f32[2,128]{1,0:T(2,128)}, f32[2,128]{1,0:T(2,128)S(1)}, u32[]{:S(2)}) copy-start(f32[2,128]{1,0:T(2,128)S(1)} %log_add_fusion.1) | copy-start | bytes 3076
  2343.5 54.0 %copy-start.136 = (f32[128]{0:T(128)S(1)}, f32[128]{0:T(128)}, u32[]{:S(2)}) copy-start(f32[128]{0:T(128)} %copy-done.135) | copy-start | bytes 1540
  2407.8 138.6 %reduce-scatter.4.cloned.1.call-start = ((), (), s32[]{:S(2)}) async-start(), calls=%async_computation.12 | async-start | bytes 2359296 | tf_op jit(solution)/shard_map/reduce_scatter | solution.py:184
  2423.5 15.9 copy-start.105
  2423.5 15.9 copy-start.117
  2423.5 187.5 %all-reduce.14.cloned.1.call-start = ((), (), s32[]{:S(2)}) async-start(), calls=%async_computation.15 | async-start | bytes 4194304 | tf_op jit(solution)/shard_map/psum | solution.py:91
  2423.7 15.7 copy-start.49
  2439.4 14.1 copy-start.29
  2546.4 14.2 copy-start.67
  2560.3 266.9 %all-reduce.16.cloned.1.call-start = ((), (), s32[]{:S(2)}) async-start(), calls=%async_computation.16 | async-start | bytes 4653056 | tf_op jit(solution)/shard_map/psum | solution.py:448
  2575.4 38.1 copy-start.134
  2620.3 1677.1 %reduce-scatter.8.cloned.1.call-start = ((), (), s32[]{:S(2)}) async-start(), calls=%async_computation.14 | async-start | bytes 113246208 | tf_op jit(solution)/shard_map/reduce_scatter | solution.py:207
  2799.2 27.9 copy-start.129
  2799.2 27.9 copy-start.130
  2799.2 27.9 copy-start.93
  2831.7 1478.7 %copy-start.56 = (f32[64,768]{1,0:T(8,128)S(1)}, f32[64,768]{1,0:T(8,128)}, u32[]{:S(2)}) copy-start(f32[64,768]{1,0:T(8,128)} %get-tuple-element.105) | copy-start | bytes 589828
  2831.7 1524.9 %copy-start.38 = (f32[16,64,32]{1,2,0:T(8,128)S(1)}, f32[16,64,32]{1,2,0:T(8,128)}, u32[]{:S(2)}) copy-start(f32[16,64,32]{1,2,0:T(8,128)} %param.39) | copy-start | bytes 393220
  2831.7 1524.9 %copy-start.78 = (f32[16,64,32]{1,2,0:T(8,128)S(1)}, f32[16,64,32]{1,2,0:T(8,128)}, u32[]{:S(2)}) copy-start(f32[16,64,32]{1,2,0:T(8,128)} %param.40) | copy-start | bytes 393220
  2831.7 1524.9 %copy-start.79 = (f32[16,64,32]{1,2,0:T(8,128)S(1)}, f32[16,64,32]{1,2,0:T(8,128)}, u32[]{:S(2)}) copy-start(f32[16,64,32]{1,2,0:T(8,128)} %param.41) | copy-start | bytes 393220
  4557.7 37.5 copy-start.73
  4557.7 37.5 copy-start.95
  4557.7 37.5 copy-start.96
  4557.7 40.3 copy-start.47
  4557.7 40.3 copy-start.80
  4557.7 40.3 copy-start.81
  4557.8 43.2 copy-start.112
  4557.8 43.2 copy-start.131
  4557.8 43.2 copy-start.132
  4557.8 45.8 copy-start.31
  4595.2 8.4 copy-start.17
  4607.7 9.6 copy-start.32
  (89 other events, 179.4 us)
Sparse Core Ops, SparseCore 0:
  31.5 1898.7 all-gather.4
  1942.4 49.2 all-gather.6
  1994.5 47.7 all-gather.8
  2052.8 49.8 all-reduce.7
  2138.2 52.5 all-reduce.9
  2293.4 16.7 all-gather.10
  2343.0 51.3 all-reduce.11
  2407.9 67.7 reduce-scatter.5
  2479.7 66.6 reduce-scatter.3
  2560.5 50.4 all-reduce.13
  2620.4 136.2 all-reduce.15
  2760.9 1536.3 reduce-scatter.7
where the time goes:
time: 4640 us; the launch traced here: 4630 us
  waiting for transfers between devices  3710 us (80%)
  local copies, waits for them, and re-layouts  311 us (7%)
  other arithmetic  248 us (5%)
  matrix products  197 us (4%)
  blocking collectives  121 us (3%)
    all_gather x1, waiting for transfers between devices, per_device(): lax.all_gather(abd_weights.astype(jnp.bfloat16), 'dp', axis=0, tiled=True)  1890 us
    reduce_scatter x1, waiting for transfers between devices, abd_backward(): lax.psum_scatter(jnp.concatenate([jnp.einsum('tc,htk->chk', pieces[0], tr...  1470 us
    unnamed x285, local copies, waits for them, and re-layouts  268 us
    psum x4, waiting for transfers between devices, head_total(): return lax.psum(values, 'head')  146 us
  transfers between devices with their start and end apart: 14, of which 13 were waited for; matrix products, arithmetic and copies ran while one was open for 6% of the time, Pallas kernels for 0%

commit v1 on v0

v1 whole, which is shorter than its diff:
```python
import jax
import jax.experimental.pallas as pl
import jax.experimental.pallas.tpu as pltpu
import jax.numpy as jnp
from jax import lax
from jax.sharding import Mesh
from jax.sharding import PartitionSpec as P

H = 8
AH = 8
STEP = 10
HD = 512
FF = 16384


EPS_NORM = 1e-05
CLIP_LIMIT = 0.01
LEARN_RATE = 0.3
BETA_FIRST = 0.9
BETA_SECOND = 0.999
ADAM_EPSILON = 1e-08
WEIGHT_DECAY = 0.01


def layer_norm(values, gain_row):
    center = jnp.mean(values, axis=-1, keepdims=True)
    centred = values - center
    spread = jnp.mean(centred * centred, axis=-1, keepdims=True)
    return centred * lax.rsqrt(spread + EPS_NORM) * gain_row


def gelu_apply(values):
    return 0.5 * values * (1.0 + lax.erf(values * 0.7071067811865476))


def norm_back(values, gain_row, upstream):
    unused_value, pull_back = jax.vjp(layer_norm, values, gain_row)
    return pull_back(upstream)


def gelu_back(values, upstream):
    unused_value, pull_back = jax.vjp(gelu_apply, values)
    return pull_back(upstream)[0]


def attend_keys(queries, key_rows, value_rows, factor):
    scores = (
        jnp.einsum("...qd,...kd->...qk", queries, key_rows, preferred_element_type=jnp.float32)
        * factor
    )
    highest = jnp.max(scores, axis=-1, keepdims=True)
    weights = jnp.exp(scores - highest)
    totals = jnp.sum(weights, axis=-1, keepdims=True)
    result = jnp.einsum(
        "...qk,...kd->...qd",
        (weights / totals).astype(jnp.bfloat16),
        value_rows,
        preferred_element_type=jnp.float32,
    )
    return (result, highest + jnp.log(totals))


def attend_back(queries, key_rows, value_rows, log_total, result_grad, factor):
    scores = (
        jnp.einsum("...qd,...kd->...qk", queries, key_rows, preferred_element_type=jnp.float32)
        * factor
    )
    softmax_probs = jnp.exp(scores - log_total)
    prob_grad = jnp.einsum(
        "...qd,...kd->...qk", result_grad, value_rows, preferred_element_type=jnp.float32
    )
    score_grad = softmax_probs * (
        prob_grad - jnp.sum(softmax_probs * prob_grad, axis=-1, keepdims=True)
    )
    score_grad = score_grad.astype(jnp.bfloat16)
    query_grad = (
        jnp.einsum("...qk,...kd->...qd", score_grad, key_rows, preferred_element_type=jnp.float32)
        * factor
    )
    key_grad = (
        jnp.einsum("...qk,...qd->...kd", score_grad, queries, preferred_element_type=jnp.float32)
        * factor
    )
    value_grad = jnp.einsum(
        "...qk,...qd->...kd",
        softmax_probs.astype(jnp.bfloat16),
        result_grad,
        preferred_element_type=jnp.float32,
    )
    return (query_grad, key_grad, value_grad)


def aba_forward(row_block, weights, gain_rows):
    embed_width = weights.shape[0]
    row_count = row_block.shape[0]
    attr_count = row_block.shape[1] // embed_width
    size_each = embed_width // AH
    inputs = row_block.reshape(row_count, attr_count, embed_width)
    normed = layer_norm(inputs, gain_rows[0]).astype(jnp.bfloat16)
    projection = weights[:, : 3 * embed_width].reshape(embed_width, 3, AH, size_each)
    triple = jnp.einsum(
        "rfe,eshd->srhfd", normed, projection, preferred_element_type=jnp.float32
    ).astype(jnp.bfloat16)
    attended, log_total = attend_keys(triple[0], triple[1], triple[2], size_each ** (-0.5))
    attended = attended.astype(jnp.bfloat16)
    out_proj = weights[:, 3 * embed_width : 4 * embed_width].reshape(embed_width, AH, size_each)
    middle = inputs + jnp.einsum(
        "rhfd,ohd->rfo", attended, out_proj, preferred_element_type=jnp.float32
    )
    second = layer_norm(middle, gain_rows[1]).astype(jnp.bfloat16)
    before = jnp.einsum(
        "rfe,eu->rfu",
        second,
        weights[:, 4 * embed_width : 8 * embed_width],
        preferred_element_type=jnp.float32,
    )
    hidden = gelu_apply(before).astype(jnp.bfloat16)
    after = middle + jnp.einsum(
        "rfu,ou->rfo", hidden, weights[:, 8 * embed_width :], preferred_element_type=jnp.float32
    )
    return (
        after.reshape(row_count, attr_count * embed_width),
        (inputs, normed, triple, log_total, attended, middle, second, before, hidden),
    )


def aba_backward(upstream, stored, weights, gain_rows):
    inputs, normed, triple, log_total, attended, middle, second, before, hidden = stored
    row_count, attr_count, embed_width = inputs.shape
    size_each = embed_width // AH
    upstream = upstream.reshape(row_count, attr_count, embed_width)
    down_grad = upstream.astype(jnp.bfloat16)
    hidden_grad = jnp.einsum(
        "rfo,ou->rfu", down_grad, weights[:, 8 * embed_width :], preferred_element_type=jnp.float32
    )
    before_grad = gelu_back(before, hidden_grad).astype(jnp.bfloat16)
    second_grad = jnp.einsum(
        "rfu,eu->rfe",
        before_grad,
        weights[:, 4 * embed_width : 8 * embed_width],
        preferred_element_type=jnp.float32,
    )
    middle_part, gain_two = norm_back(middle, gain_rows[1], second_grad)
    middle_grad = upstream + middle_part
    branch_grad = middle_grad.astype(jnp.bfloat16)
    out_proj = weights[:, 3 * embed_width : 4 * embed_width].reshape(embed_width, AH, size_each)
    attended_grad = jnp.einsum(
        "rfo,ohd->rhfd", branch_grad, out_proj, preferred_element_type=jnp.float32
    ).astype(jnp.bfloat16)
    query_grad, key_grad, value_grad = attend_back(
        triple[0], triple[1], triple[2], log_total, attended_grad, size_each ** (-0.5)
    )
    triple_grad = jnp.stack([query_grad, key_grad, value_grad]).astype(jnp.bfloat16)
    projection = weights[:, : 3 * embed_width].reshape(embed_width, 3, AH, size_each)
    normed_grad = jnp.einsum(
        "srhfd,eshd->rfe", triple_grad, projection, preferred_element_type=jnp.float32
    )
    input_part, gain_one = norm_back(inputs, gain_rows[0], normed_grad)
    input_grad = middle_grad + input_part
    weight_grad = jnp.concatenate(
        [
            jnp.einsum(
                "rfe,srhfd->eshd", normed, triple_grad, preferred_element_type=jnp.float32
            ).reshape(embed_width, 3 * embed_width),
            jnp.einsum(
                "rfo,rhfd->ohd", branch_grad, attended, preferred_element_type=jnp.float32
            ).reshape(embed_width, embed_width),
            jnp.einsum("rfe,rfu->eu", second, before_grad, preferred_element_type=jnp.float32),
            jnp.einsum("rfo,rfu->ou", down_grad, hidden, preferred_element_type=jnp.float32),
        ],
        axis=1,
    )
    return (
        input_grad.reshape(row_count, attr_count * embed_width),
        weight_grad,
        jnp.stack([gain_one, gain_two]),
    )


def moments_of(weight, gradient, first, second, clip_factor, decay):
    scaled = gradient * clip_factor
    first_new = BETA_FIRST * first + (1.0 - BETA_FIRST) * scaled
    second_new = BETA_SECOND * second + (1.0 - BETA_SECOND) * scaled * scaled
    update = (
        first_new
        / (1.0 - BETA_FIRST**STEP)
        / (jnp.sqrt(second_new / (1.0 - BETA_SECOND**STEP)) + ADAM_EPSILON)
        + decay * weight
    )
    return (first_new, second_new, update)


def apply_trust(weight, update, weight_sq, update_sq):
    trust_ratio = jnp.sqrt(weight_sq) / (jnp.sqrt(update_sq) + 1e-06)
    return weight - LEARN_RATE * trust_ratio * update


def local_step(weight, gradient, first, second, clip_factor, decay):
    first_new, second_new, update = moments_of(weight, gradient, first, second, clip_factor, decay)
    return (
        apply_trust(weight, update, jnp.sum(weight * weight), jnp.sum(update * update)),
        first_new,
        second_new,
    )


LOW = jnp.bfloat16
WIDE = jnp.float32
GROUP = ("x", "h")
MEMBERS = 8
FIRST_SCALE = 1.0 / (1.0 - BETA_FIRST**STEP)
SECOND_SCALE = 1.0 / (1.0 - BETA_SECOND**STEP)


def dot(left, right, left_dim=1, right_dim=0):
    return lax.dot_general(
        left, right, (((left_dim,), (right_dim,)), ((), ())), preferred_element_type=WIDE
    )


def native_view(values):
    rows, heads, columns = values.shape
    return (
        values.reshape(rows, heads, columns // 128, 128)
        .transpose(0, 2, 1, 3)
        .reshape(rows, columns // 128 * heads, 128)
    )


def from_native(values, heads):
    rows, count, width = values.shape
    return (
        values.reshape(rows, count // heads, heads, width)
        .transpose(0, 2, 1, 3)
        .reshape(rows, heads, count // heads * width)
    )


def split_kernel(side_ref, weight_ref, own_ref, other_ref):
    first = side_ref[0] == 0
    for start in range(0, weight_ref.shape[1], 8):
        turned = jnp.swapaxes(weight_ref[:, start : start + 8, :], 0, 1)
        for pair in range(4):
            lanes = pl.ds((start // 2 + pair) * 128, 128)
            left, right = turned[2 * pair], turned[2 * pair + 1]
            own_ref[:, lanes] = jnp.where(first, left, right).astype(LOW)
            other_ref[:, lanes] = jnp.where(first, right, left).astype(LOW)


def split_heads(view, side, offset, width):
    rows = view.shape[0]
    depth = width // 64
    block = 64
    return pl.pallas_call(
        split_kernel,
        out_shape=[jax.ShapeDtypeStruct((rows, width), LOW)] * 2,
        grid=(rows // block,),
        in_specs=[
            pl.BlockSpec(memory_space=pltpu.SMEM),
            pl.BlockSpec((block, depth, 128), lambda i: (i, offset // width, 0)),
        ],
        out_specs=[pl.BlockSpec((block, width), lambda i: (i, 0))] * 2,
        compiler_params=pltpu.CompilerParams(vmem_limit_bytes=40 * 2**20),
        cost_estimate=pl.CostEstimate(
            flops=rows * width * 2, bytes_accessed=rows * width * 12, transcendentals=0
        ),
    )(side, view)


def moments_kernel(side_ref, clip_ref, weight_ref, first_ref, second_ref, *rest):
    gradients, (first_out, second_out, update_out, total_ref) = rest[:-4], rest[-4:]
    first = side_ref[0] == 0
    clip = clip_ref[0]

    @pl.when(pl.program_id(0) == 0)
    def _():
        total_ref[...] = jnp.zeros_like(total_ref)

    update_sq = jnp.zeros((8, 128), WIDE)
    weight_sq = jnp.zeros((8, 128), WIDE)
    start = 0
    for own_ref, other_ref in zip(gradients[0::2], gradients[1::2]):
        for column in range(0, own_ref.shape[1], 512):
            parts = []
            for lane in range(column, column + 512, 128):
                own = own_ref[:, lane : lane + 128].astype(WIDE)
                other = other_ref[:, lane : lane + 128].astype(WIDE)
                parts += [jnp.where(first, own, other), jnp.where(first, other, own)]
            scaled = jnp.swapaxes(jnp.stack(parts, axis=0), 0, 1) * clip
            here = pl.ds(start, 8)
            weight = weight_ref[:, here, :]
            first_new = BETA_FIRST * first_ref[:, here, :] + (1.0 - BETA_FIRST) * scaled
            second_new = (
                BETA_SECOND * second_ref[:, here, :] + (1.0 - BETA_SECOND) * scaled * scaled
            )
            first_out[:, here, :] = first_new
            second_out[:, here, :] = second_new
            update = (
                first_new * FIRST_SCALE / (jnp.sqrt(second_new * SECOND_SCALE) + ADAM_EPSILON)
                + WEIGHT_DECAY * weight
            )
            update_out[:, here, :] = update.astype(update_out.dtype)
            update_sq += jnp.sum(update * update, axis=0)
            weight_sq += jnp.sum(weight * weight, axis=0)
            start += 8
    total_ref[0] += update_sq
    total_ref[1] += weight_sq


def moments_step(side, clip, weight, first, second, gradients):
    rows, depth, _ = weight.shape
    block = 32
    whole = pl.BlockSpec((block, depth, 128), lambda i: (i, 0, 0))
    shape = jax.ShapeDtypeStruct(weight.shape, WIDE)
    return pl.pallas_call(
        moments_kernel,
        out_shape=[
            shape,
            shape,
            jax.ShapeDtypeStruct(weight.shape, LOW),
            jax.ShapeDtypeStruct((2, 8, 128), WIDE),
        ],
        grid=(rows // block,),
        in_specs=[pl.BlockSpec(memory_space=pltpu.SMEM)] * 2
        + [whole] * 3
        + [pl.BlockSpec((block, g.shape[1]), lambda i: (i, 0)) for g in gradients],
        out_specs=[whole] * 3 + [pl.BlockSpec((2, 8, 128), lambda i: (0, 0, 0))],
        compiler_params=pltpu.CompilerParams(vmem_limit_bytes=48 * 2**20),
        cost_estimate=pl.CostEstimate(
            flops=weight.size * 20, bytes_accessed=weight.size * 24, transcendentals=weight.size
        ),
    )(side, clip, weight, first, second, *gradients)


class Grid:
    def __init__(self, line, share, heads):
        self.line, self.share, self.heads = line, share, heads

    def place(self):
        return lax.axis_index("z"), lax.axis_index("x"), lax.axis_index("h")

    def pair(self, values, step):
        return lax.ppermute(values, GROUP, [(i, i ^ step) for i in range(MEMBERS)])

    def along(self, values, step):
        return lax.ppermute(values, "z", [(i, i ^ step) for i in range(self.line)])

    def flip(self, values):
        if self.share == 1:
            return values
        half = values.shape[-1] // 2
        return jnp.concatenate([values[..., half:], values[..., :half]], axis=-1)

    def absolute(self, values):
        if self.share == 1:
            return values
        return jnp.where(lax.axis_index("x") == 1, self.flip(values), values)

    def crossed(self, values, step):
        return self.flip(values) if step >= self.heads else values

    def spread(self, own):
        parts = [own] + [self.crossed(self.pair(own, d), d) for d in (2, 4, 6)]
        half = jnp.concatenate(parts, axis=0)
        return jnp.concatenate([half, self.pair(half, 1)], axis=0)

    def gathered_sum(self, values):
        rows = values.shape[0] // MEMBERS
        both = values[: 4 * rows].astype(WIDE) + self.pair(values[4 * rows :], 1).astype(WIDE)
        total = both[:rows]
        for k, d in enumerate((2, 4, 6), 1):
            sent = both[k * rows : (k + 1) * rows].astype(LOW)
            total = total + self.crossed(self.pair(sent, d), d).astype(WIDE)
        return total

    def group_total(self, values):
        values = values + self.pair(values, 1)
        return values + self.pair(values, 2) + self.pair(values, 4) + self.pair(values, 6)

    def line_list(self, values):
        if self.line == 4:
            return [values] + [self.along(values, d) for d in (1, 2, 3)]
        every = lax.all_gather(values, "z", axis=0)
        return [every[i] for i in range(self.line)]

    def line_total(self, values):
        if self.line == 4:
            return sum(self.line_list(values))
        return lax.psum(values, "z")

    def total(self, values):
        return self.line_total(self.group_total(values))

    def ordered(self, parts):
        z = lax.axis_index("z")
        low, high = z % 2 == 1, z // 2 == 1
        parts = [jnp.where(low, parts[q ^ 1], parts[q]) for q in range(4)]
        return [jnp.where(high, parts[q ^ 2], parts[q]) for q in range(4)]

    def line_gather(self, values):
        if self.line == 4:
            return self.ordered(self.line_list(values))
        return self.line_list(values)

    def to_rows(self, values):
        rows = values.shape[0] // self.line
        values = self.absolute(values)
        if self.line != 4:
            return lax.all_to_all(values, "z", split_axis=0, concat_axis=1, tiled=True)
        z = lax.axis_index("z")
        blocks = values.reshape(self.line, rows, values.shape[1])
        parts = [lax.dynamic_index_in_dim(blocks, z ^ d, 0, False) for d in range(4)]
        parts = [parts[0]] + [self.along(parts[d], d) for d in (1, 2, 3)]
        return jnp.concatenate(self.ordered(parts), axis=1)

    def from_rows(self, values):
        if self.line != 4:
            moved = lax.all_to_all(values, "z", split_axis=1, concat_axis=0, tiled=True)
            return self.absolute(moved)
        z = lax.axis_index("z")
        width = values.shape[1] // self.line
        parts = [
            lax.dynamic_slice_in_dim(values, (z ^ d) * width, width, 1) for d in range(4)
        ]
        parts = [parts[0]] + [self.along(parts[d], d) for d in (1, 2, 3)]
        return self.absolute(jnp.concatenate(self.ordered(parts), axis=0))

    def line_sum(self, values, pieces=8):
        if self.line != 4:
            return lax.psum(values.astype(WIDE), "z")
        z = lax.axis_index("z")
        rows = values.shape[0] // pieces
        chunks = [values[i * rows : (i + 1) * rows] for i in range(pieces)]
        upward, downward = [(0, 1), (1, 2), (2, 3)], [(3, 2), (2, 1), (1, 0)]
        ups, downs = [], []
        for step in range(pieces + 2):
            held = [chunks[min(max(step - i, 0), pieces - 1)] for i in range(3)]
            up = lax.select_n(jnp.minimum(z, 2), *held)
            down = lax.select_n(jnp.minimum(3 - z, 2), *held)
            if step > 0:
                up = (up.astype(WIDE) + ups[-1].astype(WIDE)).astype(LOW)
                down = (down.astype(WIDE) + downs[-1].astype(WIDE)).astype(LOW)
            ups.append(lax.ppermute(up, "z", upward))
            downs.append(lax.ppermute(down, "z", downward))
        results = []
        for i in range(pieces):
            below = lax.select_n(jnp.maximum(z - 1, 0), ups[i], ups[i + 1], ups[i + 2])
            above = lax.select_n(jnp.maximum(2 - z, 0), downs[i], downs[i + 1], downs[i + 2])
            results.append(chunks[i].astype(WIDE) + below.astype(WIDE) + above.astype(WIDE))
        return jnp.concatenate(results, axis=0)

    def trade(self, values):
        return lax.ppermute(values, "x", [(0, 1), (1, 0)])

    def into(self, acts, weights):
        width = acts.shape[1] // self.share
        return sum(
            dot(acts[:, i * width : (i + 1) * width], weights[i]) for i in range(self.share)
        )

    def out_of(self, acts, weights):
        return jnp.concatenate([dot(acts, w, 1, 1) for w in weights], axis=1)

    def local(self, values, axis):
        z, x, _ = self.place()
        size = values.shape[axis] // (self.line * self.share)
        blocks = [
            lax.dynamic_slice_in_dim(values, (z * self.share + (x ^ i)) * size, size, axis)
            for i in range(self.share)
        ]
        return jnp.concatenate(blocks, axis=axis)

    def line_stats(self, values, count):
        center = jnp.mean(values, axis=1)
        spread = jnp.sum(jnp.square(values - center[:, None]), axis=1)
        parts = self.line_list(jnp.stack([center, spread]))
        mean = sum(part[0] for part in parts) / self.line
        size = count // self.line
        square = sum(part[1] + size * jnp.square(part[0] - mean) for part in parts)
        return mean[:, None], lax.rsqrt(square / count + EPS_NORM)[:, None]


def split_three(values):
    high = lax.reduce_precision(values, 8, 7)
    rest = values - high
    middle = lax.reduce_precision(rest, 8, 7)
    return high.astype(LOW), middle.astype(LOW), (rest - middle).astype(LOW)


def per_device(grid, *arguments):
    (
        cell_ids,
        cell_mask,
        labels,
        abd_weights,
        abd_first,
        abd_second,
        abd_gains,
        abd_gains_first,
        abd_gains_second,
        aba_weights,
        aba_first,
        aba_second,
        aba_gains,
        aba_gains_first,
        aba_gains_second,
        embed_table,
        embed_first,
        embed_second,
        output_table,
        output_first,
        output_second,
    ) = arguments
    z, x, h = grid.place()
    share, line = grid.share, grid.line
    attr_count, classes, embed_width = (
        embed_table.shape[0],
        output_table.shape[2],
        embed_table.shape[2],
    )
    model_width = attr_count * embed_width
    own_tokens = cell_ids.shape[0] // grid.heads
    first_device = ((z == 0) & (x == 0)).astype(WIDE)
    lead = ((z == 0) & (x == 0) & (h == 0)).astype(WIDE)
    side = x.astype(jnp.int32)[None]
    unit = FF // H
    sections = ((0, 3 * HD), (3 * HD, HD), (4 * HD, unit), (4 * HD + unit, unit))

    weights = []
    if share == 2:
        weight_view = native_view(abd_weights)
        for offset, width in sections:
            own, other = split_heads(weight_view, side, offset, width)
            weights.append([own, grid.trade(other)])
    else:
        for offset, width in sections:
            weights.append([abd_weights[:, 0, offset : offset + width].astype(LOW)])
    qkv_w, out_w, up_w, down_w = weights

    def own_rows(values):
        return lax.dynamic_slice_in_dim(values, h * own_tokens, own_tokens, 0)

    picked = own_rows(jnp.where(cell_mask == 1, classes, cell_ids)).astype(LOW)
    picked = grid.local(jnp.concatenate(grid.line_gather(picked), axis=0), 1)
    picked = grid.spread(picked)
    local_attrs = picked.shape[1]
    entries = classes + 1
    table_rows = jnp.arange(local_attrs * entries, dtype=jnp.int32)
    row_attr, row_entry = table_rows // entries, table_rows % entries
    expand = (jnp.arange(local_attrs, dtype=jnp.int32)[:, None] == row_attr[None, :]).astype(LOW)
    hot = (dot(picked, expand) == row_entry.astype(WIDE)[None, :]).astype(LOW)
    own_block = row_attr[:, None] == (
        jnp.arange(local_attrs * embed_width, dtype=jnp.int32) // embed_width
    )
    table_local = grid.local(embed_table, 0).reshape(local_attrs * entries, embed_width)
    table_wide = jnp.where(own_block, jnp.tile(table_local, (1, local_attrs)), 0.0)
    high, middle_bits, low_bits = split_three(table_wide)
    embedded = dot(
        jnp.concatenate([hot, hot, hot], axis=1),
        jnp.concatenate([high, middle_bits, low_bits], axis=0),
    )
    tokens = embedded.shape[0]
    held = tokens // MEMBERS

    mask_own = own_rows(cell_mask).astype(WIDE)
    labels_own = own_rows(lax.all_gather(labels, "h", axis=1, tiled=True))
    label_hot = (labels_own[:, :, None] == jnp.arange(classes, dtype=jnp.int32)).astype(WIDE)
    counts = lax.psum(jnp.sum(mask_own[:, :, None] * label_hot, axis=0), ("z", "x", "h"))
    class_weight = lax.rsqrt(1.0 + counts)
    weight_total = jnp.sum(counts * class_weight)
    output_low = lax.all_gather(output_table.astype(LOW), "h", axis=0, tiled=True)

    gains = grid.local(abd_gains, 1)
    mean_one, scale_one = grid.line_stats(embedded, model_width)
    hat_one = (embedded - mean_one) * scale_one
    normed = (hat_one * gains[0]).astype(LOW)
    triple = grid.line_sum(grid.into(normed, qkv_w).astype(LOW)).astype(LOW)
    queries, key_rows, value_rows = triple[:, :HD], triple[:, HD : 2 * HD], triple[:, 2 * HD :]
    factor = HD ** (-0.5)
    scores = dot(queries, key_rows, 1, 1) * factor
    shifted = jnp.exp(scores - jnp.max(scores, axis=1, keepdims=True))
    probs = shifted / jnp.sum(shifted, axis=1, keepdims=True)
    probs_low = probs.astype(LOW)
    attended = dot(probs_low, value_rows).astype(LOW)
    middle = embedded[:held] + grid.gathered_sum(grid.out_of(attended, out_w).astype(LOW))
    mean_two, scale_two = grid.line_stats(middle, model_width)
    hat_two = (middle - mean_two) * scale_two
    second = grid.spread((hat_two * gains[1]).astype(LOW))
    before = grid.line_sum(grid.into(second, up_w).astype(LOW))
    hidden = gelu_apply(before).astype(LOW)
    after = middle + grid.gathered_sum(grid.out_of(hidden, down_w).astype(LOW))

    aba_low = aba_weights.astype(LOW)
    final, aba_stored = aba_forward(grid.to_rows(after), aba_low, aba_gains)
    final_low = final.reshape(own_tokens, attr_count, embed_width).astype(LOW)
    logits = jnp.einsum("tfe,fec->tfc", final_low, output_low, preferred_element_type=WIDE)
    highest = jnp.max(logits, axis=-1, keepdims=True)
    exped = jnp.exp(logits - highest)
    totals = jnp.sum(exped, axis=-1, keepdims=True)
    log_total = (highest + jnp.log(totals))[:, :, 0]
    cell_weight = mask_own * jnp.sum(label_hot * class_weight[None], axis=-1)
    loss_local = jnp.sum(cell_weight * (log_total - jnp.sum(label_hot * logits, axis=-1)))
    logit_grad = ((cell_weight / weight_total)[:, :, None] * (exped / totals - label_hot)).astype(
        LOW
    )
    final_grad = jnp.einsum("tfc,fec->tfe", logit_grad, output_low, preferred_element_type=WIDE)
    output_part = jnp.einsum("tfe,tfc->fec", final_low, logit_grad, preferred_element_type=WIDE)
    rows_grad, aba_grad, aba_gains_grad = aba_backward(
        final_grad.reshape(own_tokens, model_width), aba_stored, aba_low, aba_gains
    )
    aba_grad, aba_gains_grad = lax.psum((aba_grad, aba_gains_grad), ("z", "x", "h"))
    output_grad = lax.psum(
        lax.psum_scatter(output_part, "h", scatter_dimension=0, tiled=True), ("z", "x")
    )

    upstream = grid.from_rows(rows_grad.astype(LOW))
    down_grad = grid.spread(upstream)
    hidden_grad = grid.line_sum(grid.into(down_grad, down_w).astype(LOW))
    before_grad = gelu_back(before, hidden_grad).astype(LOW)
    second_grad = grid.gathered_sum(grid.out_of(before_grad, up_w).astype(LOW))
    gained = second_grad * gains[1]
    sums = grid.line_total(jnp.stack([jnp.sum(gained, axis=1), jnp.sum(gained * hat_two, axis=1)]))
    sums = sums / model_width
    middle_grad = upstream.astype(WIDE) + scale_two * (
        gained - sums[0][:, None] - hat_two * sums[1][:, None]
    )
    gain_two = jnp.sum(second_grad * hat_two, axis=0)
    branch_grad = grid.spread(middle_grad.astype(LOW))
    attended_grad = grid.line_sum(grid.into(branch_grad, out_w).astype(LOW)).astype(LOW)
    prob_grad = dot(attended_grad, value_rows, 1, 1)
    score_grad = probs * (prob_grad - jnp.sum(probs * prob_grad, axis=1, keepdims=True))
    score_grad = score_grad.astype(LOW)
    query_grad = dot(score_grad, key_rows) * factor
    key_grad = dot(score_grad, queries, 0, 0) * factor
    value_grad = dot(probs_low, attended_grad, 0, 0)
    triple_grad = jnp.concatenate([query_grad, key_grad, value_grad], axis=1).astype(LOW)

    width = normed.shape[1] // share
    gradients, gradient_sq = [], 0.0
    for acts, upper in (
        (down_grad, hidden),
        (second, before_grad),
        (branch_grad, attended),
        (normed, triple_grad),
    ):
        parts = [
            dot(acts[:, i * width : (i + 1) * width], upper, 0, 0).astype(LOW)
            for i in range(share)
        ]
        for part in parts:
            gradient_sq = gradient_sq + jnp.sum(jnp.square(part.astype(WIDE)))
        if share == 2:
            parts[1] = grid.trade(parts[1])
        gradients = parts + gradients

    normed_grad = grid.out_of(triple_grad, qkv_w)
    gained = normed_grad * gains[0]
    sums = jnp.stack([jnp.sum(gained, axis=1), jnp.sum(gained * hat_one, axis=1)])
    places = (0, 2, 4, 6, 1, 3, 5, 7)
    own_sums = sums[:, :held]
    for k in range(1, MEMBERS):
        own_sums = own_sums + grid.pair(sums[:, k * held : (k + 1) * held], places[k])
    own_sums = grid.line_total(own_sums) / model_width
    gain_one = jnp.sum(normed_grad * hat_one, axis=0)
    own_part = middle_grad - scale_one[:held] * (
        own_sums[0][:, None] + hat_one[:held] * own_sums[1][:, None]
    )
    spread_grad = scale_one * gained
    table_grad = 0.0
    for piece in split_three(spread_grad)[:2]:
        table_grad = table_grad + dot(hot, piece, 0, 0)
    for piece in split_three(own_part)[:2]:
        table_grad = table_grad + dot(hot[:held], piece, 0, 0)
    fold = (
        jnp.arange(local_attrs * embed_width, dtype=jnp.int32)[:, None] % embed_width
        == jnp.arange(embed_width, dtype=jnp.int32)
    ).astype(WIDE)
    table_grad = jnp.dot(
        jnp.where(own_block, table_grad, 0.0), fold, precision=lax.Precision.HIGHEST
    )
    table_grad = table_grad.reshape(share, -1)
    gain_grad = jnp.stack([gain_one, gain_two]).reshape(2, share, -1).transpose(1, 0, 2)
    packed = jnp.concatenate([table_grad, gain_grad.reshape(share, -1)], axis=1)
    if share == 2:
        packed = jnp.where(x == 1, packed[::-1], packed)
    table_size = table_grad.shape[1]
    packed = packed.reshape(-1, 128)
    packed = jnp.stack(grid.line_gather(grid.group_total(packed)))
    packed = packed.reshape(line * share, -1)
    embed_grad = packed[:, :table_size].reshape(embed_table.shape)
    abd_gains_grad = (
        packed[:, table_size:].reshape(line * share, 2, -1).transpose(1, 0, 2).reshape(2, -1)
    )

    output_sq = first_device * jnp.sum(output_grad * output_grad)
    summed = grid.total(jnp.stack([gradient_sq, output_sq, loss_local]))
    replicated_sq = (
        jnp.sum(abd_gains_grad * abd_gains_grad)
        + jnp.sum(aba_grad * aba_grad)
        + jnp.sum(aba_gains_grad * aba_gains_grad)
        + jnp.sum(embed_grad * embed_grad)
    )
    grad_norm = jnp.sqrt(summed[0] + summed[1] + replicated_sq)
    loss_sum = summed[2]
    clip_factor = jnp.minimum(1.0, CLIP_LIMIT / (grad_norm + 1e-06))
    if share == 2:
        first_view, second_view, abd_update, squares = moments_step(
            side,
            clip_factor[None],
            weight_view,
            native_view(abd_first),
            native_view(abd_second),
            gradients,
        )
        abd_first_new = from_native(first_view, share)
        abd_second_new = from_native(second_view, share)
        abd_update_sq, abd_weight_sq = jnp.sum(squares[0]), jnp.sum(squares[1])
    else:
        abd_grad = jnp.concatenate(gradients, axis=1)[:, None, :].astype(WIDE)
        abd_first_new, abd_second_new, abd_update = moments_of(
            abd_weights, abd_grad, abd_first, abd_second, clip_factor, WEIGHT_DECAY
        )
        abd_update_sq, abd_weight_sq = (
            jnp.sum(abd_update * abd_update),
            jnp.sum(abd_weights * abd_weights),
        )
    output_first_new, output_second_new, output_update = moments_of(
        output_table, output_grad, output_first, output_second, clip_factor, WEIGHT_DECAY
    )
    trust_sums = grid.total(
        jnp.stack(
            [
                abd_update_sq,
                first_device * jnp.sum(output_update * output_update),
                abd_weight_sq,
                first_device * jnp.sum(output_table * output_table),
            ]
        )
    )
    if share == 2:
        abd_new = from_native(
            apply_trust(weight_view, abd_update.astype(WIDE), trust_sums[2], trust_sums[0]), share
        )
    else:
        abd_new = apply_trust(abd_weights, abd_update, trust_sums[2], trust_sums[0])
    output_new = apply_trust(output_table, output_update, trust_sums[3], trust_sums[1])
    gain_triple = local_step(
        abd_gains, abd_gains_grad, abd_gains_first, abd_gains_second, clip_factor, 0.0
    )
    aba_triple = local_step(aba_weights, aba_grad, aba_first, aba_second, clip_factor, WEIGHT_DECAY)
    aba_gain_triple = local_step(
        aba_gains, aba_gains_grad, aba_gains_first, aba_gains_second, clip_factor, 0.0
    )
    embed_triple = local_step(
        embed_table, embed_grad, embed_first, embed_second, clip_factor, WEIGHT_DECAY
    )
    return (
        loss_sum,
        weight_total,
        grad_norm,
        abd_new,
        abd_first_new,
        abd_second_new,
        *gain_triple,
        *aba_triple,
        *aba_gain_triple,
        *embed_triple,
        output_new,
        output_first_new,
        output_second_new,
    )


def solution(mesh):
    rows, heads = mesh.shape["dp"], mesh.shape["head"]
    share = H // heads
    line = rows // share
    devices = Mesh(mesh.devices.reshape(line, share, heads), ("z", "x", "h"))
    tokens, table = P(("z", "x"), None), P("h", None, None)
    weight = P(("z", "x"), "h", None)
    in_specs = (
        (tokens, tokens, P(("z", "x"), "h"), weight, weight, weight) + (P(),) * 12 + (table,) * 3
    )
    out_specs = (P(),) * 3 + (weight,) * 3 + (P(),) * 12 + (table,) * 3

    def step(*arguments):
        return per_device(Grid(line, share, heads), *arguments)

    return jax.shard_map(
        step, mesh=devices, in_specs=in_specs, out_specs=out_specs, check_vma=False
    )
```

time: 4640 us -> 1830 us (0.39)
  waiting for transfers between devices: 3710 us -> 922 us
  starting transfers between devices: 10.1 us -> 321 us
  local copies, waits for them, and re-layouts: 311 us -> 73.2 us
  other arithmetic: 248 us -> 148 us
  Pallas kernels: 0 us -> 83.5 us
  matrix products: 197 us -> 129 us
    all_gather x4 -> x0, waiting for transfers between devices: 2000 us -> none  [the longest x1 1890 us: per_device(): lax.all_gather(abd_weights.astype(jnp.bfloat16), 'dp', axis=0, tiled=True)]
    reduce_scatter x3 -> x1, waiting for transfers between devices: 1550 us -> 0.01 us  [per_device(): lax.psum_scatter(output_part, 'h', scatter_dimension=0, tiled=True)]
    ppermute x0 -> x165, waiting for transfers between devices: none -> 775 us  [the longest x40 299 us: line_sum(): downs.append(lax.ppermute(down, 'z', downward))]
    ppermute x0 -> x165, starting transfers between devices: none -> 321 us  [the longest x40 171 us: line_sum(): ups.append(lax.ppermute(up, 'z', upward))]
    unnamed x285 -> x358, local copies, waits for them, and re-layouts: 268 us -> 21.8 us
    pallas_call x0 -> x5, Pallas kernels: none -> 83.5 us  [the longest x1 60.1 us: moments_step(): pl.pallas_call(moments_kernel, out_shape=[shape, shape, jax.ShapeDtypeStr...]
    reduce_sum x5 -> x11, other arithmetic: 87.8 us -> 9.84 us  [the longest x1 1.62 us: per_device(): output_sq = first_device * jnp.sum(output_grad * output_grad)]
    concatenate x1 -> x17, other arithmetic: 67.7 us -> 5.41 us  [the longest x4 3.53 us: line_sum(): return jnp.concatenate(results, axis=0)]
  transfers between devices with their start and end apart: 14 -> 168, of which waited for: 13 -> 111; matrix products, arithmetic and copies ran while one was open for 6% -> 8% of each run, Pallas kernels for 0% -> 1%
where the time goes in v1:
time: 1830 us; the launch traced here: 1810 us
  waiting for transfers between devices  922 us (50%)
  starting transfers between devices  321 us (18%)
  other arithmetic  148 us (8%)
  matrix products  129 us (7%)
  blocking collectives  94.9 us (5%)
  Pallas kernels  83.5 us (5%)
  local copies, waits for them, and re-layouts  73.2 us (4%)
  between operations  40.9 us (2%)
    ppermute x40, waiting for transfers between devices, line_sum(): downs.append(lax.ppermute(down, 'z', downward))  299 us
    ppermute x40, waiting for transfers between devices, line_sum(): ups.append(lax.ppermute(up, 'z', upward))  221 us
    ppermute x47, waiting for transfers between devices, pair(): return lax.ppermute(values, GROUP, [(i, i ^ step) for i in range(MEMBERS)])  215 us
    ppermute x40, starting transfers between devices, line_sum(): ups.append(lax.ppermute(up, 'z', upward))  171 us
    dot_general x36, matrix products, dot(): lax.dot_general(left, right, (((left_dim,), (right_dim,)), ((), ())), pre...  95.8 us
    psum x1, waiting for transfers between devices, per_device(): lax.psum((aba_grad, aba_gains_grad), ('z', 'x', 'h'))  73.5 us
    psum x1, waiting for transfers between devices, per_device(): lax.psum(lax.psum_scatter(output_part, 'h', scatter_dimension=0, tiled=Tr...  73.1 us
    pallas_call x1, Pallas kernels, moments_step(): pl.pallas_call(moments_kernel, out_shape=[shape, shape, jax.ShapeDtypeStr...  60.1 us
  transfers between devices with their start and end apart: 168, of which 111 were waited for; matrix products, arithmetic and copies ran while one was open for 8% of the time, Pallas kernels for 1%

profile of v1, /device:TPU:0, one launch (start us, length us, event | category | flops | bytes accessed | tf_op | source)
XLA Modules:
  0.0 1812.0 jit_solution(15741628134198004030)
XLA Ops:
  39.8 16.9 collective-permute-done.4
  83.1 7.3 collective-permute-done.11
  96.7 6.3 collective-permute-done.12
  128.8 6.1 collective-permute-done.19
  140.5 7.9 collective-permute-done.21
  153.3 9.2 collective-permute-done.23
  168.6 7.2 collective-permute-done.25
  191.1 13.3 collective-permute-done.15
  223.3 7.2 collective-permute-done.18
  232.5 8.1 collective-permute-done.20
  242.5 12.9 collective-permute-done.22
  257.3 12.6 collective-permute-done.24
  271.7 11.9 collective-permute-done.26
  285.4 8.0 collective-permute-done.28
  295.6 7.6 collective-permute-done.30
  317.4 6.6 collective-permute-done.35
  334.8 6.7 shard_map.366
  345.4 50.3 %collective-permute-done.40 = bf16[128,1024]{1,0:T(8,128)(2,1)S(1)} collective-permute-done((bf16[128,1024]{1,0:T(8,128)(2,1)S(1)}, bf16[128,1024]{1,0:T(8,128)(2,1)S(1)}, u32[]{:S(2)}, u32[]{:S(2)}) %collective-permute-start.40) | collective-permute-done | bytes 262176 | tf_op jit(solution)/shard_map/ppermute | solution.py:343
  408.7 14.6 collective-permute-done.47
  424.8 13.7 collective-permute-done.48
  440.3 12.8 collective-permute-done.49
  454.8 11.9 collective-permute-done.51
  468.3 11.0 collective-permute-done.53
  485.5 5.9 collective-permute-done.55
  493.0 11.0 collective-permute-done.57
  526.1 11.3 collective-permute-done.46
  542.8 12.0 collective-permute-done.50
  560.1 11.1 collective-permute-done.52
  576.6 10.3 collective-permute-done.54
  592.3 9.4 collective-permute-done.56
  608.3 7.1 collective-permute-done.58
  620.7 9.3 collective-permute-done.60
  637.4 6.8 shard_map.367
  651.0 22.1 %collective-permute-done.64 = bf16[512,2048]{1,0:T(8,128)(2,1)S(1)} collective-permute-done((bf16[512,2048]{1,0:T(8,128)(2,1)S(1)}, bf16[512,2048]{1,0:T(8,128)(2,1)S(1)}, u32[]{:S(2)}, u32[]{:S(2)}) %collective-permute-start.64) | collective-permute-done | bytes 2097184 | tf_op jit(solution)/shard_map/ppermute | solution.py:453
  684.8 40.6 %psum.28 = f32[64,32]{1,0:T(8,128)S(1)} all-reduce(f32[64,32]{1,0:T(8,128)S(1)} %select_reduce_fusion.2), channel_id=1, replica_groups=mesh['z'=4,'x'=2,'h'=4] {'z','x','h'}, use_global_device_ids=true, to_apply=%region_1.2 | all-reduce | flops 2048 | bytes 16384 | tf_op jit(solution)/shard_map/psum | solution.py:568
  747.4 8.0 all_gather.7
  841.1 5.8 collective-permute-done.76
  861.2 14.6 collective-permute-done.82
  877.4 13.7 collective-permute-done.83
  892.7 12.8 collective-permute-done.84
  907.2 12.1 collective-permute-done.86
  921.4 11.2 collective-permute-done.88
  938.8 6.1 collective-permute-done.90
  946.6 10.4 collective-permute-done.92
  977.6 9.8 collective-permute-done.81
  992.7 10.9 collective-permute-done.85
  1009.0 12.1 collective-permute-done.87
  1026.4 11.4 collective-permute-done.89
  1043.2 10.6 collective-permute-done.91
  1060.4 8.4 collective-permute-done.93
  1074.2 10.6 collective-permute-done.95
  1115.8 6.6 collective-permute-done.102
  1142.4 5.8 collective-permute-done.107
  1191.8 41.1 %psum.31 = f32[2,64]{1,0:T(2,128)S(1)} all-reduce(f32[2,64]{1,0:T(2,128)S(1)} %pad_maximum_fusion.19), channel_id=1, replica_groups=mesh['z'=4,'x'=2,'h'=4] {'z','x','h'}, use_global_device_ids=true, to_apply=%region_48.49 | all-reduce | flops 128 | bytes 1024 | tf_op jit(solution)/shard_map/psum | solution.py:611
  1235.4 73.5 %all-reduce.5.cloned.1.call-done = f32[64,768]{1,0:T(8,128)} async-done(((f32[64,768]{1,0:T(8,128)}), f32[64,768]{1,0:T(8,128)}) %all-reduce.5.cloned.1.call-update) | async-done | bytes 196624 | tf_op jit(solution)/shard_map/psum | solution.py:611
  1310.5 73.1 %all-reduce.3.cloned.1.call-done = f32[16,64,32]{1,2,0:T(8,128)} async-done(((f32[16,64,32]{1,2,0:T(8,128)}), f32[16,64,32]{1,2,0:T(8,128)}) %all-reduce.3.cloned.1.call-update) | async-done | bytes 131088 | tf_op jit(solution)/shard_map/psum | solution.py:612
  1389.3 6.9 multiply_reduce_fusion.8
  1409.3 6.9 multiply_reduce_fusion.6
  1452.0 5.7 collective-permute-done.117
  1513.6 6.3 multiply_reduce_fusion.11
  1561.7 71.2 %collective-permute-done.133 = f32[3]{0:T(128)S(1)} collective-permute-done((f32[3]{0:T(128)S(1)}, f32[3]{0:T(128)S(1)}, u32[]{:S(2)}, u32[]{:S(2)}) %collective-permute-start.133) | collective-permute-done | bytes 44 | tf_op jit(solution)/shard_map/ppermute | solution.py:343
  1672.1 7.0 multiply_reduce_fusion.13
  1701.0 60.1 %shard_map.368 = (f32[512,96,128]{2,1,0:T(8,128)}, f32[512,96,128]{2,1,0:T(8,128)}, bf16[512,96,128]{2,1,0:T(8,128)(2,1)}, f32[2,8,128]{2,1,0:T(8,128)S(1)}) custom-call(s32[1]{0:T(128)} %bitcast.10.side_ref, f32[1]{0:T(128)} %bitcast.89.clip_ref, f32[512,96,128]{2,1,0:T(8,128)} %bitcast.360, f32[512,96,128]{2,1,0:T(8,128)} %bitcast.367, ...), custom_call_target="tpu_custom_call" | custom-call | flops 125829120 | bytes 150994944 | tf_op jit(solution)/shard_map/pallas_call | solution.py:315
  1781.3 20.8 %multiply_subtract_fusion = f32[512,96,128]{2,1,0:T(8,128)} fusion(f32[512,96,128]{2,1,0:T(8,128)} %bitcast.361, bf16[512,96,128]{2,1,0:T(8,128)(2,1)} %get-tuple-element.42, f32[]{:T(128)} %bitcast.100), kind=kLoop, calls=%fused_computation | loop fusion | flops 18874368 | bytes 62914564 | tf_op jit(solution)/shard_map/sub | solution.py:195
  (975 shorter events, 790.8 us)
Async XLA Ops:
  8.0 1225.4 %reduce-scatter.2.cloned.1.call-start = ((), (), s32[]{:S(2)}) async-start(), calls=%async_computation.1 | async-start | bytes 1310720 | tf_op jit(solution)/shard_map/reduce_scatter | solution.py:613
  9.5 25.8 %collective-permute-start = (bf16[32,64]{0,1:T(8,128)(2,1)S(1)}, bf16[32,64]{0,1:T(8,128)(2,1)S(1)}, u32[]{:S(2)}, u32[]{:S(2)}) collective-permute-start(bf16[32,64]{0,1:T(8,128)(2,1)S(1)} %get-tuple-element.256), channel_id=1, source_target_pairs={{0,24},{8,16},{16,8},{24,0},{1,25},{9,17},{17,9},{25,1},{2,26},{10... | collective-permute-start | bytes 12296 | tf_op jit(solution)/shard_map/ppermute | solution.py:346
  14.6 20.8 %collective-permute-start.1 = (bf16[32,64]{0,1:T(8,128)(2,1)S(1)}, bf16[32,64]{0,1:T(8,128)(2,1)S(1)}, u32[]{:S(2)}, u32[]{:S(2)}) collective-permute-start(bf16[32,64]{0,1:T(8,128)(2,1)S(1)} %get-tuple-element.256), channel_id=1, source_target_pairs={{0,16},{8,24},{16,0},{24,8},{1,17},{9,25},{17,1},{25,9},{2,18},{10... | collective-permute-start | bytes 12296 | tf_op jit(solution)/shard_map/ppermute | solution.py:346
  14.6 20.8 %collective-permute-start.2 = (bf16[32,64]{0,1:T(8,128)(2,1)S(1)}, bf16[32,64]{0,1:T(8,128)(2,1)S(1)}, u32[]{:S(2)}, u32[]{:S(2)}) collective-permute-start(bf16[32,64]{0,1:T(8,128)(2,1)S(1)} %get-tuple-element.256), channel_id=1, source_target_pairs={{0,8},{8,0},{16,24},{24,16},{1,9},{9,1},{17,25},{25,17},{2,10},{10... | collective-permute-start | bytes 12296 | tf_op jit(solution)/shard_map/ppermute | solution.py:346
  20.9 56.2 %collective-permute-start.10 = (bf16[512,1536]{1,0:T(8,128)(2,1)S(1)}, bf16[512,1536]{1,0:T(8,128)(2,1)}, u32[]{:S(2)}, u32[]{:S(2)}) collective-permute-start(bf16[512,1536]{1,0:T(8,128)(2,1)S(1)} %get-tuple-element.34), channel_id=1, source_target_pairs={{0,4},{4,0},{1,5},{5,1},{2,6},{6,2},{3,7},{7,3},{8,12},{12,8},{9,1... | collective-permute-start | bytes 4718600 | tf_op jit(solution)/shard_map/ppermute | solution.py:453
  35.5 21.2 %collective-permute-start.4 = (bf16[128,16]{0,1:T(8,128)(2,1)S(1)}, bf16[128,16]{0,1:T(8,128)(2,1)S(1)}, u32[]{:S(2)}, u32[]{:S(2)}) collective-permute-start(bf16[128,16]{0,1:T(8,128)(2,1)S(1)} %get-tuple-element.282), channel_id=1, source_target_pairs={{0,4},{1,5},{2,6},{3,7},{4,0},{5,1},{6,2},{7,3},{8,12},{9,13},{10,... | collective-permute-start | bytes 12296 | tf_op jit(solution)/shard_map/ppermute | solution.py:343
  37.0 19.7 %collective-permute-start.3 = (bf16[128,16]{0,1:T(8,128)(2,1)S(1)}, bf16[128,16]{0,1:T(8,128)(2,1)S(1)}, u32[]{:S(2)}, u32[]{:S(2)}) collective-permute-start(bf16[128,16]{0,1:T(8,128)(2,1)S(1)} %get-tuple-element.282), channel_id=1, source_target_pairs={{0,2},{1,3},{2,0},{3,1},{4,6},{5,7},{6,4},{7,5},{8,10},{9,11},{10,... | collective-permute-start | bytes 12296 | tf_op jit(solution)/shard_map/ppermute | solution.py:343
  38.6 19.1 %collective-permute-start.5 = (bf16[128,16]{0,1:T(8,128)(2,1)S(1)}, bf16[128,16]{0,1:T(8,128)(2,1)S(1)}, u32[]{:S(2)}, u32[]{:S(2)}) collective-permute-start(bf16[128,16]{0,1:T(8,128)(2,1)S(1)} %get-tuple-element.282), channel_id=1, source_target_pairs={{0,6},{1,7},{2,4},{3,5},{4,2},{5,3},{6,0},{7,1},{8,14},{9,15},{10,... | collective-permute-start | bytes 12296 | tf_op jit(solution)/shard_map/ppermute | solution.py:343
  148.5 13.9 collective-permute-start.23
  162.7 13.1 collective-permute-start.25
  167.3 15.5 collective-permute-start.14
  189.8 14.6 collective-permute-start.15
  211.9 96.8 %collective-permute-start.31 = (bf16[512,512]{1,0:T(8,128)(2,1)S(1)}, bf16[512,512]{1,0:T(8,128)(2,1)}, u32[]{:S(2)}, u32[]{:S(2)}) collective-permute-start(bf16[512,512]{1,0:T(8,128)(2,1)S(1)} %get-tuple-element.36), channel_id=1, source_target_pairs={{0,4},{4,0},{1,5},{5,1},{2,6},{6,2},{3,7},{7,3},{8,12},{12,8},{9,1... | collective-permute-start | bytes 1572872 | tf_op jit(solution)/shard_map/ppermute | solution.py:453
  213.5 82.1 %collective-permute-start.29 = (bf16[128,1536]{1,0:T(8,128)(2,1)}, bf16[128,1536]{1,0:T(8,128)(2,1)S(1)}, u32[]{:S(2)}, u32[]{:S(2)}) collective-permute-start(bf16[128,1536]{1,0:T(8,128)(2,1)} %get-tuple-element.182), channel_id=1, source_target_pairs={{0,8},{8,16},{16,24},{1,9},{9,17},{17,25},{2,10},{10,18},{18,26},{... | collective-permute-start | bytes 1179656 | tf_op jit(solution)/shard_map/ppermute | solution.py:443
  240.8 14.6 collective-permute-start.22
  255.6 14.3 collective-permute-start.24
  270.1 13.5 collective-permute-start.26
  313.9 14.1 collective-permute-start.34
  341.5 61.1 %collective-permute-start.43 = (bf16[512,2048]{1,0:T(8,128)(2,1)S(1)}, bf16[512,2048]{1,0:T(8,128)(2,1)S(1)}, u32[]{:S(2)}, u32[]{:S(2)}) collective-permute-start(bf16[512,2048]{1,0:T(8,128)(2,1)S(1)} %get-tuple-element.38), channel_id=1, source_target_pairs={{0,4},{4,0},{1,5},{5,1},{2,6},{6,2},{3,7},{7,3},{8,12},{12,8},{9,1... | collective-permute-start | bytes 6291464 | tf_op jit(solution)/shard_map/ppermute | solution.py:453
  341.8 53.9 %collective-permute-start.40 = (bf16[128,1024]{1,0:T(8,128)(2,1)S(1)}, bf16[128,1024]{1,0:T(8,128)(2,1)S(1)}, u32[]{:S(2)}, u32[]{:S(2)}) collective-permute-start(bf16[128,1024]{1,0:T(8,128)(2,1)S(1)} %get-tuple-element.135), channel_id=1, source_target_pairs={{0,4},{1,5},{2,6},{3,7},{4,0},{5,1},{6,2},{7,3},{8,12},{9,13},{10,... | collective-permute-start | bytes 786440 | tf_op jit(solution)/shard_map/ppermute | solution.py:343
  343.8 55.7 %collective-permute-start.41 = (bf16[128,1024]{1,0:T(8,128)(2,1)S(1)}, bf16[128,1024]{1,0:T(8,128)(2,1)S(1)}, u32[]{:S(2)}, u32[]{:S(2)}) collective-permute-start(bf16[128,1024]{1,0:T(8,128)(2,1)S(1)} %get-tuple-element.135), channel_id=1, source_target_pairs={{0,6},{1,7},{2,4},{3,5},{4,2},{5,3},{6,0},{7,1},{8,14},{9,15},{10,... | collective-permute-start | bytes 786440 | tf_op jit(solution)/shard_map/ppermute | solution.py:343
  344.1 55.4 %collective-permute-start.39 = (bf16[128,1024]{1,0:T(8,128)(2,1)S(1)}, bf16[128,1024]{1,0:T(8,128)(2,1)S(1)}, u32[]{:S(2)}, u32[]{:S(2)}) collective-permute-start(bf16[128,1024]{1,0:T(8,128)(2,1)S(1)} %get-tuple-element.135), channel_id=1, source_target_pairs={{0,2},{1,3},{2,0},{3,1},{4,6},{5,7},{6,4},{7,5},{8,10},{9,11},{10,... | collective-permute-start | bytes 786440 | tf_op jit(solution)/shard_map/ppermute | solution.py:343
  407.4 15.9 collective-permute-start.47
  423.5 15.0 collective-permute-start.48
  438.9 14.3 collective-permute-start.49
  453.5 13.2 collective-permute-start.51
  505.9 15.1 collective-permute-start.45
  521.7 15.8 collective-permute-start.46
  538.4 16.4 collective-permute-start.50
  555.7 15.6 collective-permute-start.52
  572.1 14.7 collective-permute-start.54
  587.8 13.8 collective-permute-start.56
  607.0 13.7 collective-permute-start.61
  616.2 13.8 collective-permute-start.60
  630.8 13.8 collective-permute-start.63
  644.2 28.9 %collective-permute-start.64 = (bf16[512,2048]{1,0:T(8,128)(2,1)S(1)}, bf16[512,2048]{1,0:T(8,128)(2,1)S(1)}, u32[]{:S(2)}, u32[]{:S(2)}) collective-permute-start(bf16[512,2048]{1,0:T(8,128)(2,1)S(1)} %get-tuple-element.40), channel_id=1, source_target_pairs={{0,4},{4,0},{1,5},{5,1},{2,6},{6,2},{3,7},{7,3},{8,12},{12,8},{9,1... | collective-permute-start | bytes 6291464 | tf_op jit(solution)/shard_map/ppermute | solution.py:453
  684.0 46.3 %collective-permute-start.67 = (bf16[128,1024]{1,0:T(8,128)(2,1)}, bf16[128,1024]{1,0:T(8,128)(2,1)S(1)}, u32[]{:S(2)}, u32[]{:S(2)}) collective-permute-start(bf16[128,1024]{1,0:T(8,128)(2,1)} %get-tuple-element.195), channel_id=1, source_target_pairs={{0,4},{1,5},{2,6},{3,7},{4,0},{5,1},{6,2},{7,3},{8,12},{9,13},{10,... | collective-permute-start | bytes 786440 | tf_op jit(solution)/shard_map/ppermute | solution.py:343
  741.6 13.9 collective-permute-start.69
  859.9 15.9 collective-permute-start.82
  876.1 15.0 collective-permute-start.83
  891.4 14.1 collective-permute-start.84
  905.9 13.4 collective-permute-start.86
  958.9 13.6 collective-permute-start.80
  973.1 14.2 collective-permute-start.81
  988.3 15.4 collective-permute-start.85
  1004.6 16.5 collective-permute-start.87
  1022.0 15.8 collective-permute-start.89
  1038.7 15.0 collective-permute-start.91
  1054.6 14.1 collective-permute-start.93
  1059.1 15.1 collective-permute-start.96
  1069.6 15.2 collective-permute-start.95
  1157.8 151.1 %all-reduce.5.cloned.1.call-start = ((), (), s32[]{:S(2)}) async-start(), calls=%async_computation.3 | async-start | bytes 393216 | tf_op jit(solution)/shard_map/psum | solution.py:611
  1186.0 197.6 %all-reduce.3.cloned.1.call-start = ((), (), s32[]{:S(2)}) async-start(), calls=%async_computation.2 | async-start | bytes 524288 | tf_op jit(solution)/shard_map/psum | solution.py:612
  1187.4 46.1 %collective-permute-start.116 = (bf16[128,512]{1,0:T(8,128)(2,1)S(1)}, bf16[128,512]{1,0:T(8,128)(2,1)S(1)}, u32[]{:S(2)}, u32[]{:S(2)}) collective-permute-start(bf16[128,512]{1,0:T(8,128)(2,1)S(1)} %add_convert_fusion.79), channel_id=1, source_target_pairs={{0,8},{8,16},{16,24},{1,9},{9,17},{17,25},{2,10},{10,18},{18,26},{... | collective-permute-start | bytes 393224 | tf_op jit(solution)/shard_map/ppermute | solution.py:443
  1233.6 152.3 %collective-permute-start.118 = (bf16[128,512]{1,0:T(8,128)(2,1)S(1)}, bf16[128,512]{1,0:T(8,128)(2,1)S(1)}, u32[]{:S(2)}, u32[]{:S(2)}) collective-permute-start(bf16[128,512]{1,0:T(8,128)(2,1)S(1)} %add_convert_fusion.76), channel_id=1, source_target_pairs={{0,8},{8,16},{16,24},{1,9},{9,17},{17,25},{2,10},{10,18},{18,26},{... | collective-permute-start | bytes 393224 | tf_op jit(solution)/shard_map/ppermute | solution.py:443
  1416.1 13.7 collective-permute-start.113
  1444.0 50.6 %collective-permute-start.128 = (bf16[128,512]{1,0:T(8,128)(2,1)}, bf16[128,512]{1,0:T(8,128)(2,1)S(1)}, u32[]{:S(2)}, u32[]{:S(2)}) collective-permute-start(bf16[128,512]{1,0:T(8,128)(2,1)} %get-tuple-element.189), channel_id=1, source_target_pairs={{0,8},{8,16},{16,24},{1,9},{9,17},{17,25},{2,10},{10,18},{18,26},{... | collective-permute-start | bytes 393224 | tf_op jit(solution)/shard_map/ppermute | solution.py:443
  1540.1 160.9 %collective-permute-start.157 = (bf16[512,2048]{1,0:T(8,128)(2,1)}, bf16[512,2048]{1,0:T(8,128)(2,1)}, u32[]{:S(2)}, u32[]{:S(2)}) collective-permute-start(bf16[512,2048]{1,0:T(8,128)(2,1)} %get-tuple-element.320), channel_id=1, source_target_pairs={{0,4},{4,0},{1,5},{5,1},{2,6},{6,2},{3,7},{7,3},{8,12},{12,8},{9,1... | collective-permute-start | bytes 6291464 | tf_op jit(solution)/shard_map/ppermute | solution.py:453
  1541.0 160.0 %collective-permute-start.156 = (bf16[512,2048]{1,0:T(8,128)(2,1)}, bf16[512,2048]{1,0:T(8,128)(2,1)}, u32[]{:S(2)}, u32[]{:S(2)}) collective-permute-start(bf16[512,2048]{1,0:T(8,128)(2,1)} %get-tuple-element.324), channel_id=1, source_target_pairs={{0,4},{4,0},{1,5},{5,1},{2,6},{6,2},{3,7},{7,3},{8,12},{12,8},{9,1... | collective-permute-start | bytes 6291464 | tf_op jit(solution)/shard_map/ppermute | solution.py:453
  1558.1 74.8 %collective-permute-start.133 = (f32[3]{0:T(128)S(1)}, f32[3]{0:T(128)S(1)}, u32[]{:S(2)}, u32[]{:S(2)}) collective-permute-start(f32[3]{0:T(128)S(1)} %fusion.333), channel_id=1, source_target_pairs={{0,6},{1,7},{2,4},{3,5},{4,2},{5,3},{6,0},{7,1},{8,14},{9,15},{10,... | collective-permute-start | bytes 44 | tf_op jit(solution)/shard_map/ppermute | solution.py:343
  1559.9 73.8 %collective-permute-start.132 = (f32[3]{0:T(128)S(1)}, f32[3]{0:T(128)S(1)}, u32[]{:S(2)}, u32[]{:S(2)}) collective-permute-start(f32[3]{0:T(128)S(1)} %fusion.333), channel_id=1, source_target_pairs={{0,4},{1,5},{2,6},{3,7},{4,0},{5,1},{6,2},{7,3},{8,12},{9,13},{10,... | collective-permute-start | bytes 44 | tf_op jit(solution)/shard_map/ppermute | solution.py:343
  1561.1 73.8 %collective-permute-start.131 = (f32[3]{0:T(128)S(1)}, f32[3]{0:T(128)S(1)}, u32[]{:S(2)}, u32[]{:S(2)}) collective-permute-start(f32[3]{0:T(128)S(1)} %fusion.333), channel_id=1, source_target_pairs={{0,2},{1,3},{2,0},{3,1},{4,6},{5,7},{6,4},{7,5},{8,10},{9,11},{10,... | collective-permute-start | bytes 44 | tf_op jit(solution)/shard_map/ppermute | solution.py:343
  1651.4 49.5 %collective-permute-start.155 = (bf16[512,512]{1,0:T(8,128)(2,1)}, bf16[512,512]{1,0:T(8,128)(2,1)}, u32[]{:S(2)}, u32[]{:S(2)}) collective-permute-start(bf16[512,512]{1,0:T(8,128)(2,1)} %get-tuple-element.328), channel_id=1, source_target_pairs={{0,4},{4,0},{1,5},{5,1},{2,6},{6,2},{3,7},{7,3},{8,12},{12,8},{9,1... | collective-permute-start | bytes 1572872 | tf_op jit(solution)/shard_map/ppermute | solution.py:453
  1654.3 46.7 %collective-permute-start.154 = (bf16[512,1536]{1,0:T(8,128)(2,1)}, bf16[512,1536]{1,0:T(8,128)(2,1)S(1)}, u32[]{:S(2)}, u32[]{:S(2)}) collective-permute-start(bf16[512,1536]{1,0:T(8,128)(2,1)} %get-tuple-element.334), channel_id=1, source_target_pairs={{0,4},{4,0},{1,5},{5,1},{2,6},{6,2},{3,7},{7,3},{8,12},{12,8},{9,1... | collective-permute-start | bytes 4718600 | tf_op jit(solution)/shard_map/ppermute | solution.py:453
  (278 other events, 3708.6 us)
Sparse Core Ops, SparseCore 0:
  1157.9 24.4 reduce-scatter.1
Sparse Core Ops, SparseCore 1:
  1186.1 122.8 all-reduce.4
  1312.5 71.0 all-reduce.2

commit v2 on v1

v2 whole, which is shorter than its diff:
```python
import functools

import jax
import jax.experimental.pallas as pl
import jax.experimental.pallas.tpu as pltpu
import jax.numpy as jnp
from jax import lax
from jax.sharding import Mesh
from jax.sharding import PartitionSpec as P

H = 8
AH = 8
STEP = 10
HD = 512
FF = 16384


EPS_NORM = 1e-05
CLIP_LIMIT = 0.01
LEARN_RATE = 0.3
BETA_FIRST = 0.9
BETA_SECOND = 0.999
ADAM_EPSILON = 1e-08
WEIGHT_DECAY = 0.01


def layer_norm(values, gain_row):
    center = jnp.mean(values, axis=-1, keepdims=True)
    centred = values - center
    spread = jnp.mean(centred * centred, axis=-1, keepdims=True)
    return centred * lax.rsqrt(spread + EPS_NORM) * gain_row


def gelu_apply(values):
    return 0.5 * values * (1.0 + lax.erf(values * 0.7071067811865476))


def norm_back(values, gain_row, upstream):
    unused_value, pull_back = jax.vjp(layer_norm, values, gain_row)
    return pull_back(upstream)


def gelu_back(values, upstream):
    unused_value, pull_back = jax.vjp(gelu_apply, values)
    return pull_back(upstream)[0]


def attend_keys(queries, key_rows, value_rows, factor):
    scores = (
        jnp.einsum("...qd,...kd->...qk", queries, key_rows, preferred_element_type=jnp.float32)
        * factor
    )
    highest = jnp.max(scores, axis=-1, keepdims=True)
    weights = jnp.exp(scores - highest)
    totals = jnp.sum(weights, axis=-1, keepdims=True)
    result = jnp.einsum(
        "...qk,...kd->...qd",
        (weights / totals).astype(jnp.bfloat16),
        value_rows,
        preferred_element_type=jnp.float32,
    )
    return (result, highest + jnp.log(totals))


def attend_back(queries, key_rows, value_rows, log_total, result_grad, factor):
    scores = (
        jnp.einsum("...qd,...kd->...qk", queries, key_rows, preferred_element_type=jnp.float32)
        * factor
    )
    softmax_probs = jnp.exp(scores - log_total)
    prob_grad = jnp.einsum(
        "...qd,...kd->...qk", result_grad, value_rows, preferred_element_type=jnp.float32
    )
    score_grad = softmax_probs * (
        prob_grad - jnp.sum(softmax_probs * prob_grad, axis=-1, keepdims=True)
    )
    score_grad = score_grad.astype(jnp.bfloat16)
    query_grad = (
        jnp.einsum("...qk,...kd->...qd", score_grad, key_rows, preferred_element_type=jnp.float32)
        * factor
    )
    key_grad = (
        jnp.einsum("...qk,...qd->...kd", score_grad, queries, preferred_element_type=jnp.float32)
        * factor
    )
    value_grad = jnp.einsum(
        "...qk,...qd->...kd",
        softmax_probs.astype(jnp.bfloat16),
        result_grad,
        preferred_element_type=jnp.float32,
    )
    return (query_grad, key_grad, value_grad)


def aba_forward(row_block, weights, gain_rows):
    embed_width = weights.shape[0]
    row_count = row_block.shape[0]
    attr_count = row_block.shape[1] // embed_width
    size_each = embed_width // AH
    inputs = row_block.reshape(row_count, attr_count, embed_width)
    normed = layer_norm(inputs, gain_rows[0]).astype(jnp.bfloat16)
    projection = weights[:, : 3 * embed_width].reshape(embed_width, 3, AH, size_each)
    triple = jnp.einsum(
        "rfe,eshd->srhfd", normed, projection, preferred_element_type=jnp.float32
    ).astype(jnp.bfloat16)
    attended, log_total = attend_keys(triple[0], triple[1], triple[2], size_each ** (-0.5))
    attended = attended.astype(jnp.bfloat16)
    out_proj = weights[:, 3 * embed_width : 4 * embed_width].reshape(embed_width, AH, size_each)
    middle = inputs + jnp.einsum(
        "rhfd,ohd->rfo", attended, out_proj, preferred_element_type=jnp.float32
    )
    second = layer_norm(middle, gain_rows[1]).astype(jnp.bfloat16)
    before = jnp.einsum(
        "rfe,eu->rfu",
        second,
        weights[:, 4 * embed_width : 8 * embed_width],
        preferred_element_type=jnp.float32,
    )
    hidden = gelu_apply(before).astype(jnp.bfloat16)
    after = middle + jnp.einsum(
        "rfu,ou->rfo", hidden, weights[:, 8 * embed_width :], preferred_element_type=jnp.float32
    )
    return (
        after.reshape(row_count, attr_count * embed_width),
        (inputs, normed, triple, log_total, attended, middle, second, before, hidden),
    )


def aba_backward(upstream, stored, weights, gain_rows):
    inputs, normed, triple, log_total, attended, middle, second, before, hidden = stored
    row_count, attr_count, embed_width = inputs.shape
    size_each = embed_width // AH
    upstream = upstream.reshape(row_count, attr_count, embed_width)
    down_grad = upstream.astype(jnp.bfloat16)
    hidden_grad = jnp.einsum(
        "rfo,ou->rfu", down_grad, weights[:, 8 * embed_width :], preferred_element_type=jnp.float32
    )
    before_grad = gelu_back(before, hidden_grad).astype(jnp.bfloat16)
    second_grad = jnp.einsum(
        "rfu,eu->rfe",
        before_grad,
        weights[:, 4 * embed_width : 8 * embed_width],
        preferred_element_type=jnp.float32,
    )
    middle_part, gain_two = norm_back(middle, gain_rows[1], second_grad)
    middle_grad = upstream + middle_part
    branch_grad = middle_grad.astype(jnp.bfloat16)
    out_proj = weights[:, 3 * embed_width : 4 * embed_width].reshape(embed_width, AH, size_each)
    attended_grad = jnp.einsum(
        "rfo,ohd->rhfd", branch_grad, out_proj, preferred_element_type=jnp.float32
    ).astype(jnp.bfloat16)
    query_grad, key_grad, value_grad = attend_back(
        triple[0], triple[1], triple[2], log_total, attended_grad, size_each ** (-0.5)
    )
    triple_grad = jnp.stack([query_grad, key_grad, value_grad]).astype(jnp.bfloat16)
    projection = weights[:, : 3 * embed_width].reshape(embed_width, 3, AH, size_each)
    normed_grad = jnp.einsum(
        "srhfd,eshd->rfe", triple_grad, projection, preferred_element_type=jnp.float32
    )
    input_part, gain_one = norm_back(inputs, gain_rows[0], normed_grad)
    input_grad = middle_grad + input_part
    weight_grad = jnp.concatenate(
        [
            jnp.einsum(
                "rfe,srhfd->eshd", normed, triple_grad, preferred_element_type=jnp.float32
            ).reshape(embed_width, 3 * embed_width),
            jnp.einsum(
                "rfo,rhfd->ohd", branch_grad, attended, preferred_element_type=jnp.float32
            ).reshape(embed_width, embed_width),
            jnp.einsum("rfe,rfu->eu", second, before_grad, preferred_element_type=jnp.float32),
            jnp.einsum("rfo,rfu->ou", down_grad, hidden, preferred_element_type=jnp.float32),
        ],
        axis=1,
    )
    return (
        input_grad.reshape(row_count, attr_count * embed_width),
        weight_grad,
        jnp.stack([gain_one, gain_two]),
    )


def moments_of(weight, gradient, first, second, clip_factor, decay):
    scaled = gradient * clip_factor
    first_new = BETA_FIRST * first + (1.0 - BETA_FIRST) * scaled
    second_new = BETA_SECOND * second + (1.0 - BETA_SECOND) * scaled * scaled
    update = (
        first_new
        / (1.0 - BETA_FIRST**STEP)
        / (jnp.sqrt(second_new / (1.0 - BETA_SECOND**STEP)) + ADAM_EPSILON)
        + decay * weight
    )
    return (first_new, second_new, update)


def apply_trust(weight, update, weight_sq, update_sq):
    trust_ratio = jnp.sqrt(weight_sq) / (jnp.sqrt(update_sq) + 1e-06)
    return weight - LEARN_RATE * trust_ratio * update


def local_step(weight, gradient, first, second, clip_factor, decay):
    first_new, second_new, update = moments_of(weight, gradient, first, second, clip_factor, decay)
    return (
        apply_trust(weight, update, jnp.sum(weight * weight), jnp.sum(update * update)),
        first_new,
        second_new,
    )


LOW = jnp.bfloat16
WIDE = jnp.float32
SHARERS = 4
FIRST_SCALE = 1.0 / (1.0 - BETA_FIRST**STEP)
SECOND_SCALE = 1.0 / (1.0 - BETA_SECOND**STEP)
UNITS = FF // H
SECTIONS = ((0, 3, HD), (3 * HD, 1, HD), (4 * HD, 1, UNITS), (4 * HD + UNITS, 1, UNITS))


def dot(left, right, left_dim=1, right_dim=0):
    return lax.dot_general(
        left, right, (((left_dim,), (right_dim,)), ((), ())), preferred_element_type=WIDE
    )


def native_view(values):
    rows, heads, columns = values.shape
    return (
        values.reshape(rows, heads, columns // 128, 128)
        .transpose(0, 2, 1, 3)
        .reshape(rows, columns // 128 * heads, 128)
    )


def from_native(values, heads):
    rows, count, width = values.shape
    return (
        values.reshape(rows, count // heads, heads, width)
        .transpose(0, 2, 1, 3)
        .reshape(rows, heads, count // heads * width)
    )


def tile_pairs(parts, width):
    each = width // 128
    return [
        (part * each + i, part * each + each // 2 + i)
        for part in range(parts)
        for i in range(each // 2)
    ]


def exchange(flag, left, right):
    return jnp.where(flag, right, left), jnp.where(flag, left, right)


def cross(q_flag, p_flag, values):
    a, b = exchange(p_flag, values[0], values[1])
    c, d = exchange(p_flag, values[2], values[3])
    a, c = exchange(q_flag, a, c)
    b, d = exchange(q_flag, b, d)
    return a, b, c, d


def split_kernel(parts, width, side_ref, weight_ref, *out_refs):
    q_flag, p_flag = side_ref[0] == 1, side_ref[1] == 1
    turned = {}
    for tile, (left, right) in enumerate(tile_pairs(parts, width)):
        for place in (left, right):
            group = place // 4
            if group not in turned:
                turned[group] = jnp.swapaxes(weight_ref[:, group * 8 : group * 8 + 8, :], 0, 1)
        values = [turned[t // 4][t % 4 * 2 + head] for head in range(2) for t in (left, right)]
        lanes = pl.ds(tile * 128, 128)
        for ref, value in zip(out_refs, cross(q_flag, p_flag, values)):
            ref[:, lanes] = value.astype(LOW)


def split_weights(view, side, offset, parts, width):
    rows = view.shape[0]
    total = parts * width
    depth = total // 64
    block = 32
    return pl.pallas_call(
        functools.partial(split_kernel, parts, width),
        out_shape=[jax.ShapeDtypeStruct((rows, total // 2), LOW)] * SHARERS,
        grid=(rows // block,),
        in_specs=[
            pl.BlockSpec(memory_space=pltpu.SMEM),
            pl.BlockSpec((block, depth, 128), lambda i: (i, offset // total, 0)),
        ],
        out_specs=[pl.BlockSpec((block, total // 2), lambda i: (i, 0))] * SHARERS,
        compiler_params=pltpu.CompilerParams(vmem_limit_bytes=40 * 2**20),
        cost_estimate=pl.CostEstimate(
            flops=rows * total * 2, bytes_accessed=rows * total * 12, transcendentals=0
        ),
    )(side, view)


def moments_kernel(side_ref, clip_ref, weight_ref, first_ref, second_ref, *rest):
    gradients, (first_out, second_out, update_out, total_ref) = rest[:-4], rest[-4:]
    q_flag, p_flag = side_ref[0] == 1, side_ref[1] == 1
    clip = clip_ref[0]

    @pl.when(pl.program_id(0) == 0)
    def _():
        total_ref[...] = jnp.zeros_like(total_ref)

    update_sq = jnp.zeros((8, 128), WIDE)
    weight_sq = jnp.zeros((8, 128), WIDE)
    for index, (offset, parts, width) in enumerate(SECTIONS):
        refs = gradients[SHARERS * index : SHARERS * (index + 1)]
        places = {}
        for tile, (left, right) in enumerate(tile_pairs(parts, width)):
            values = [ref[:, tile * 128 : tile * 128 + 128].astype(WIDE) for ref in refs]
            a, b, c, d = cross(q_flag, p_flag, values)
            places[2 * left], places[2 * right] = a, b
            places[2 * left + 1], places[2 * right + 1] = c, d
            for group in (left // 4, right // 4):
                rows = range(group * 8, group * 8 + 8)
                if any(row not in places for row in rows):
                    continue
                scaled = jnp.swapaxes(jnp.stack([places.pop(r) for r in rows], axis=0), 0, 1) * clip
                here = pl.ds(offset // 64 + group * 8, 8)
                weight = weight_ref[:, here, :]
                first_new = BETA_FIRST * first_ref[:, here, :] + (1.0 - BETA_FIRST) * scaled
                second_new = (
                    BETA_SECOND * second_ref[:, here, :] + (1.0 - BETA_SECOND) * scaled * scaled
                )
                first_out[:, here, :] = first_new
                second_out[:, here, :] = second_new
                update = (
                    first_new * FIRST_SCALE / (jnp.sqrt(second_new * SECOND_SCALE) + ADAM_EPSILON)
                    + WEIGHT_DECAY * weight
                )
                update_out[:, here, :] = update.astype(update_out.dtype)
                update_sq += jnp.sum(update * update, axis=0)
                weight_sq += jnp.sum(weight * weight, axis=0)
    total_ref[0] += update_sq
    total_ref[1] += weight_sq


def moments_step(side, clip, weight, first, second, gradients):
    rows, depth, _ = weight.shape
    block = 32
    whole = pl.BlockSpec((block, depth, 128), lambda i: (i, 0, 0))
    shape = jax.ShapeDtypeStruct(weight.shape, WIDE)
    return pl.pallas_call(
        moments_kernel,
        out_shape=[
            shape,
            shape,
            jax.ShapeDtypeStruct(weight.shape, LOW),
            jax.ShapeDtypeStruct((2, 8, 128), WIDE),
        ],
        grid=(rows // block,),
        in_specs=[pl.BlockSpec(memory_space=pltpu.SMEM)] * 2
        + [whole] * 3
        + [pl.BlockSpec((block, g.shape[1]), lambda i: (i, 0)) for g in gradients],
        out_specs=[whole] * 3 + [pl.BlockSpec((2, 8, 128), lambda i: (0, 0, 0))],
        compiler_params=pltpu.CompilerParams(vmem_limit_bytes=48 * 2**20),
        cost_estimate=pl.CostEstimate(
            flops=weight.size * 20, bytes_accessed=weight.size * 24, transcendentals=weight.size
        ),
    )(side, clip, weight, first, second, *gradients)


class Grid:
    def __init__(self, rows, heads):
        self.rows, self.heads = rows // SHARERS, heads
        self.each = H // heads
        self.parts = SHARERS // self.each
        self.members = SHARERS * heads
        self.shape = (self.rows, self.each, self.parts, heads)
        self.evens = range(2, self.members, 2)

    def sharer(self):
        return lax.axis_index("q") * self.parts + lax.axis_index("p")

    def pair(self, values, step):
        return lax.ppermute(values, ("q", "p", "h"), [(i, i ^ step) for i in range(self.members)])

    def trade(self, values, step):
        return lax.ppermute(values, ("q", "p"), [(i, i ^ step) for i in range(SHARERS)])

    def moved(self, values, step):
        turn = step // self.heads
        if turn == 0:
            return values
        blocks = jnp.split(values, SHARERS, axis=-1)
        return jnp.concatenate([blocks[j ^ turn] for j in range(SHARERS)], axis=-1)

    def spread(self, own):
        parts = [own] + [self.moved(self.pair(own, d), d) for d in self.evens]
        half = jnp.concatenate(parts, axis=0)
        return half, self.pair(half, 1)

    def gathered_sum(self, half, other):
        rows = half.shape[0] // (self.members // 2)
        both = half.astype(WIDE) + self.pair(other, 1).astype(WIDE)
        total = both[:rows]
        for k, d in enumerate(self.evens, 1):
            sent = both[k * rows : (k + 1) * rows].astype(LOW)
            total = total + self.moved(self.pair(sent, d), d).astype(WIDE)
        return total

    def group_total(self, values):
        step = 1
        while step < self.members:
            values = values + self.pair(values, step)
            step *= 2
        return values

    def facing(self, values):
        return lax.ppermute(values, "a", [(0, 1), (1, 0)])

    def row_list(self, values):
        if self.rows == 2:
            return [values, self.facing(values)]
        every = lax.all_gather(values, "a", axis=0)
        return [every[i] for i in range(self.rows)]

    def row_gather(self, values):
        parts = self.row_list(values)
        if self.rows == 2:
            flag = lax.axis_index("a") == 1
            parts = exchange(flag, *parts)
        return list(parts)

    def row_sum(self, values):
        if self.rows == 2:
            return values.astype(WIDE) + self.facing(values).astype(WIDE)
        return lax.psum(values.astype(WIDE), "a")

    def total(self, values):
        return self.row_sum(self.group_total(values))

    def ordered(self, parts):
        place = self.sharer()
        low, high = place % 2 == 1, place // 2 == 1
        parts = [jnp.where(low, parts[j ^ 1], parts[j]) for j in range(SHARERS)]
        return [jnp.where(high, parts[j ^ 2], parts[j]) for j in range(SHARERS)]

    def absolute(self, values):
        return jnp.concatenate(self.ordered(jnp.split(values, SHARERS, axis=-1)), axis=-1)

    def to_rows(self, values):
        values = self.absolute(values)
        if self.rows != 2:
            return lax.all_to_all(values, "a", split_axis=0, concat_axis=1, tiled=True)
        flag = lax.axis_index("a") == 1
        kept, sent = exchange(flag, *jnp.split(values, 2, axis=0))
        return jnp.concatenate(exchange(flag, kept, self.facing(sent)), axis=1)

    def from_rows(self, values):
        if self.rows != 2:
            return self.absolute(
                lax.all_to_all(values, "a", split_axis=1, concat_axis=0, tiled=True)
            )
        flag = lax.axis_index("a") == 1
        kept, sent = exchange(flag, *jnp.split(values, 2, axis=1))
        moved = jnp.concatenate(exchange(flag, kept, self.facing(sent)), axis=0)
        return self.absolute(moved)

    def renamed(self, values, step):
        block = values.shape[0] // self.members
        span = 1
        while span < self.members // 2:
            if step // 2 & span:
                halves = values.reshape(-1, 2, span * block, values.shape[1])
                values = jnp.stack([halves[:, 1], halves[:, 0]], axis=1).reshape(values.shape)
            span *= 2
        return values

    def columns(self, values):
        found = [values]
        for d in range(1, self.parts):
            got = lax.ppermute(values, "p", [(i, i ^ d) for i in range(self.parts)])
            found.append(self.renamed(got, d * self.heads))
        return jnp.concatenate(found, axis=1)

    def local(self, values, axis):
        size = values.shape[axis] // (self.rows * SHARERS)
        first, place = lax.axis_index("a") * SHARERS, self.sharer()
        return [
            lax.dynamic_slice_in_dim(values, (first + (place ^ j)) * size, size, axis)
            for j in range(SHARERS)
        ]

    def stats(self, values, count):
        center = jnp.mean(values, axis=1)
        spread = jnp.sum(jnp.square(values - center[:, None]), axis=1)
        parts = self.row_list(jnp.stack([center, spread]))
        mean = sum(part[0] for part in parts) / self.rows
        size = count // self.rows
        square = sum(part[1] + size * jnp.square(part[0] - mean) for part in parts)
        return mean[:, None], lax.rsqrt(square / count + EPS_NORM)[:, None]

    def split_plain(self, values, parts, width):
        rows = values.shape[0]
        values = values.astype(LOW).reshape(rows, self.each, parts, self.parts, -1)
        values = values.transpose(1, 3, 0, 2, 4).reshape(SHARERS, rows, -1)
        return [
            lax.dynamic_index_in_dim(values, self.sharer() ^ j, 0, False) for j in range(SHARERS)
        ]

    def merge_plain(self, pieces, parts, width):
        values = jnp.stack(self.ordered(pieces))
        rows = values.shape[1]
        values = values.reshape(self.each, self.parts, rows, parts, -1)
        return values.transpose(2, 0, 3, 1, 4).reshape(rows, self.each, parts * width)


def tied(*values):
    return lax.optimization_barrier(values)


def split_three(values):
    high = lax.reduce_precision(values, 8, 7)
    rest = values - high
    middle = lax.reduce_precision(rest, 8, 7)
    return high.astype(LOW), middle.astype(LOW), (rest - middle).astype(LOW)


def per_device(grid, *arguments):
    (
        cell_ids,
        cell_mask,
        labels,
        abd_weights,
        abd_first,
        abd_second,
        abd_gains,
        abd_gains_first,
        abd_gains_second,
        aba_weights,
        aba_first,
        aba_second,
        aba_gains,
        aba_gains_first,
        aba_gains_second,
        embed_table,
        embed_first,
        embed_second,
        output_table,
        output_first,
        output_second,
    ) = arguments
    h = lax.axis_index("h")
    attr_count, entries, embed_width = embed_table.shape
    classes = output_table.shape[2]
    model_width = attr_count * embed_width
    own_tokens = cell_ids.shape[0] // grid.heads
    first_device = ((lax.axis_index("a") == 0) & (grid.sharer() == 0)).astype(WIDE)
    native = grid.each == 2
    side = jnp.stack([lax.axis_index("q"), lax.axis_index("p")]).astype(jnp.int32)

    pieces = []
    weight_view = native_view(abd_weights) if native else None
    for offset, parts, width in SECTIONS:
        if native:
            pieces.append(split_weights(weight_view, side, offset, parts, width))
        else:
            columns = abd_weights[:, :, offset : offset + parts * width]
            pieces.append(grid.split_plain(columns, parts, width))
    qkv_pieces, out_pieces, up_pieces, down_pieces = pieces

    def traded(values):
        return [values[0]] + [grid.trade(values[j], j) for j in (1, 2, 3)]

    qkv_w = jnp.concatenate(traded(qkv_pieces), axis=0)

    def own_rows(values):
        return lax.dynamic_slice_in_dim(values, h * own_tokens, own_tokens, 0)

    picked = own_rows(jnp.where(cell_mask == 1, classes, cell_ids)).astype(LOW)
    picked = jnp.concatenate(grid.row_gather(picked), axis=0)
    picked = grid.spread(jnp.concatenate(grid.local(picked, 1), axis=1))
    picked = jnp.concatenate(picked, axis=0)
    local_attrs = picked.shape[1]
    tokens = picked.shape[0]
    held = tokens // grid.members
    block_attrs = local_attrs // SHARERS
    table_rows = jnp.arange(block_attrs * entries, dtype=jnp.int32)
    row_attr, row_entry = table_rows // entries, (table_rows % entries).astype(WIDE)
    own_block = row_attr[:, None] == (
        jnp.arange(block_attrs * embed_width, dtype=jnp.int32) // embed_width
    )
    hots, embedded = [], []
    for j, table in enumerate(grid.local(embed_table, 0)):
        expand = (
            jnp.arange(local_attrs, dtype=jnp.int32)[:, None]
            == j * block_attrs + row_attr[None, :]
        ).astype(LOW)
        hot = (dot(picked, expand) == row_entry[None, :]).astype(LOW)
        hots.append(hot)
        table = table.reshape(block_attrs * entries, embed_width)
        table = jnp.where(own_block, jnp.tile(table, (1, block_attrs)), 0.0)
        embedded.append(
            dot(
                jnp.concatenate([hot, hot, hot], axis=1),
                jnp.concatenate(split_three(table), axis=0),
            )
        )
    embedded = jnp.concatenate(embedded, axis=1)

    mask_own = own_rows(cell_mask).astype(WIDE)
    label_parts = labels.reshape(grid.heads, own_tokens, -1).astype(LOW)
    label_sent = [
        lax.dynamic_index_in_dim(label_parts, h ^ d, 0, False) for d in range(grid.heads)
    ]
    tables_low = output_table.astype(LOW)
    label_got, table_got = [label_sent[0]], [tables_low]
    for d in range(1, grid.heads):
        label_got.append(grid.pair(label_sent[d], d))
        table_got.append(grid.pair(tables_low, d))

    def by_head(parts):
        for bit in range((grid.heads - 1).bit_length()):
            flag = (h >> bit) % 2 == 1
            parts = [
                jnp.where(flag, parts[d ^ (1 << bit)], parts[d]) for d in range(grid.heads)
            ]
        return parts

    labels_own = jnp.concatenate(by_head(label_got), axis=1).astype(jnp.int32)
    output_low = jnp.concatenate(by_head(table_got), axis=0)
    label_hot = (labels_own[:, :, None] == jnp.arange(classes, dtype=jnp.int32)).astype(WIDE)
    counts = jnp.sum(mask_own[:, :, None] * label_hot, axis=0)

    gains = jnp.concatenate(grid.local(abd_gains, 1), axis=1)
    mean_one, scale_one = grid.stats(embedded, model_width)
    hat_one = (embedded - mean_one) * scale_one
    normed = (hat_one * gains[0]).astype(LOW)
    triple, out_pieces, up_pieces = tied(dot(normed, qkv_w).astype(LOW), out_pieces, up_pieces)
    triple = grid.row_sum(triple).astype(LOW)
    out_w = jnp.concatenate(traded(out_pieces), axis=0)
    up_w = jnp.concatenate(traded(up_pieces), axis=0)
    counts = grid.total(counts)
    triple, out_w, up_w, counts, label_hot, output_low, down_pieces = tied(
        triple, out_w, up_w, counts, label_hot, output_low, down_pieces
    )
    class_weight = lax.rsqrt(1.0 + counts)
    weight_total = jnp.sum(counts * class_weight)
    part = HD // grid.parts
    query_own, key_own, value_own = (triple[:, i * part : (i + 1) * part] for i in range(3))
    queries, key_rows = grid.columns(query_own), grid.columns(key_own)
    value_rows = grid.columns(value_own)
    factor = HD ** (-0.5)
    scores = dot(queries, key_rows, 1, 1) * factor
    shifted = jnp.exp(scores - jnp.max(scores, axis=1, keepdims=True))
    probs = shifted / jnp.sum(shifted, axis=1, keepdims=True)
    probs_low = probs.astype(LOW)
    attended = jnp.split(dot(probs_low, value_own).astype(LOW), 2, axis=0)
    branch = [dot(a, out_w, 1, 1).astype(LOW) for a in attended]
    middle = embedded[:held] + grid.gathered_sum(*branch)
    mean_two, scale_two = grid.stats(middle, model_width)
    hat_two = (middle - mean_two) * scale_two
    second = grid.spread((hat_two * gains[1]).astype(LOW))
    before, down_pieces = tied([dot(a, up_w).astype(LOW) for a in second], down_pieces)
    before = [grid.row_sum(b) for b in before]
    down_w = jnp.concatenate(traded(down_pieces), axis=0)
    before, down_w = tied(before, down_w)
    hidden = [gelu_apply(b).astype(LOW) for b in before]
    after = middle + grid.gathered_sum(*[dot(a, down_w, 1, 1).astype(LOW) for a in hidden])

    aba_low = aba_weights.astype(LOW)
    final, aba_stored = aba_forward(grid.to_rows(after), aba_low, aba_gains)
    final_low = final.reshape(own_tokens, attr_count, embed_width).astype(LOW)
    logits = jnp.einsum("tfe,fec->tfc", final_low, output_low, preferred_element_type=WIDE)
    highest = jnp.max(logits, axis=-1, keepdims=True)
    exped = jnp.exp(logits - highest)
    totals = jnp.sum(exped, axis=-1, keepdims=True)
    log_total = (highest + jnp.log(totals))[:, :, 0]
    cell_weight = mask_own * jnp.sum(label_hot * class_weight[None], axis=-1)
    loss_local = jnp.sum(cell_weight * (log_total - jnp.sum(label_hot * logits, axis=-1)))
    logit_grad = ((cell_weight / weight_total)[:, :, None] * (exped / totals - label_hot)).astype(
        LOW
    )
    final_grad = jnp.einsum("tfc,fec->tfe", logit_grad, output_low, preferred_element_type=WIDE)
    output_part = jnp.einsum("tfe,tfc->fec", final_low, logit_grad, preferred_element_type=WIDE)
    rows_grad, aba_part, aba_gains_part = aba_backward(
        final_grad.reshape(own_tokens, model_width), aba_stored, aba_low, aba_gains
    )

    width = normed.shape[1] // SHARERS
    gradient_sq = []

    def row_gradients(acts, uppers):
        found = []
        for j in range(SHARERS):
            cut = slice(j * width, (j + 1) * width)
            piece = sum(dot(a[:, cut], u, 0, 0) for a, u in zip(acts, uppers)).astype(LOW)
            gradient_sq.append(jnp.sum(jnp.square(piece.astype(WIDE))))
            found.append(piece)
        return found

    upstream = grid.from_rows(rows_grad.astype(LOW))
    down_grad = grid.spread(upstream)
    hidden_grad, output_part, aba_part, aba_gains_part = tied(
        [dot(a, down_w).astype(LOW) for a in down_grad], output_part, aba_part, aba_gains_part
    )
    hidden_grad = [grid.row_sum(g) for g in hidden_grad]
    down_gradient = traded(row_gradients(down_grad, hidden))

    small = jnp.concatenate([aba_part.reshape(-1), aba_gains_part.reshape(-1)])
    blocks = output_part.reshape(grid.heads, -1)
    bits = (grid.heads - 1).bit_length()
    for bit in range(bits):
        flag = (h >> bit) % 2 == 1
        halves = blocks.reshape(-1, 2, blocks.shape[1])
        kept, sent = exchange(flag, halves[:, 0], halves[:, 1])
        got = grid.pair(jnp.concatenate([sent.reshape(-1), small]).reshape(-1, 128), 1 << bit)
        got = got.reshape(-1)
        blocks = kept + got[: sent.size].reshape(kept.shape)
        small = small + got[sent.size :]
    packed = jnp.concatenate([blocks.reshape(-1), small]).reshape(-1, 128)
    for step in (grid.heads, 2 * grid.heads):
        packed = packed + grid.pair(packed, step)
    packed = grid.row_sum(packed).reshape(-1)
    output_grad = packed[: blocks.size].reshape(output_table.shape)
    aba_grad = packed[blocks.size : blocks.size + aba_weights.size].reshape(aba_weights.shape)
    aba_gains_grad = packed[blocks.size + aba_weights.size :].reshape(aba_gains.shape)

    hidden_grad, down_gradient, output_grad, aba_grad, aba_gains_grad = tied(
        hidden_grad, down_gradient, output_grad, aba_grad, aba_gains_grad
    )

    before_grad = [gelu_back(b, g).astype(LOW) for b, g in zip(before, hidden_grad)]
    second_grad = grid.gathered_sum(*[dot(a, up_w, 1, 1).astype(LOW) for a in before_grad])
    gained = second_grad * gains[1]
    sums = jnp.stack([jnp.sum(gained, axis=1), jnp.sum(gained * hat_two, axis=1)])
    sums = sum(grid.row_list(sums)) / model_width
    middle_grad = upstream.astype(WIDE) + scale_two * (
        gained - sums[0][:, None] - hat_two * sums[1][:, None]
    )
    gain_two = jnp.sum(second_grad * hat_two, axis=0)
    branch_grad = grid.spread(middle_grad.astype(LOW))
    attended_grad, up_gradient, out_gradient = tied(
        jnp.concatenate([dot(a, out_w).astype(LOW) for a in branch_grad], axis=0),
        row_gradients(second, before_grad),
        row_gradients(branch_grad, attended),
    )
    attended_grad = grid.row_sum(attended_grad).astype(LOW)
    up_gradient, out_gradient = traded(up_gradient), traded(out_gradient)
    prob_grad = dot(grid.columns(attended_grad), value_rows, 1, 1)
    score_grad = probs * (prob_grad - jnp.sum(probs * prob_grad, axis=1, keepdims=True))
    score_grad = score_grad.astype(LOW)
    query_grad = dot(score_grad, key_own) * factor
    key_grad = dot(score_grad, query_own, 0, 0) * factor
    value_grad = dot(probs_low, attended_grad, 0, 0)
    triple_grad = jnp.concatenate([query_grad, key_grad, value_grad], axis=1).astype(LOW)
    table_part = [
        sum(dot(hot[:held], piece, 0, 0) for piece in split_three(block)[:2])
        for hot, block in zip(hots, jnp.split(middle_grad, SHARERS, axis=1))
    ]
    triple_grad, up_gradient, out_gradient, table_part = tied(
        triple_grad, up_gradient, out_gradient, table_part
    )
    qkv_gradient = traded(row_gradients([normed], [triple_grad]))
    gradients = qkv_gradient + out_gradient + up_gradient + down_gradient

    normed_grad = dot(triple_grad, qkv_w, 1, 1)
    gained = normed_grad * gains[0]
    sums = jnp.stack([jnp.sum(gained, axis=1), jnp.sum(gained * hat_one, axis=1)])
    sums = sum(grid.row_list(sums)) / model_width
    gain_one = jnp.sum(normed_grad * hat_one, axis=0)
    spread_grad = scale_one * (gained - sums[0][:, None] - hat_one * sums[1][:, None])
    fold = (
        jnp.arange(block_attrs * embed_width, dtype=jnp.int32)[:, None] % embed_width
        == jnp.arange(embed_width, dtype=jnp.int32)
    ).astype(WIDE)
    records = []
    for j, block in enumerate(jnp.split(spread_grad, SHARERS, axis=1)):
        grad = table_part[j] + sum(dot(hots[j], piece, 0, 0) for piece in split_three(block)[:2])
        grad = jnp.dot(jnp.where(own_block, grad, 0.0), fold, precision=lax.Precision.HIGHEST)
        cut = slice(j * width, (j + 1) * width)
        records.append(jnp.concatenate([grad.reshape(-1), gain_one[cut], gain_two[cut]]))
    table_size = block_attrs * entries * embed_width
    packed = jnp.stack(grid.ordered(records)).reshape(-1, 128)
    packed = jnp.stack(grid.row_gather(grid.group_total(packed)))
    packed = packed.reshape(grid.rows * SHARERS, -1)
    embed_grad = packed[:, :table_size].reshape(embed_table.shape)
    abd_gains_grad = packed[:, table_size:].reshape(-1, 2, width).transpose(1, 0, 2)
    abd_gains_grad = abd_gains_grad.reshape(2, model_width)

    output_sq = first_device * jnp.sum(output_grad * output_grad)
    summed = grid.total(jnp.stack([sum(gradient_sq), output_sq, loss_local]))
    replicated_sq = (
        jnp.sum(abd_gains_grad * abd_gains_grad)
        + jnp.sum(aba_grad * aba_grad)
        + jnp.sum(aba_gains_grad * aba_gains_grad)
        + jnp.sum(embed_grad * embed_grad)
    )
    grad_norm = jnp.sqrt(summed[0] + summed[1] + replicated_sq)
    loss_sum = summed[2]
    clip_factor = jnp.minimum(1.0, CLIP_LIMIT / (grad_norm + 1e-06))
    if native:
        first_view, second_view, abd_update, squares = moments_step(
            side,
            clip_factor[None],
            weight_view,
            native_view(abd_first),
            native_view(abd_second),
            gradients,
        )
        abd_first_new = from_native(first_view, grid.each)
        abd_second_new = from_native(second_view, grid.each)
        abd_update_sq, abd_weight_sq = jnp.sum(squares[0]), jnp.sum(squares[1])
    else:
        merged = [
            grid.merge_plain(gradients[SHARERS * i : SHARERS * (i + 1)], parts, width)
            for i, (_, parts, width) in enumerate(SECTIONS)
        ]
        abd_grad = jnp.concatenate(merged, axis=2).astype(WIDE)
        abd_first_new, abd_second_new, abd_update = moments_of(
            abd_weights, abd_grad, abd_first, abd_second, clip_factor, WEIGHT_DECAY
        )
        abd_update_sq, abd_weight_sq = (
            jnp.sum(abd_update * abd_update),
            jnp.sum(abd_weights * abd_weights),
        )
    output_first_new, output_second_new, output_update = moments_of(
        output_table, output_grad, output_first, output_second, clip_factor, WEIGHT_DECAY
    )
    trust_sums = grid.total(
        jnp.stack(
            [
                abd_update_sq,
                first_device * jnp.sum(output_update * output_update),
                abd_weight_sq,
                first_device * jnp.sum(output_table * output_table),
            ]
        )
    )
    if native:
        abd_new = from_native(
            apply_trust(weight_view, abd_update.astype(WIDE), trust_sums[2], trust_sums[0]),
            grid.each,
        )
    else:
        abd_new = apply_trust(abd_weights, abd_update, trust_sums[2], trust_sums[0])
    output_new = apply_trust(output_table, output_update, trust_sums[3], trust_sums[1])
    gain_triple = local_step(
        abd_gains, abd_gains_grad, abd_gains_first, abd_gains_second, clip_factor, 0.0
    )
    aba_triple = local_step(aba_weights, aba_grad, aba_first, aba_second, clip_factor, WEIGHT_DECAY)
    aba_gain_triple = local_step(
        aba_gains, aba_gains_grad, aba_gains_first, aba_gains_second, clip_factor, 0.0
    )
    embed_triple = local_step(
        embed_table, embed_grad, embed_first, embed_second, clip_factor, WEIGHT_DECAY
    )
    return (
        loss_sum,
        weight_total,
        grad_norm,
        abd_new,
        abd_first_new,
        abd_second_new,
        *gain_triple,
        *aba_triple,
        *aba_gain_triple,
        *embed_triple,
        output_new,
        output_first_new,
        output_second_new,
    )


def solution(mesh):
    grid = Grid(mesh.shape["dp"], mesh.shape["head"])
    devices = Mesh(mesh.devices.reshape(grid.shape), ("a", "q", "p", "h"))
    rows = ("a", "q", "p")
    tokens, table = P(rows, None), P("h", None, None)
    weight = P(rows, "h", None)
    in_specs = (tokens, tokens, P(rows, "h"), weight, weight, weight) + (P(),) * 12 + (table,) * 3
    out_specs = (P(),) * 3 + (weight,) * 3 + (P(),) * 12 + (table,) * 3
    return jax.shard_map(
        functools.partial(per_device, grid),
        mesh=devices,
        in_specs=in_specs,
        out_specs=out_specs,
        check_vma=False,
    )
```

time: 1830 us -> 1540 us (0.84)
  starting transfers between devices: 321 us -> 139 us
  waiting for transfers between devices: 922 us -> 767 us
  blocking collectives: 94.9 us -> 0 us
  local copies, waits for them, and re-layouts: 73.2 us -> 145 us
  matrix products: 129 us -> 180 us
  other arithmetic: 148 us -> 171 us
    ppermute x165 -> x128, starting transfers between devices: 321 us -> 139 us  [the longest x82 80.3 us: pair(): lax.ppermute(values, ('q', 'p', 'h'), [(i, i ^ step) for i in range(self....]
    psum x2 -> x0, waiting for transfers between devices: 147 us -> none  [the longest x1 73.5 us: per_device(): lax.psum((aba_grad, aba_gains_grad), ('z', 'x', 'h'))]
    psum x2 -> x0, blocking collectives: 81.7 us -> none  [the longest x1 41.1 us: per_device(): lax.psum((aba_grad, aba_gains_grad), ('z', 'x', 'h'))]
    dot_general x36 -> x72, matrix products: 95.8 us -> 146 us  [dot(): lax.dot_general(left, right, (((left_dim,), (right_dim,)), ((), ())), pre...]
    convert_element_type x68 -> x11, other arithmetic: 41.8 us -> 8.84 us  [the longest x2 4.31 us: per_device(): gelu_back(b, g).astype(LOW)]
    concatenate x17 -> x34, other arithmetic: 5.41 us -> 28.2 us  [the longest x21 17.4 us: moved(): return jnp.concatenate([blocks[j ^ turn] for j in range(SHARERS)], axis=-1)]
    add x10 -> x33, other arithmetic: 3.43 us -> 25.6 us  [the longest x16 10.4 us: group_total(): values = values + self.pair(values, step)]
    concatenate x13 -> x12, local copies, waits for them, and re-layouts: 12.5 us -> 32.3 us  [the longest x4 21.5 us: spread(): half = jnp.concatenate(parts, axis=0)]
  transfers between devices with their start and end apart: 168 -> 128, of which waited for: 111 -> 65; matrix products, arithmetic and copies ran while one was open for 8% -> 16% of each run, Pallas kernels for 1% -> 2%
where the time goes in v2:
time: 1540 us; the launch traced here: 1530 us
  waiting for transfers between devices  767 us (50%)
  matrix products  180 us (12%)
  other arithmetic  171 us (11%)
  local copies, waits for them, and re-layouts  145 us (9%)
  starting transfers between devices  139 us (9%)
  Pallas kernels  94.4 us (6%)
  between operations  30.7 us (2%)
    ppermute x82, waiting for transfers between devices, pair(): lax.ppermute(values, ('q', 'p', 'h'), [(i, i ^ step) for i in range(self....  440 us
    ppermute x18, waiting for transfers between devices, facing(): return lax.ppermute(values, 'a', [(0, 1), (1, 0)])  189 us
    dot_general x72, matrix products, dot(): lax.dot_general(left, right, (((left_dim,), (right_dim,)), ((), ())), pre...  146 us
    ppermute x82, starting transfers between devices, pair(): lax.ppermute(values, ('q', 'p', 'h'), [(i, i ^ step) for i in range(self....  80.3 us
    ppermute x24, waiting for transfers between devices, trade(): lax.ppermute(values, ('q', 'p'), [(i, i ^ step) for i in range(SHARERS)])  79.6 us
    ppermute x4, waiting for transfers between devices, columns(): got = lax.ppermute(values, 'p', [(i, i ^ d) for i in range(self.parts)])  58.7 us
    pallas_call x1, Pallas kernels, moments_step(): pl.pallas_call(moments_kernel, out_shape=[shape, shape, jax.ShapeDtypeStr...  56.7 us
    unnamed x410, local copies, waits for them, and re-layouts  41.2 us
  transfers between devices with their start and end apart: 128, of which 65 were waited for; matrix products, arithmetic and copies ran while one was open for 16% of the time, Pallas kernels for 2%

profile of v2, /device:TPU:0, one launch (start us, length us, event | category | flops | bytes accessed | tf_op | source)
XLA Modules:
  0.0 1526.4 jit_solution(5596119612977138824)
XLA Ops:
  2.1 4.0 collective-permute-start
  6.3 9.4 shard_map.364
  56.1 30.3 %collective-permute-done.4 = bf16[64,32]{0,1:T(8,128)(2,1)S(1)} collective-permute-done((bf16[64,32]{0,1:T(8,128)(2,1)S(1)}, bf16[64,32]{0,1:T(8,128)(2,1)S(1)}, u32[]{:S(2)}, u32[]{:S(2)}) %collective-permute-start.4) | collective-permute-done | bytes 4128 | tf_op jit(solution)/shard_map/ppermute | solution.py:379
  136.1 7.8 shard_map.365
  143.9 10.3 shard_map.366
  157.7 4.7 pad_maximum_fusion
  169.2 5.6 convolution_convert_fusion.7
  187.2 28.5 %collective-permute-done.16 = bf16[512,256]{1,0:T(8,128)(2,1)S(1)} collective-permute-done((bf16[512,256]{1,0:T(8,128)(2,1)S(1)}, bf16[512,256]{1,0:T(8,128)(2,1)S(1)}, u32[]{:S(2)}, u32[]{:S(2)}) %collective-permute-start.16) | collective-permute-done | bytes 262176 | tf_op jit(solution)/shard_map/ppermute | solution.py:382
  218.2 10.2 shard_map.367
  229.7 39.4 %collective-permute-done.15 = bf16[512,256]{1,0:T(8,128)(2,1)S(1)} collective-permute-done((bf16[512,256]{1,0:T(8,128)(2,1)S(1)}, bf16[512,256]{1,0:T(8,128)(2,1)S(1)}, u32[]{:S(2)}, u32[]{:S(2)}) %collective-permute-start.15) | collective-permute-done | bytes 262176 | tf_op jit(solution)/shard_map/ppermute | solution.py:382
  270.6 5.3 collective-permute-done.14
  282.0 12.8 collective-permute-done.32
  294.9 7.8 collective-permute-done.31
  308.1 4.1 collective-permute-done.33
  320.4 14.9 collective-permute-done.38
  335.9 10.7 collective-permute-done.40
  347.3 9.7 collective-permute-done.39
  357.0 7.0 collective-permute-done.36
  364.1 8.9 collective-permute-done.35
  373.1 6.0 fusion.343
  390.7 8.6 collective-permute-done.45
  399.5 15.2 collective-permute-done.46
  417.5 16.7 %collective-permute-done.44 = bf16[64,2048]{0,1:T(8,128)(2,1)S(1)} collective-permute-done((bf16[64,2048]{0,1:T(8,128)(2,1)S(1)}, bf16[64,2048]{0,1:T(8,128)(2,1)S(1)}, u32[]{:S(2)}, u32[]{:S(2)}) %collective-permute-start.44) | collective-permute-done | bytes 262176 | tf_op jit(solution)/shard_map/ppermute | solution.py:379
  437.9 6.8 concatenate.451
  444.9 5.3 convolution_convert_fusion.11
  459.1 65.5 %collective-permute-done.50 = bf16[512,1024]{1,0:T(8,128)(2,1)S(1)} collective-permute-done((bf16[512,1024]{1,0:T(8,128)(2,1)S(1)}, bf16[512,1024]{1,0:T(8,128)(2,1)S(1)}, u32[]{:S(2)}, u32[]{:S(2)}) %collective-permute-start.50) | collective-permute-done | bytes 1048608 | tf_op jit(solution)/shard_map/ppermute | solution.py:413
  525.0 21.5 %collective-permute-done.51 = bf16[512,1024]{1,0:T(8,128)(2,1)S(1)} collective-permute-done((bf16[512,1024]{1,0:T(8,128)(2,1)S(1)}, bf16[512,1024]{1,0:T(8,128)(2,1)S(1)}, u32[]{:S(2)}, u32[]{:S(2)}) %collective-permute-start.51) | collective-permute-done | bytes 1048608 | tf_op jit(solution)/shard_map/ppermute | solution.py:413
  555.2 4.4 fusion.407
  567.2 9.2 collective-permute-done.59
  581.8 15.6 %collective-permute-done.58 = bf16[64,2048]{0,1:T(8,128)(2,1)S(1)} collective-permute-done((bf16[64,2048]{0,1:T(8,128)(2,1)}, bf16[64,2048]{0,1:T(8,128)(2,1)S(1)}, u32[]{:S(2)}, u32[]{:S(2)}) %collective-permute-start.58) | collective-permute-done | bytes 262176 | tf_op jit(solution)/shard_map/ppermute | solution.py:379
  597.4 10.4 collective-permute-done.61
  607.9 10.6 collective-permute-done.62
  618.6 6.2 fusion.90
  633.4 9.5 collective-permute-done.63
  718.2 24.5 %collective-permute-done.64 = bf16[32,2048]{0,1:T(8,128)(2,1)S(1)} collective-permute-done((bf16[32,2048]{0,1:T(8,128)(2,1)S(1)}, bf16[32,2048]{0,1:T(8,128)(2,1)S(1)}, u32[]{:S(2)}, u32[]{:S(2)}) %collective-permute-start.64) | collective-permute-done | bytes 131104 | tf_op jit(solution)/shard_map/ppermute | solution.py:413
  762.6 9.2 collective-permute-done.69
  774.1 21.8 %collective-permute-done.66 = bf16[64,2048]{0,1:T(8,128)(2,1)S(1)} collective-permute-done((bf16[64,2048]{0,1:T(8,128)(2,1)}, bf16[64,2048]{0,1:T(8,128)(2,1)S(1)}, u32[]{:S(2)}, u32[]{:S(2)}) %collective-permute-start.66) | collective-permute-done | bytes 262176 | tf_op jit(solution)/shard_map/ppermute | solution.py:379
  795.9 9.6 collective-permute-done.67
  809.3 6.6 concatenate.472
  828.4 5.0 convolution_convert_fusion.8
  862.3 5.3 collective-permute-done.79
  871.0 6.2 collective-permute-done.80
  877.9 27.0 %collective-permute-done.73 = bf16[512,1024]{1,0:T(8,128)(2,1)} collective-permute-done((bf16[512,1024]{1,0:T(8,128)(2,1)}, bf16[512,1024]{1,0:T(8,128)(2,1)}, u32[]{:S(2)}, u32[]{:S(2)}) %collective-permute-start.73) | collective-permute-done | bytes 1048608 | tf_op jit(solution)/shard_map/ppermute | solution.py:413
  908.2 51.8 %collective-permute-done.81 = f32[641,128]{1,0:T(8,128)S(1)} collective-permute-done((f32[641,128]{1,0:T(8,128)S(1)}, f32[641,128]{1,0:T(8,128)S(1)}, u32[]{:S(2)}, u32[]{:S(2)}) %collective-permute-start.81) | collective-permute-done | bytes 328224 | tf_op jit(solution)/shard_map/ppermute | solution.py:379
  963.4 13.0 collective-permute-done.82
  1014.2 28.3 %collective-permute-done.88 = bf16[64,2048]{0,1:T(8,128)(2,1)S(1)} collective-permute-done((bf16[64,2048]{0,1:T(8,128)(2,1)S(1)}, bf16[64,2048]{0,1:T(8,128)(2,1)S(1)}, u32[]{:S(2)}, u32[]{:S(2)}) %collective-permute-start.88) | collective-permute-done | bytes 262176 | tf_op jit(solution)/shard_map/ppermute | solution.py:379
  1045.0 8.0 collective-permute-done.89
  1053.1 11.0 collective-permute-done.85
  1064.3 5.3 multiply_reduce_fusion.22
  1082.6 7.1 collective-permute-done.95
  1090.0 17.0 %collective-permute-done.96 = bf16[64,2048]{0,1:T(8,128)(2,1)S(1)} collective-permute-done((bf16[64,2048]{0,1:T(8,128)(2,1)S(1)}, bf16[64,2048]{0,1:T(8,128)(2,1)S(1)}, u32[]{:S(2)}, u32[]{:S(2)}) %collective-permute-start.96) | collective-permute-done | bytes 262176 | tf_op jit(solution)/shard_map/ppermute | solution.py:379
  1109.6 19.9 %collective-permute-done.94 = bf16[64,2048]{0,1:T(8,128)(2,1)S(1)} collective-permute-done((bf16[64,2048]{0,1:T(8,128)(2,1)S(1)}, bf16[64,2048]{0,1:T(8,128)(2,1)S(1)}, u32[]{:S(2)}, u32[]{:S(2)}) %collective-permute-start.94) | collective-permute-done | bytes 262176 | tf_op jit(solution)/shard_map/ppermute | solution.py:379
  1133.3 6.6 concatenate.490
  1181.2 14.1 collective-permute-done.100
  1201.2 38.0 %collective-permute-done.101 = bf16[1024,256]{1,0:T(8,128)(2,1)S(1)} collective-permute-done((bf16[1024,256]{1,0:T(8,128)(2,1)S(1)}, bf16[1024,256]{1,0:T(8,128)(2,1)S(1)}, u32[]{:S(2)}, u32[]{:S(2)}) %collective-permute-start.101) | collective-permute-done | bytes 524320 | tf_op jit(solution)/shard_map/ppermute | solution.py:476
  1247.7 5.0 collective-permute-done.108.rest_7_
  1258.2 9.2 multiply_reduce_fusion.1
  1272.1 6.9 subtract_multiply_fusion
  1297.8 4.3 multiply_reduce_fusion.18
  1338.8 9.4 collective-permute-done.111
  1348.7 24.3 %collective-permute-done.112 = f32[3]{0:T(128)S(1)} collective-permute-done((f32[3]{0:T(128)S(1)}, f32[3]{0:T(128)S(1)}, u32[]{:S(2)}, u32[]{:S(2)}) %collective-permute-start.112) | collective-permute-done | bytes 44 | tf_op jit(solution)/shard_map/ppermute | solution.py:379
  1394.6 56.7 %shard_map.368 = (f32[512,96,128]{2,1,0:T(8,128)}, f32[512,96,128]{2,1,0:T(8,128)}, bf16[512,96,128]{2,1,0:T(8,128)(2,1)}, f32[2,8,128]{2,1,0:T(8,128)S(1)}) custom-call(s32[2]{0:T(128)S(1)} %copy-done.8, f32[1]{0:T(128)} %bitcast.105.clip_ref, f32[512,96,128]{2,1,0:T(8,128)} %bitcast.384, f32[512,96,128]{2,1,0:T(8,128)} %bitcast.389, ...), custom_call_target="tpu_custom_call" | custom-call | flops 125829120 | bytes 150994944 | tf_op jit(solution)/shard_map/pallas_call | solution.py:346
  1465.4 6.2 multiply_reduce_fusion.20
  1504.3 20.8 %multiply_subtract_fusion = f32[512,96,128]{2,1,0:T(8,128)} fusion(f32[512,96,128]{2,1,0:T(8,128)} %bitcast.385, bf16[512,96,128]{2,1,0:T(8,128)(2,1)} %get-tuple-element.186, f32[]{:T(128)} %bitcast.116), kind=kLoop, calls=%fused_computation | loop fusion | flops 18874368 | bytes 62914564 | tf_op jit(solution)/shard_map/sub | solution.py:197
  (1002 shorter events, 574.5 us)
Async XLA Ops:
  2.1 51.0 %collective-permute-start = (bf16[32,64]{0,1:T(8,128)(2,1)}, bf16[32,64]{0,1:T(8,128)(2,1)}, u32[]{:S(2)}, u32[]{:S(2)}) collective-permute-start(bf16[32,64]{0,1:T(8,128)(2,1)} %get-tuple-element.562), channel_id=1, source_target_pairs={{0,16},{16,0},{1,17},{17,1},{2,18},{18,2},{3,19},{19,3},{4,20},{20... | collective-permute-start | bytes 12296 | tf_op jit(solution)/shard_map/ppermute | solution.py:413
  15.6 146.8 %collective-permute-start.10 = (bf16[512,768]{1,0:T(8,128)(2,1)S(1)}, bf16[512,768]{1,0:T(8,128)(2,1)}, u32[]{:S(2)}, u32[]{:S(2)}) collective-permute-start(bf16[512,768]{1,0:T(8,128)(2,1)S(1)} %get-tuple-element.106), channel_id=1, source_target_pairs={{0,4},{4,0},{8,12},{12,8},{1,5},{5,1},{9,13},{13,9},{2,6},{6,2},{1... | collective-permute-start | bytes 2359304 | tf_op jit(solution)/shard_map/ppermute | solution.py:382
  18.5 31.2 %collective-permute-start.20 = (bf16[32,16]{0,1:T(8,128)(2,1)}, bf16[32,16]{0,1:T(8,128)(2,1)}, u32[]{:S(2)}, u32[]{:S(2)}) collective-permute-start(bf16[32,16]{0,1:T(8,128)(2,1)} %bitcast.379), channel_id=1, source_target_pairs={{0,3},{1,2},{2,1},{3,0},{4,7},{5,6},{6,5},{7,4},{8,11},{9,10},{10,... | collective-permute-start | bytes 3080 | tf_op jit(solution)/shard_map/ppermute | solution.py:379
  19.5 31.8 %collective-permute-start.21 = (bf16[32,16]{0,1:T(8,128)(2,1)}, bf16[32,16]{0,1:T(8,128)(2,1)}, u32[]{:S(2)}, u32[]{:S(2)}) collective-permute-start(bf16[32,16]{0,1:T(8,128)(2,1)} %bitcast.378), channel_id=1, source_target_pairs={{0,2},{1,3},{2,0},{3,1},{4,6},{5,7},{6,4},{7,5},{8,10},{9,11},{10,... | collective-permute-start | bytes 3080 | tf_op jit(solution)/shard_map/ppermute | solution.py:379
  21.2 30.5 %collective-permute-start.22 = (bf16[32,16]{0,1:T(8,128)(2,1)}, bf16[32,16]{0,1:T(8,128)(2,1)}, u32[]{:S(2)}, u32[]{:S(2)}) collective-permute-start(bf16[32,16]{0,1:T(8,128)(2,1)} %bitcast.377), channel_id=1, source_target_pairs={{0,1},{1,0},{2,3},{3,2},{4,5},{5,4},{6,7},{7,6},{8,9},{9,8},{10,11... | collective-permute-start | bytes 3080 | tf_op jit(solution)/shard_map/ppermute | solution.py:379
  49.7 115.3 %collective-permute-start.11 = (bf16[512,768]{1,0:T(8,128)(2,1)S(1)}, bf16[512,768]{1,0:T(8,128)(2,1)}, u32[]{:S(2)}, u32[]{:S(2)}) collective-permute-start(bf16[512,768]{1,0:T(8,128)(2,1)S(1)} %get-tuple-element.107), channel_id=1, source_target_pairs={{0,8},{4,12},{8,0},{12,4},{1,9},{5,13},{9,1},{13,5},{2,10},{6,14},... | collective-permute-start | bytes 2359304 | tf_op jit(solution)/shard_map/ppermute | solution.py:382
  51.3 115.8 %collective-permute-start.12 = (bf16[512,768]{1,0:T(8,128)(2,1)S(1)}, bf16[512,768]{1,0:T(8,128)(2,1)}, u32[]{:S(2)}, u32[]{:S(2)}) collective-permute-start(bf16[512,768]{1,0:T(8,128)(2,1)S(1)} %get-tuple-element.108), channel_id=1, source_target_pairs={{0,12},{4,8},{8,4},{12,0},{1,13},{5,9},{9,5},{13,1},{2,14},{6,10},... | collective-permute-start | bytes 2359304 | tf_op jit(solution)/shard_map/ppermute | solution.py:382
  54.0 32.4 %collective-permute-start.4 = (bf16[64,32]{0,1:T(8,128)(2,1)S(1)}, bf16[64,32]{0,1:T(8,128)(2,1)S(1)}, u32[]{:S(2)}, u32[]{:S(2)}) collective-permute-start(bf16[64,32]{0,1:T(8,128)(2,1)S(1)} %pad_maximum_fusion.43), channel_id=1, source_target_pairs={{0,8},{1,9},{2,10},{3,11},{4,12},{5,13},{6,14},{7,15},{8,0},{9,1},... | collective-permute-start | bytes 12296 | tf_op jit(solution)/shard_map/ppermute | solution.py:379
  56.0 55.1 %collective-permute-start.23 = (f32[64,32]{1,0:T(8,128)S(1)}, f32[64,32]{1,0:T(8,128)S(1)}, u32[]{:S(2)}, u32[]{:S(2)}) collective-permute-start(f32[64,32]{1,0:T(8,128)S(1)} %select_reduce_fusion), channel_id=1, source_target_pairs={{0,1},{1,0},{2,3},{3,2},{4,5},{5,4},{6,7},{7,6},{8,9},{9,8},{10,11... | collective-permute-start | bytes 24584 | tf_op jit(solution)/shard_map/ppermute | solution.py:379
  119.9 34.3 %collective-permute-start.26 = (f32[64,32]{1,0:T(8,128)S(1)}, f32[64,32]{1,0:T(8,128)}, u32[]{:S(2)}, u32[]{:S(2)}) collective-permute-start(f32[64,32]{1,0:T(8,128)S(1)} %add.791), channel_id=1, source_target_pairs={{0,8},{1,9},{2,10},{3,11},{4,12},{5,13},{6,14},{7,15},{8,0},{9,1},... | collective-permute-start | bytes 24584 | tf_op jit(solution)/shard_map/ppermute | solution.py:379
  174.7 103.8 %collective-permute-start.13 = (bf16[1024,768]{1,0:T(8,128)(2,1)S(1)}, bf16[1024,768]{1,0:T(8,128)(2,1)S(1)}, u32[]{:S(2)}, u32[]{:S(2)}) collective-permute-start(bf16[1024,768]{1,0:T(8,128)(2,1)S(1)} %convolution_convert_fusion.7), channel_id=1, source_target_pairs={{0,16},{16,0},{1,17},{17,1},{2,18},{18,2},{3,19},{19,3},{4,20},{20... | collective-permute-start | bytes 4718600 | tf_op jit(solution)/shard_map/ppermute | solution.py:413
  175.1 40.5 %collective-permute-start.16 = (bf16[512,256]{1,0:T(8,128)(2,1)S(1)}, bf16[512,256]{1,0:T(8,128)(2,1)S(1)}, u32[]{:S(2)}, u32[]{:S(2)}) collective-permute-start(bf16[512,256]{1,0:T(8,128)(2,1)S(1)} %get-tuple-element.121), channel_id=1, source_target_pairs={{0,12},{4,8},{8,4},{12,0},{1,13},{5,9},{9,5},{13,1},{2,14},{6,10},... | collective-permute-start | bytes 786440 | tf_op jit(solution)/shard_map/ppermute | solution.py:382
  181.9 94.1 %collective-permute-start.19 = (bf16[512,1024]{1,0:T(8,128)(2,1)S(1)}, bf16[512,1024]{1,0:T(8,128)(2,1)S(1)}, u32[]{:S(2)}, u32[]{:S(2)}) collective-permute-start(bf16[512,1024]{1,0:T(8,128)(2,1)S(1)} %get-tuple-element.125), channel_id=1, source_target_pairs={{0,12},{4,8},{8,4},{12,0},{1,13},{5,9},{9,5},{13,1},{2,14},{6,10},... | collective-permute-start | bytes 3145736 | tf_op jit(solution)/shard_map/ppermute | solution.py:382
  184.5 91.5 %collective-permute-start.18 = (bf16[512,1024]{1,0:T(8,128)(2,1)S(1)}, bf16[512,1024]{1,0:T(8,128)(2,1)S(1)}, u32[]{:S(2)}, u32[]{:S(2)}) collective-permute-start(bf16[512,1024]{1,0:T(8,128)(2,1)S(1)} %get-tuple-element.124), channel_id=1, source_target_pairs={{0,8},{4,12},{8,0},{12,4},{1,9},{5,13},{9,1},{13,5},{2,10},{6,14},... | collective-permute-start | bytes 3145736 | tf_op jit(solution)/shard_map/ppermute | solution.py:382
  185.7 90.3 %collective-permute-start.17 = (bf16[512,1024]{1,0:T(8,128)(2,1)S(1)}, bf16[512,1024]{1,0:T(8,128)(2,1)S(1)}, u32[]{:S(2)}, u32[]{:S(2)}) collective-permute-start(bf16[512,1024]{1,0:T(8,128)(2,1)S(1)} %get-tuple-element.123), channel_id=1, source_target_pairs={{0,4},{4,0},{8,12},{12,8},{1,5},{5,1},{9,13},{13,9},{2,6},{6,2},{1... | collective-permute-start | bytes 3145736 | tf_op jit(solution)/shard_map/ppermute | solution.py:382
  215.7 53.5 %collective-permute-start.15 = (bf16[512,256]{1,0:T(8,128)(2,1)S(1)}, bf16[512,256]{1,0:T(8,128)(2,1)S(1)}, u32[]{:S(2)}, u32[]{:S(2)}) collective-permute-start(bf16[512,256]{1,0:T(8,128)(2,1)S(1)} %get-tuple-element.120), channel_id=1, source_target_pairs={{0,8},{4,12},{8,0},{12,4},{1,9},{5,13},{9,1},{13,5},{2,10},{6,14},... | collective-permute-start | bytes 786440 | tf_op jit(solution)/shard_map/ppermute | solution.py:382
  314.0 32.6 %collective-permute-start.40 = (bf16[64,2048]{0,1:T(8,128)(2,1)S(1)}, bf16[64,2048]{0,1:T(8,128)(2,1)S(1)}, u32[]{:S(2)}, u32[]{:S(2)}) collective-permute-start(bf16[64,2048]{0,1:T(8,128)(2,1)S(1)} %get-tuple-element.384), channel_id=1, source_target_pairs={{0,14},{1,15},{2,12},{3,13},{4,10},{5,11},{6,8},{7,9},{8,6},{9,7},... | collective-permute-start | bytes 786440 | tf_op jit(solution)/shard_map/ppermute | solution.py:379
  316.8 40.2 %collective-permute-start.39 = (bf16[64,2048]{0,1:T(8,128)(2,1)S(1)}, bf16[64,2048]{0,1:T(8,128)(2,1)S(1)}, u32[]{:S(2)}, u32[]{:S(2)}) collective-permute-start(bf16[64,2048]{0,1:T(8,128)(2,1)S(1)} %get-tuple-element.385), channel_id=1, source_target_pairs={{0,12},{1,13},{2,14},{3,15},{4,8},{5,9},{6,10},{7,11},{8,4},{9,5},... | collective-permute-start | bytes 786440 | tf_op jit(solution)/shard_map/ppermute | solution.py:379
  317.3 55.7 %collective-permute-start.37 = (bf16[64,2048]{0,1:T(8,128)(2,1)S(1)}, bf16[64,2048]{0,1:T(8,128)(2,1)S(1)}, u32[]{:S(2)}, u32[]{:S(2)}) collective-permute-start(bf16[64,2048]{0,1:T(8,128)(2,1)S(1)} %get-tuple-element.387), channel_id=1, source_target_pairs={{0,8},{1,9},{2,10},{3,11},{4,12},{5,13},{6,14},{7,15},{8,0},{9,1},... | collective-permute-start | bytes 786440 | tf_op jit(solution)/shard_map/ppermute | solution.py:379
  319.8 44.3 %collective-permute-start.36 = (bf16[64,2048]{0,1:T(8,128)(2,1)S(1)}, bf16[64,2048]{0,1:T(8,128)(2,1)S(1)}, u32[]{:S(2)}, u32[]{:S(2)}) collective-permute-start(bf16[64,2048]{0,1:T(8,128)(2,1)S(1)} %get-tuple-element.388), channel_id=1, source_target_pairs={{0,6},{1,7},{2,4},{3,5},{4,2},{5,3},{6,0},{7,1},{8,14},{9,15},{10,... | collective-permute-start | bytes 786440 | tf_op jit(solution)/shard_map/ppermute | solution.py:379
  335.4 37.6 %collective-permute-start.35 = (bf16[64,2048]{0,1:T(8,128)(2,1)S(1)}, bf16[64,2048]{0,1:T(8,128)(2,1)S(1)}, u32[]{:S(2)}, u32[]{:S(2)}) collective-permute-start(bf16[64,2048]{0,1:T(8,128)(2,1)S(1)} %get-tuple-element.389), channel_id=1, source_target_pairs={{0,4},{1,5},{2,6},{3,7},{4,0},{5,1},{6,2},{7,3},{8,12},{9,13},{10,... | collective-permute-start | bytes 786440 | tf_op jit(solution)/shard_map/ppermute | solution.py:379
  387.2 50.7 %collective-permute-start.42 = (bf16[64,2048]{0,1:T(8,128)(2,1)S(1)}, bf16[64,2048]{0,1:T(8,128)(2,1)}, u32[]{:S(2)}, u32[]{:S(2)}) collective-permute-start(bf16[64,2048]{0,1:T(8,128)(2,1)S(1)} %multiply_convert_fusion.9), channel_id=1, source_target_pairs={{0,2},{1,3},{2,0},{3,1},{4,6},{5,7},{6,4},{7,5},{8,10},{9,11},{10,... | collective-permute-start | bytes 786440 | tf_op jit(solution)/shard_map/ppermute | solution.py:379
  388.4 45.7 %collective-permute-start.44 = (bf16[64,2048]{0,1:T(8,128)(2,1)S(1)}, bf16[64,2048]{0,1:T(8,128)(2,1)S(1)}, u32[]{:S(2)}, u32[]{:S(2)}) collective-permute-start(bf16[64,2048]{0,1:T(8,128)(2,1)S(1)} %multiply_convert_fusion.9), channel_id=1, source_target_pairs={{0,6},{1,7},{2,4},{3,5},{4,2},{5,3},{6,0},{7,1},{8,14},{9,15},{10,... | collective-permute-start | bytes 786440 | tf_op jit(solution)/shard_map/ppermute | solution.py:379
  399.3 36.7 %collective-permute-start.47 = (bf16[64,2048]{0,1:T(8,128)(2,1)S(1)}, bf16[64,2048]{0,1:T(8,128)(2,1)S(1)}, u32[]{:S(2)}, u32[]{:S(2)}) collective-permute-start(bf16[64,2048]{0,1:T(8,128)(2,1)S(1)} %multiply_convert_fusion.9), channel_id=1, source_target_pairs={{0,12},{1,13},{2,14},{3,15},{4,8},{5,9},{6,10},{7,11},{8,4},{9,5},... | collective-permute-start | bytes 786440 | tf_op jit(solution)/shard_map/ppermute | solution.py:379
  452.6 72.0 %collective-permute-start.50 = (bf16[512,1024]{1,0:T(8,128)(2,1)S(1)}, bf16[512,1024]{1,0:T(8,128)(2,1)S(1)}, u32[]{:S(2)}, u32[]{:S(2)}) collective-permute-start(bf16[512,1024]{1,0:T(8,128)(2,1)S(1)} %convolution_convert_fusion.11), channel_id=1, source_target_pairs={{0,16},{16,0},{1,17},{17,1},{2,18},{18,2},{3,19},{19,3},{4,20},{20... | collective-permute-start | bytes 3145736 | tf_op jit(solution)/shard_map/ppermute | solution.py:413
  454.7 91.8 %collective-permute-start.51 = (bf16[512,1024]{1,0:T(8,128)(2,1)S(1)}, bf16[512,1024]{1,0:T(8,128)(2,1)S(1)}, u32[]{:S(2)}, u32[]{:S(2)}) collective-permute-start(bf16[512,1024]{1,0:T(8,128)(2,1)S(1)} %convolution_convert_fusion.10), channel_id=1, source_target_pairs={{0,16},{16,0},{1,17},{17,1},{2,18},{18,2},{3,19},{19,3},{4,20},{20... | collective-permute-start | bytes 3145736 | tf_op jit(solution)/shard_map/ppermute | solution.py:413
  455.6 91.3 %collective-permute-start.54 = (bf16[512,1024]{1,0:T(8,128)(2,1)S(1)}, bf16[512,1024]{1,0:T(8,128)(2,1)S(1)}, u32[]{:S(2)}, u32[]{:S(2)}) collective-permute-start(bf16[512,1024]{1,0:T(8,128)(2,1)S(1)} %copy-done.10), channel_id=1, source_target_pairs={{0,12},{4,8},{8,4},{12,0},{1,13},{5,9},{9,5},{13,1},{2,14},{6,10},... | collective-permute-start | bytes 3145736 | tf_op jit(solution)/shard_map/ppermute | solution.py:382
  457.2 90.5 %collective-permute-start.53 = (bf16[512,1024]{1,0:T(8,128)(2,1)S(1)}, bf16[512,1024]{1,0:T(8,128)(2,1)S(1)}, u32[]{:S(2)}, u32[]{:S(2)}) collective-permute-start(bf16[512,1024]{1,0:T(8,128)(2,1)S(1)} %get-tuple-element.144), channel_id=1, source_target_pairs={{0,8},{4,12},{8,0},{12,4},{1,9},{5,13},{9,1},{13,5},{2,10},{6,14},... | collective-permute-start | bytes 3145736 | tf_op jit(solution)/shard_map/ppermute | solution.py:382
  458.1 89.6 %collective-permute-start.52 = (bf16[512,1024]{1,0:T(8,128)(2,1)S(1)}, bf16[512,1024]{1,0:T(8,128)(2,1)S(1)}, u32[]{:S(2)}, u32[]{:S(2)}) collective-permute-start(bf16[512,1024]{1,0:T(8,128)(2,1)S(1)} %get-tuple-element.143), channel_id=1, source_target_pairs={{0,4},{4,0},{8,12},{12,8},{1,5},{5,1},{9,13},{13,9},{2,6},{6,2},{1... | collective-permute-start | bytes 3145736 | tf_op jit(solution)/shard_map/ppermute | solution.py:382
  562.5 56.1 %collective-permute-start.56 = (bf16[64,2048]{0,1:T(8,128)(2,1)S(1)}, bf16[64,2048]{0,1:T(8,128)(2,1)S(1)}, u32[]{:S(2)}, u32[]{:S(2)}) collective-permute-start(bf16[64,2048]{0,1:T(8,128)(2,1)S(1)} %get-tuple-element.382), channel_id=1, source_target_pairs={{0,2},{1,3},{2,0},{3,1},{4,6},{5,7},{6,4},{7,5},{8,10},{9,11},{10,... | collective-permute-start | bytes 786440 | tf_op jit(solution)/shard_map/ppermute | solution.py:379
  563.2 34.2 %collective-permute-start.58 = (bf16[64,2048]{0,1:T(8,128)(2,1)}, bf16[64,2048]{0,1:T(8,128)(2,1)S(1)}, u32[]{:S(2)}, u32[]{:S(2)}) collective-permute-start(bf16[64,2048]{0,1:T(8,128)(2,1)} %get-tuple-element.380), channel_id=1, source_target_pairs={{0,6},{1,7},{2,4},{3,5},{4,2},{5,3},{6,0},{7,1},{8,14},{9,15},{10,... | collective-permute-start | bytes 786440 | tf_op jit(solution)/shard_map/ppermute | solution.py:379
  565.0 53.6 %collective-permute-start.60 = (bf16[64,2048]{0,1:T(8,128)(2,1)S(1)}, bf16[64,2048]{0,1:T(8,128)(2,1)S(1)}, u32[]{:S(2)}, u32[]{:S(2)}) collective-permute-start(bf16[64,2048]{0,1:T(8,128)(2,1)S(1)} %get-tuple-element.378), channel_id=1, source_target_pairs={{0,10},{1,11},{2,8},{3,9},{4,14},{5,15},{6,12},{7,13},{8,2},{9,3},... | collective-permute-start | bytes 786440 | tf_op jit(solution)/shard_map/ppermute | solution.py:379
  576.4 31.5 %collective-permute-start.61 = (bf16[64,2048]{0,1:T(8,128)(2,1)}, bf16[64,2048]{0,1:T(8,128)(2,1)S(1)}, u32[]{:S(2)}, u32[]{:S(2)}) collective-permute-start(bf16[64,2048]{0,1:T(8,128)(2,1)} %get-tuple-element.377), channel_id=1, source_target_pairs={{0,12},{1,13},{2,14},{3,15},{4,8},{5,9},{6,10},{7,11},{8,4},{9,5},... | collective-permute-start | bytes 786440 | tf_op jit(solution)/shard_map/ppermute | solution.py:379
  577.8 40.7 %collective-permute-start.62 = (bf16[64,2048]{0,1:T(8,128)(2,1)}, bf16[64,2048]{0,1:T(8,128)(2,1)S(1)}, u32[]{:S(2)}, u32[]{:S(2)}) collective-permute-start(bf16[64,2048]{0,1:T(8,128)(2,1)} %get-tuple-element.376), channel_id=1, source_target_pairs={{0,14},{1,15},{2,12},{3,13},{4,10},{5,11},{6,8},{7,9},{8,6},{9,7},... | collective-permute-start | bytes 786440 | tf_op jit(solution)/shard_map/ppermute | solution.py:379
  717.1 38.6 %collective-permute-start.102 = (bf16[1024,256]{1,0:T(8,128)(2,1)}, bf16[1024,256]{1,0:T(8,128)(2,1)}, u32[]{:S(2)}, u32[]{:S(2)}) collective-permute-start(bf16[1024,256]{1,0:T(8,128)(2,1)} %get-tuple-element.390), channel_id=1, source_target_pairs={{0,4},{4,0},{1,5},{5,1},{2,6},{6,2},{3,7},{7,3},{8,12},{12,8},{9,1... | collective-permute-start | bytes 1572872 | tf_op jit(solution)/shard_map/ppermute | solution.py:476
  757.6 51.8 %collective-permute-start.65 = (bf16[64,2048]{0,1:T(8,128)(2,1)}, bf16[64,2048]{0,1:T(8,128)(2,1)}, u32[]{:S(2)}, u32[]{:S(2)}) collective-permute-start(bf16[64,2048]{0,1:T(8,128)(2,1)} %pad_maximum_fusion.19), channel_id=1, source_target_pairs={{0,2},{1,3},{2,0},{3,1},{4,6},{5,7},{6,4},{7,5},{8,10},{9,11},{10,... | collective-permute-start | bytes 786440 | tf_op jit(solution)/shard_map/ppermute | solution.py:379
  758.3 37.5 %collective-permute-start.66 = (bf16[64,2048]{0,1:T(8,128)(2,1)}, bf16[64,2048]{0,1:T(8,128)(2,1)S(1)}, u32[]{:S(2)}, u32[]{:S(2)}) collective-permute-start(bf16[64,2048]{0,1:T(8,128)(2,1)} %pad_maximum_fusion.19), channel_id=1, source_target_pairs={{0,4},{1,5},{2,6},{3,7},{4,0},{5,1},{6,2},{7,3},{8,12},{9,13},{10,... | collective-permute-start | bytes 786440 | tf_op jit(solution)/shard_map/ppermute | solution.py:379
  759.3 46.3 %collective-permute-start.67 = (bf16[64,2048]{0,1:T(8,128)(2,1)}, bf16[64,2048]{0,1:T(8,128)(2,1)S(1)}, u32[]{:S(2)}, u32[]{:S(2)}) collective-permute-start(bf16[64,2048]{0,1:T(8,128)(2,1)} %pad_maximum_fusion.19), channel_id=1, source_target_pairs={{0,6},{1,7},{2,4},{3,5},{4,2},{5,3},{6,0},{7,1},{8,14},{9,15},{10,... | collective-permute-start | bytes 786440 | tf_op jit(solution)/shard_map/ppermute | solution.py:379
  761.1 46.3 %collective-permute-start.70 = (bf16[64,2048]{0,1:T(8,128)(2,1)}, bf16[64,2048]{0,1:T(8,128)(2,1)S(1)}, u32[]{:S(2)}, u32[]{:S(2)}) collective-permute-start(bf16[64,2048]{0,1:T(8,128)(2,1)} %pad_maximum_fusion.19), channel_id=1, source_target_pairs={{0,12},{1,13},{2,14},{3,15},{4,8},{5,9},{6,10},{7,11},{8,4},{9,5},... | collective-permute-start | bytes 786440 | tf_op jit(solution)/shard_map/ppermute | solution.py:379
  771.9 35.6 %collective-permute-start.71 = (bf16[64,2048]{0,1:T(8,128)(2,1)}, bf16[64,2048]{0,1:T(8,128)(2,1)S(1)}, u32[]{:S(2)}, u32[]{:S(2)}) collective-permute-start(bf16[64,2048]{0,1:T(8,128)(2,1)} %pad_maximum_fusion.19), channel_id=1, source_target_pairs={{0,14},{1,15},{2,12},{3,13},{4,10},{5,11},{6,8},{7,9},{8,6},{9,7},... | collective-permute-start | bytes 786440 | tf_op jit(solution)/shard_map/ppermute | solution.py:379
  833.4 71.6 %collective-permute-start.73 = (bf16[512,1024]{1,0:T(8,128)(2,1)}, bf16[512,1024]{1,0:T(8,128)(2,1)}, u32[]{:S(2)}, u32[]{:S(2)}) collective-permute-start(bf16[512,1024]{1,0:T(8,128)(2,1)} %convolution_convert_fusion.9), channel_id=1, source_target_pairs={{0,16},{16,0},{1,17},{17,1},{2,18},{18,2},{3,19},{19,3},{4,20},{20... | collective-permute-start | bytes 3145736 | tf_op jit(solution)/shard_map/ppermute | solution.py:413
  833.8 126.3 %collective-permute-start.74 = (bf16[512,1024]{1,0:T(8,128)(2,1)}, bf16[512,1024]{1,0:T(8,128)(2,1)}, u32[]{:S(2)}, u32[]{:S(2)}) collective-permute-start(bf16[512,1024]{1,0:T(8,128)(2,1)} %convolution_convert_fusion.8), channel_id=1, source_target_pairs={{0,16},{16,0},{1,17},{17,1},{2,18},{18,2},{3,19},{19,3},{4,20},{20... | collective-permute-start | bytes 3145736 | tf_op jit(solution)/shard_map/ppermute | solution.py:413
  840.4 137.3 %collective-permute-start.75 = (bf16[512,1024]{1,0:T(8,128)(2,1)}, bf16[512,1024]{1,0:T(8,128)(2,1)}, u32[]{:S(2)}, u32[]{:S(2)}) collective-permute-start(bf16[512,1024]{1,0:T(8,128)(2,1)} %get-tuple-element.672), channel_id=1, source_target_pairs={{0,4},{4,0},{8,12},{12,8},{1,5},{5,1},{9,13},{13,9},{2,6},{6,2},{1... | collective-permute-start | bytes 3145736 | tf_op jit(solution)/shard_map/ppermute | solution.py:382
  860.1 117.6 %collective-permute-start.76 = (bf16[512,1024]{1,0:T(8,128)(2,1)}, bf16[512,1024]{1,0:T(8,128)(2,1)}, u32[]{:S(2)}, u32[]{:S(2)}) collective-permute-start(bf16[512,1024]{1,0:T(8,128)(2,1)} %get-tuple-element.674), channel_id=1, source_target_pairs={{0,8},{4,12},{8,0},{12,4},{1,9},{5,13},{9,1},{13,5},{2,10},{6,14},... | collective-permute-start | bytes 3145736 | tf_op jit(solution)/shard_map/ppermute | solution.py:382
  877.2 100.4 %collective-permute-start.77 = (bf16[512,1024]{1,0:T(8,128)(2,1)}, bf16[512,1024]{1,0:T(8,128)(2,1)S(1)}, u32[]{:S(2)}, u32[]{:S(2)}) collective-permute-start(bf16[512,1024]{1,0:T(8,128)(2,1)} %get-tuple-element.676), channel_id=1, source_target_pairs={{0,12},{4,8},{8,4},{12,0},{1,13},{5,9},{9,5},{13,1},{2,14},{6,10},... | collective-permute-start | bytes 3145736 | tf_op jit(solution)/shard_map/ppermute | solution.py:382
  905.0 55.0 %collective-permute-start.81 = (f32[641,128]{1,0:T(8,128)S(1)}, f32[641,128]{1,0:T(8,128)S(1)}, u32[]{:S(2)}, u32[]{:S(2)}) collective-permute-start(f32[641,128]{1,0:T(8,128)S(1)} %fusion.321), channel_id=1, source_target_pairs={{0,8},{1,9},{2,10},{3,11},{4,12},{5,13},{6,14},{7,15},{8,0},{9,1},... | collective-permute-start | bytes 984584 | tf_op jit(solution)/shard_map/ppermute | solution.py:379
  1004.2 39.3 %collective-permute-start.90 = (bf16[64,2048]{0,1:T(8,128)(2,1)S(1)}, bf16[64,2048]{0,1:T(8,128)(2,1)S(1)}, u32[]{:S(2)}, u32[]{:S(2)}) collective-permute-start(bf16[64,2048]{0,1:T(8,128)(2,1)S(1)} %get-tuple-element.368), channel_id=1, source_target_pairs={{0,14},{1,15},{2,12},{3,13},{4,10},{5,11},{6,8},{7,9},{8,6},{9,7},... | collective-permute-start | bytes 786440 | tf_op jit(solution)/shard_map/ppermute | solution.py:379
  1004.9 37.6 %collective-permute-start.88 = (bf16[64,2048]{0,1:T(8,128)(2,1)S(1)}, bf16[64,2048]{0,1:T(8,128)(2,1)S(1)}, u32[]{:S(2)}, u32[]{:S(2)}) collective-permute-start(bf16[64,2048]{0,1:T(8,128)(2,1)S(1)} %get-tuple-element.370), channel_id=1, source_target_pairs={{0,10},{1,11},{2,8},{3,9},{4,14},{5,15},{6,12},{7,13},{8,2},{9,3},... | collective-permute-start | bytes 786440 | tf_op jit(solution)/shard_map/ppermute | solution.py:379
  1009.9 43.1 %collective-permute-start.89 = (bf16[64,2048]{0,1:T(8,128)(2,1)S(1)}, bf16[64,2048]{0,1:T(8,128)(2,1)S(1)}, u32[]{:S(2)}, u32[]{:S(2)}) collective-permute-start(bf16[64,2048]{0,1:T(8,128)(2,1)S(1)} %get-tuple-element.369), channel_id=1, source_target_pairs={{0,12},{1,13},{2,14},{3,15},{4,8},{5,9},{6,10},{7,11},{8,4},{9,5},... | collective-permute-start | bytes 786440 | tf_op jit(solution)/shard_map/ppermute | solution.py:379
  1010.3 53.9 %collective-permute-start.87 = (bf16[64,2048]{0,1:T(8,128)(2,1)S(1)}, bf16[64,2048]{0,1:T(8,128)(2,1)S(1)}, u32[]{:S(2)}, u32[]{:S(2)}) collective-permute-start(bf16[64,2048]{0,1:T(8,128)(2,1)S(1)} %get-tuple-element.371), channel_id=1, source_target_pairs={{0,8},{1,9},{2,10},{3,11},{4,12},{5,13},{6,14},{7,15},{8,0},{9,1},... | collective-permute-start | bytes 786440 | tf_op jit(solution)/shard_map/ppermute | solution.py:379
  1012.4 40.7 %collective-permute-start.86 = (bf16[64,2048]{0,1:T(8,128)(2,1)S(1)}, bf16[64,2048]{0,1:T(8,128)(2,1)S(1)}, u32[]{:S(2)}, u32[]{:S(2)}) collective-permute-start(bf16[64,2048]{0,1:T(8,128)(2,1)S(1)} %get-tuple-element.372), channel_id=1, source_target_pairs={{0,6},{1,7},{2,4},{3,5},{4,2},{5,3},{6,0},{7,1},{8,14},{9,15},{10,... | collective-permute-start | bytes 786440 | tf_op jit(solution)/shard_map/ppermute | solution.py:379
  1074.8 32.2 %collective-permute-start.96 = (bf16[64,2048]{0,1:T(8,128)(2,1)S(1)}, bf16[64,2048]{0,1:T(8,128)(2,1)S(1)}, u32[]{:S(2)}, u32[]{:S(2)}) collective-permute-start(bf16[64,2048]{0,1:T(8,128)(2,1)S(1)} %get-tuple-element.349), channel_id=1, source_target_pairs={{0,10},{1,11},{2,8},{3,9},{4,14},{5,15},{6,12},{7,13},{8,2},{9,3},... | collective-permute-start | bytes 786440 | tf_op jit(solution)/shard_map/ppermute | solution.py:379
  1079.1 54.2 %collective-permute-start.92 = (bf16[64,2048]{0,1:T(8,128)(2,1)S(1)}, bf16[64,2048]{0,1:T(8,128)(2,1)}, u32[]{:S(2)}, u32[]{:S(2)}) collective-permute-start(bf16[64,2048]{0,1:T(8,128)(2,1)S(1)} %get-tuple-element.349), channel_id=1, source_target_pairs={{0,2},{1,3},{2,0},{3,1},{4,6},{5,7},{6,4},{7,5},{8,10},{9,11},{10,... | collective-permute-start | bytes 786440 | tf_op jit(solution)/shard_map/ppermute | solution.py:379
  1081.5 48.0 %collective-permute-start.94 = (bf16[64,2048]{0,1:T(8,128)(2,1)S(1)}, bf16[64,2048]{0,1:T(8,128)(2,1)S(1)}, u32[]{:S(2)}, u32[]{:S(2)}) collective-permute-start(bf16[64,2048]{0,1:T(8,128)(2,1)S(1)} %get-tuple-element.349), channel_id=1, source_target_pairs={{0,6},{1,7},{2,4},{3,5},{4,2},{5,3},{6,0},{7,1},{8,14},{9,15},{10,... | collective-permute-start | bytes 786440 | tf_op jit(solution)/shard_map/ppermute | solution.py:379
  1089.6 41.8 %collective-permute-start.97 = (bf16[64,2048]{0,1:T(8,128)(2,1)S(1)}, bf16[64,2048]{0,1:T(8,128)(2,1)S(1)}, u32[]{:S(2)}, u32[]{:S(2)}) collective-permute-start(bf16[64,2048]{0,1:T(8,128)(2,1)S(1)} %get-tuple-element.349), channel_id=1, source_target_pairs={{0,12},{1,13},{2,14},{3,15},{4,8},{5,9},{6,10},{7,11},{8,4},{9,5},... | collective-permute-start | bytes 786440 | tf_op jit(solution)/shard_map/ppermute | solution.py:379
  1174.5 79.0 %collective-permute-start.103 = (bf16[512,1024]{1,0:T(8,128)(2,1)}, bf16[512,1024]{1,0:T(8,128)(2,1)S(1)}, u32[]{:S(2)}, u32[]{:S(2)}) collective-permute-start(bf16[512,1024]{1,0:T(8,128)(2,1)} %get-tuple-element.158), channel_id=1, source_target_pairs={{0,4},{4,0},{8,12},{12,8},{1,5},{5,1},{9,13},{13,9},{2,6},{6,2},{1... | collective-permute-start | bytes 3145736 | tf_op jit(solution)/shard_map/ppermute | solution.py:382
  1175.1 78.3 %collective-permute-start.104 = (bf16[512,1024]{1,0:T(8,128)(2,1)}, bf16[512,1024]{1,0:T(8,128)(2,1)S(1)}, u32[]{:S(2)}, u32[]{:S(2)}) collective-permute-start(bf16[512,1024]{1,0:T(8,128)(2,1)} %get-tuple-element.159), channel_id=1, source_target_pairs={{0,8},{4,12},{8,0},{12,4},{1,9},{5,13},{9,1},{13,5},{2,10},{6,14},... | collective-permute-start | bytes 3145736 | tf_op jit(solution)/shard_map/ppermute | solution.py:382
  1176.7 77.7 %collective-permute-start.105 = (bf16[512,1024]{1,0:T(8,128)(2,1)}, bf16[512,1024]{1,0:T(8,128)(2,1)}, u32[]{:S(2)}, u32[]{:S(2)}) collective-permute-start(bf16[512,1024]{1,0:T(8,128)(2,1)} %get-tuple-element.160), channel_id=1, source_target_pairs={{0,12},{4,8},{8,4},{12,0},{1,13},{5,9},{9,5},{13,1},{2,14},{6,10},... | collective-permute-start | bytes 3145736 | tf_op jit(solution)/shard_map/ppermute | solution.py:382
  1178.0 66.4 %collective-permute-start.106 = (bf16[512,256]{1,0:T(8,128)(2,1)}, bf16[512,256]{1,0:T(8,128)(2,1)S(1)}, u32[]{:S(2)}, u32[]{:S(2)}) collective-permute-start(bf16[512,256]{1,0:T(8,128)(2,1)} %get-tuple-element.162), channel_id=1, source_target_pairs={{0,4},{4,0},{8,12},{12,8},{1,5},{5,1},{9,13},{13,9},{2,6},{6,2},{1... | collective-permute-start | bytes 786440 | tf_op jit(solution)/shard_map/ppermute | solution.py:382
  1196.6 42.6 %collective-permute-start.101 = (bf16[1024,256]{1,0:T(8,128)(2,1)S(1)}, bf16[1024,256]{1,0:T(8,128)(2,1)S(1)}, u32[]{:S(2)}, u32[]{:S(2)}) collective-permute-start(bf16[1024,256]{1,0:T(8,128)(2,1)S(1)} %add_convert_fusion.12), channel_id=1, source_target_pairs={{0,4},{4,0},{1,5},{5,1},{2,6},{6,2},{3,7},{7,3},{8,12},{12,8},{9,1... | collective-permute-start | bytes 1572872 | tf_op jit(solution)/shard_map/ppermute | solution.py:476
  1327.9 62.9 %collective-permute-start.120 = (bf16[512,768]{1,0:T(8,128)(2,1)}, bf16[512,768]{1,0:T(8,128)(2,1)S(1)}, u32[]{:S(2)}, u32[]{:S(2)}) collective-permute-start(bf16[512,768]{1,0:T(8,128)(2,1)} %get-tuple-element.700), channel_id=1, source_target_pairs={{0,4},{4,0},{8,12},{12,8},{1,5},{5,1},{9,13},{13,9},{2,6},{6,2},{1... | collective-permute-start | bytes 2359304 | tf_op jit(solution)/shard_map/ppermute | solution.py:382
  1329.0 61.8 %collective-permute-start.121 = (bf16[512,768]{1,0:T(8,128)(2,1)}, bf16[512,768]{1,0:T(8,128)(2,1)S(1)}, u32[]{:S(2)}, u32[]{:S(2)}) collective-permute-start(bf16[512,768]{1,0:T(8,128)(2,1)} %get-tuple-element.702), channel_id=1, source_target_pairs={{0,8},{4,12},{8,0},{12,4},{1,9},{5,13},{9,1},{13,5},{2,10},{6,14},... | collective-permute-start | bytes 2359304 | tf_op jit(solution)/shard_map/ppermute | solution.py:382
  1329.8 61.0 %collective-permute-start.122 = (bf16[512,768]{1,0:T(8,128)(2,1)}, bf16[512,768]{1,0:T(8,128)(2,1)}, u32[]{:S(2)}, u32[]{:S(2)}) collective-permute-start(bf16[512,768]{1,0:T(8,128)(2,1)} %get-tuple-element.704), channel_id=1, source_target_pairs={{0,12},{4,8},{8,4},{12,0},{1,13},{5,9},{9,5},{13,1},{2,14},{6,10},... | collective-permute-start | bytes 2359304 | tf_op jit(solution)/shard_map/ppermute | solution.py:382
  1334.4 45.0 %collective-permute-start.119 = (f32[560,128]{1,0:T(8,128)S(1)}, f32[560,128]{1,0:T(8,128)S(1)}, u32[]{:S(2)}, u32[]{:S(2)}) collective-permute-start(f32[560,128]{1,0:T(8,128)S(1)} %add.904), channel_id=1, source_target_pairs={{0,16},{16,0},{1,17},{17,1},{2,18},{18,2},{3,19},{19,3},{4,20},{20... | collective-permute-start | bytes 860168 | tf_op jit(solution)/shard_map/ppermute | solution.py:413
  (261 other events, 3524.5 us)

commit v3 on v2

--- a/solution.py
+++ b/solution.py
@@ -212,6 +212,7 @@
 FIRST_SCALE = 1.0 / (1.0 - BETA_FIRST**STEP)
 SECOND_SCALE = 1.0 / (1.0 - BETA_SECOND**STEP)
 UNITS = FF // H
+SOURCES = ((0, 0), (1, 0), (1, HD // 2), (2, 0))
 SECTIONS = ((0, 3, HD), (3 * HD, 1, HD), (4 * HD, 1, UNITS), (4 * HD + UNITS, 1, UNITS))
 
 
@@ -260,39 +261,45 @@
     return a, b, c, d
 
 
-def split_kernel(parts, width, side_ref, weight_ref, *out_refs):
+def split_kernel(sections, side_ref, *refs):
+    weight_refs, out_refs = refs[: len(sections)], refs[len(sections) :]
     q_flag, p_flag = side_ref[0] == 1, side_ref[1] == 1
-    turned = {}
-    for tile, (left, right) in enumerate(tile_pairs(parts, width)):
-        for place in (left, right):
-            group = place // 4
-            if group not in turned:
-                turned[group] = jnp.swapaxes(weight_ref[:, group * 8 : group * 8 + 8, :], 0, 1)
-        values = [turned[t // 4][t % 4 * 2 + head] for head in range(2) for t in (left, right)]
-        lanes = pl.ds(tile * 128, 128)
-        for ref, value in zip(out_refs, cross(q_flag, p_flag, values)):
-            ref[:, lanes] = value.astype(LOW)
-
-
-def split_weights(view, side, offset, parts, width):
+    lane = 0
+    for weight_ref, (_, parts, width) in zip(weight_refs, sections):
+        turned = {}
+        for left, right in tile_pairs(parts, width):
+            for group in (left // 4, right // 4):
+                if group not in turned:
+                    rows = weight_ref[:, group * 8 : group * 8 + 8, :]
+                    turned[group] = jnp.swapaxes(rows, 0, 1)
+            values = [
+                turned[t // 4][t % 4 * 2 + head] for head in range(2) for t in (left, right)
+            ]
+            for ref, value in zip(out_refs, cross(q_flag, p_flag, values)):
+                ref[:, lane : lane + 128] = value.astype(LOW)
+            lane += 128
+
+
+def split_weights(view, side, sections):
     rows = view.shape[0]
-    total = parts * width
-    depth = total // 64
+    total = sum(parts * width for _, parts, width in sections)
     block = 32
+
+    def section_spec(offset, size):
+        return pl.BlockSpec((block, size // 64, 128), lambda i: (i, offset // size, 0))
+
     return pl.pallas_call(
-        functools.partial(split_kernel, parts, width),
+        functools.partial(split_kernel, sections),
         out_shape=[jax.ShapeDtypeStruct((rows, total // 2), LOW)] * SHARERS,
         grid=(rows // block,),
-        in_specs=[
-            pl.BlockSpec(memory_space=pltpu.SMEM),
-            pl.BlockSpec((block, depth, 128), lambda i: (i, offset // total, 0)),
-        ],
+        in_specs=[pl.BlockSpec(memory_space=pltpu.SMEM)]
+        + [section_spec(offset, parts * width) for offset, parts, width in sections],
         out_specs=[pl.BlockSpec((block, total // 2), lambda i: (i, 0))] * SHARERS,
         compiler_params=pltpu.CompilerParams(vmem_limit_bytes=40 * 2**20),
         cost_estimate=pl.CostEstimate(
             flops=rows * total * 2, bytes_accessed=rows * total * 12, transcendentals=0
         ),
-    )(side, view)
+    )(side, *[view] * len(sections))
 
 
 def moments_kernel(side_ref, clip_ref, weight_ref, first_ref, second_ref, *rest):
@@ -306,11 +313,12 @@
 
     update_sq = jnp.zeros((8, 128), WIDE)
     weight_sq = jnp.zeros((8, 128), WIDE)
-    for index, (offset, parts, width) in enumerate(SECTIONS):
+    for (offset, parts, width), (index, lane) in zip(SECTIONS, SOURCES):
         refs = gradients[SHARERS * index : SHARERS * (index + 1)]
         places = {}
         for tile, (left, right) in enumerate(tile_pairs(parts, width)):
-            values = [ref[:, tile * 128 : tile * 128 + 128].astype(WIDE) for ref in refs]
+            lanes = slice(lane + tile * 128, lane + tile * 128 + 128)
+            values = [ref[:, lanes].astype(WIDE) for ref in refs]
             a, b, c, d = cross(q_flag, p_flag, values)
             places[2 * left], places[2 * right] = a, b
             places[2 * left + 1], places[2 * right + 1] = c, d
@@ -363,6 +371,53 @@
     )(side, clip, weight, first, second, *gradients)
 
 
+def join_kernel(*refs):
+    rows = refs[0].shape[0]
+    for k, ref in enumerate(refs[:-1]):
+        refs[-1][k * rows : (k + 1) * rows, :] = ref[...]
+
+
+def join_blocks(parts, turns):
+    rows, columns = parts[0].shape
+    width = columns // SHARERS
+    return pl.pallas_call(
+        join_kernel,
+        out_shape=jax.ShapeDtypeStruct((len(parts) * rows, columns), parts[0].dtype),
+        grid=(SHARERS,),
+        in_specs=[pl.BlockSpec((rows, width), lambda j, t=t: (0, j ^ t)) for t in turns],
+        out_specs=pl.BlockSpec((len(parts) * rows, width), lambda j: (0, j)),
+        cost_estimate=pl.CostEstimate(
+            flops=0, bytes_accessed=4 * len(parts) * rows * columns, transcendentals=0
+        ),
+    )(*parts)
+
+
+def part_kernel(*refs):
+    count = len(refs) // 3
+    for left, right, out in zip(refs[:count], refs[count : 2 * count], refs[2 * count :]):
+        out[...] = (left[...].astype(WIDE) + right[...].astype(WIDE)).astype(out.dtype)
+
+
+def part_sums(left, right, turns):
+    rows, columns = left.shape[0] // len(turns), left.shape[1]
+    width = columns // SHARERS
+    specs = [
+        pl.BlockSpec((rows, width), lambda j, k=k, t=t: (k, j ^ t)) for k, t in enumerate(turns)
+    ]
+    return pl.pallas_call(
+        part_kernel,
+        out_shape=[
+            jax.ShapeDtypeStruct((rows, columns), LOW if k else WIDE) for k in range(len(turns))
+        ],
+        grid=(SHARERS,),
+        in_specs=specs + specs,
+        out_specs=[pl.BlockSpec((rows, width), lambda j: (0, j))] * len(turns),
+        cost_estimate=pl.CostEstimate(
+            flops=left.size, bytes_accessed=6 * left.size, transcendentals=0
+        ),
+    )(*[left] * len(turns), *[right] * len(turns))
+
+
 class Grid:
     def __init__(self, rows, heads):
         self.rows, self.heads = rows // SHARERS, heads
@@ -381,31 +436,37 @@
     def trade(self, values, step):
         return lax.ppermute(values, ("q", "p"), [(i, i ^ step) for i in range(SHARERS)])
 
-    def moved(self, values, step):
-        turn = step // self.heads
-        if turn == 0:
-            return values
-        blocks = jnp.split(values, SHARERS, axis=-1)
-        return jnp.concatenate([blocks[j ^ turn] for j in range(SHARERS)], axis=-1)
+    def turns(self):
+        return [0] + [d // self.heads for d in self.evens]
 
     def spread(self, own):
-        parts = [own] + [self.moved(self.pair(own, d), d) for d in self.evens]
-        half = jnp.concatenate(parts, axis=0)
+        parts = [own] + [self.pair(own, d) for d in self.evens]
+        half = join_blocks(parts, self.turns())
         return half, self.pair(half, 1)
 
     def gathered_sum(self, half, other):
-        rows = half.shape[0] // (self.members // 2)
-        both = half.astype(WIDE) + self.pair(other, 1).astype(WIDE)
-        total = both[:rows]
-        for k, d in enumerate(self.evens, 1):
-            sent = both[k * rows : (k + 1) * rows].astype(LOW)
-            total = total + self.moved(self.pair(sent, d), d).astype(WIDE)
+        parts = part_sums(half, self.pair(other, 1), self.turns())
+        total = parts[0]
+        for part, d in zip(parts[1:], self.evens):
+            total = total + self.pair(part, d).astype(WIDE)
         return total
 
     def group_total(self, values):
         step = 1
         while step < self.members:
             values = values + self.pair(values, step)
+            step *= 2
+        return values
+
+    def every(self, values):
+        step = 1
+        while step < self.members:
+            values = jnp.concatenate([values, self.pair(values, step)], axis=0)
+            step *= 2
+        step = 1
+        while step < self.rows:
+            moved = lax.ppermute(values, "a", [(i, i ^ step) for i in range(self.rows)])
+            values = jnp.concatenate([values, moved], axis=0)
             step *= 2
         return values
 
@@ -553,65 +614,18 @@
     native = grid.each == 2
     side = jnp.stack([lax.axis_index("q"), lax.axis_index("p")]).astype(jnp.int32)
 
-    pieces = []
-    weight_view = native_view(abd_weights) if native else None
-    for offset, parts, width in SECTIONS:
-        if native:
-            pieces.append(split_weights(weight_view, side, offset, parts, width))
-        else:
-            columns = abd_weights[:, :, offset : offset + parts * width]
-            pieces.append(grid.split_plain(columns, parts, width))
-    qkv_pieces, out_pieces, up_pieces, down_pieces = pieces
-
-    def traded(values):
-        return [values[0]] + [grid.trade(values[j], j) for j in (1, 2, 3)]
-
-    qkv_w = jnp.concatenate(traded(qkv_pieces), axis=0)
-
     def own_rows(values):
         return lax.dynamic_slice_in_dim(values, h * own_tokens, own_tokens, 0)
 
-    picked = own_rows(jnp.where(cell_mask == 1, classes, cell_ids)).astype(LOW)
-    picked = jnp.concatenate(grid.row_gather(picked), axis=0)
-    picked = grid.spread(jnp.concatenate(grid.local(picked, 1), axis=1))
-    picked = jnp.concatenate(picked, axis=0)
-    local_attrs = picked.shape[1]
-    tokens = picked.shape[0]
-    held = tokens // grid.members
-    block_attrs = local_attrs // SHARERS
-    table_rows = jnp.arange(block_attrs * entries, dtype=jnp.int32)
-    row_attr, row_entry = table_rows // entries, (table_rows % entries).astype(WIDE)
-    own_block = row_attr[:, None] == (
-        jnp.arange(block_attrs * embed_width, dtype=jnp.int32) // embed_width
-    )
-    hots, embedded = [], []
-    for j, table in enumerate(grid.local(embed_table, 0)):
-        expand = (
-            jnp.arange(local_attrs, dtype=jnp.int32)[:, None]
-            == j * block_attrs + row_attr[None, :]
-        ).astype(LOW)
-        hot = (dot(picked, expand) == row_entry[None, :]).astype(LOW)
-        hots.append(hot)
-        table = table.reshape(block_attrs * entries, embed_width)
-        table = jnp.where(own_block, jnp.tile(table, (1, block_attrs)), 0.0)
-        embedded.append(
-            dot(
-                jnp.concatenate([hot, hot, hot], axis=1),
-                jnp.concatenate(split_three(table), axis=0),
-            )
-        )
-    embedded = jnp.concatenate(embedded, axis=1)
-
-    mask_own = own_rows(cell_mask).astype(WIDE)
-    label_parts = labels.reshape(grid.heads, own_tokens, -1).astype(LOW)
-    label_sent = [
-        lax.dynamic_index_in_dim(label_parts, h ^ d, 0, False) for d in range(grid.heads)
-    ]
-    tables_low = output_table.astype(LOW)
-    label_got, table_got = [label_sent[0]], [tables_low]
-    for d in range(1, grid.heads):
-        label_got.append(grid.pair(label_sent[d], d))
-        table_got.append(grid.pair(tables_low, d))
+    attrs_held = labels.shape[1]
+    mask_held = lax.dynamic_slice_in_dim(cell_mask, h * attrs_held, attrs_held, 1)
+    codes = jnp.where(mask_held == 1, labels, -1).reshape(own_tokens, attr_count)
+    picked = own_rows(jnp.where(cell_mask == 1, classes, cell_ids))
+    gathered = grid.every(jnp.concatenate([picked, codes], axis=1).astype(LOW))
+    tokens = gathered.shape[0]
+    picked_all = gathered[:, :attr_count]
+    codes_all = gathered[:, attr_count:].reshape(-1, grid.heads, own_tokens, attr_count)
+    device = (lax.axis_index("a") * SHARERS + grid.sharer()) * grid.heads + h
 
     def by_head(parts):
         for bit in range((grid.heads - 1).bit_length()):
@@ -621,25 +635,89 @@
             ]
         return parts
 
-    labels_own = jnp.concatenate(by_head(label_got), axis=1).astype(jnp.int32)
-    output_low = jnp.concatenate(by_head(table_got), axis=0)
-    label_hot = (labels_own[:, :, None] == jnp.arange(classes, dtype=jnp.int32)).astype(WIDE)
-    counts = jnp.sum(mask_own[:, :, None] * label_hot, axis=0)
-
+    def pieces_of(sections):
+        if native:
+            return split_weights(weight_view, side, sections)
+        found = []
+        for offset, parts, size in sections:
+            columns = abd_weights[:, :, offset : offset + parts * size]
+            found.append(grid.split_plain(columns, parts, size))
+        return [jnp.concatenate(piece, axis=1) for piece in zip(*found)]
+
+    def traded(values):
+        return [values[0]] + [grid.trade(values[j], j) for j in (1, 2, 3)]
+
+    weight_view = native_view(abd_weights) if native else None
+    qkv_pieces, picked_all, side = tied(pieces_of(SECTIONS[:1]), picked_all, side)
+    qkv_w = traded(qkv_pieces)
+    qkv_w, other_pieces = tied(qkv_w, pieces_of(SECTIONS[1:]))
+    qkv_w = jnp.concatenate(qkv_w, axis=0)
+    others = traded(other_pieces)
+
+    held = tokens // grid.members
+    place = jnp.arange(tokens, dtype=jnp.int32)
+    owner, inside = place // held, place % held
+    owner = 2 * (owner % (grid.members // 2)) + owner // (grid.members // 2)
+    owner = owner ^ (grid.sharer() * grid.heads + h)
+    source = (inside // own_tokens * grid.members + owner) ^ device
+    row_of = source * own_tokens + inside % own_tokens
+    picked = dot((row_of[:, None] == place[None, :]).astype(LOW), picked_all).astype(LOW)
+    picked = jnp.concatenate(grid.local(picked, 1), axis=1)
+    local_attrs = picked.shape[1]
+    block_attrs = local_attrs // SHARERS
+    table_rows = jnp.arange(block_attrs * entries, dtype=jnp.int32)
+    row_attr, row_entry = table_rows // entries, (table_rows % entries).astype(WIDE)
+    block_columns = jnp.arange(block_attrs * embed_width, dtype=jnp.int32)
+    own_block = row_attr[:, None] == block_columns // embed_width
+    fold = (
+        block_columns[:, None] % embed_width == jnp.arange(embed_width, dtype=jnp.int32)
+    ).astype(LOW)
+    table = jnp.concatenate(grid.local(embed_table, 0), axis=0).reshape(-1, embed_width)
+    tables = [dot(piece, fold, 1, 1).astype(LOW) for piece in split_three(table)]
+    hots, embedded = [], []
+    for j in range(SHARERS):
+        expand = (
+            jnp.arange(local_attrs, dtype=jnp.int32)[:, None]
+            == j * block_attrs + row_attr[None, :]
+        ).astype(LOW)
+        hot = (dot(picked, expand) == row_entry[None, :]).astype(LOW)
+        hots.append(hot)
+        cut = slice(j * row_attr.size, (j + 1) * row_attr.size)
+        wide = [jnp.where(own_block, piece[cut], 0.0) for piece in tables]
+        embedded.append(
+            dot(jnp.concatenate([hot, hot, hot], axis=1), jnp.concatenate(wide, axis=0))
+        )
+    embedded = jnp.concatenate(embedded, axis=1)
+
+    kinds = jnp.arange(classes, dtype=jnp.int32).astype(WIDE)
+    mask_own = own_rows(cell_mask).astype(WIDE)
+    counts, own_codes = [], []
+    for d in range(grid.heads):
+        found = (codes_all[:, d].reshape(-1, attr_count)[:, :, None].astype(WIDE) == kinds)
+        found = jnp.sum(found.astype(WIDE), axis=0)
+        counts.append(jnp.sum(found.reshape(-1, attrs_held, classes), axis=0))
+        own_codes.append(own_rows(codes_all[0, d].reshape(-1, attrs_held)))
+    counts = jnp.concatenate(by_head(counts), axis=0)
+    own_codes = jnp.concatenate(by_head(own_codes), axis=1)
+    label_hot = (own_codes.astype(WIDE)[:, :, None] == kinds).astype(WIDE)
+    class_weight = lax.rsqrt(1.0 + counts)
+    weight_total = jnp.sum(counts * class_weight)
+    tables_low = output_table.astype(LOW)[None]
+    step = 1
+    while step < grid.heads:
+        tables_low = jnp.concatenate([tables_low, grid.pair(tables_low, step)], axis=0)
+        step *= 2
+    output_low = jnp.concatenate(by_head(list(tables_low)), axis=0)
+
+    out_size, up_size = HD * grid.each // SHARERS, UNITS * grid.each // SHARERS
     gains = jnp.concatenate(grid.local(abd_gains, 1), axis=1)
     mean_one, scale_one = grid.stats(embedded, model_width)
     hat_one = (embedded - mean_one) * scale_one
     normed = (hat_one * gains[0]).astype(LOW)
-    triple, out_pieces, up_pieces = tied(dot(normed, qkv_w).astype(LOW), out_pieces, up_pieces)
-    triple = grid.row_sum(triple).astype(LOW)
-    out_w = jnp.concatenate(traded(out_pieces), axis=0)
-    up_w = jnp.concatenate(traded(up_pieces), axis=0)
-    counts = grid.total(counts)
-    triple, out_w, up_w, counts, label_hot, output_low, down_pieces = tied(
-        triple, out_w, up_w, counts, label_hot, output_low, down_pieces
-    )
-    class_weight = lax.rsqrt(1.0 + counts)
-    weight_total = jnp.sum(counts * class_weight)
+    triple = grid.row_sum(dot(normed, qkv_w).astype(LOW)).astype(LOW)
+    triple, class_weight, weight_total, label_hot, output_low = tied(
+        triple, class_weight, weight_total, label_hot, output_low
+    )
     part = HD // grid.parts
     query_own, key_own, value_own = (triple[:, i * part : (i + 1) * part] for i in range(3))
     queries, key_rows = grid.columns(query_own), grid.columns(key_own)
@@ -649,16 +727,19 @@
     shifted = jnp.exp(scores - jnp.max(scores, axis=1, keepdims=True))
     probs = shifted / jnp.sum(shifted, axis=1, keepdims=True)
     probs_low = probs.astype(LOW)
-    attended = jnp.split(dot(probs_low, value_own).astype(LOW), 2, axis=0)
+    attended, others = tied(dot(probs_low, value_own).astype(LOW), others)
+    out_w, up_w, down_w = (
+        jnp.concatenate([piece[:, start : start + size] for piece in others], axis=0)
+        for start, size in ((0, out_size), (out_size, up_size), (out_size + up_size, up_size))
+    )
+    attended = jnp.split(attended, 2, axis=0)
     branch = [dot(a, out_w, 1, 1).astype(LOW) for a in attended]
     middle = embedded[:held] + grid.gathered_sum(*branch)
     mean_two, scale_two = grid.stats(middle, model_width)
     hat_two = (middle - mean_two) * scale_two
     second = grid.spread((hat_two * gains[1]).astype(LOW))
-    before, down_pieces = tied([dot(a, up_w).astype(LOW) for a in second], down_pieces)
-    before = [grid.row_sum(b) for b in before]
-    down_w = jnp.concatenate(traded(down_pieces), axis=0)
-    before, down_w = tied(before, down_w)
+    before = jnp.concatenate([dot(a, up_w).astype(LOW) for a in second], axis=0)
+    before = jnp.split(grid.row_sum(before), 2, axis=0)
     hidden = [gelu_apply(b).astype(LOW) for b in before]
     after = middle + grid.gathered_sum(*[dot(a, down_w, 1, 1).astype(LOW) for a in hidden])
 
@@ -696,9 +777,12 @@
     upstream = grid.from_rows(rows_grad.astype(LOW))
     down_grad = grid.spread(upstream)
     hidden_grad, output_part, aba_part, aba_gains_part = tied(
-        [dot(a, down_w).astype(LOW) for a in down_grad], output_part, aba_part, aba_gains_part
-    )
-    hidden_grad = [grid.row_sum(g) for g in hidden_grad]
+        jnp.concatenate([dot(a, down_w).astype(LOW) for a in down_grad], axis=0),
+        output_part,
+        aba_part,
+        aba_gains_part,
+    )
+    hidden_grad = grid.row_sum(hidden_grad)
     down_gradient = traded(row_gradients(down_grad, hidden))
 
     small = jnp.concatenate([aba_part.reshape(-1), aba_gains_part.reshape(-1)])
@@ -724,7 +808,7 @@
         hidden_grad, down_gradient, output_grad, aba_grad, aba_gains_grad
     )
 
-    before_grad = [gelu_back(b, g).astype(LOW) for b, g in zip(before, hidden_grad)]
+    before_grad = [gelu_back(b, g).astype(LOW) for b, g in zip(before, jnp.split(hidden_grad, 2, axis=0))]
     second_grad = grid.gathered_sum(*[dot(a, up_w, 1, 1).astype(LOW) for a in before_grad])
     gained = second_grad * gains[1]
     sums = jnp.stack([jnp.sum(gained, axis=1), jnp.sum(gained * hat_two, axis=1)])
@@ -734,13 +818,16 @@
     )
     gain_two = jnp.sum(second_grad * hat_two, axis=0)
     branch_grad = grid.spread(middle_grad.astype(LOW))
-    attended_grad, up_gradient, out_gradient = tied(
-        jnp.concatenate([dot(a, out_w).astype(LOW) for a in branch_grad], axis=0),
+    attended_grad = jnp.concatenate([dot(a, out_w).astype(LOW) for a in branch_grad], axis=0)
+    attended_grad, second, attended = tied(attended_grad, second, attended)
+    attended_grad = grid.row_sum(attended_grad).astype(LOW)
+    out_gradient, up_gradient = (
+        row_gradients(branch_grad, attended),
         row_gradients(second, before_grad),
-        row_gradients(branch_grad, attended),
-    )
-    attended_grad = grid.row_sum(attended_grad).astype(LOW)
-    up_gradient, out_gradient = traded(up_gradient), traded(out_gradient)
+    )
+    other_gradient = traded(
+        [jnp.concatenate(pair, axis=1) for pair in zip(out_gradient, up_gradient)]
+    )
     prob_grad = dot(grid.columns(attended_grad), value_rows, 1, 1)
     score_grad = probs * (prob_grad - jnp.sum(probs * prob_grad, axis=1, keepdims=True))
     score_grad = score_grad.astype(LOW)
@@ -749,14 +836,12 @@
     value_grad = dot(probs_low, attended_grad, 0, 0)
     triple_grad = jnp.concatenate([query_grad, key_grad, value_grad], axis=1).astype(LOW)
     table_part = [
-        sum(dot(hot[:held], piece, 0, 0) for piece in split_three(block)[:2])
-        for hot, block in zip(hots, jnp.split(middle_grad, SHARERS, axis=1))
+        dot(hot[:held], block, 0, 0)
+        for hot, block in zip(hots, jnp.split(middle_grad.astype(LOW), SHARERS, axis=1))
     ]
-    triple_grad, up_gradient, out_gradient, table_part = tied(
-        triple_grad, up_gradient, out_gradient, table_part
-    )
-    qkv_gradient = traded(row_gradients([normed], [triple_grad]))
-    gradients = qkv_gradient + out_gradient + up_gradient + down_gradient
+    triple_grad, table_part = tied(triple_grad, table_part)
+    qkv_gradient = row_gradients([normed], [triple_grad])
+    triple_grad, qkv_gradient = tied(triple_grad, qkv_gradient)
 
     normed_grad = dot(triple_grad, qkv_w, 1, 1)
     gained = normed_grad * gains[0]
@@ -764,19 +849,19 @@
     sums = sum(grid.row_list(sums)) / model_width
     gain_one = jnp.sum(normed_grad * hat_one, axis=0)
     spread_grad = scale_one * (gained - sums[0][:, None] - hat_one * sums[1][:, None])
-    fold = (
-        jnp.arange(block_attrs * embed_width, dtype=jnp.int32)[:, None] % embed_width
-        == jnp.arange(embed_width, dtype=jnp.int32)
-    ).astype(WIDE)
     records = []
-    for j, block in enumerate(jnp.split(spread_grad, SHARERS, axis=1)):
-        grad = table_part[j] + sum(dot(hots[j], piece, 0, 0) for piece in split_three(block)[:2])
-        grad = jnp.dot(jnp.where(own_block, grad, 0.0), fold, precision=lax.Precision.HIGHEST)
+    for j, block in enumerate(jnp.split(spread_grad.astype(LOW), SHARERS, axis=1)):
+        grad = table_part[j] + dot(hots[j], block, 0, 0)
+        grad = jnp.where(own_block, grad, 0.0)
+        grad = jnp.dot(grad, fold.astype(WIDE), precision=lax.Precision.HIGHEST)
         cut = slice(j * width, (j + 1) * width)
         records.append(jnp.concatenate([grad.reshape(-1), gain_one[cut], gain_two[cut]]))
     table_size = block_attrs * entries * embed_width
     packed = jnp.stack(grid.ordered(records)).reshape(-1, 128)
-    packed = jnp.stack(grid.row_gather(grid.group_total(packed)))
+    packed = grid.group_total(packed)
+    packed, qkv_gradient = tied(packed, traded(qkv_gradient))
+    gradients = qkv_gradient + other_gradient + down_gradient
+    packed = jnp.stack(grid.row_gather(packed))
     packed = packed.reshape(grid.rows * SHARERS, -1)
     embed_grad = packed[:, :table_size].reshape(embed_table.shape)
     abd_gains_grad = packed[:, table_size:].reshape(-1, 2, width).transpose(1, 0, 2)
@@ -806,9 +891,11 @@
         abd_second_new = from_native(second_view, grid.each)
         abd_update_sq, abd_weight_sq = jnp.sum(squares[0]), jnp.sum(squares[1])
     else:
+        qkv_g, other_g, down_g = (gradients[SHARERS * i : SHARERS * (i + 1)] for i in range(3))
+        split_g = (qkv_g, [g[:, :out_size] for g in other_g], [g[:, out_size:] for g in other_g], down_g)
         merged = [
-            grid.merge_plain(gradients[SHARERS * i : SHARERS * (i + 1)], parts, width)
-            for i, (_, parts, width) in enumerate(SECTIONS)
+            grid.merge_plain(pieces, parts, size)
+            for pieces, (_, parts, size) in zip(split_g, SECTIONS)
         ]
         abd_grad = jnp.concatenate(merged, axis=2).astype(WIDE)
         abd_first_new, abd_second_new, abd_update = moments_of(

time: 1540 us -> 1340 us (0.87)
  waiting for transfers between devices: 767 us -> 667 us
  local copies, waits for them, and re-layouts: 145 us -> 97.4 us
  other arithmetic: 171 us -> 126 us
  starting transfers between devices: 139 us -> 116 us
    ppermute x82 -> x70, waiting for transfers between devices: 440 us -> 297 us  [pair(): lax.ppermute(values, ('q', 'p', 'h'), [(i, i ^ step) for i in range(self....]
    ppermute x4, waiting for transfers between devices: 58.7 us -> 131 us  [columns(): got = lax.ppermute(values, 'p', [(i, i ^ d) for i in range(self.parts)])]
    ppermute x24 -> x15, waiting for transfers between devices: 79.6 us -> 12 us  [trade(): lax.ppermute(values, ('q', 'p'), [(i, i ^ step) for i in range(SHARERS)])]
    ppermute x18 -> x14, waiting for transfers between devices: 189 us -> 223 us  [facing(): return lax.ppermute(values, 'a', [(0, 1), (1, 0)])]
    concatenate x6 -> x4, local copies, waits for them, and re-layouts: 25.2 us -> 1.55 us  [the longest x1 1.19 us: per_device(): qkv_w = jnp.concatenate(qkv_w, axis=0)]
    another operation x16 -> x5, local copies, waits for them, and re-layouts: 20.9 us -> 0.46 us  [the longest x4 0.33 us: per_device(): own_codes.append(own_rows(codes_all[0, d].reshape(-1, attrs_held)))]
    ppermute x18 -> x14, starting transfers between devices: 26.9 us -> 10 us  [facing(): return lax.ppermute(values, 'a', [(0, 1), (1, 0)])]
    pallas_call x4 -> x8, Pallas kernels: 37.7 us -> 50.8 us  [the longest x2 25.8 us: split_weights(): pl.pallas_call(functools.partial(split_kernel, sections), out_shape=[jax....]
  transfers between devices with their start and end apart: 128 -> 104, of which waited for: 65 -> 67; matrix products, arithmetic and copies ran while one was open for 16% -> 12% of each run, Pallas kernels for 2% -> 2%
where the time goes in v3:
time: 1340 us; the launch traced here: 1330 us
  waiting for transfers between devices  667 us (50%)
  matrix products  185 us (14%)
  other arithmetic  126 us (9%)
  starting transfers between devices  116 us (9%)
  Pallas kernels  108 us (8%)
  local copies, waits for them, and re-layouts  97.4 us (7%)
  between operations  30.1 us (2%)
    ppermute x70, waiting for transfers between devices, pair(): lax.ppermute(values, ('q', 'p', 'h'), [(i, i ^ step) for i in range(self....  297 us
    ppermute x14, waiting for transfers between devices, facing(): return lax.ppermute(values, 'a', [(0, 1), (1, 0)])  223 us
    dot_general x68, matrix products, dot(): lax.dot_general(left, right, (((left_dim,), (right_dim,)), ((), ())), pre...  154 us
    ppermute x4, waiting for transfers between devices, columns(): got = lax.ppermute(values, 'p', [(i, i ^ d) for i in range(self.parts)])  131 us
    ppermute x70, starting transfers between devices, pair(): lax.ppermute(values, ('q', 'p', 'h'), [(i, i ^ step) for i in range(self....  80.1 us
    pallas_call x1, Pallas kernels, moments_step(): pl.pallas_call(moments_kernel, out_shape=[shape, shape, jax.ShapeDtypeStr...  57.2 us
    unnamed x417, local copies, waits for them, and re-layouts  43.3 us
  transfers between devices with their start and end apart: 104, of which 67 were waited for; matrix products, arithmetic and copies ran while one was open for 12% of the time, Pallas kernels for 2%

profile of v3, /device:TPU:0, one launch (start us, length us, event | category | flops | bytes accessed | tf_op | source)
XLA Modules:
  0.0 1329.5 jit_solution(8450524634214420684)
XLA Ops:
  16.7 11.2 shard_map.364
  41.1 3.8 collective-permute-start.4
  56.9 4.2 fusion.314
  64.4 3.8 fusion.316
  71.1 4.1 fusion.315
  78.1 3.5 multiply_reduce_fusion.3
  88.4 14.7 %shard_map.365 = (bf16[512,2304]{1,0:T(8,128)(2,1)S(1)}, bf16[512,2304]{1,0:T(8,128)(2,1)S(1)}, bf16[512,2304]{1,0:T(8,128)(2,1)S(1)}, bf16[512,2304]{1,0:T(8,128)(2,1)S(1)}) custom-call(s32[2]{0:T(128)S(1)} %pad_add_fusion.side_ref, f32[512,96,128]{2,1,0:T(8,128)} %bitcast.386, f32[512,96,128]{2,1,0:T(8,128)} %bitcast.387, f32[512,96,128]{2,1,0:T(8,128)} %bitcast.388), custom_call_target="tpu_custom_call" | custom-call | flops 4718592 | bytes 28311552 | tf_op jit(solution)/shard_map/pallas_call | solution.py:291
  105.9 4.3 pad_maximum_fusion
  110.3 6.4 collective-permute-done.8
  118.1 4.6 convolution_convert_fusion.10
  127.8 60.2 %collective-permute-done.9 = bf16[1024,768]{1,0:T(8,128)(2,1)} collective-permute-done((bf16[1024,768]{1,0:T(8,128)(2,1)}, bf16[1024,768]{1,0:T(8,128)(2,1)}, u32[]{:S(2)}, u32[]{:S(2)}) %collective-permute-start.9) | collective-permute-done | bytes 1572896 | tf_op jit(solution)/shard_map/ppermute | solution.py:474
  196.9 9.3 collective-permute-done.13
  206.4 110.3 %collective-permute-done.12 = bf16[1024,256]{1,0:T(8,128)(2,1)S(1)} collective-permute-done((bf16[1024,256]{1,0:T(8,128)(2,1)S(1)}, bf16[1024,256]{1,0:T(8,128)(2,1)S(1)}, u32[]{:S(2)}, u32[]{:S(2)}) %collective-permute-start.12) | collective-permute-done | bytes 524320 | tf_op jit(solution)/shard_map/ppermute | solution.py:537
  328.5 4.4 shard_map.366
  345.7 4.1 collective-permute-done.23
  350.3 9.2 collective-permute-done.22
  359.5 3.9 collective-permute-done.21
  367.8 3.6 collective-permute-done.25
  378.7 10.9 collective-permute-done.26.refs_1_
  389.9 4.5 collective-permute-start.32
  397.5 4.1 collective-permute-done.32.refs_7_
  401.7 3.9 shard_map.367
  419.5 92.7 %collective-permute-done.34 = bf16[1024,1024]{1,0:T(8,128)(2,1)S(1)} collective-permute-done((bf16[1024,1024]{1,0:T(8,128)(2,1)S(1)}, bf16[1024,1024]{1,0:T(8,128)(2,1)S(1)}, u32[]{:S(2)}, u32[]{:S(2)}) %collective-permute-start.34) | collective-permute-done | bytes 2097184 | tf_op jit(solution)/shard_map/ppermute | solution.py:474
  515.1 6.6 convolution_convert_fusion.2
  521.8 7.6 convolution_convert_fusion.3.refs_0_.refs_1_.refs_2_.refs_3_.refs_4_.refs_5_.refs_6_.refs_7_
  530.8 4.7 shard_map.368
  541.9 4.9 collective-permute-done.42
  552.9 9.3 collective-permute-done.40
  570.9 12.8 collective-permute-done.43
  643.2 8.6 collective-permute-done.44
  664.2 6.6 collective-permute-done.47.refs_3_
  671.9 6.3 collective-permute-done.50.refs_6_
  681.9 3.8 shard_map.369
  697.4 4.2 convolution_convert_fusion.11
  719.1 3.4 collective-permute-done.58
  728.9 19.4 %collective-permute-done.59 = f32[641,128]{1,0:T(8,128)S(1)} collective-permute-done((f32[641,128]{1,0:T(8,128)S(1)}, f32[641,128]{1,0:T(8,128)S(1)}, u32[]{:S(2)}, u32[]{:S(2)}) %collective-permute-start.59) | collective-permute-done | bytes 328224 | tf_op jit(solution)/shard_map/ppermute | solution.py:434
  755.0 52.1 %collective-permute-done.60 = f32[641,128]{1,0:T(8,128)S(1)} collective-permute-done((f32[641,128]{1,0:T(8,128)S(1)}, f32[641,128]{1,0:T(8,128)S(1)}, u32[]{:S(2)}, u32[]{:S(2)}) %collective-permute-start.60) | collective-permute-done | bytes 328224 | tf_op jit(solution)/shard_map/ppermute | solution.py:434
  809.1 11.7 collective-permute-done.61
  826.0 5.6 collective-permute-done.56.rest_11_
  833.7 6.8 convolution_convert_fusion
  840.6 7.6 convolution_convert_fusion.1.refs_0_.refs_1_.refs_2_.refs_3_.refs_4_.refs_5_.refs_6_.refs_7_
  848.2 4.2 shard_map.370
  860.1 3.7 collective-permute-done.69
  864.8 4.3 collective-permute-done.68
  869.9 9.3 collective-permute-done.67
  879.2 4.0 collective-permute-done.66
  908.3 3.4 collective-permute-start.77
  916.1 4.3 collective-permute-done.75.refs_5_
  920.4 5.2 collective-permute-done.76.refs_6_
  929.2 4.0 shard_map.371
  975.1 19.4 %collective-permute-done.79 = bf16[1024,256]{1,0:T(8,128)(2,1)S(1)} collective-permute-done((bf16[1024,256]{1,0:T(8,128)(2,1)S(1)}, bf16[1024,256]{1,0:T(8,128)(2,1)S(1)}, u32[]{:S(2)}, u32[]{:S(2)}) %collective-permute-start.79) | collective-permute-done | bytes 524320 | tf_op jit(solution)/shard_map/ppermute | solution.py:474
  996.9 11.7 collective-permute-done.80
  1026.2 10.1 multiply_reduce_fusion.1
  1036.5 4.5 collective-permute-done.87
  1041.1 5.8 multiply_convert_fusion
  1088.1 23.2 %collective-permute-done.90 = f32[560,128]{1,0:T(8,128)S(1)} collective-permute-done((f32[560,128]{1,0:T(8,128)S(1)}, f32[560,128]{1,0:T(8,128)S(1)}, u32[]{:S(2)}, u32[]{:S(2)}) %collective-permute-start.90) | collective-permute-done | bytes 286752 | tf_op jit(solution)/shard_map/ppermute | solution.py:434
  1115.0 4.5 collective-permute-done.91
  1127.3 17.1 %collective-permute-done.84 = f32[3]{0:T(128)S(1)} collective-permute-done((f32[3]{0:T(128)S(1)}, f32[3]{0:T(128)S(1)}, u32[]{:S(2)}, u32[]{:S(2)}) %collective-permute-start.84) | collective-permute-done | bytes 44 | tf_op jit(solution)/shard_map/ppermute | solution.py:434
  1146.5 36.6 %collective-permute-done.85 = f32[3]{0:T(128)S(1)} collective-permute-done((f32[3]{0:T(128)S(1)}, f32[3]{0:T(128)S(1)}, u32[]{:S(2)}, u32[]{:S(2)}) %collective-permute-start.85) | collective-permute-done | bytes 44 | tf_op jit(solution)/shard_map/ppermute | solution.py:434
  1184.0 3.5 collective-permute-done.86
  1196.3 57.2 %shard_map.372 = (f32[512,96,128]{2,1,0:T(8,128)}, f32[512,96,128]{2,1,0:T(8,128)}, bf16[512,96,128]{2,1,0:T(8,128)(2,1)}, f32[2,8,128]{2,1,0:T(8,128)S(1)}) custom-call(s32[2]{0:T(128)S(1)} %pad_add_fusion.side_ref, f32[1]{0:T(128)} %bitcast.111.clip_ref, f32[512,96,128]{2,1,0:T(8,128)} %bitcast.389, f32[512,96,128]{2,1,0:T(8,128)} %bitcast.394, ...), custom_call_target="tpu_custom_call" | custom-call | flops 125829120 | bytes 150994944 | tf_op jit(solution)/shard_map/pallas_call | solution.py:354
  1268.5 6.3 multiply_reduce_fusion.20
  1299.1 3.5 collective-permute-done.103
  1307.4 20.8 %multiply_subtract_fusion = f32[512,96,128]{2,1,0:T(8,128)} fusion(f32[512,96,128]{2,1,0:T(8,128)} %bitcast.390, bf16[512,96,128]{2,1,0:T(8,128)(2,1)} %get-tuple-element.202, f32[]{:T(128)} %bitcast.122), kind=kLoop, calls=%fused_computation | loop fusion | flops 18874368 | bytes 62914564 | tf_op jit(solution)/shard_map/sub | solution.py:197
  (911 shorter events, 469.5 us)
Async XLA Ops:
  3.3 24.5 %collective-permute-start = (bf16[32,128]{1,0:T(8,128)(2,1)S(1)}, bf16[32,128]{1,0:T(8,128)(2,1)S(1)}, u32[]{:S(2)}, u32[]{:S(2)}) collective-permute-start(bf16[32,128]{1,0:T(8,128)(2,1)S(1)} %get-tuple-element.296), channel_id=1, source_target_pairs={{0,1},{1,0},{2,3},{3,2},{4,5},{5,4},{6,7},{7,6},{8,9},{9,8},{10,11... | collective-permute-start | bytes 24584 | tf_op jit(solution)/shard_map/ppermute | solution.py:434
  5.5 33.3 %collective-permute-start.10 = (bf16[1,16,64,32]{2,3,1,0:T(8,128)(2,1)S(1)}, bf16[1,16,64,32]{2,3,1,0:T(8,128)(2,1)S(1)}, u32[]{:S(2)}, u32[]{:S(2)}) collective-permute-start(bf16[1,16,64,32]{2,3,1,0:T(8,128)(2,1)S(1)} %bitcast.399), channel_id=1, source_target_pairs={{0,1},{1,0},{2,3},{3,2},{4,5},{5,4},{6,7},{7,6},{8,9},{9,8},{10,11... | collective-permute-start | bytes 196616 | tf_op jit(solution)/shard_map/ppermute | solution.py:434
  81.6 24.2 %collective-permute-start.5 = (f32[2,1024]{1,0:T(2,128)S(1)}, f32[2,1024]{1,0:T(2,128)S(1)}, u32[]{:S(2)}, u32[]{:S(2)}) collective-permute-start(f32[2,1024]{1,0:T(2,128)S(1)} %pad_maximum_fusion.39), channel_id=1, source_target_pairs={{0,16},{16,0},{1,17},{17,1},{2,18},{18,2},{3,19},{19,3},{4,20},{20... | collective-permute-start | bytes 24584 | tf_op jit(solution)/shard_map/ppermute | solution.py:474
  83.3 26.9 %collective-permute-start.6 = (bf16[512,768]{1,0:T(8,128)(2,1)}, bf16[512,768]{1,0:T(8,128)(2,1)S(1)}, u32[]{:S(2)}, u32[]{:S(2)}) collective-permute-start(bf16[512,768]{1,0:T(8,128)(2,1)} %get-tuple-element.119), channel_id=1, source_target_pairs={{0,4},{4,0},{8,12},{12,8},{1,5},{5,1},{9,13},{13,9},{2,6},{6,2},{1... | collective-permute-start | bytes 2359304 | tf_op jit(solution)/shard_map/ppermute | solution.py:437
  84.8 25.5 %collective-permute-start.7 = (bf16[512,768]{1,0:T(8,128)(2,1)}, bf16[512,768]{1,0:T(8,128)(2,1)S(1)}, u32[]{:S(2)}, u32[]{:S(2)}) collective-permute-start(bf16[512,768]{1,0:T(8,128)(2,1)} %get-tuple-element.120), channel_id=1, source_target_pairs={{0,8},{4,12},{8,0},{12,4},{1,9},{5,13},{9,1},{13,5},{2,10},{6,14},... | collective-permute-start | bytes 2359304 | tf_op jit(solution)/shard_map/ppermute | solution.py:437
  87.0 29.7 %collective-permute-start.8 = (bf16[512,768]{1,0:T(8,128)(2,1)}, bf16[512,768]{1,0:T(8,128)(2,1)}, u32[]{:S(2)}, u32[]{:S(2)}) collective-permute-start(bf16[512,768]{1,0:T(8,128)(2,1)} %get-tuple-element.121), channel_id=1, source_target_pairs={{0,12},{4,8},{8,4},{12,0},{1,13},{5,9},{9,5},{13,1},{2,14},{6,10},... | collective-permute-start | bytes 2359304 | tf_op jit(solution)/shard_map/ppermute | solution.py:437
  122.6 65.4 %collective-permute-start.9 = (bf16[1024,768]{1,0:T(8,128)(2,1)}, bf16[1024,768]{1,0:T(8,128)(2,1)}, u32[]{:S(2)}, u32[]{:S(2)}) collective-permute-start(bf16[1024,768]{1,0:T(8,128)(2,1)} %convolution_convert_fusion.10), channel_id=1, source_target_pairs={{0,16},{16,0},{1,17},{17,1},{2,18},{18,2},{3,19},{19,3},{4,20},{20... | collective-permute-start | bytes 4718600 | tf_op jit(solution)/shard_map/ppermute | solution.py:474
  192.9 128.3 %collective-permute-start.14 = (bf16[512,2304]{1,0:T(8,128)(2,1)S(1)}, bf16[512,2304]{1,0:T(8,128)(2,1)S(1)}, u32[]{:S(2)}, u32[]{:S(2)}) collective-permute-start(bf16[512,2304]{1,0:T(8,128)(2,1)S(1)} %copy-done.5), channel_id=1, source_target_pairs={{0,4},{4,0},{8,12},{12,8},{1,5},{5,1},{9,13},{13,9},{2,6},{6,2},{1... | collective-permute-start | bytes 7077896 | tf_op jit(solution)/shard_map/ppermute | solution.py:437
  193.4 127.8 %collective-permute-start.15 = (bf16[512,2304]{1,0:T(8,128)(2,1)S(1)}, bf16[512,2304]{1,0:T(8,128)(2,1)S(1)}, u32[]{:S(2)}, u32[]{:S(2)}) collective-permute-start(bf16[512,2304]{1,0:T(8,128)(2,1)S(1)} %copy-done.3), channel_id=1, source_target_pairs={{0,8},{4,12},{8,0},{12,4},{1,9},{5,13},{9,1},{13,5},{2,10},{6,14},... | collective-permute-start | bytes 7077896 | tf_op jit(solution)/shard_map/ppermute | solution.py:437
  193.4 127.8 %collective-permute-start.16 = (bf16[512,2304]{1,0:T(8,128)(2,1)S(1)}, bf16[512,2304]{1,0:T(8,128)(2,1)S(1)}, u32[]{:S(2)}, u32[]{:S(2)}) collective-permute-start(bf16[512,2304]{1,0:T(8,128)(2,1)S(1)} %copy-done.1), channel_id=1, source_target_pairs={{0,12},{4,8},{8,4},{12,0},{1,13},{5,9},{9,5},{13,1},{2,14},{6,10},... | collective-permute-start | bytes 7077896 | tf_op jit(solution)/shard_map/ppermute | solution.py:437
  196.4 120.2 %collective-permute-start.12 = (bf16[1024,256]{1,0:T(8,128)(2,1)S(1)}, bf16[1024,256]{1,0:T(8,128)(2,1)S(1)}, u32[]{:S(2)}, u32[]{:S(2)}) collective-permute-start(bf16[1024,256]{1,0:T(8,128)(2,1)S(1)} %get-tuple-element.313), channel_id=1, source_target_pairs={{0,4},{4,0},{1,5},{5,1},{2,6},{6,2},{3,7},{7,3},{8,12},{12,8},{9,1... | collective-permute-start | bytes 1572872 | tf_op jit(solution)/shard_map/ppermute | solution.py:537
  334.1 15.7 %collective-permute-start.23 = (bf16[64,2048]{1,0:T(8,128)(2,1)}, bf16[64,2048]{1,0:T(8,128)(2,1)S(1)}, u32[]{:S(2)}, u32[]{:S(2)}) collective-permute-start(bf16[64,2048]{1,0:T(8,128)(2,1)} %get-tuple-element.151), channel_id=1, source_target_pairs={{0,12},{1,13},{2,14},{3,15},{4,8},{5,9},{6,10},{7,11},{8,4},{9,5},... | collective-permute-start | bytes 786440 | tf_op jit(solution)/shard_map/ppermute | solution.py:434
  336.8 22.6 %collective-permute-start.22 = (bf16[64,2048]{1,0:T(8,128)(2,1)}, bf16[64,2048]{1,0:T(8,128)(2,1)S(1)}, u32[]{:S(2)}, u32[]{:S(2)}) collective-permute-start(bf16[64,2048]{1,0:T(8,128)(2,1)} %get-tuple-element.150), channel_id=1, source_target_pairs={{0,10},{1,11},{2,8},{3,9},{4,14},{5,15},{6,12},{7,13},{8,2},{9,3},... | collective-permute-start | bytes 786440 | tf_op jit(solution)/shard_map/ppermute | solution.py:434
  336.9 26.4 %collective-permute-start.21 = (bf16[64,2048]{1,0:T(8,128)(2,1)}, bf16[64,2048]{1,0:T(8,128)(2,1)S(1)}, u32[]{:S(2)}, u32[]{:S(2)}) collective-permute-start(bf16[64,2048]{1,0:T(8,128)(2,1)} %get-tuple-element.149), channel_id=1, source_target_pairs={{0,8},{1,9},{2,10},{3,11},{4,12},{5,13},{6,14},{7,15},{8,0},{9,1},... | collective-permute-start | bytes 786440 | tf_op jit(solution)/shard_map/ppermute | solution.py:434
  338.8 24.6 %collective-permute-start.20 = (bf16[64,2048]{1,0:T(8,128)(2,1)}, bf16[64,2048]{1,0:T(8,128)(2,1)S(1)}, u32[]{:S(2)}, u32[]{:S(2)}) collective-permute-start(bf16[64,2048]{1,0:T(8,128)(2,1)} %get-tuple-element.148), channel_id=1, source_target_pairs={{0,6},{1,7},{2,4},{3,5},{4,2},{5,3},{6,0},{7,1},{8,14},{9,15},{10,... | collective-permute-start | bytes 786440 | tf_op jit(solution)/shard_map/ppermute | solution.py:434
  344.2 19.8 %collective-permute-start.19 = (bf16[64,2048]{1,0:T(8,128)(2,1)}, bf16[64,2048]{1,0:T(8,128)(2,1)S(1)}, u32[]{:S(2)}, u32[]{:S(2)}) collective-permute-start(bf16[64,2048]{1,0:T(8,128)(2,1)} %get-tuple-element.147), channel_id=1, source_target_pairs={{0,4},{1,5},{2,6},{3,7},{4,0},{5,1},{6,2},{7,3},{8,12},{9,13},{10,... | collective-permute-start | bytes 786440 | tf_op jit(solution)/shard_map/ppermute | solution.py:434
  349.8 15.2 %collective-permute-start.18 = (bf16[64,2048]{1,0:T(8,128)(2,1)}, bf16[64,2048]{1,0:T(8,128)(2,1)S(1)}, u32[]{:S(2)}, u32[]{:S(2)}) collective-permute-start(bf16[64,2048]{1,0:T(8,128)(2,1)} %get-tuple-element.146), channel_id=1, source_target_pairs={{0,2},{1,3},{2,0},{3,1},{4,6},{5,7},{6,4},{7,5},{8,10},{9,11},{10,... | collective-permute-start | bytes 786440 | tf_op jit(solution)/shard_map/ppermute | solution.py:434
  372.2 17.4 %collective-permute-start.26 = (bf16[64,2048]{1,0:T(8,128)(2,1)S(1)}, bf16[64,2048]{1,0:T(8,128)(2,1)S(1)}, u32[]{:S(2)}, u32[]{:S(2)}) collective-permute-start(bf16[64,2048]{1,0:T(8,128)(2,1)S(1)} %multiply_convert_fusion.11.refs_0_), channel_id=1, source_target_pairs={{0,2},{1,3},{2,0},{3,1},{4,6},{5,7},{6,4},{7,5},{8,10},{9,11},{10,... | collective-permute-start | bytes 786440 | tf_op jit(solution)/shard_map/ppermute | solution.py:434
  373.7 16.2 %collective-permute-start.27 = (bf16[64,2048]{1,0:T(8,128)(2,1)S(1)}, bf16[64,2048]{1,0:T(8,128)(2,1)S(1)}, u32[]{:S(2)}, u32[]{:S(2)}) collective-permute-start(bf16[64,2048]{1,0:T(8,128)(2,1)S(1)} %multiply_convert_fusion.11.refs_0_), channel_id=1, source_target_pairs={{0,4},{1,5},{2,6},{3,7},{4,0},{5,1},{6,2},{7,3},{8,12},{9,13},{10,... | collective-permute-start | bytes 786440 | tf_op jit(solution)/shard_map/ppermute | solution.py:434
  374.8 19.7 %collective-permute-start.28 = (bf16[64,2048]{1,0:T(8,128)(2,1)S(1)}, bf16[64,2048]{1,0:T(8,128)(2,1)S(1)}, u32[]{:S(2)}, u32[]{:S(2)}) collective-permute-start(bf16[64,2048]{1,0:T(8,128)(2,1)S(1)} %multiply_convert_fusion.11.refs_0_), channel_id=1, source_target_pairs={{0,6},{1,7},{2,4},{3,5},{4,2},{5,3},{6,0},{7,1},{8,14},{9,15},{10,... | collective-permute-start | bytes 786440 | tf_op jit(solution)/shard_map/ppermute | solution.py:434
  375.7 18.7 %collective-permute-start.29 = (bf16[64,2048]{1,0:T(8,128)(2,1)S(1)}, bf16[64,2048]{1,0:T(8,128)(2,1)S(1)}, u32[]{:S(2)}, u32[]{:S(2)}) collective-permute-start(bf16[64,2048]{1,0:T(8,128)(2,1)S(1)} %multiply_convert_fusion.11.refs_0_), channel_id=1, source_target_pairs={{0,8},{1,9},{2,10},{3,11},{4,12},{5,13},{6,14},{7,15},{8,0},{9,1},... | collective-permute-start | bytes 786440 | tf_op jit(solution)/shard_map/ppermute | solution.py:434
  375.8 18.6 %collective-permute-start.30 = (bf16[64,2048]{1,0:T(8,128)(2,1)S(1)}, bf16[64,2048]{1,0:T(8,128)(2,1)S(1)}, u32[]{:S(2)}, u32[]{:S(2)}) collective-permute-start(bf16[64,2048]{1,0:T(8,128)(2,1)S(1)} %multiply_convert_fusion.11.refs_0_), channel_id=1, source_target_pairs={{0,10},{1,11},{2,8},{3,9},{4,14},{5,15},{6,12},{7,13},{8,2},{9,3},... | collective-permute-start | bytes 786440 | tf_op jit(solution)/shard_map/ppermute | solution.py:434
  419.2 93.0 %collective-permute-start.34 = (bf16[1024,1024]{1,0:T(8,128)(2,1)S(1)}, bf16[1024,1024]{1,0:T(8,128)(2,1)S(1)}, u32[]{:S(2)}, u32[]{:S(2)}) collective-permute-start(bf16[1024,1024]{1,0:T(8,128)(2,1)S(1)} %pad_maximum_fusion.3), channel_id=1, source_target_pairs={{0,16},{16,0},{1,17},{17,1},{2,18},{18,2},{3,19},{19,3},{4,20},{20... | collective-permute-start | bytes 6291464 | tf_op jit(solution)/shard_map/ppermute | solution.py:474
  535.5 15.3 %collective-permute-start.41 = (bf16[64,2048]{1,0:T(8,128)(2,1)}, bf16[64,2048]{1,0:T(8,128)(2,1)S(1)}, u32[]{:S(2)}, u32[]{:S(2)}) collective-permute-start(bf16[64,2048]{1,0:T(8,128)(2,1)} %get-tuple-element.159), channel_id=1, source_target_pairs={{0,12},{1,13},{2,14},{3,15},{4,8},{5,9},{6,10},{7,11},{8,4},{9,5},... | collective-permute-start | bytes 786440 | tf_op jit(solution)/shard_map/ppermute | solution.py:434
  537.9 24.2 %collective-permute-start.40 = (bf16[64,2048]{1,0:T(8,128)(2,1)}, bf16[64,2048]{1,0:T(8,128)(2,1)S(1)}, u32[]{:S(2)}, u32[]{:S(2)}) collective-permute-start(bf16[64,2048]{1,0:T(8,128)(2,1)} %get-tuple-element.158), channel_id=1, source_target_pairs={{0,10},{1,11},{2,8},{3,9},{4,14},{5,15},{6,12},{7,13},{8,2},{9,3},... | collective-permute-start | bytes 786440 | tf_op jit(solution)/shard_map/ppermute | solution.py:434
  538.9 26.1 %collective-permute-start.39 = (bf16[64,2048]{1,0:T(8,128)(2,1)}, bf16[64,2048]{1,0:T(8,128)(2,1)S(1)}, u32[]{:S(2)}, u32[]{:S(2)}) collective-permute-start(bf16[64,2048]{1,0:T(8,128)(2,1)} %get-tuple-element.157), channel_id=1, source_target_pairs={{0,8},{1,9},{2,10},{3,11},{4,12},{5,13},{6,14},{7,15},{8,0},{9,1},... | collective-permute-start | bytes 786440 | tf_op jit(solution)/shard_map/ppermute | solution.py:434
  541.4 23.6 %collective-permute-start.38 = (bf16[64,2048]{1,0:T(8,128)(2,1)}, bf16[64,2048]{1,0:T(8,128)(2,1)S(1)}, u32[]{:S(2)}, u32[]{:S(2)}) collective-permute-start(bf16[64,2048]{1,0:T(8,128)(2,1)} %get-tuple-element.156), channel_id=1, source_target_pairs={{0,6},{1,7},{2,4},{3,5},{4,2},{5,3},{6,0},{7,1},{8,14},{9,15},{10,... | collective-permute-start | bytes 786440 | tf_op jit(solution)/shard_map/ppermute | solution.py:434
  546.7 19.3 %collective-permute-start.37 = (bf16[64,2048]{1,0:T(8,128)(2,1)}, bf16[64,2048]{1,0:T(8,128)(2,1)S(1)}, u32[]{:S(2)}, u32[]{:S(2)}) collective-permute-start(bf16[64,2048]{1,0:T(8,128)(2,1)} %get-tuple-element.155), channel_id=1, source_target_pairs={{0,4},{1,5},{2,6},{3,7},{4,0},{5,1},{6,2},{7,3},{8,12},{9,13},{10,... | collective-permute-start | bytes 786440 | tf_op jit(solution)/shard_map/ppermute | solution.py:434
  550.9 17.2 %collective-permute-start.36 = (bf16[64,2048]{1,0:T(8,128)(2,1)}, bf16[64,2048]{1,0:T(8,128)(2,1)S(1)}, u32[]{:S(2)}, u32[]{:S(2)}) collective-permute-start(bf16[64,2048]{1,0:T(8,128)(2,1)} %get-tuple-element.154), channel_id=1, source_target_pairs={{0,2},{1,3},{2,0},{3,1},{4,6},{5,7},{6,4},{7,5},{8,10},{9,11},{10,... | collective-permute-start | bytes 786440 | tf_op jit(solution)/shard_map/ppermute | solution.py:434
  653.5 17.3 %collective-permute-start.47 = (bf16[64,2048]{1,0:T(8,128)(2,1)S(1)}, bf16[64,2048]{1,0:T(8,128)(2,1)S(1)}, u32[]{:S(2)}, u32[]{:S(2)}) collective-permute-start(bf16[64,2048]{1,0:T(8,128)(2,1)S(1)} %pad_maximum_fusion.25.refs_0_), channel_id=1, source_target_pairs={{0,6},{1,7},{2,4},{3,5},{4,2},{5,3},{6,0},{7,1},{8,14},{9,15},{10,... | collective-permute-start | bytes 786440 | tf_op jit(solution)/shard_map/ppermute | solution.py:434
  655.5 15.3 %collective-permute-start.48 = (bf16[64,2048]{1,0:T(8,128)(2,1)S(1)}, bf16[64,2048]{1,0:T(8,128)(2,1)S(1)}, u32[]{:S(2)}, u32[]{:S(2)}) collective-permute-start(bf16[64,2048]{1,0:T(8,128)(2,1)S(1)} %pad_maximum_fusion.25.refs_0_), channel_id=1, source_target_pairs={{0,8},{1,9},{2,10},{3,11},{4,12},{5,13},{6,14},{7,15},{8,0},{9,1},... | collective-permute-start | bytes 786440 | tf_op jit(solution)/shard_map/ppermute | solution.py:434
  655.5 16.4 %collective-permute-start.49 = (bf16[64,2048]{1,0:T(8,128)(2,1)S(1)}, bf16[64,2048]{1,0:T(8,128)(2,1)S(1)}, u32[]{:S(2)}, u32[]{:S(2)}) collective-permute-start(bf16[64,2048]{1,0:T(8,128)(2,1)S(1)} %pad_maximum_fusion.25.refs_0_), channel_id=1, source_target_pairs={{0,10},{1,11},{2,8},{3,9},{4,14},{5,15},{6,12},{7,13},{8,2},{9,3},... | collective-permute-start | bytes 786440 | tf_op jit(solution)/shard_map/ppermute | solution.py:434
  660.3 17.8 %collective-permute-start.50 = (bf16[64,2048]{1,0:T(8,128)(2,1)S(1)}, bf16[64,2048]{1,0:T(8,128)(2,1)S(1)}, u32[]{:S(2)}, u32[]{:S(2)}) collective-permute-start(bf16[64,2048]{1,0:T(8,128)(2,1)S(1)} %pad_maximum_fusion.25.refs_0_), channel_id=1, source_target_pairs={{0,12},{1,13},{2,14},{3,15},{4,8},{5,9},{6,10},{7,11},{8,4},{9,5},... | collective-permute-start | bytes 786440 | tf_op jit(solution)/shard_map/ppermute | solution.py:434
  662.5 19.4 %collective-permute-start.51 = (bf16[64,2048]{1,0:T(8,128)(2,1)S(1)}, bf16[64,2048]{1,0:T(8,128)(2,1)}, u32[]{:S(2)}, u32[]{:S(2)}) collective-permute-start(bf16[64,2048]{1,0:T(8,128)(2,1)S(1)} %pad_maximum_fusion.25.refs_0_), channel_id=1, source_target_pairs={{0,14},{1,15},{2,12},{3,13},{4,10},{5,11},{6,8},{7,9},{8,6},{9,7},... | collective-permute-start | bytes 786440 | tf_op jit(solution)/shard_map/ppermute | solution.py:434
  708.8 113.9 %collective-permute-start.53 = (bf16[1024,1024]{1,0:T(8,128)(2,1)}, bf16[1024,1024]{1,0:T(8,128)(2,1)}, u32[]{:S(2)}, u32[]{:S(2)}) collective-permute-start(bf16[1024,1024]{1,0:T(8,128)(2,1)} %pad_maximum_fusion.4), channel_id=1, source_target_pairs={{0,16},{16,0},{1,17},{17,1},{2,18},{18,2},{3,19},{19,3},{4,20},{20... | collective-permute-start | bytes 6291464 | tf_op jit(solution)/shard_map/ppermute | solution.py:474
  716.3 109.6 %collective-permute-start.54 = (bf16[512,1024]{1,0:T(8,128)(2,1)}, bf16[512,1024]{1,0:T(8,128)(2,1)S(1)}, u32[]{:S(2)}, u32[]{:S(2)}) collective-permute-start(bf16[512,1024]{1,0:T(8,128)(2,1)} %get-tuple-element.466), channel_id=1, source_target_pairs={{0,4},{4,0},{8,12},{12,8},{1,5},{5,1},{9,13},{13,9},{2,6},{6,2},{1... | collective-permute-start | bytes 3145736 | tf_op jit(solution)/shard_map/ppermute | solution.py:437
  722.6 25.7 %collective-permute-start.59 = (f32[641,128]{1,0:T(8,128)S(1)}, f32[641,128]{1,0:T(8,128)S(1)}, u32[]{:S(2)}, u32[]{:S(2)}) collective-permute-start(f32[641,128]{1,0:T(8,128)S(1)} %maximum_bitcast_fusion.2), channel_id=1, source_target_pairs={{0,4},{1,5},{2,6},{3,7},{4,0},{5,1},{6,2},{7,3},{8,12},{9,13},{10,... | collective-permute-start | bytes 984584 | tf_op jit(solution)/shard_map/ppermute | solution.py:434
  726.0 100.0 %collective-permute-start.55 = (bf16[512,1024]{1,0:T(8,128)(2,1)}, bf16[512,1024]{1,0:T(8,128)(2,1)}, u32[]{:S(2)}, u32[]{:S(2)}) collective-permute-start(bf16[512,1024]{1,0:T(8,128)(2,1)} %get-tuple-element.468), channel_id=1, source_target_pairs={{0,8},{4,12},{8,0},{12,4},{1,9},{5,13},{9,1},{13,5},{2,10},{6,14},... | collective-permute-start | bytes 3145736 | tf_op jit(solution)/shard_map/ppermute | solution.py:437
  748.4 58.8 %collective-permute-start.60 = (f32[641,128]{1,0:T(8,128)S(1)}, f32[641,128]{1,0:T(8,128)S(1)}, u32[]{:S(2)}, u32[]{:S(2)}) collective-permute-start(f32[641,128]{1,0:T(8,128)S(1)} %fusion.272), channel_id=1, source_target_pairs={{0,8},{1,9},{2,10},{3,11},{4,12},{5,13},{6,14},{7,15},{8,0},{9,1},... | collective-permute-start | bytes 984584 | tf_op jit(solution)/shard_map/ppermute | solution.py:434
  751.9 79.6 %collective-permute-start.56 = (bf16[512,1024]{1,0:T(8,128)(2,1)}, bf16[512,1024]{1,0:T(8,128)(2,1)}, u32[]{:S(2)}, u32[]{:S(2)}) collective-permute-start(bf16[512,1024]{1,0:T(8,128)(2,1)} %get-tuple-element.470), channel_id=1, source_target_pairs={{0,12},{4,8},{8,4},{12,0},{1,13},{5,9},{9,5},{13,1},{2,14},{6,10},... | collective-permute-start | bytes 3145736 | tf_op jit(solution)/shard_map/ppermute | solution.py:437
  852.8 16.3 %collective-permute-start.68 = (bf16[64,2048]{1,0:T(8,128)(2,1)}, bf16[64,2048]{1,0:T(8,128)(2,1)S(1)}, u32[]{:S(2)}, u32[]{:S(2)}) collective-permute-start(bf16[64,2048]{1,0:T(8,128)(2,1)} %get-tuple-element.172), channel_id=1, source_target_pairs={{0,12},{1,13},{2,14},{3,15},{4,8},{5,9},{6,10},{7,11},{8,4},{9,5},... | collective-permute-start | bytes 786440 | tf_op jit(solution)/shard_map/ppermute | solution.py:434
  856.2 23.0 %collective-permute-start.67 = (bf16[64,2048]{1,0:T(8,128)(2,1)}, bf16[64,2048]{1,0:T(8,128)(2,1)S(1)}, u32[]{:S(2)}, u32[]{:S(2)}) collective-permute-start(bf16[64,2048]{1,0:T(8,128)(2,1)} %get-tuple-element.171), channel_id=1, source_target_pairs={{0,10},{1,11},{2,8},{3,9},{4,14},{5,15},{6,12},{7,13},{8,2},{9,3},... | collective-permute-start | bytes 786440 | tf_op jit(solution)/shard_map/ppermute | solution.py:434
  856.2 27.1 %collective-permute-start.66 = (bf16[64,2048]{1,0:T(8,128)(2,1)}, bf16[64,2048]{1,0:T(8,128)(2,1)S(1)}, u32[]{:S(2)}, u32[]{:S(2)}) collective-permute-start(bf16[64,2048]{1,0:T(8,128)(2,1)} %get-tuple-element.170), channel_id=1, source_target_pairs={{0,8},{1,9},{2,10},{3,11},{4,12},{5,13},{6,14},{7,15},{8,0},{9,1},... | collective-permute-start | bytes 786440 | tf_op jit(solution)/shard_map/ppermute | solution.py:434
  858.5 24.8 %collective-permute-start.65 = (bf16[64,2048]{1,0:T(8,128)(2,1)}, bf16[64,2048]{1,0:T(8,128)(2,1)S(1)}, u32[]{:S(2)}, u32[]{:S(2)}) collective-permute-start(bf16[64,2048]{1,0:T(8,128)(2,1)} %get-tuple-element.169), channel_id=1, source_target_pairs={{0,6},{1,7},{2,4},{3,5},{4,2},{5,3},{6,0},{7,1},{8,14},{9,15},{10,... | collective-permute-start | bytes 786440 | tf_op jit(solution)/shard_map/ppermute | solution.py:434
  863.8 20.4 %collective-permute-start.64 = (bf16[64,2048]{1,0:T(8,128)(2,1)}, bf16[64,2048]{1,0:T(8,128)(2,1)S(1)}, u32[]{:S(2)}, u32[]{:S(2)}) collective-permute-start(bf16[64,2048]{1,0:T(8,128)(2,1)} %get-tuple-element.168), channel_id=1, source_target_pairs={{0,4},{1,5},{2,6},{3,7},{4,0},{5,1},{6,2},{7,3},{8,12},{9,13},{10,... | collective-permute-start | bytes 786440 | tf_op jit(solution)/shard_map/ppermute | solution.py:434
  869.1 16.0 %collective-permute-start.63 = (bf16[64,2048]{1,0:T(8,128)(2,1)}, bf16[64,2048]{1,0:T(8,128)(2,1)S(1)}, u32[]{:S(2)}, u32[]{:S(2)}) collective-permute-start(bf16[64,2048]{1,0:T(8,128)(2,1)} %get-tuple-element.167), channel_id=1, source_target_pairs={{0,2},{1,3},{2,0},{3,1},{4,6},{5,7},{6,4},{7,5},{8,10},{9,11},{10,... | collective-permute-start | bytes 786440 | tf_op jit(solution)/shard_map/ppermute | solution.py:434
  887.5 17.4 %collective-permute-start.81 = (bf16[1024,256]{1,0:T(8,128)(2,1)}, bf16[1024,256]{1,0:T(8,128)(2,1)}, u32[]{:S(2)}, u32[]{:S(2)}) collective-permute-start(bf16[1024,256]{1,0:T(8,128)(2,1)} %get-tuple-element.311), channel_id=1, source_target_pairs={{0,4},{4,0},{1,5},{5,1},{2,6},{6,2},{3,7},{7,3},{8,12},{12,8},{9,1... | collective-permute-start | bytes 1572872 | tf_op jit(solution)/shard_map/ppermute | solution.py:537
  891.8 15.7 %collective-permute-start.71 = (bf16[64,2048]{1,0:T(8,128)(2,1)S(1)}, bf16[64,2048]{1,0:T(8,128)(2,1)}, u32[]{:S(2)}, u32[]{:S(2)}) collective-permute-start(bf16[64,2048]{1,0:T(8,128)(2,1)S(1)} %add_convert_fusion.14.refs_0_), channel_id=1, source_target_pairs={{0,2},{1,3},{2,0},{3,1},{4,6},{5,7},{6,4},{7,5},{8,10},{9,11},{10,... | collective-permute-start | bytes 786440 | tf_op jit(solution)/shard_map/ppermute | solution.py:434
  904.9 15.5 %collective-permute-start.75 = (bf16[64,2048]{1,0:T(8,128)(2,1)S(1)}, bf16[64,2048]{1,0:T(8,128)(2,1)S(1)}, u32[]{:S(2)}, u32[]{:S(2)}) collective-permute-start(bf16[64,2048]{1,0:T(8,128)(2,1)S(1)} %add_convert_fusion.14.refs_0_), channel_id=1, source_target_pairs={{0,10},{1,11},{2,8},{3,9},{4,14},{5,15},{6,12},{7,13},{8,2},{9,3},... | collective-permute-start | bytes 786440 | tf_op jit(solution)/shard_map/ppermute | solution.py:434
  907.6 18.0 %collective-permute-start.76 = (bf16[64,2048]{1,0:T(8,128)(2,1)S(1)}, bf16[64,2048]{1,0:T(8,128)(2,1)S(1)}, u32[]{:S(2)}, u32[]{:S(2)}) collective-permute-start(bf16[64,2048]{1,0:T(8,128)(2,1)S(1)} %add_convert_fusion.14.refs_0_), channel_id=1, source_target_pairs={{0,12},{1,13},{2,14},{3,15},{4,8},{5,9},{6,10},{7,11},{8,4},{9,5},... | collective-permute-start | bytes 786440 | tf_op jit(solution)/shard_map/ppermute | solution.py:434
  908.3 20.9 %collective-permute-start.77 = (bf16[64,2048]{1,0:T(8,128)(2,1)S(1)}, bf16[64,2048]{1,0:T(8,128)(2,1)}, u32[]{:S(2)}, u32[]{:S(2)}) collective-permute-start(bf16[64,2048]{1,0:T(8,128)(2,1)S(1)} %add_convert_fusion.14.refs_0_), channel_id=1, source_target_pairs={{0,14},{1,15},{2,12},{3,13},{4,10},{5,11},{6,8},{7,9},{8,6},{9,7},... | collective-permute-start | bytes 786440 | tf_op jit(solution)/shard_map/ppermute | solution.py:434
  933.1 17.7 %collective-permute-start.78 = (bf16[512,2048]{1,0:T(8,128)(2,1)}, bf16[512,2048]{1,0:T(8,128)(2,1)}, u32[]{:S(2)}, u32[]{:S(2)}) collective-permute-start(bf16[512,2048]{1,0:T(8,128)(2,1)} %shard_map.371), channel_id=1, source_target_pairs={{0,1},{1,0},{2,3},{3,2},{4,5},{5,4},{6,7},{7,6},{8,9},{9,8},{10,11... | collective-permute-start | bytes 6291464 | tf_op jit(solution)/shard_map/ppermute | solution.py:434
  968.2 26.2 %collective-permute-start.79 = (bf16[1024,256]{1,0:T(8,128)(2,1)S(1)}, bf16[1024,256]{1,0:T(8,128)(2,1)S(1)}, u32[]{:S(2)}, u32[]{:S(2)}) collective-permute-start(bf16[1024,256]{1,0:T(8,128)(2,1)S(1)} %pad_maximum_fusion.20), channel_id=1, source_target_pairs={{0,16},{16,0},{1,17},{17,1},{2,18},{18,2},{3,19},{19,3},{4,20},{20... | collective-permute-start | bytes 1572872 | tf_op jit(solution)/shard_map/ppermute | solution.py:474
  1068.5 51.3 %collective-permute-start.92 = (bf16[512,768]{1,0:T(8,128)(2,1)}, bf16[512,768]{1,0:T(8,128)(2,1)}, u32[]{:S(2)}, u32[]{:S(2)}) collective-permute-start(bf16[512,768]{1,0:T(8,128)(2,1)} %get-tuple-element.187), channel_id=1, source_target_pairs={{0,4},{4,0},{8,12},{12,8},{1,5},{5,1},{9,13},{13,9},{2,6},{6,2},{1... | collective-permute-start | bytes 2359304 | tf_op jit(solution)/shard_map/ppermute | solution.py:437
  1069.5 52.6 %collective-permute-start.93 = (bf16[512,768]{1,0:T(8,128)(2,1)}, bf16[512,768]{1,0:T(8,128)(2,1)}, u32[]{:S(2)}, u32[]{:S(2)}) collective-permute-start(bf16[512,768]{1,0:T(8,128)(2,1)} %get-tuple-element.188), channel_id=1, source_target_pairs={{0,8},{4,12},{8,0},{12,4},{1,9},{5,13},{9,1},{13,5},{2,10},{6,14},... | collective-permute-start | bytes 2359304 | tf_op jit(solution)/shard_map/ppermute | solution.py:437
  1069.5 53.8 %collective-permute-start.94 = (bf16[512,768]{1,0:T(8,128)(2,1)}, bf16[512,768]{1,0:T(8,128)(2,1)}, u32[]{:S(2)}, u32[]{:S(2)}) collective-permute-start(bf16[512,768]{1,0:T(8,128)(2,1)} %get-tuple-element.189), channel_id=1, source_target_pairs={{0,12},{4,8},{8,4},{12,0},{1,13},{5,9},{9,5},{13,1},{2,14},{6,10},... | collective-permute-start | bytes 2359304 | tf_op jit(solution)/shard_map/ppermute | solution.py:437
  1074.3 36.9 %collective-permute-start.90 = (f32[560,128]{1,0:T(8,128)S(1)}, f32[560,128]{1,0:T(8,128)S(1)}, u32[]{:S(2)}, u32[]{:S(2)}) collective-permute-start(f32[560,128]{1,0:T(8,128)S(1)} %add.910), channel_id=1, source_target_pairs={{0,4},{1,5},{2,6},{3,7},{4,0},{5,1},{6,2},{7,3},{8,12},{9,13},{10,... | collective-permute-start | bytes 860168 | tf_op jit(solution)/shard_map/ppermute | solution.py:434
  1113.2 83.0 %collective-permute-start.96 = (bf16[512,1280]{1,0:T(8,128)(2,1)}, bf16[512,1280]{1,0:T(8,128)(2,1)}, u32[]{:S(2)}, u32[]{:S(2)}) collective-permute-start(bf16[512,1280]{1,0:T(8,128)(2,1)} %pad_maximum_fusion.8), channel_id=1, source_target_pairs={{0,4},{4,0},{8,12},{12,8},{1,5},{5,1},{9,13},{13,9},{2,6},{6,2},{1... | collective-permute-start | bytes 3932168 | tf_op jit(solution)/shard_map/ppermute | solution.py:437
  1119.4 76.8 %collective-permute-start.97 = (bf16[512,1280]{1,0:T(8,128)(2,1)}, bf16[512,1280]{1,0:T(8,128)(2,1)}, u32[]{:S(2)}, u32[]{:S(2)}) collective-permute-start(bf16[512,1280]{1,0:T(8,128)(2,1)} %pad_maximum_fusion.9), channel_id=1, source_target_pairs={{0,8},{4,12},{8,0},{12,4},{1,9},{5,13},{9,1},{13,5},{2,10},{6,14},... | collective-permute-start | bytes 3932168 | tf_op jit(solution)/shard_map/ppermute | solution.py:437
  1119.8 76.5 %collective-permute-start.98 = (bf16[512,1280]{1,0:T(8,128)(2,1)}, bf16[512,1280]{1,0:T(8,128)(2,1)}, u32[]{:S(2)}, u32[]{:S(2)}) collective-permute-start(bf16[512,1280]{1,0:T(8,128)(2,1)} %pad_maximum_fusion.10), channel_id=1, source_target_pairs={{0,12},{4,8},{8,4},{12,0},{1,13},{5,9},{9,5},{13,1},{2,14},{6,10},... | collective-permute-start | bytes 3932168 | tf_op jit(solution)/shard_map/ppermute | solution.py:437
  1123.3 66.1 %collective-permute-start.95 = (f32[560,128]{1,0:T(8,128)S(1)}, f32[560,128]{1,0:T(8,128)S(1)}, u32[]{:S(2)}, u32[]{:S(2)}) collective-permute-start(f32[560,128]{1,0:T(8,128)S(1)} %add.912), channel_id=1, source_target_pairs={{0,16},{16,0},{1,17},{17,1},{2,18},{18,2},{3,19},{19,3},{4,20},{20... | collective-permute-start | bytes 860168 | tf_op jit(solution)/shard_map/ppermute | solution.py:474
  1126.3 18.2 %collective-permute-start.84 = (f32[3]{0:T(128)S(1)}, f32[3]{0:T(128)S(1)}, u32[]{:S(2)}, u32[]{:S(2)}) collective-permute-start(f32[3]{0:T(128)S(1)} %fusion.403), channel_id=1, source_target_pairs={{0,4},{1,5},{2,6},{3,7},{4,0},{5,1},{6,2},{7,3},{8,12},{9,13},{10,... | collective-permute-start | bytes 44 | tf_op jit(solution)/shard_map/ppermute | solution.py:434
  1144.5 38.6 %collective-permute-start.85 = (f32[3]{0:T(128)S(1)}, f32[3]{0:T(128)S(1)}, u32[]{:S(2)}, u32[]{:S(2)}) collective-permute-start(f32[3]{0:T(128)S(1)} %add.899), channel_id=1, source_target_pairs={{0,8},{1,9},{2,10},{3,11},{4,12},{5,13},{6,14},{7,15},{8,0},{9,1},... | collective-permute-start | bytes 44 | tf_op jit(solution)/shard_map/ppermute | solution.py:434
  1258.4 26.6 %collective-permute-start.99 = (f32[4]{0:T(128)S(1)}, f32[4]{0:T(128)S(1)}, u32[]{:S(2)}, u32[]{:S(2)}) collective-permute-start(f32[4]{0:T(128)S(1)} %pad_maximum_fusion.45), channel_id=1, source_target_pairs={{0,1},{1,0},{2,3},{3,2},{4,5},{5,4},{6,7},{7,6},{8,9},{9,8},{10,11... | collective-permute-start | bytes 56 | tf_op jit(solution)/shard_map/ppermute | solution.py:434
  (239 other events, 2944.7 us)

commit v4 on v3

--- a/solution.py
+++ b/solution.py
@@ -212,7 +212,7 @@
 FIRST_SCALE = 1.0 / (1.0 - BETA_FIRST**STEP)
 SECOND_SCALE = 1.0 / (1.0 - BETA_SECOND**STEP)
 UNITS = FF // H
-SOURCES = ((0, 0), (1, 0), (1, HD // 2), (2, 0))
+SOURCES = ((0, 0), (0, 3 * HD // 2), (1, 0), (2, 0))
 SECTIONS = ((0, 3, HD), (3 * HD, 1, HD), (4 * HD, 1, UNITS), (4 * HD + UNITS, 1, UNITS))
 
 
@@ -296,9 +296,7 @@
         + [section_spec(offset, parts * width) for offset, parts, width in sections],
         out_specs=[pl.BlockSpec((block, total // 2), lambda i: (i, 0))] * SHARERS,
         compiler_params=pltpu.CompilerParams(vmem_limit_bytes=40 * 2**20),
-        cost_estimate=pl.CostEstimate(
-            flops=rows * total * 2, bytes_accessed=rows * total * 12, transcendentals=0
-        ),
+        cost_estimate=pl.CostEstimate(flops=1, bytes_accessed=1, transcendentals=0),
     )(side, *[view] * len(sections))
 
 
@@ -371,6 +369,42 @@
     )(side, clip, weight, first, second, *gradients)
 
 
+def embed_kernel(picked_ref, expand_ref, entry_ref, table_ref, fold_ref, block_ref, hot_ref, out_ref):
+    hot = (dot(picked_ref[...], expand_ref[0]) == entry_ref[...]).astype(LOW)
+    hot_ref[0] = hot
+    total = 0.0
+    for i in (2, 1, 0):
+        wide = (dot(table_ref[0, i], fold_ref[...], 1, 1) * block_ref[...]).astype(LOW)
+        total = total + dot(hot, wide)
+    out_ref[...] = total
+
+
+def embed_tokens(picked, expand, entry, table, fold, block):
+    tokens, rows, width = picked.shape[0], entry.shape[1], fold.shape[0]
+    return pl.pallas_call(
+        embed_kernel,
+        out_shape=[
+            jax.ShapeDtypeStruct((SHARERS, tokens, rows), LOW),
+            jax.ShapeDtypeStruct((tokens, SHARERS * width), WIDE),
+        ],
+        grid=(SHARERS,),
+        in_specs=[
+            pl.BlockSpec(picked.shape, lambda j: (0, 0)),
+            pl.BlockSpec((1, *expand.shape[1:]), lambda j: (j, 0, 0)),
+            pl.BlockSpec(entry.shape, lambda j: (0, 0)),
+            pl.BlockSpec((1, *table.shape[1:]), lambda j: (j, 0, 0, 0)),
+            pl.BlockSpec(fold.shape, lambda j: (0, 0)),
+            pl.BlockSpec(block.shape, lambda j: (0, 0)),
+        ],
+        out_specs=[
+            pl.BlockSpec((1, tokens, rows), lambda j: (j, 0, 0)),
+            pl.BlockSpec((tokens, width), lambda j: (0, j)),
+        ],
+        compiler_params=pltpu.CompilerParams(vmem_limit_bytes=40 * 2**20),
+        cost_estimate=pl.CostEstimate(flops=1, bytes_accessed=1, transcendentals=0),
+    )(picked, expand, entry, table, fold, block)
+
+
 def join_kernel(*refs):
     rows = refs[0].shape[0]
     for k, ref in enumerate(refs[:-1]):
@@ -648,9 +682,12 @@
         return [values[0]] + [grid.trade(values[j], j) for j in (1, 2, 3)]
 
     weight_view = native_view(abd_weights) if native else None
-    qkv_pieces, picked_all, side = tied(pieces_of(SECTIONS[:1]), picked_all, side)
+    qkv_pieces, picked_all, side, table = tied(
+        pieces_of(SECTIONS[:1]), picked_all, side, embed_table
+    )
     qkv_w = traded(qkv_pieces)
-    qkv_w, other_pieces = tied(qkv_w, pieces_of(SECTIONS[1:]))
+    picked_all, other_pieces = tied(picked_all, pieces_of(SECTIONS[1:3]))
+    qkv_w, other_pieces, side = tied(qkv_w, other_pieces, side)
     qkv_w = jnp.concatenate(qkv_w, axis=0)
     others = traded(other_pieces)
 
@@ -672,22 +709,19 @@
     fold = (
         block_columns[:, None] % embed_width == jnp.arange(embed_width, dtype=jnp.int32)
     ).astype(LOW)
-    table = jnp.concatenate(grid.local(embed_table, 0), axis=0).reshape(-1, embed_width)
-    tables = [dot(piece, fold, 1, 1).astype(LOW) for piece in split_three(table)]
-    hots, embedded = [], []
-    for j in range(SHARERS):
-        expand = (
-            jnp.arange(local_attrs, dtype=jnp.int32)[:, None]
-            == j * block_attrs + row_attr[None, :]
-        ).astype(LOW)
-        hot = (dot(picked, expand) == row_entry[None, :]).astype(LOW)
-        hots.append(hot)
-        cut = slice(j * row_attr.size, (j + 1) * row_attr.size)
-        wide = [jnp.where(own_block, piece[cut], 0.0) for piece in tables]
-        embedded.append(
-            dot(jnp.concatenate([hot, hot, hot], axis=1), jnp.concatenate(wide, axis=0))
-        )
-    embedded = jnp.concatenate(embedded, axis=1)
+    table = jnp.stack(grid.local(table, 0)).reshape(SHARERS, row_attr.size, embed_width)
+    places = jnp.arange(local_attrs, dtype=jnp.int32)
+    expand = places[None, :, None] == (
+        jnp.arange(SHARERS, dtype=jnp.int32)[:, None, None] * block_attrs + row_attr[None, None, :]
+    )
+    hots, embedded = embed_tokens(
+        picked,
+        expand.astype(LOW),
+        row_entry[None, :],
+        jnp.stack(split_three(table), axis=1),
+        fold,
+        own_block.astype(WIDE),
+    )
 
     kinds = jnp.arange(classes, dtype=jnp.int32).astype(WIDE)
     mask_own = own_rows(cell_mask).astype(WIDE)
@@ -715,8 +749,8 @@
     hat_one = (embedded - mean_one) * scale_one
     normed = (hat_one * gains[0]).astype(LOW)
     triple = grid.row_sum(dot(normed, qkv_w).astype(LOW)).astype(LOW)
-    triple, class_weight, weight_total, label_hot, output_low = tied(
-        triple, class_weight, weight_total, label_hot, output_low
+    triple, others, class_weight, weight_total, label_hot, output_low, down_pieces = tied(
+        triple, others, class_weight, weight_total, label_hot, output_low, pieces_of(SECTIONS[3:])
     )
     part = HD // grid.parts
     query_own, key_own, value_own = (triple[:, i * part : (i + 1) * part] for i in range(3))
@@ -727,11 +761,9 @@
     shifted = jnp.exp(scores - jnp.max(scores, axis=1, keepdims=True))
     probs = shifted / jnp.sum(shifted, axis=1, keepdims=True)
     probs_low = probs.astype(LOW)
-    attended, others = tied(dot(probs_low, value_own).astype(LOW), others)
-    out_w, up_w, down_w = (
-        jnp.concatenate([piece[:, start : start + size] for piece in others], axis=0)
-        for start, size in ((0, out_size), (out_size, up_size), (out_size + up_size, up_size))
-    )
+    attended = dot(probs_low, value_own).astype(LOW)
+    out_w = jnp.concatenate([piece[:, :out_size] for piece in others], axis=0)
+    up_w = jnp.concatenate([piece[:, out_size:] for piece in others], axis=0)
     attended = jnp.split(attended, 2, axis=0)
     branch = [dot(a, out_w, 1, 1).astype(LOW) for a in attended]
     middle = embedded[:held] + grid.gathered_sum(*branch)
@@ -739,7 +771,12 @@
     hat_two = (middle - mean_two) * scale_two
     second = grid.spread((hat_two * gains[1]).astype(LOW))
     before = jnp.concatenate([dot(a, up_w).astype(LOW) for a in second], axis=0)
-    before = jnp.split(grid.row_sum(before), 2, axis=0)
+    before, down_pieces = tied(before, down_pieces)
+    before, down_w, up_turned, qkv_turned = tied(
+        grid.row_sum(before), traded(down_pieces), up_w.T, qkv_w.T
+    )
+    down_w = jnp.concatenate(down_w, axis=0)
+    before = jnp.split(before, 2, axis=0)
     hidden = [gelu_apply(b).astype(LOW) for b in before]
     after = middle + grid.gathered_sum(*[dot(a, down_w, 1, 1).astype(LOW) for a in hidden])
 
@@ -757,7 +794,7 @@
         LOW
     )
     final_grad = jnp.einsum("tfc,fec->tfe", logit_grad, output_low, preferred_element_type=WIDE)
-    output_part = jnp.einsum("tfe,tfc->fec", final_low, logit_grad, preferred_element_type=WIDE)
+    output_part = jnp.einsum("tfe,tfc->fce", final_low, logit_grad, preferred_element_type=WIDE)
     rows_grad, aba_part, aba_gains_part = aba_backward(
         final_grad.reshape(own_tokens, model_width), aba_stored, aba_low, aba_gains
     )
@@ -776,14 +813,13 @@
 
     upstream = grid.from_rows(rows_grad.astype(LOW))
     down_grad = grid.spread(upstream)
-    hidden_grad, output_part, aba_part, aba_gains_part = tied(
-        jnp.concatenate([dot(a, down_w).astype(LOW) for a in down_grad], axis=0),
-        output_part,
-        aba_part,
-        aba_gains_part,
-    )
+    hidden_grad = jnp.concatenate([dot(a, down_w).astype(LOW) for a in down_grad], axis=0)
     hidden_grad = grid.row_sum(hidden_grad)
     down_gradient = traded(row_gradients(down_grad, hidden))
+
+    hidden_grad, down_gradient, output_part, aba_part, aba_gains_part = tied(
+        hidden_grad, down_gradient, output_part, aba_part, aba_gains_part
+    )
 
     small = jnp.concatenate([aba_part.reshape(-1), aba_gains_part.reshape(-1)])
     blocks = output_part.reshape(grid.heads, -1)
@@ -800,34 +836,29 @@
     for step in (grid.heads, 2 * grid.heads):
         packed = packed + grid.pair(packed, step)
     packed = grid.row_sum(packed).reshape(-1)
-    output_grad = packed[: blocks.size].reshape(output_table.shape)
+    output_grad = packed[: blocks.size].reshape(-1, classes, embed_width)
     aba_grad = packed[blocks.size : blocks.size + aba_weights.size].reshape(aba_weights.shape)
     aba_gains_grad = packed[blocks.size + aba_weights.size :].reshape(aba_gains.shape)
 
-    hidden_grad, down_gradient, output_grad, aba_grad, aba_gains_grad = tied(
-        hidden_grad, down_gradient, output_grad, aba_grad, aba_gains_grad
-    )
 
     before_grad = [gelu_back(b, g).astype(LOW) for b, g in zip(before, jnp.split(hidden_grad, 2, axis=0))]
-    second_grad = grid.gathered_sum(*[dot(a, up_w, 1, 1).astype(LOW) for a in before_grad])
+    second_grad = grid.gathered_sum(*[dot(a, up_turned).astype(LOW) for a in before_grad])
     gained = second_grad * gains[1]
     sums = jnp.stack([jnp.sum(gained, axis=1), jnp.sum(gained * hat_two, axis=1)])
     sums = sum(grid.row_list(sums)) / model_width
     middle_grad = upstream.astype(WIDE) + scale_two * (
         gained - sums[0][:, None] - hat_two * sums[1][:, None]
     )
+    middle_grad, up_gradient, output_grad, aba_grad, aba_gains_grad = tied(
+        middle_grad, row_gradients(second, before_grad), output_grad, aba_grad, aba_gains_grad
+    )
+    up_gradient = traded(up_gradient)
     gain_two = jnp.sum(second_grad * hat_two, axis=0)
     branch_grad = grid.spread(middle_grad.astype(LOW))
     attended_grad = jnp.concatenate([dot(a, out_w).astype(LOW) for a in branch_grad], axis=0)
-    attended_grad, second, attended = tied(attended_grad, second, attended)
-    attended_grad = grid.row_sum(attended_grad).astype(LOW)
-    out_gradient, up_gradient = (
-        row_gradients(branch_grad, attended),
-        row_gradients(second, before_grad),
-    )
-    other_gradient = traded(
-        [jnp.concatenate(pair, axis=1) for pair in zip(out_gradient, up_gradient)]
-    )
+    attended_grad, attended = tied(attended_grad, attended)
+    attended_grad, up_gradient = tied(grid.row_sum(attended_grad).astype(LOW), up_gradient)
+    out_gradient = row_gradients(branch_grad, attended)
     prob_grad = dot(grid.columns(attended_grad), value_rows, 1, 1)
     score_grad = probs * (prob_grad - jnp.sum(probs * prob_grad, axis=1, keepdims=True))
     score_grad = score_grad.astype(LOW)
@@ -839,11 +870,12 @@
         dot(hot[:held], block, 0, 0)
         for hot, block in zip(hots, jnp.split(middle_grad.astype(LOW), SHARERS, axis=1))
     ]
-    triple_grad, table_part = tied(triple_grad, table_part)
+    triple_grad, table_part, out_gradient = tied(triple_grad, table_part, out_gradient)
     qkv_gradient = row_gradients([normed], [triple_grad])
+    qkv_gradient = [jnp.concatenate(pair, axis=1) for pair in zip(qkv_gradient, out_gradient)]
     triple_grad, qkv_gradient = tied(triple_grad, qkv_gradient)
 
-    normed_grad = dot(triple_grad, qkv_w, 1, 1)
+    normed_grad = dot(triple_grad, qkv_turned)
     gained = normed_grad * gains[0]
     sums = jnp.stack([jnp.sum(gained, axis=1), jnp.sum(gained * hat_one, axis=1)])
     sums = sum(grid.row_list(sums)) / model_width
@@ -858,17 +890,27 @@
         records.append(jnp.concatenate([grad.reshape(-1), gain_one[cut], gain_two[cut]]))
     table_size = block_attrs * entries * embed_width
     packed = jnp.stack(grid.ordered(records)).reshape(-1, 128)
-    packed = grid.group_total(packed)
+    output_sq = first_device * jnp.sum(output_grad * output_grad)
+    scalars = jnp.stack([sum(gradient_sq), output_sq, loss_local])
+    lane = jnp.arange(8 * 128, dtype=jnp.int32).reshape(8, 128)
+    scalars = sum(jnp.where(lane == i, scalars[i], 0.0) for i in range(3))
     packed, qkv_gradient = tied(packed, traded(qkv_gradient))
-    gradients = qkv_gradient + other_gradient + down_gradient
-    packed = jnp.stack(grid.row_gather(packed))
-    packed = packed.reshape(grid.rows * SHARERS, -1)
-    embed_grad = packed[:, :table_size].reshape(embed_table.shape)
+    gradients = qkv_gradient + up_gradient + down_gradient
+    packed = jnp.stack(
+        grid.row_gather(grid.group_total(jnp.concatenate([scalars, packed], axis=0)))
+    )
+    summed = jnp.sum(packed[:, 0, :3], axis=0)
+    packed = packed[:, 8:].reshape(grid.rows * SHARERS, -1)
+    embed_grad = packed[:, :table_size].reshape(embed_table.shape).transpose(1, 0, 2)
     abd_gains_grad = packed[:, table_size:].reshape(-1, 2, width).transpose(1, 0, 2)
     abd_gains_grad = abd_gains_grad.reshape(2, model_width)
 
-    output_sq = first_device * jnp.sum(output_grad * output_grad)
-    summed = grid.total(jnp.stack([sum(gradient_sq), output_sq, loss_local]))
+    output_table, output_first, output_second = (
+        values.transpose(0, 2, 1) for values in (output_table, output_first, output_second)
+    )
+    embed_table, embed_first, embed_second = (
+        values.transpose(1, 0, 2) for values in (embed_table, embed_first, embed_second)
+    )
     replicated_sq = (
         jnp.sum(abd_gains_grad * abd_gains_grad)
         + jnp.sum(aba_grad * aba_grad)
@@ -891,8 +933,13 @@
         abd_second_new = from_native(second_view, grid.each)
         abd_update_sq, abd_weight_sq = jnp.sum(squares[0]), jnp.sum(squares[1])
     else:
-        qkv_g, other_g, down_g = (gradients[SHARERS * i : SHARERS * (i + 1)] for i in range(3))
-        split_g = (qkv_g, [g[:, :out_size] for g in other_g], [g[:, out_size:] for g in other_g], down_g)
+        first_g, up_g, down_g = (gradients[SHARERS * i : SHARERS * (i + 1)] for i in range(3))
+        split_g = (
+            [g[:, : 3 * out_size] for g in first_g],
+            [g[:, 3 * out_size :] for g in first_g],
+            up_g,
+            down_g,
+        )
         merged = [
             grid.merge_plain(pieces, parts, size)
             for pieces, (_, parts, size) in zip(split_g, SECTIONS)
@@ -946,10 +993,8 @@
         *gain_triple,
         *aba_triple,
         *aba_gain_triple,
-        *embed_triple,
-        output_new,
-        output_first_new,
-        output_second_new,
+        *[values.transpose(1, 0, 2) for values in embed_triple],
+        *[values.transpose(0, 2, 1) for values in (output_new, output_first_new, output_second_new)],
     )
 
 

time: 1340 us -> 1200 us (0.90)
  waiting for transfers between devices: 667 us -> 550 us
  matrix products: 185 us -> 151 us
  Pallas kernels: 108 us -> 124 us
    ppermute x70 -> x66, waiting for transfers between devices: 297 us -> 181 us  [pair(): lax.ppermute(values, ('q', 'p', 'h'), [(i, i ^ step) for i in range(self....]
    ppermute x4, waiting for transfers between devices: 131 us -> 25.9 us  [columns(): got = lax.ppermute(values, 'p', [(i, i ^ d) for i in range(self.parts)])]
    ppermute x15 -> x18, waiting for transfers between devices: 12 us -> 73.3 us  [trade(): lax.ppermute(values, ('q', 'p'), [(i, i ^ step) for i in range(SHARERS)])]
    ppermute x14 -> x13, waiting for transfers between devices: 223 us -> 266 us  [facing(): return lax.ppermute(values, 'a', [(0, 1), (1, 0)])]
    dot_general x68 -> x57, matrix products: 154 us -> 119 us  [dot(): lax.dot_general(left, right, (((left_dim,), (right_dim,)), ((), ())), pre...]
    ppermute x70 -> x66, starting transfers between devices: 80.1 us -> 70.3 us  [pair(): lax.ppermute(values, ('q', 'p', 'h'), [(i, i ^ step) for i in range(self....]
    pallas_call x2 -> x3, Pallas kernels: 25.8 us -> 32.5 us  [split_weights(): pl.pallas_call(functools.partial(split_kernel, sections), out_shape=[jax....]
    unnamed x417 -> x385, local copies, waits for them, and re-layouts: 43.3 us -> 39.9 us
  transfers between devices with their start and end apart: 104 -> 102, of which waited for: 67 -> 73; matrix products, arithmetic and copies ran while one was open for 12% -> 13% of each run, Pallas kernels for 2% -> 2%
where the time goes in v4:
time: 1200 us; the launch traced here: 1190 us
  waiting for transfers between devices  550 us (46%)
  matrix products  151 us (13%)
  other arithmetic  124 us (10%)
  Pallas kernels  124 us (10%)
  starting transfers between devices  114 us (10%)
  local copies, waits for them, and re-layouts  95.7 us (8%)
  between operations  30.3 us (3%)
    ppermute x13, waiting for transfers between devices, facing(): return lax.ppermute(values, 'a', [(0, 1), (1, 0)])  266 us
    ppermute x66, waiting for transfers between devices, pair(): lax.ppermute(values, ('q', 'p', 'h'), [(i, i ^ step) for i in range(self....  181 us
    dot_general x57, matrix products, dot(): lax.dot_general(left, right, (((left_dim,), (right_dim,)), ((), ())), pre...  119 us
    ppermute x18, waiting for transfers between devices, trade(): lax.ppermute(values, ('q', 'p'), [(i, i ^ step) for i in range(SHARERS)])  73.3 us
    ppermute x66, starting transfers between devices, pair(): lax.ppermute(values, ('q', 'p', 'h'), [(i, i ^ step) for i in range(self....  70.3 us
    pallas_call x1, Pallas kernels, moments_step(): pl.pallas_call(moments_kernel, out_shape=[shape, shape, jax.ShapeDtypeStr...  56.5 us
    unnamed x385, local copies, waits for them, and re-layouts  39.9 us
    pallas_call x3, Pallas kernels, split_weights(): pl.pallas_call(functools.partial(split_kernel, sections), out_shape=[jax....  32.5 us
  transfers between devices with their start and end apart: 102, of which 73 were waited for; matrix products, arithmetic and copies ran while one was open for 13% of the time, Pallas kernels for 2%

profile of v4, /device:TPU:0, one launch (start us, length us, event | category | flops | bytes accessed | tf_op | source)
XLA Modules:
  0.0 1189.4 jit_solution(645830309545963649)
XLA Ops:
  5.7 9.4 shard_map.364
  30.9 3.8 collective-permute-start.4
  39.3 12.5 %shard_map.365 = (bf16[512,1280]{1,0:T(8,128)(2,1)S(1)}, bf16[512,1280]{1,0:T(8,128)(2,1)}, bf16[512,1280]{1,0:T(8,128)(2,1)}, bf16[512,1280]{1,0:T(8,128)(2,1)}) custom-call(s32[2]{0:T(128)S(1)} %pad_add_fusion.side_ref, f32[512,96,128]{2,1,0:T(8,128)} %bitcast.469, f32[512,96,128]{2,1,0:T(8,128)} %bitcast.470), custom_call_target="tpu_custom_call" | custom-call | flops 1 | bytes 1 | tf_op jit(solution)/shard_map/pallas_call | solution.py:291
  72.9 10.3 shard_map.366
  88.3 3.9 reduce_sum.679
  92.3 4.5 multiply_reduce_fusion.3
  104.3 11.8 collective-permute-done.6
  116.2 4.6 collective-permute-done.7
  120.8 10.9 collective-permute-done.8
  132.0 4.5 convolution_convert_fusion.7
  145.2 10.6 shard_map.367
  155.9 46.1 %collective-permute-done.9 = bf16[1024,768]{1,0:T(8,128)(2,1)} collective-permute-done((bf16[1024,768]{1,0:T(8,128)(2,1)}, bf16[1024,768]{1,0:T(8,128)(2,1)}, u32[]{:S(2)}, u32[]{:S(2)}) %collective-permute-start.9) | collective-permute-done | bytes 1572896 | tf_op jit(solution)/shard_map/ppermute | solution.py:508
  205.0 20.9 %collective-permute-done.12 = bf16[512,1280]{1,0:T(8,128)(2,1)} collective-permute-done((bf16[512,1280]{1,0:T(8,128)(2,1)}, bf16[512,1280]{1,0:T(8,128)(2,1)}, u32[]{:S(2)}, u32[]{:S(2)}) %collective-permute-start.12) | collective-permute-done | bytes 1310752 | tf_op jit(solution)/shard_map/ppermute | solution.py:471
  232.0 9.7 collective-permute-done.16
  241.7 6.4 collective-permute-done.15
  257.9 4.2 shard_map.368
  262.2 3.9 collective-permute-start.23
  274.9 4.2 collective-permute-done.23
  279.6 9.1 collective-permute-done.22
  288.7 3.9 collective-permute-done.21
  307.9 10.5 collective-permute-done.26.refs_1_
  326.9 3.8 collective-permute-done.32.refs_7_
  330.7 3.9 shard_map.369
  354.8 85.1 %collective-permute-done.34 = bf16[1024,1024]{1,0:T(8,128)(2,1)S(1)} collective-permute-done((bf16[1024,1024]{1,0:T(8,128)(2,1)S(1)}, bf16[1024,1024]{1,0:T(8,128)(2,1)S(1)}, u32[]{:S(2)}, u32[]{:S(2)}) %collective-permute-start.34) | collective-permute-done | bytes 2097184 | tf_op jit(solution)/shard_map/ppermute | solution.py:508
  446.2 3.7 convolution_convert_fusion.3.refs_0_.refs_1_.refs_2_.refs_3_.refs_4_.refs_5_.refs_6_.refs_7_
  451.6 4.4 shard_map.370
  468.4 5.0 collective-permute-done.44
  473.5 8.6 collective-permute-done.43
  482.0 4.3 collective-permute-done.42
  492.3 12.1 %collective-permute-done.46 = f32[32,2048]{1,0:T(8,128)S(1)} collective-permute-done((f32[32,2048]{1,0:T(8,128)S(1)}, f32[32,2048]{1,0:T(8,128)S(1)}, u32[]{:S(2)}, u32[]{:S(2)}) %collective-permute-start.46) | collective-permute-done | bytes 262176 | tf_op jit(solution)/shard_map/ppermute | solution.py:508
  565.6 8.3 collective-permute-done.47
  586.7 6.5 collective-permute-done.50.refs_3_
  595.6 4.9 collective-permute-done.53.refs_6_
  601.3 4.2 collective-permute-done.54.refs_7_
  605.5 3.9 shard_map.371
  620.4 4.0 convolution_convert_fusion.8
  643.8 74.1 %collective-permute-done.56 = bf16[1024,1024]{1,0:T(8,128)(2,1)S(1)} collective-permute-done((bf16[1024,1024]{1,0:T(8,128)(2,1)S(1)}, bf16[1024,1024]{1,0:T(8,128)(2,1)S(1)}, u32[]{:S(2)}, u32[]{:S(2)}) %collective-permute-start.56) | collective-permute-done | bytes 2097184 | tf_op jit(solution)/shard_map/ppermute | solution.py:508
  718.9 7.6 collective-permute-done.59.rest_11_
  732.4 6.0 convolution_convert_fusion.1.refs_0_.refs_1_.refs_2_.refs_3_.refs_4_.refs_5_.refs_6_.refs_7_
  744.5 4.9 collective-permute-done.70
  752.9 6.1 collective-permute-done.71
  762.2 5.4 collective-permute-done.72
  771.6 4.4 shard_map.372
  785.6 4.3 collective-permute-done.67
  790.9 4.3 collective-permute-done.66
  800.5 5.2 collective-permute-done.65
  805.7 4.2 collective-permute-done.64
  821.7 3.8 collective-permute-done.74.refs_1_
  828.6 6.8 collective-permute-done.76.refs_3_
  837.1 5.5 collective-permute-done.79.refs_6_
  846.1 3.8 shard_map.373
  890.6 24.7 %collective-permute-done.82 = bf16[1024,256]{1,0:T(8,128)(2,1)S(1)} collective-permute-done((bf16[1024,256]{1,0:T(8,128)(2,1)S(1)}, bf16[1024,256]{1,0:T(8,128)(2,1)S(1)}, u32[]{:S(2)}, u32[]{:S(2)}) %collective-permute-start.82) | collective-permute-done | bytes 524320 | tf_op jit(solution)/shard_map/ppermute | solution.py:508
  922.7 6.5 collective-permute-done.86
  946.9 7.9 multiply_reduce_fusion.1
  962.0 7.6 multiply_convert_fusion
  986.6 13.8 %collective-permute-done.91.rest_3_ = bf16[512,1024]{1,0:T(8,128)(2,1)} collective-permute-done((bf16[512,1024]{1,0:T(8,128)(2,1)}, bf16[512,1024]{1,0:T(8,128)(2,1)}, u32[]{:S(2)}, u32[]{:S(2)}) %collective-permute-start.91) | collective-permute-done | bytes 1048608 | tf_op jit(solution)/shard_map/ppermute | solution.py:471
  1003.0 8.1 collective-permute-done.93
  1012.2 7.1 collective-permute-done.94
  1020.9 5.7 collective-permute-done.95
  1033.1 7.2 collective-permute-done.96
  1058.0 56.5 %shard_map.374 = (f32[512,96,128]{2,1,0:T(8,128)}, f32[512,96,128]{2,1,0:T(8,128)}, bf16[512,96,128]{2,1,0:T(8,128)(2,1)}, f32[2,8,128]{2,1,0:T(8,128)S(1)}) custom-call(s32[2]{0:T(128)S(1)} %copy-done.4, f32[1]{0:T(128)} %bitcast.118.clip_ref, f32[512,96,128]{2,1,0:T(8,128)} %bitcast.472, f32[512,96,128]{2,1,0:T(8,128)} %bitcast.477, ...), custom_call_target="tpu_custom_call" | custom-call | flops 125829120 | bytes 150994944 | tf_op jit(solution)/shard_map/pallas_call | solution.py:352
  1130.6 4.5 fusion.25
  1135.9 3.7 copy_subtract_fusion
  1166.5 20.8 %multiply_subtract_fusion = f32[512,96,128]{2,1,0:T(8,128)} fusion(f32[512,96,128]{2,1,0:T(8,128)} %bitcast.473, bf16[512,96,128]{2,1,0:T(8,128)(2,1)} %get-tuple-element.280, f32[]{:T(128)} %bitcast.132), kind=kLoop, calls=%fused_computation | loop fusion | flops 18874368 | bytes 62914564 | tf_op jit(solution)/shard_map/sub | solution.py:197
  (875 shorter events, 470.3 us)
Async XLA Ops:
  2.7 15.0 %collective-permute-start = (bf16[32,128]{1,0:T(8,128)(2,1)S(1)}, bf16[32,128]{1,0:T(8,128)(2,1)S(1)}, u32[]{:S(2)}, u32[]{:S(2)}) collective-permute-start(bf16[32,128]{1,0:T(8,128)(2,1)S(1)} %get-tuple-element.393), channel_id=1, source_target_pairs={{0,1},{1,0},{2,3},{3,2},{4,5},{5,4},{6,7},{7,6},{8,9},{9,8},{10,11... | collective-permute-start | bytes 24584 | tf_op jit(solution)/shard_map/ppermute | solution.py:468
  4.1 24.5 %collective-permute-start.13 = (bf16[1,16,64,32]{2,3,1,0:T(8,128)(2,1)S(1)}, bf16[1,16,64,32]{2,3,1,0:T(8,128)(2,1)S(1)}, u32[]{:S(2)}, u32[]{:S(2)}) collective-permute-start(bf16[1,16,64,32]{2,3,1,0:T(8,128)(2,1)S(1)} %convert_bitcast_fusion), channel_id=1, source_target_pairs={{0,1},{1,0},{2,3},{3,2},{4,5},{5,4},{6,7},{7,6},{8,9},{9,8},{10,11... | collective-permute-start | bytes 196616 | tf_op jit(solution)/shard_map/ppermute | solution.py:468
  98.5 17.7 %collective-permute-start.6 = (bf16[512,768]{1,0:T(8,128)(2,1)}, bf16[512,768]{1,0:T(8,128)(2,1)S(1)}, u32[]{:S(2)}, u32[]{:S(2)}) collective-permute-start(bf16[512,768]{1,0:T(8,128)(2,1)} %copy-done.14), channel_id=1, source_target_pairs={{0,4},{4,0},{8,12},{12,8},{1,5},{5,1},{9,13},{13,9},{2,6},{6,2},{1... | collective-permute-start | bytes 2359304 | tf_op jit(solution)/shard_map/ppermute | solution.py:471
  99.9 20.8 %collective-permute-start.7 = (bf16[512,768]{1,0:T(8,128)(2,1)}, bf16[512,768]{1,0:T(8,128)(2,1)S(1)}, u32[]{:S(2)}, u32[]{:S(2)}) collective-permute-start(bf16[512,768]{1,0:T(8,128)(2,1)} %copy-done.13), channel_id=1, source_target_pairs={{0,8},{4,12},{8,0},{12,4},{1,9},{5,13},{9,1},{13,5},{2,10},{6,14},... | collective-permute-start | bytes 2359304 | tf_op jit(solution)/shard_map/ppermute | solution.py:471
  102.1 29.6 %collective-permute-start.8 = (bf16[512,768]{1,0:T(8,128)(2,1)S(1)}, bf16[512,768]{1,0:T(8,128)(2,1)S(1)}, u32[]{:S(2)}, u32[]{:S(2)}) collective-permute-start(bf16[512,768]{1,0:T(8,128)(2,1)S(1)} %copy-done.12), channel_id=1, source_target_pairs={{0,12},{4,8},{8,4},{12,0},{1,13},{5,9},{9,5},{13,1},{2,14},{6,10},... | collective-permute-start | bytes 2359304 | tf_op jit(solution)/shard_map/ppermute | solution.py:471
  136.5 65.5 %collective-permute-start.9 = (bf16[1024,768]{1,0:T(8,128)(2,1)}, bf16[1024,768]{1,0:T(8,128)(2,1)}, u32[]{:S(2)}, u32[]{:S(2)}) collective-permute-start(bf16[1024,768]{1,0:T(8,128)(2,1)} %convolution_convert_fusion.7), channel_id=1, source_target_pairs={{0,16},{16,0},{1,17},{17,1},{2,18},{18,2},{3,19},{19,3},{4,20},{20... | collective-permute-start | bytes 4718600 | tf_op jit(solution)/shard_map/ppermute | solution.py:508
  138.7 65.6 %collective-permute-start.10 = (bf16[512,1280]{1,0:T(8,128)(2,1)}, bf16[512,1280]{1,0:T(8,128)(2,1)}, u32[]{:S(2)}, u32[]{:S(2)}) collective-permute-start(bf16[512,1280]{1,0:T(8,128)(2,1)} %get-tuple-element.178), channel_id=1, source_target_pairs={{0,4},{4,0},{8,12},{12,8},{1,5},{5,1},{9,13},{13,9},{2,6},{6,2},{1... | collective-permute-start | bytes 3932168 | tf_op jit(solution)/shard_map/ppermute | solution.py:471
  140.2 64.7 %collective-permute-start.11 = (bf16[512,1280]{1,0:T(8,128)(2,1)}, bf16[512,1280]{1,0:T(8,128)(2,1)}, u32[]{:S(2)}, u32[]{:S(2)}) collective-permute-start(bf16[512,1280]{1,0:T(8,128)(2,1)} %get-tuple-element.179), channel_id=1, source_target_pairs={{0,8},{4,12},{8,0},{12,4},{1,9},{5,13},{9,1},{13,5},{2,10},{6,14},... | collective-permute-start | bytes 3932168 | tf_op jit(solution)/shard_map/ppermute | solution.py:471
  142.0 83.9 %collective-permute-start.12 = (bf16[512,1280]{1,0:T(8,128)(2,1)}, bf16[512,1280]{1,0:T(8,128)(2,1)}, u32[]{:S(2)}, u32[]{:S(2)}) collective-permute-start(bf16[512,1280]{1,0:T(8,128)(2,1)} %get-tuple-element.180), channel_id=1, source_target_pairs={{0,12},{4,8},{8,4},{12,0},{1,13},{5,9},{9,5},{13,1},{2,14},{6,10},... | collective-permute-start | bytes 3932168 | tf_op jit(solution)/shard_map/ppermute | solution.py:471
  226.8 14.9 %collective-permute-start.16 = (bf16[1024,256]{1,0:T(8,128)(2,1)S(1)}, bf16[1024,256]{1,0:T(8,128)(2,1)S(1)}, u32[]{:S(2)}, u32[]{:S(2)}) collective-permute-start(bf16[1024,256]{1,0:T(8,128)(2,1)S(1)} %get-tuple-element.399), channel_id=1, source_target_pairs={{0,4},{4,0},{1,5},{5,1},{2,6},{6,2},{3,7},{7,3},{8,12},{12,8},{9,1... | collective-permute-start | bytes 1572872 | tf_op jit(solution)/shard_map/ppermute | solution.py:571
  228.2 19.9 %collective-permute-start.15 = (bf16[1024,256]{1,0:T(8,128)(2,1)S(1)}, bf16[1024,256]{1,0:T(8,128)(2,1)S(1)}, u32[]{:S(2)}, u32[]{:S(2)}) collective-permute-start(bf16[1024,256]{1,0:T(8,128)(2,1)S(1)} %get-tuple-element.400), channel_id=1, source_target_pairs={{0,4},{4,0},{1,5},{5,1},{2,6},{6,2},{3,7},{7,3},{8,12},{12,8},{9,1... | collective-permute-start | bytes 1572872 | tf_op jit(solution)/shard_map/ppermute | solution.py:571
  262.2 16.9 %collective-permute-start.23 = (bf16[64,2048]{1,0:T(8,128)(2,1)}, bf16[64,2048]{1,0:T(8,128)(2,1)S(1)}, u32[]{:S(2)}, u32[]{:S(2)}) collective-permute-start(bf16[64,2048]{1,0:T(8,128)(2,1)} %get-tuple-element.201), channel_id=1, source_target_pairs={{0,12},{1,13},{2,14},{3,15},{4,8},{5,9},{6,10},{7,11},{8,4},{9,5},... | collective-permute-start | bytes 786440 | tf_op jit(solution)/shard_map/ppermute | solution.py:468
  266.1 22.6 %collective-permute-start.22 = (bf16[64,2048]{1,0:T(8,128)(2,1)}, bf16[64,2048]{1,0:T(8,128)(2,1)S(1)}, u32[]{:S(2)}, u32[]{:S(2)}) collective-permute-start(bf16[64,2048]{1,0:T(8,128)(2,1)} %get-tuple-element.200), channel_id=1, source_target_pairs={{0,10},{1,11},{2,8},{3,9},{4,14},{5,15},{6,12},{7,13},{8,2},{9,3},... | collective-permute-start | bytes 786440 | tf_op jit(solution)/shard_map/ppermute | solution.py:468
  266.1 26.4 %collective-permute-start.21 = (bf16[64,2048]{1,0:T(8,128)(2,1)}, bf16[64,2048]{1,0:T(8,128)(2,1)S(1)}, u32[]{:S(2)}, u32[]{:S(2)}) collective-permute-start(bf16[64,2048]{1,0:T(8,128)(2,1)} %get-tuple-element.199), channel_id=1, source_target_pairs={{0,8},{1,9},{2,10},{3,11},{4,12},{5,13},{6,14},{7,15},{8,0},{9,1},... | collective-permute-start | bytes 786440 | tf_op jit(solution)/shard_map/ppermute | solution.py:468
  268.1 24.5 %collective-permute-start.20 = (bf16[64,2048]{1,0:T(8,128)(2,1)}, bf16[64,2048]{1,0:T(8,128)(2,1)S(1)}, u32[]{:S(2)}, u32[]{:S(2)}) collective-permute-start(bf16[64,2048]{1,0:T(8,128)(2,1)} %get-tuple-element.198), channel_id=1, source_target_pairs={{0,6},{1,7},{2,4},{3,5},{4,2},{5,3},{6,0},{7,1},{8,14},{9,15},{10,... | collective-permute-start | bytes 786440 | tf_op jit(solution)/shard_map/ppermute | solution.py:468
  273.5 19.8 %collective-permute-start.19 = (bf16[64,2048]{1,0:T(8,128)(2,1)}, bf16[64,2048]{1,0:T(8,128)(2,1)S(1)}, u32[]{:S(2)}, u32[]{:S(2)}) collective-permute-start(bf16[64,2048]{1,0:T(8,128)(2,1)} %get-tuple-element.197), channel_id=1, source_target_pairs={{0,4},{1,5},{2,6},{3,7},{4,0},{5,1},{6,2},{7,3},{8,12},{9,13},{10,... | collective-permute-start | bytes 786440 | tf_op jit(solution)/shard_map/ppermute | solution.py:468
  279.1 15.1 %collective-permute-start.18 = (bf16[64,2048]{1,0:T(8,128)(2,1)}, bf16[64,2048]{1,0:T(8,128)(2,1)S(1)}, u32[]{:S(2)}, u32[]{:S(2)}) collective-permute-start(bf16[64,2048]{1,0:T(8,128)(2,1)} %get-tuple-element.196), channel_id=1, source_target_pairs={{0,2},{1,3},{2,0},{3,1},{4,6},{5,7},{6,4},{7,5},{8,10},{9,11},{10,... | collective-permute-start | bytes 786440 | tf_op jit(solution)/shard_map/ppermute | solution.py:468
  301.4 17.0 %collective-permute-start.26 = (bf16[64,2048]{1,0:T(8,128)(2,1)S(1)}, bf16[64,2048]{1,0:T(8,128)(2,1)S(1)}, u32[]{:S(2)}, u32[]{:S(2)}) collective-permute-start(bf16[64,2048]{1,0:T(8,128)(2,1)S(1)} %multiply_convert_fusion.11.refs_0_), channel_id=1, source_target_pairs={{0,2},{1,3},{2,0},{3,1},{4,6},{5,7},{6,4},{7,5},{8,10},{9,11},{10,... | collective-permute-start | bytes 786440 | tf_op jit(solution)/shard_map/ppermute | solution.py:468
  302.9 18.6 %collective-permute-start.27 = (bf16[64,2048]{1,0:T(8,128)(2,1)S(1)}, bf16[64,2048]{1,0:T(8,128)(2,1)S(1)}, u32[]{:S(2)}, u32[]{:S(2)}) collective-permute-start(bf16[64,2048]{1,0:T(8,128)(2,1)S(1)} %multiply_convert_fusion.11.refs_0_), channel_id=1, source_target_pairs={{0,4},{1,5},{2,6},{3,7},{4,0},{5,1},{6,2},{7,3},{8,12},{9,13},{10,... | collective-permute-start | bytes 786440 | tf_op jit(solution)/shard_map/ppermute | solution.py:468
  303.9 19.5 %collective-permute-start.28 = (bf16[64,2048]{1,0:T(8,128)(2,1)S(1)}, bf16[64,2048]{1,0:T(8,128)(2,1)S(1)}, u32[]{:S(2)}, u32[]{:S(2)}) collective-permute-start(bf16[64,2048]{1,0:T(8,128)(2,1)S(1)} %multiply_convert_fusion.11.refs_0_), channel_id=1, source_target_pairs={{0,6},{1,7},{2,4},{3,5},{4,2},{5,3},{6,0},{7,1},{8,14},{9,15},{10,... | collective-permute-start | bytes 786440 | tf_op jit(solution)/shard_map/ppermute | solution.py:468
  305.0 18.5 %collective-permute-start.29 = (bf16[64,2048]{1,0:T(8,128)(2,1)S(1)}, bf16[64,2048]{1,0:T(8,128)(2,1)S(1)}, u32[]{:S(2)}, u32[]{:S(2)}) collective-permute-start(bf16[64,2048]{1,0:T(8,128)(2,1)S(1)} %multiply_convert_fusion.11.refs_0_), channel_id=1, source_target_pairs={{0,8},{1,9},{2,10},{3,11},{4,12},{5,13},{6,14},{7,15},{8,0},{9,1},... | collective-permute-start | bytes 786440 | tf_op jit(solution)/shard_map/ppermute | solution.py:468
  306.8 16.6 %collective-permute-start.30 = (bf16[64,2048]{1,0:T(8,128)(2,1)S(1)}, bf16[64,2048]{1,0:T(8,128)(2,1)S(1)}, u32[]{:S(2)}, u32[]{:S(2)}) collective-permute-start(bf16[64,2048]{1,0:T(8,128)(2,1)S(1)} %multiply_convert_fusion.11.refs_0_), channel_id=1, source_target_pairs={{0,10},{1,11},{2,8},{3,9},{4,14},{5,15},{6,12},{7,13},{8,2},{9,3},... | collective-permute-start | bytes 786440 | tf_op jit(solution)/shard_map/ppermute | solution.py:468
  345.8 94.0 %collective-permute-start.34 = (bf16[1024,1024]{1,0:T(8,128)(2,1)S(1)}, bf16[1024,1024]{1,0:T(8,128)(2,1)S(1)}, u32[]{:S(2)}, u32[]{:S(2)}) collective-permute-start(bf16[1024,1024]{1,0:T(8,128)(2,1)S(1)} %pad_maximum_fusion.1), channel_id=1, source_target_pairs={{0,16},{16,0},{1,17},{17,1},{2,18},{18,2},{3,19},{19,3},{4,20},{20... | collective-permute-start | bytes 6291464 | tf_op jit(solution)/shard_map/ppermute | solution.py:508
  348.5 92.3 %collective-permute-start.35 = (bf16[512,1024]{1,0:T(8,128)(2,1)S(1)}, bf16[512,1024]{1,0:T(8,128)(2,1)S(1)}, u32[]{:S(2)}, u32[]{:S(2)}) collective-permute-start(bf16[512,1024]{1,0:T(8,128)(2,1)S(1)} %copy-done.10), channel_id=1, source_target_pairs={{0,4},{4,0},{8,12},{12,8},{1,5},{5,1},{9,13},{13,9},{2,6},{6,2},{1... | collective-permute-start | bytes 3145736 | tf_op jit(solution)/shard_map/ppermute | solution.py:471
  349.5 91.3 %collective-permute-start.36 = (bf16[512,1024]{1,0:T(8,128)(2,1)S(1)}, bf16[512,1024]{1,0:T(8,128)(2,1)S(1)}, u32[]{:S(2)}, u32[]{:S(2)}) collective-permute-start(bf16[512,1024]{1,0:T(8,128)(2,1)S(1)} %copy-done.8), channel_id=1, source_target_pairs={{0,8},{4,12},{8,0},{12,4},{1,9},{5,13},{9,1},{13,5},{2,10},{6,14},... | collective-permute-start | bytes 3145736 | tf_op jit(solution)/shard_map/ppermute | solution.py:471
  352.0 89.2 %collective-permute-start.37 = (bf16[512,1024]{1,0:T(8,128)(2,1)S(1)}, bf16[512,1024]{1,0:T(8,128)(2,1)S(1)}, u32[]{:S(2)}, u32[]{:S(2)}) collective-permute-start(bf16[512,1024]{1,0:T(8,128)(2,1)S(1)} %copy-done.6), channel_id=1, source_target_pairs={{0,12},{4,8},{8,4},{12,0},{1,13},{5,9},{9,5},{13,1},{2,14},{6,10},... | collective-permute-start | bytes 3145736 | tf_op jit(solution)/shard_map/ppermute | solution.py:471
  457.6 15.8 %collective-permute-start.44 = (bf16[64,2048]{1,0:T(8,128)(2,1)}, bf16[64,2048]{1,0:T(8,128)(2,1)S(1)}, u32[]{:S(2)}, u32[]{:S(2)}) collective-permute-start(bf16[64,2048]{1,0:T(8,128)(2,1)} %get-tuple-element.223), channel_id=1, source_target_pairs={{0,12},{1,13},{2,14},{3,15},{4,8},{5,9},{6,10},{7,11},{8,4},{9,5},... | collective-permute-start | bytes 786440 | tf_op jit(solution)/shard_map/ppermute | solution.py:468
  460.4 21.7 %collective-permute-start.43 = (bf16[64,2048]{1,0:T(8,128)(2,1)}, bf16[64,2048]{1,0:T(8,128)(2,1)S(1)}, u32[]{:S(2)}, u32[]{:S(2)}) collective-permute-start(bf16[64,2048]{1,0:T(8,128)(2,1)} %get-tuple-element.222), channel_id=1, source_target_pairs={{0,10},{1,11},{2,8},{3,9},{4,14},{5,15},{6,12},{7,13},{8,2},{9,3},... | collective-permute-start | bytes 786440 | tf_op jit(solution)/shard_map/ppermute | solution.py:468
  460.6 25.7 %collective-permute-start.42 = (bf16[64,2048]{1,0:T(8,128)(2,1)}, bf16[64,2048]{1,0:T(8,128)(2,1)S(1)}, u32[]{:S(2)}, u32[]{:S(2)}) collective-permute-start(bf16[64,2048]{1,0:T(8,128)(2,1)} %get-tuple-element.221), channel_id=1, source_target_pairs={{0,8},{1,9},{2,10},{3,11},{4,12},{5,13},{6,14},{7,15},{8,0},{9,1},... | collective-permute-start | bytes 786440 | tf_op jit(solution)/shard_map/ppermute | solution.py:468
  461.9 24.4 %collective-permute-start.41 = (bf16[64,2048]{1,0:T(8,128)(2,1)}, bf16[64,2048]{1,0:T(8,128)(2,1)S(1)}, u32[]{:S(2)}, u32[]{:S(2)}) collective-permute-start(bf16[64,2048]{1,0:T(8,128)(2,1)} %get-tuple-element.220), channel_id=1, source_target_pairs={{0,6},{1,7},{2,4},{3,5},{4,2},{5,3},{6,0},{7,1},{8,14},{9,15},{10,... | collective-permute-start | bytes 786440 | tf_op jit(solution)/shard_map/ppermute | solution.py:468
  467.3 20.4 %collective-permute-start.40 = (bf16[64,2048]{1,0:T(8,128)(2,1)}, bf16[64,2048]{1,0:T(8,128)(2,1)S(1)}, u32[]{:S(2)}, u32[]{:S(2)}) collective-permute-start(bf16[64,2048]{1,0:T(8,128)(2,1)} %get-tuple-element.219), channel_id=1, source_target_pairs={{0,4},{1,5},{2,6},{3,7},{4,0},{5,1},{6,2},{7,3},{8,12},{9,13},{10,... | collective-permute-start | bytes 786440 | tf_op jit(solution)/shard_map/ppermute | solution.py:468
  473.4 14.5 %collective-permute-start.39 = (bf16[64,2048]{1,0:T(8,128)(2,1)}, bf16[64,2048]{1,0:T(8,128)(2,1)S(1)}, u32[]{:S(2)}, u32[]{:S(2)}) collective-permute-start(bf16[64,2048]{1,0:T(8,128)(2,1)} %get-tuple-element.218), channel_id=1, source_target_pairs={{0,2},{1,3},{2,0},{3,1},{4,6},{5,7},{6,4},{7,5},{8,10},{9,11},{10,... | collective-permute-start | bytes 786440 | tf_op jit(solution)/shard_map/ppermute | solution.py:468
  489.6 14.8 %collective-permute-start.46 = (f32[32,2048]{1,0:T(8,128)S(1)}, f32[32,2048]{1,0:T(8,128)S(1)}, u32[]{:S(2)}, u32[]{:S(2)}) collective-permute-start(f32[32,2048]{1,0:T(8,128)S(1)} %slice_select_fusion.1), channel_id=1, source_target_pairs={{0,16},{16,0},{1,17},{17,1},{2,18},{18,2},{3,19},{19,3},{4,20},{20... | collective-permute-start | bytes 786440 | tf_op jit(solution)/shard_map/ppermute | solution.py:508
  577.0 16.1 %collective-permute-start.50 = (bf16[64,2048]{1,0:T(8,128)(2,1)S(1)}, bf16[64,2048]{1,0:T(8,128)(2,1)S(1)}, u32[]{:S(2)}, u32[]{:S(2)}) collective-permute-start(bf16[64,2048]{1,0:T(8,128)(2,1)S(1)} %pad_maximum_fusion.24.refs_0_), channel_id=1, source_target_pairs={{0,6},{1,7},{2,4},{3,5},{4,2},{5,3},{6,0},{7,1},{8,14},{9,15},{10,... | collective-permute-start | bytes 786440 | tf_op jit(solution)/shard_map/ppermute | solution.py:468
  577.7 15.5 %collective-permute-start.51 = (bf16[64,2048]{1,0:T(8,128)(2,1)S(1)}, bf16[64,2048]{1,0:T(8,128)(2,1)S(1)}, u32[]{:S(2)}, u32[]{:S(2)}) collective-permute-start(bf16[64,2048]{1,0:T(8,128)(2,1)S(1)} %pad_maximum_fusion.24.refs_0_), channel_id=1, source_target_pairs={{0,8},{1,9},{2,10},{3,11},{4,12},{5,13},{6,14},{7,15},{8,0},{9,1},... | collective-permute-start | bytes 786440 | tf_op jit(solution)/shard_map/ppermute | solution.py:468
  577.7 17.9 %collective-permute-start.52 = (bf16[64,2048]{1,0:T(8,128)(2,1)S(1)}, bf16[64,2048]{1,0:T(8,128)(2,1)S(1)}, u32[]{:S(2)}, u32[]{:S(2)}) collective-permute-start(bf16[64,2048]{1,0:T(8,128)(2,1)S(1)} %pad_maximum_fusion.24.refs_0_), channel_id=1, source_target_pairs={{0,10},{1,11},{2,8},{3,9},{4,14},{5,15},{6,12},{7,13},{8,2},{9,3},... | collective-permute-start | bytes 786440 | tf_op jit(solution)/shard_map/ppermute | solution.py:468
  582.5 18.0 %collective-permute-start.53 = (bf16[64,2048]{1,0:T(8,128)(2,1)S(1)}, bf16[64,2048]{1,0:T(8,128)(2,1)S(1)}, u32[]{:S(2)}, u32[]{:S(2)}) collective-permute-start(bf16[64,2048]{1,0:T(8,128)(2,1)S(1)} %pad_maximum_fusion.24.refs_0_), channel_id=1, source_target_pairs={{0,12},{1,13},{2,14},{3,15},{4,8},{5,9},{6,10},{7,11},{8,4},{9,5},... | collective-permute-start | bytes 786440 | tf_op jit(solution)/shard_map/ppermute | solution.py:468
  585.2 20.3 %collective-permute-start.54 = (bf16[64,2048]{1,0:T(8,128)(2,1)S(1)}, bf16[64,2048]{1,0:T(8,128)(2,1)}, u32[]{:S(2)}, u32[]{:S(2)}) collective-permute-start(bf16[64,2048]{1,0:T(8,128)(2,1)S(1)} %pad_maximum_fusion.24.refs_0_), channel_id=1, source_target_pairs={{0,14},{1,15},{2,12},{3,13},{4,10},{5,11},{6,8},{7,9},{8,6},{9,7},... | collective-permute-start | bytes 786440 | tf_op jit(solution)/shard_map/ppermute | solution.py:468
  624.5 93.4 %collective-permute-start.56 = (bf16[1024,1024]{1,0:T(8,128)(2,1)S(1)}, bf16[1024,1024]{1,0:T(8,128)(2,1)S(1)}, u32[]{:S(2)}, u32[]{:S(2)}) collective-permute-start(bf16[1024,1024]{1,0:T(8,128)(2,1)S(1)} %pad_maximum_fusion.2), channel_id=1, source_target_pairs={{0,16},{16,0},{1,17},{17,1},{2,18},{18,2},{3,19},{19,3},{4,20},{20... | collective-permute-start | bytes 6291464 | tf_op jit(solution)/shard_map/ppermute | solution.py:508
  629.0 89.9 %collective-permute-start.57 = (bf16[512,1024]{1,0:T(8,128)(2,1)S(1)}, bf16[512,1024]{1,0:T(8,128)(2,1)S(1)}, u32[]{:S(2)}, u32[]{:S(2)}) collective-permute-start(bf16[512,1024]{1,0:T(8,128)(2,1)S(1)} %get-tuple-element.532), channel_id=1, source_target_pairs={{0,4},{4,0},{8,12},{12,8},{1,5},{5,1},{9,13},{13,9},{2,6},{6,2},{1... | collective-permute-start | bytes 3145736 | tf_op jit(solution)/shard_map/ppermute | solution.py:471
  633.4 85.5 %collective-permute-start.58 = (bf16[512,1024]{1,0:T(8,128)(2,1)S(1)}, bf16[512,1024]{1,0:T(8,128)(2,1)S(1)}, u32[]{:S(2)}, u32[]{:S(2)}) collective-permute-start(bf16[512,1024]{1,0:T(8,128)(2,1)S(1)} %get-tuple-element.534), channel_id=1, source_target_pairs={{0,8},{4,12},{8,0},{12,4},{1,9},{5,13},{9,1},{13,5},{2,10},{6,14},... | collective-permute-start | bytes 3145736 | tf_op jit(solution)/shard_map/ppermute | solution.py:471
  637.9 88.6 %collective-permute-start.59 = (bf16[512,1024]{1,0:T(8,128)(2,1)S(1)}, bf16[512,1024]{1,0:T(8,128)(2,1)S(1)}, u32[]{:S(2)}, u32[]{:S(2)}) collective-permute-start(bf16[512,1024]{1,0:T(8,128)(2,1)S(1)} %get-tuple-element.536), channel_id=1, source_target_pairs={{0,12},{4,8},{8,4},{12,0},{1,13},{5,9},{9,5},{13,1},{2,14},{6,10},... | collective-permute-start | bytes 3145736 | tf_op jit(solution)/shard_map/ppermute | solution.py:471
  741.7 28.6 %collective-permute-start.60 = (bf16[512,2048]{1,0:T(8,128)(2,1)S(1)}, bf16[512,2048]{1,0:T(8,128)(2,1)S(1)}, u32[]{:S(2)}, u32[]{:S(2)}) collective-permute-start(bf16[512,2048]{1,0:T(8,128)(2,1)S(1)} %convolution_convert_fusion), channel_id=1, source_target_pairs={{0,1},{1,0},{2,3},{3,2},{4,5},{5,4},{6,7},{7,6},{8,9},{9,8},{10,11... | collective-permute-start | bytes 6291464 | tf_op jit(solution)/shard_map/ppermute | solution.py:468
  767.6 16.5 %collective-permute-start.73 = (f32[641,128]{1,0:T(8,128)S(1)}, f32[641,128]{1,0:T(8,128)}, u32[]{:S(2)}, u32[]{:S(2)}) collective-permute-start(f32[641,128]{1,0:T(8,128)S(1)} %fusion.362), channel_id=1, source_target_pairs={{0,16},{16,0},{1,17},{17,1},{2,18},{18,2},{3,19},{19,3},{4,20},{20... | collective-permute-start | bytes 984584 | tf_op jit(solution)/shard_map/ppermute | solution.py:508
  776.0 13.9 %collective-permute-start.67 = (bf16[64,2048]{1,0:T(8,128)(2,1)}, bf16[64,2048]{1,0:T(8,128)(2,1)S(1)}, u32[]{:S(2)}, u32[]{:S(2)}) collective-permute-start(bf16[64,2048]{1,0:T(8,128)(2,1)} %get-tuple-element.234), channel_id=1, source_target_pairs={{0,14},{1,15},{2,12},{3,13},{4,10},{5,11},{6,8},{7,9},{8,6},{9,7},... | collective-permute-start | bytes 786440 | tf_op jit(solution)/shard_map/ppermute | solution.py:468
  778.7 16.4 %collective-permute-start.66 = (bf16[64,2048]{1,0:T(8,128)(2,1)}, bf16[64,2048]{1,0:T(8,128)(2,1)S(1)}, u32[]{:S(2)}, u32[]{:S(2)}) collective-permute-start(bf16[64,2048]{1,0:T(8,128)(2,1)} %get-tuple-element.233), channel_id=1, source_target_pairs={{0,12},{1,13},{2,14},{3,15},{4,8},{5,9},{6,10},{7,11},{8,4},{9,5},... | collective-permute-start | bytes 786440 | tf_op jit(solution)/shard_map/ppermute | solution.py:468
  781.6 24.1 %collective-permute-start.65 = (bf16[64,2048]{1,0:T(8,128)(2,1)S(1)}, bf16[64,2048]{1,0:T(8,128)(2,1)S(1)}, u32[]{:S(2)}, u32[]{:S(2)}) collective-permute-start(bf16[64,2048]{1,0:T(8,128)(2,1)S(1)} %copy-done.178), channel_id=1, source_target_pairs={{0,10},{1,11},{2,8},{3,9},{4,14},{5,15},{6,12},{7,13},{8,2},{9,3},... | collective-permute-start | bytes 786440 | tf_op jit(solution)/shard_map/ppermute | solution.py:468
  783.8 26.1 %collective-permute-start.64 = (bf16[64,2048]{1,0:T(8,128)(2,1)S(1)}, bf16[64,2048]{1,0:T(8,128)(2,1)S(1)}, u32[]{:S(2)}, u32[]{:S(2)}) collective-permute-start(bf16[64,2048]{1,0:T(8,128)(2,1)S(1)} %copy-done.177), channel_id=1, source_target_pairs={{0,8},{1,9},{2,10},{3,11},{4,12},{5,13},{6,14},{7,15},{8,0},{9,1},... | collective-permute-start | bytes 786440 | tf_op jit(solution)/shard_map/ppermute | solution.py:468
  784.1 25.8 %collective-permute-start.63 = (bf16[64,2048]{1,0:T(8,128)(2,1)S(1)}, bf16[64,2048]{1,0:T(8,128)(2,1)S(1)}, u32[]{:S(2)}, u32[]{:S(2)}) collective-permute-start(bf16[64,2048]{1,0:T(8,128)(2,1)S(1)} %copy-done.176), channel_id=1, source_target_pairs={{0,6},{1,7},{2,4},{3,5},{4,2},{5,3},{6,0},{7,1},{8,14},{9,15},{10,... | collective-permute-start | bytes 786440 | tf_op jit(solution)/shard_map/ppermute | solution.py:468
  789.9 20.9 %collective-permute-start.62 = (bf16[64,2048]{1,0:T(8,128)(2,1)S(1)}, bf16[64,2048]{1,0:T(8,128)(2,1)S(1)}, u32[]{:S(2)}, u32[]{:S(2)}) collective-permute-start(bf16[64,2048]{1,0:T(8,128)(2,1)S(1)} %copy-done.175), channel_id=1, source_target_pairs={{0,4},{1,5},{2,6},{3,7},{4,0},{5,1},{6,2},{7,3},{8,12},{9,13},{10,... | collective-permute-start | bytes 786440 | tf_op jit(solution)/shard_map/ppermute | solution.py:468
  795.2 16.5 %collective-permute-start.61 = (bf16[64,2048]{1,0:T(8,128)(2,1)S(1)}, bf16[64,2048]{1,0:T(8,128)(2,1)S(1)}, u32[]{:S(2)}, u32[]{:S(2)}) collective-permute-start(bf16[64,2048]{1,0:T(8,128)(2,1)S(1)} %copy-done.174), channel_id=1, source_target_pairs={{0,2},{1,3},{2,0},{3,1},{4,6},{5,7},{6,4},{7,5},{8,10},{9,11},{10,... | collective-permute-start | bytes 786440 | tf_op jit(solution)/shard_map/ppermute | solution.py:468
  819.4 16.0 %collective-permute-start.76 = (bf16[64,2048]{1,0:T(8,128)(2,1)S(1)}, bf16[64,2048]{1,0:T(8,128)(2,1)S(1)}, u32[]{:S(2)}, u32[]{:S(2)}) collective-permute-start(bf16[64,2048]{1,0:T(8,128)(2,1)S(1)} %multiply_add_fusion.1.refs_0_), channel_id=1, source_target_pairs={{0,6},{1,7},{2,4},{3,5},{4,2},{5,3},{6,0},{7,1},{8,14},{9,15},{10,... | collective-permute-start | bytes 786440 | tf_op jit(solution)/shard_map/ppermute | solution.py:468
  820.7 32.6 %collective-permute-start.87 = (bf16[1024,256]{1,0:T(8,128)(2,1)}, bf16[1024,256]{1,0:T(8,128)(2,1)S(1)}, u32[]{:S(2)}, u32[]{:S(2)}) collective-permute-start(bf16[1024,256]{1,0:T(8,128)(2,1)} %get-tuple-element.398), channel_id=1, source_target_pairs={{0,4},{4,0},{1,5},{5,1},{2,6},{6,2},{3,7},{7,3},{8,12},{12,8},{9,1... | collective-permute-start | bytes 1572872 | tf_op jit(solution)/shard_map/ppermute | solution.py:571
  821.7 13.7 %collective-permute-start.77 = (bf16[64,2048]{1,0:T(8,128)(2,1)S(1)}, bf16[64,2048]{1,0:T(8,128)(2,1)S(1)}, u32[]{:S(2)}, u32[]{:S(2)}) collective-permute-start(bf16[64,2048]{1,0:T(8,128)(2,1)S(1)} %multiply_add_fusion.1.refs_0_), channel_id=1, source_target_pairs={{0,8},{1,9},{2,10},{3,11},{4,12},{5,13},{6,14},{7,15},{8,0},{9,1},... | collective-permute-start | bytes 786440 | tf_op jit(solution)/shard_map/ppermute | solution.py:468
  827.6 15.0 %collective-permute-start.79 = (bf16[64,2048]{1,0:T(8,128)(2,1)S(1)}, bf16[64,2048]{1,0:T(8,128)(2,1)}, u32[]{:S(2)}, u32[]{:S(2)}) collective-permute-start(bf16[64,2048]{1,0:T(8,128)(2,1)S(1)} %multiply_add_fusion.1.refs_0_), channel_id=1, source_target_pairs={{0,12},{1,13},{2,14},{3,15},{4,8},{5,9},{6,10},{7,11},{8,4},{9,5},... | collective-permute-start | bytes 786440 | tf_op jit(solution)/shard_map/ppermute | solution.py:468
  849.9 24.7 %collective-permute-start.81 = (bf16[512,2048]{1,0:T(8,128)(2,1)}, bf16[512,2048]{1,0:T(8,128)(2,1)}, u32[]{:S(2)}, u32[]{:S(2)}) collective-permute-start(bf16[512,2048]{1,0:T(8,128)(2,1)} %shard_map.373), channel_id=1, source_target_pairs={{0,1},{1,0},{2,3},{3,2},{4,5},{5,4},{6,7},{7,6},{8,9},{9,8},{10,11... | collective-permute-start | bytes 6291464 | tf_op jit(solution)/shard_map/ppermute | solution.py:468
  860.1 55.4 %collective-permute-start.83 = (bf16[512,1024]{1,0:T(8,128)(2,1)}, bf16[512,1024]{1,0:T(8,128)(2,1)}, u32[]{:S(2)}, u32[]{:S(2)}) collective-permute-start(bf16[512,1024]{1,0:T(8,128)(2,1)} %get-tuple-element.243), channel_id=1, source_target_pairs={{0,4},{4,0},{8,12},{12,8},{1,5},{5,1},{9,13},{13,9},{2,6},{6,2},{1... | collective-permute-start | bytes 3145736 | tf_op jit(solution)/shard_map/ppermute | solution.py:471
  861.1 54.3 %collective-permute-start.84 = (bf16[512,1024]{1,0:T(8,128)(2,1)}, bf16[512,1024]{1,0:T(8,128)(2,1)}, u32[]{:S(2)}, u32[]{:S(2)}) collective-permute-start(bf16[512,1024]{1,0:T(8,128)(2,1)} %get-tuple-element.244), channel_id=1, source_target_pairs={{0,8},{4,12},{8,0},{12,4},{1,9},{5,13},{9,1},{13,5},{2,10},{6,14},... | collective-permute-start | bytes 3145736 | tf_op jit(solution)/shard_map/ppermute | solution.py:471
  861.1 57.0 %collective-permute-start.85 = (bf16[512,1024]{1,0:T(8,128)(2,1)}, bf16[512,1024]{1,0:T(8,128)(2,1)}, u32[]{:S(2)}, u32[]{:S(2)}) collective-permute-start(bf16[512,1024]{1,0:T(8,128)(2,1)} %get-tuple-element.245), channel_id=1, source_target_pairs={{0,12},{4,8},{8,4},{12,0},{1,13},{5,9},{9,5},{13,1},{2,14},{6,10},... | collective-permute-start | bytes 3145736 | tf_op jit(solution)/shard_map/ppermute | solution.py:471
  877.0 38.4 %collective-permute-start.82 = (bf16[1024,256]{1,0:T(8,128)(2,1)S(1)}, bf16[1024,256]{1,0:T(8,128)(2,1)S(1)}, u32[]{:S(2)}, u32[]{:S(2)}) collective-permute-start(bf16[1024,256]{1,0:T(8,128)(2,1)S(1)} %pad_maximum_fusion.18), channel_id=1, source_target_pairs={{0,16},{16,0},{1,17},{17,1},{2,18},{18,2},{3,19},{19,3},{4,20},{20... | collective-permute-start | bytes 1572872 | tf_op jit(solution)/shard_map/ppermute | solution.py:508
  955.2 31.4 %collective-permute-start.89 = (bf16[512,1024]{1,0:T(8,128)(2,1)}, bf16[512,1024]{1,0:T(8,128)(2,1)S(1)}, u32[]{:S(2)}, u32[]{:S(2)}) collective-permute-start(bf16[512,1024]{1,0:T(8,128)(2,1)} %pad_maximum_fusion.7), channel_id=1, source_target_pairs={{0,4},{4,0},{8,12},{12,8},{1,5},{5,1},{9,13},{13,9},{2,6},{6,2},{1... | collective-permute-start | bytes 3145736 | tf_op jit(solution)/shard_map/ppermute | solution.py:471
  956.2 30.4 %collective-permute-start.90 = (bf16[512,1024]{1,0:T(8,128)(2,1)}, bf16[512,1024]{1,0:T(8,128)(2,1)}, u32[]{:S(2)}, u32[]{:S(2)}) collective-permute-start(bf16[512,1024]{1,0:T(8,128)(2,1)} %pad_maximum_fusion.8), channel_id=1, source_target_pairs={{0,8},{4,12},{8,0},{12,4},{1,9},{5,13},{9,1},{13,5},{2,10},{6,14},... | collective-permute-start | bytes 3145736 | tf_op jit(solution)/shard_map/ppermute | solution.py:471
  957.7 42.7 %collective-permute-start.91 = (bf16[512,1024]{1,0:T(8,128)(2,1)}, bf16[512,1024]{1,0:T(8,128)(2,1)}, u32[]{:S(2)}, u32[]{:S(2)}) collective-permute-start(bf16[512,1024]{1,0:T(8,128)(2,1)} %pad_maximum_fusion.9), channel_id=1, source_target_pairs={{0,12},{4,8},{8,4},{12,0},{1,13},{5,9},{9,5},{13,1},{2,14},{6,10},... | collective-permute-start | bytes 3145736 | tf_op jit(solution)/shard_map/ppermute | solution.py:471
  1117.9 27.2 %collective-permute-start.97 = (f32[4]{0:T(128)}, f32[4]{0:T(128)S(1)}, u32[]{:S(2)}, u32[]{:S(2)}) collective-permute-start(f32[4]{0:T(128)} %pad_maximum_fusion.43), channel_id=1, source_target_pairs={{0,1},{1,0},{2,3},{3,2},{4,5},{5,4},{6,7},{7,6},{8,9},{9,8},{10,11... | collective-permute-start | bytes 56 | tf_op jit(solution)/shard_map/ppermute | solution.py:468
  (221 other events, 2855.4 us)

commit v5 on v4

--- a/solution.py
+++ b/solution.py
@@ -346,7 +346,7 @@
 
 def moments_step(side, clip, weight, first, second, gradients):
     rows, depth, _ = weight.shape
-    block = 32
+    block = min(64, rows)
     whole = pl.BlockSpec((block, depth, 128), lambda i: (i, 0, 0))
     shape = jax.ShapeDtypeStruct(weight.shape, WIDE)
     return pl.pallas_call(
@@ -369,7 +369,7 @@
     )(side, clip, weight, first, second, *gradients)
 
 
-def embed_kernel(picked_ref, expand_ref, entry_ref, table_ref, fold_ref, block_ref, hot_ref, out_ref):
+def embed_kernel(place_ref, picked_ref, expand_ref, entry_ref, table_ref, fold_ref, block_ref, hot_ref, out_ref):
     hot = (dot(picked_ref[...], expand_ref[0]) == entry_ref[...]).astype(LOW)
     hot_ref[0] = hot
     total = 0.0
@@ -379,7 +379,7 @@
     out_ref[...] = total
 
 
-def embed_tokens(picked, expand, entry, table, fold, block):
+def embed_tokens(place, picked, expand, entry, table, fold, block):
     tokens, rows, width = picked.shape[0], entry.shape[1], fold.shape[0]
     return pl.pallas_call(
         embed_kernel,
@@ -387,22 +387,25 @@
             jax.ShapeDtypeStruct((SHARERS, tokens, rows), LOW),
             jax.ShapeDtypeStruct((tokens, SHARERS * width), WIDE),
         ],
-        grid=(SHARERS,),
-        in_specs=[
-            pl.BlockSpec(picked.shape, lambda j: (0, 0)),
-            pl.BlockSpec((1, *expand.shape[1:]), lambda j: (j, 0, 0)),
-            pl.BlockSpec(entry.shape, lambda j: (0, 0)),
-            pl.BlockSpec((1, *table.shape[1:]), lambda j: (j, 0, 0, 0)),
-            pl.BlockSpec(fold.shape, lambda j: (0, 0)),
-            pl.BlockSpec(block.shape, lambda j: (0, 0)),
-        ],
-        out_specs=[
-            pl.BlockSpec((1, tokens, rows), lambda j: (j, 0, 0)),
-            pl.BlockSpec((tokens, width), lambda j: (0, j)),
-        ],
+        grid_spec=pltpu.PrefetchScalarGridSpec(
+            num_scalar_prefetch=1,
+            grid=(SHARERS,),
+            in_specs=[
+                pl.BlockSpec(picked.shape, lambda j, place: (0, 0)),
+                pl.BlockSpec((1, *expand.shape[1:]), lambda j, place: (j, 0, 0)),
+                pl.BlockSpec(entry.shape, lambda j, place: (0, 0)),
+                pl.BlockSpec((1, *table.shape[1:]), lambda j, place: (j ^ place[0], 0, 0, 0)),
+                pl.BlockSpec(fold.shape, lambda j, place: (0, 0)),
+                pl.BlockSpec(block.shape, lambda j, place: (0, 0)),
+            ],
+            out_specs=[
+                pl.BlockSpec((1, tokens, rows), lambda j, place: (j, 0, 0)),
+                pl.BlockSpec((tokens, width), lambda j, place: (0, j)),
+            ],
+        ),
         compiler_params=pltpu.CompilerParams(vmem_limit_bytes=40 * 2**20),
         cost_estimate=pl.CostEstimate(flops=1, bytes_accessed=1, transcendentals=0),
-    )(picked, expand, entry, table, fold, block)
+    )(place, picked, expand, entry, table, fold, block)
 
 
 def join_kernel(*refs):
@@ -450,6 +453,37 @@
             flops=left.size, bytes_accessed=6 * left.size, transcendentals=0
         ),
     )(*[left] * len(turns), *[right] * len(turns))
+
+
+def small_kernel(decays, clip_ref, *refs):
+    count = len(decays)
+    clip = clip_ref[0]
+    for i, decay in enumerate(decays):
+        weight, gradient, first, second = (ref[...] for ref in refs[4 * i : 4 * i + 4])
+        outs = refs[4 * count + 3 * i : 4 * count + 3 * i + 3]
+        first_new, second_new, update = moments_of(weight, gradient, first, second, clip, decay)
+        outs[0][...] = apply_trust(
+            weight,
+            update,
+            jnp.sum(weight * weight, keepdims=True),
+            jnp.sum(update * update, keepdims=True),
+        )
+        outs[1][...] = first_new
+        outs[2][...] = second_new
+
+
+def small_steps(clip, groups, decays):
+    flat = [values for group in groups for values in group]
+    return pl.pallas_call(
+        functools.partial(small_kernel, decays),
+        out_shape=[
+            jax.ShapeDtypeStruct(group[0].shape, WIDE) for group in groups for _ in range(3)
+        ],
+        in_specs=[pl.BlockSpec(memory_space=pltpu.SMEM)]
+        + [pl.BlockSpec(memory_space=pltpu.VMEM)] * len(flat),
+        out_specs=[pl.BlockSpec(memory_space=pltpu.VMEM)] * (3 * len(groups)),
+        compiler_params=pltpu.CompilerParams(vmem_limit_bytes=48 * 2**20),
+    )(clip, *flat)
 
 
 class Grid:
@@ -687,9 +721,6 @@
     )
     qkv_w = traded(qkv_pieces)
     picked_all, other_pieces = tied(picked_all, pieces_of(SECTIONS[1:3]))
-    qkv_w, other_pieces, side = tied(qkv_w, other_pieces, side)
-    qkv_w = jnp.concatenate(qkv_w, axis=0)
-    others = traded(other_pieces)
 
     held = tokens // grid.members
     place = jnp.arange(tokens, dtype=jnp.int32)
@@ -709,12 +740,14 @@
     fold = (
         block_columns[:, None] % embed_width == jnp.arange(embed_width, dtype=jnp.int32)
     ).astype(LOW)
-    table = jnp.stack(grid.local(table, 0)).reshape(SHARERS, row_attr.size, embed_width)
+    table = lax.dynamic_slice_in_dim(table, lax.axis_index("a") * local_attrs, local_attrs, 0)
+    table = table.reshape(SHARERS, row_attr.size, embed_width)
     places = jnp.arange(local_attrs, dtype=jnp.int32)
     expand = places[None, :, None] == (
         jnp.arange(SHARERS, dtype=jnp.int32)[:, None, None] * block_attrs + row_attr[None, None, :]
     )
     hots, embedded = embed_tokens(
+        grid.sharer().astype(jnp.int32)[None],
         picked,
         expand.astype(LOW),
         row_entry[None, :],
@@ -722,6 +755,9 @@
         fold,
         own_block.astype(WIDE),
     )
+    embedded, qkv_w, other_pieces, side = tied(embedded, qkv_w, other_pieces, side)
+    qkv_w = jnp.concatenate(qkv_w, axis=0)
+    others = traded(other_pieces)
 
     kinds = jnp.arange(classes, dtype=jnp.int32).astype(WIDE)
     mask_own = own_rows(cell_mask).astype(WIDE)
@@ -770,15 +806,18 @@
     mean_two, scale_two = grid.stats(middle, model_width)
     hat_two = (middle - mean_two) * scale_two
     second = grid.spread((hat_two * gains[1]).astype(LOW))
-    before = jnp.concatenate([dot(a, up_w).astype(LOW) for a in second], axis=0)
-    before, down_pieces = tied(before, down_pieces)
-    before, down_w, up_turned, qkv_turned = tied(
-        grid.row_sum(before), traded(down_pieces), up_w.T, qkv_w.T
+    before, down_pieces = tied([dot(a, up_w).astype(LOW) for a in second], down_pieces)
+    before = [grid.row_sum(b) for b in before]
+    before[0], down_w, up_turned, qkv_turned = tied(
+        before[0], traded(down_pieces), up_w.T, qkv_w.T
     )
     down_w = jnp.concatenate(down_w, axis=0)
-    before = jnp.split(before, 2, axis=0)
-    hidden = [gelu_apply(b).astype(LOW) for b in before]
-    after = middle + grid.gathered_sum(*[dot(a, down_w, 1, 1).astype(LOW) for a in hidden])
+    hidden = [gelu_apply(before[0]).astype(LOW)]
+    down = [dot(hidden[0], down_w, 1, 1).astype(LOW)]
+    before[1], hidden[0], down[0] = tied(before[1], hidden[0], down[0])
+    hidden.append(gelu_apply(before[1]).astype(LOW))
+    down.append(dot(hidden[1], down_w, 1, 1).astype(LOW))
+    after = middle + grid.gathered_sum(*down)
 
     aba_low = aba_weights.astype(LOW)
     final, aba_stored = aba_forward(grid.to_rows(after), aba_low, aba_gains)
@@ -813,12 +852,12 @@
 
     upstream = grid.from_rows(rows_grad.astype(LOW))
     down_grad = grid.spread(upstream)
-    hidden_grad = jnp.concatenate([dot(a, down_w).astype(LOW) for a in down_grad], axis=0)
-    hidden_grad = grid.row_sum(hidden_grad)
+    hidden_grad = tied(*[dot(a, down_w).astype(LOW) for a in down_grad])
+    hidden_grad = [grid.row_sum(g) for g in hidden_grad]
     down_gradient = traded(row_gradients(down_grad, hidden))
 
-    hidden_grad, down_gradient, output_part, aba_part, aba_gains_part = tied(
-        hidden_grad, down_gradient, output_part, aba_part, aba_gains_part
+    hidden_grad[0], down_gradient, output_part, aba_part, aba_gains_part = tied(
+        hidden_grad[0], down_gradient, output_part, aba_part, aba_gains_part
     )
 
     small = jnp.concatenate([aba_part.reshape(-1), aba_gains_part.reshape(-1)])
@@ -841,8 +880,14 @@
     aba_gains_grad = packed[blocks.size + aba_weights.size :].reshape(aba_gains.shape)
 
 
-    before_grad = [gelu_back(b, g).astype(LOW) for b, g in zip(before, jnp.split(hidden_grad, 2, axis=0))]
-    second_grad = grid.gathered_sum(*[dot(a, up_turned).astype(LOW) for a in before_grad])
+    before_grad = [gelu_back(before[0], hidden_grad[0]).astype(LOW)]
+    second_grad = [dot(before_grad[0], up_turned).astype(LOW)]
+    hidden_grad[1], before_grad[0], second_grad[0] = tied(
+        hidden_grad[1], before_grad[0], second_grad[0]
+    )
+    before_grad.append(gelu_back(before[1], hidden_grad[1]).astype(LOW))
+    second_grad.append(dot(before_grad[1], up_turned).astype(LOW))
+    second_grad = grid.gathered_sum(*second_grad)
     gained = second_grad * gains[1]
     sums = jnp.stack([jnp.sum(gained, axis=1), jnp.sum(gained * hat_two, axis=1)])
     sums = sum(grid.row_list(sums)) / model_width
@@ -856,7 +901,7 @@
     gain_two = jnp.sum(second_grad * hat_two, axis=0)
     branch_grad = grid.spread(middle_grad.astype(LOW))
     attended_grad = jnp.concatenate([dot(a, out_w).astype(LOW) for a in branch_grad], axis=0)
-    attended_grad, attended = tied(attended_grad, attended)
+    attended_grad, attended, table_acts = tied(attended_grad, attended, middle_grad.astype(LOW))
     attended_grad, up_gradient = tied(grid.row_sum(attended_grad).astype(LOW), up_gradient)
     out_gradient = row_gradients(branch_grad, attended)
     prob_grad = dot(grid.columns(attended_grad), value_rows, 1, 1)
@@ -868,7 +913,7 @@
     triple_grad = jnp.concatenate([query_grad, key_grad, value_grad], axis=1).astype(LOW)
     table_part = [
         dot(hot[:held], block, 0, 0)
-        for hot, block in zip(hots, jnp.split(middle_grad.astype(LOW), SHARERS, axis=1))
+        for hot, block in zip(hots, jnp.split(table_acts, SHARERS, axis=1))
     ]
     triple_grad, table_part, out_gradient = tied(triple_grad, table_part, out_gradient)
     qkv_gradient = row_gradients([normed], [triple_grad])
@@ -973,15 +1018,15 @@
     else:
         abd_new = apply_trust(abd_weights, abd_update, trust_sums[2], trust_sums[0])
     output_new = apply_trust(output_table, output_update, trust_sums[3], trust_sums[1])
-    gain_triple = local_step(
-        abd_gains, abd_gains_grad, abd_gains_first, abd_gains_second, clip_factor, 0.0
-    )
-    aba_triple = local_step(aba_weights, aba_grad, aba_first, aba_second, clip_factor, WEIGHT_DECAY)
-    aba_gain_triple = local_step(
-        aba_gains, aba_gains_grad, aba_gains_first, aba_gains_second, clip_factor, 0.0
-    )
-    embed_triple = local_step(
-        embed_table, embed_grad, embed_first, embed_second, clip_factor, WEIGHT_DECAY
+    small = small_steps(
+        clip_factor[None],
+        (
+            (abd_gains, abd_gains_grad, abd_gains_first, abd_gains_second),
+            (aba_weights, aba_grad, aba_first, aba_second),
+            (aba_gains, aba_gains_grad, aba_gains_first, aba_gains_second),
+            (embed_table, embed_grad, embed_first, embed_second),
+        ),
+        (0.0, WEIGHT_DECAY, 0.0, WEIGHT_DECAY),
     )
     return (
         loss_sum,
@@ -990,10 +1035,8 @@
         abd_new,
         abd_first_new,
         abd_second_new,
-        *gain_triple,
-        *aba_triple,
-        *aba_gain_triple,
-        *[values.transpose(1, 0, 2) for values in embed_triple],
+        *small[:9],
+        *[values.transpose(1, 0, 2) for values in small[9:]],
         *[values.transpose(0, 2, 1) for values in (output_new, output_first_new, output_second_new)],
     )
 

time: 1200 us -> 1180 us (0.983)
  waiting for transfers between devices: 550 us -> 536 us
    ppermute x13 -> x15, waiting for transfers between devices: 266 us -> 181 us  [facing(): return lax.ppermute(values, 'a', [(0, 1), (1, 0)])]
    ppermute x18, waiting for transfers between devices: 73.3 us -> 135 us  [trade(): lax.ppermute(values, ('q', 'p'), [(i, i ^ step) for i in range(SHARERS)])]
    reduce_sum x5 -> x0, other arithmetic: 12.1 us -> none  [the longest x4 11.2 us: local_step(): jnp.sum(update * update)]
    sub x5 -> x1, other arithmetic: 26.5 us -> 20.8 us  [apply_trust(): return weight - LEARN_RATE * trust_ratio * update]
    unnamed x385 -> x417, local copies, waits for them, and re-layouts: 39.9 us -> 39.4 us
  transfers between devices with their start and end apart: 102 -> 104, of which waited for: 73 -> 72; matrix products, arithmetic and copies ran while one was open for 13% -> 13% of each run, Pallas kernels for 2% -> 3%
where the time goes in v5:
time: 1180 us; the launch traced here: 1170 us
  waiting for transfers between devices  536 us (45%)
  matrix products  153 us (13%)
  Pallas kernels  125 us (11%)
  starting transfers between devices  123 us (10%)
  other arithmetic  116 us (10%)
  local copies, waits for them, and re-layouts  90.6 us (8%)
  between operations  24.9 us (2%)
    ppermute x15, waiting for transfers between devices, facing(): return lax.ppermute(values, 'a', [(0, 1), (1, 0)])  181 us
    ppermute x66, waiting for transfers between devices, pair(): lax.ppermute(values, ('q', 'p', 'h'), [(i, i ^ step) for i in range(self....  180 us
    ppermute x18, waiting for transfers between devices, trade(): lax.ppermute(values, ('q', 'p'), [(i, i ^ step) for i in range(SHARERS)])  135 us
    dot_general x57, matrix products, dot(): lax.dot_general(left, right, (((left_dim,), (right_dim,)), ((), ())), pre...  118 us
    ppermute x66, starting transfers between devices, pair(): lax.ppermute(values, ('q', 'p', 'h'), [(i, i ^ step) for i in range(self....  73.3 us
    pallas_call x1, Pallas kernels, moments_step(): pl.pallas_call(moments_kernel, out_shape=[shape, shape, jax.ShapeDtypeStr...  53.9 us
    unnamed x417, local copies, waits for them, and re-layouts  39.4 us
    ppermute x4, waiting for transfers between devices, columns(): got = lax.ppermute(values, 'p', [(i, i ^ d) for i in range(self.parts)])  37.1 us
  transfers between devices with their start and end apart: 104, of which 72 were waited for; matrix products, arithmetic and copies ran while one was open for 13% of the time, Pallas kernels for 3%

profile of v5, /device:TPU:0, one launch (start us, length us, event | category | flops | bytes accessed | tf_op | source)
XLA Modules:
  0.0 1168.7 jit_solution(912017739486652741)
XLA Ops:
  5.7 9.4 shard_map.364
  31.8 3.8 collective-permute-start.4
  40.8 12.4 %shard_map.365 = (bf16[512,1280]{1,0:T(8,128)(2,1)S(1)}, bf16[512,1280]{1,0:T(8,128)(2,1)}, bf16[512,1280]{1,0:T(8,128)(2,1)}, bf16[512,1280]{1,0:T(8,128)(2,1)}) custom-call(s32[2]{0:T(128)S(1)} %pad_add_fusion.side_ref, f32[512,96,128]{2,1,0:T(8,128)} %bitcast.466, f32[512,96,128]{2,1,0:T(8,128)} %bitcast.467), custom_call_target="tpu_custom_call" | custom-call | flops 1 | bytes 1 | tf_op jit(solution)/shard_map/pallas_call | solution.py:291
  66.9 10.4 shard_map.366
  85.4 9.8 collective-permute-done.7
  96.1 3.8 reduce_sum.607
  100.0 4.4 multiply_reduce_fusion.3
  109.3 4.2 multiply_convert_fusion.2
  113.5 4.5 convolution_convert_fusion.7
  129.3 10.7 shard_map.367
  140.0 43.1 %collective-permute-done.9 = bf16[1024,768]{1,0:T(8,128)(2,1)} collective-permute-done((bf16[1024,768]{1,0:T(8,128)(2,1)}, bf16[1024,768]{1,0:T(8,128)(2,1)}, u32[]{:S(2)}, u32[]{:S(2)}) %collective-permute-start.9) | collective-permute-done | bytes 1572896 | tf_op jit(solution)/shard_map/ppermute | solution.py:542
  189.1 19.8 %collective-permute-done.12 = bf16[512,1280]{1,0:T(8,128)(2,1)} collective-permute-done((bf16[512,1280]{1,0:T(8,128)(2,1)}, bf16[512,1280]{1,0:T(8,128)(2,1)}, u32[]{:S(2)}, u32[]{:S(2)}) %collective-permute-start.12) | collective-permute-done | bytes 1310752 | tf_op jit(solution)/shard_map/ppermute | solution.py:505
  215.0 9.7 collective-permute-done.16
  224.7 6.5 collective-permute-done.15
  240.8 4.2 shard_map.368
  245.2 3.8 collective-permute-start.23
  257.9 4.1 collective-permute-done.23
  262.5 9.1 collective-permute-done.22
  271.6 3.9 collective-permute-done.21
  290.3 10.8 collective-permute-done.26.refs_1_
  302.1 4.1 collective-permute-start.32
  309.2 4.1 collective-permute-done.32.refs_7_
  313.3 3.8 shard_map.369
  335.7 40.0 %collective-permute-done.35 = bf16[512,1024]{1,0:T(8,128)(2,1)S(1)} collective-permute-done((bf16[512,1024]{1,0:T(8,128)(2,1)S(1)}, bf16[512,1024]{1,0:T(8,128)(2,1)S(1)}, u32[]{:S(2)}, u32[]{:S(2)}) %collective-permute-start.35) | collective-permute-done | bytes 1048608 | tf_op jit(solution)/shard_map/ppermute | solution.py:542
  376.2 23.6 %collective-permute-done.37 = bf16[512,1024]{1,0:T(8,128)(2,1)S(1)} collective-permute-done((bf16[512,1024]{1,0:T(8,128)(2,1)S(1)}, bf16[512,1024]{1,0:T(8,128)(2,1)S(1)}, u32[]{:S(2)}, u32[]{:S(2)}) %collective-permute-start.37) | collective-permute-done | bytes 1048608 | tf_op jit(solution)/shard_map/ppermute | solution.py:505
  399.7 22.2 %collective-permute-done.38 = bf16[512,1024]{1,0:T(8,128)(2,1)S(1)} collective-permute-done((bf16[512,1024]{1,0:T(8,128)(2,1)S(1)}, bf16[512,1024]{1,0:T(8,128)(2,1)S(1)}, u32[]{:S(2)}, u32[]{:S(2)}) %collective-permute-start.38) | collective-permute-done | bytes 1048608 | tf_op jit(solution)/shard_map/ppermute | solution.py:505
  422.7 3.7 convolution_convert_fusion.3.refs_0_.refs_1_.refs_2_.refs_3_.refs_4_.refs_5_.refs_6_.refs_7_
  431.0 4.1 collective-permute-done.39.refs_8_.refs_9_.refs_10_.refs_11_.refs_12_.refs_13_.refs_14_.refs_15_
  436.5 4.4 shard_map.370
  447.0 5.2 collective-permute-done.46
  458.3 8.5 collective-permute-done.44
  477.4 11.6 collective-permute-done.47
  550.2 8.7 collective-permute-done.48
  570.1 7.9 collective-permute-done.51.refs_3_
  579.1 6.2 collective-permute-done.54.refs_6_
  589.3 3.9 shard_map.371
  604.8 5.0 convolution_convert_fusion.8
  631.1 28.2 %collective-permute-done.58 = bf16[512,1024]{1,0:T(8,128)(2,1)S(1)} collective-permute-done((bf16[512,1024]{1,0:T(8,128)(2,1)S(1)}, bf16[512,1024]{1,0:T(8,128)(2,1)S(1)}, u32[]{:S(2)}, u32[]{:S(2)}) %collective-permute-start.58) | collective-permute-done | bytes 1048608 | tf_op jit(solution)/shard_map/ppermute | solution.py:542
  661.0 28.2 %collective-permute-done.60.rest_10_ = bf16[512,1024]{1,0:T(8,128)(2,1)} collective-permute-done((bf16[512,1024]{1,0:T(8,128)(2,1)S(1)}, bf16[512,1024]{1,0:T(8,128)(2,1)}, u32[]{:S(2)}, u32[]{:S(2)}) %collective-permute-start.60) | collective-permute-done | bytes 1048608 | tf_op jit(solution)/shard_map/ppermute | solution.py:505
  689.2 21.9 %collective-permute-done.61.rest_11_ = bf16[512,1024]{1,0:T(8,128)(2,1)} collective-permute-done((bf16[512,1024]{1,0:T(8,128)(2,1)S(1)}, bf16[512,1024]{1,0:T(8,128)(2,1)}, u32[]{:S(2)}, u32[]{:S(2)}) %collective-permute-start.61) | collective-permute-done | bytes 1048608 | tf_op jit(solution)/shard_map/ppermute | solution.py:505
  716.1 3.7 convolution_convert_fusion.1.refs_0_.refs_1_.refs_2_.refs_3_.refs_4_.refs_5_.refs_6_.refs_7_
  728.7 4.9 collective-permute-done.72
  737.1 5.5 collective-permute-done.73
  745.8 4.9 collective-permute-done.74
  755.8 4.2 shard_map.372
  783.9 5.2 collective-permute-done.67
  795.9 4.1 collective-permute-done.70
  805.9 13.0 %collective-permute-done.76.refs_1_ = bf16[64,2048]{1,0:T(8,128)(2,1)S(1)} collective-permute-done((bf16[64,2048]{1,0:T(8,128)(2,1)S(1)}, bf16[64,2048]{1,0:T(8,128)(2,1)S(1)}, u32[]{:S(2)}, u32[]{:S(2)}) %collective-permute-start.76) | collective-permute-done | bytes 262176 | tf_op jit(solution)/shard_map/ppermute | solution.py:502
  820.8 5.4 collective-permute-done.81.refs_6_
  828.0 3.9 shard_map.373
  833.2 13.2 %collective-permute-done.89 = bf16[1024,256]{1,0:T(8,128)(2,1)S(1)} collective-permute-done((bf16[1024,256]{1,0:T(8,128)(2,1)S(1)}, bf16[1024,256]{1,0:T(8,128)(2,1)S(1)}, u32[]{:S(2)}, u32[]{:S(2)}) %collective-permute-start.89) | collective-permute-done | bytes 524320 | tf_op jit(solution)/shard_map/ppermute | solution.py:605
  886.9 25.0 %collective-permute-done.84 = bf16[1024,256]{1,0:T(8,128)(2,1)} collective-permute-done((bf16[1024,256]{1,0:T(8,128)(2,1)S(1)}, bf16[1024,256]{1,0:T(8,128)(2,1)}, u32[]{:S(2)}, u32[]{:S(2)}) %collective-permute-start.84) | collective-permute-done | bytes 524320 | tf_op jit(solution)/shard_map/ppermute | solution.py:542
  917.8 7.7 collective-permute-done.88
  943.4 7.9 multiply_reduce_fusion.1
  961.6 7.5 multiply_convert_fusion
  996.2 5.0 collective-permute-done.93.rest_3_
  1006.7 7.2 collective-permute-done.95
  1015.0 7.3 collective-permute-done.96
  1022.6 7.0 collective-permute-done.97
  1031.6 11.4 collective-permute-done.98
  1057.2 53.9 %shard_map.374 = (f32[512,96,128]{2,1,0:T(8,128)}, f32[512,96,128]{2,1,0:T(8,128)}, bf16[512,96,128]{2,1,0:T(8,128)(2,1)}, f32[2,8,128]{2,1,0:T(8,128)S(1)}) custom-call(s32[2]{0:T(128)S(1)} %copy-done.18, f32[1]{0:T(128)} %bitcast.123.clip_ref, f32[512,96,128]{2,1,0:T(8,128)} %bitcast.469, f32[512,96,128]{2,1,0:T(8,128)} %bitcast.474, ...), custom_call_target="tpu_custom_call" | custom-call | flops 125829120 | bytes 150994944 | tf_op jit(solution)/shard_map/pallas_call | solution.py:352
  1120.3 3.9 shard_map.375
  1137.7 4.2 collective-permute-done.103
  1145.5 20.8 %multiply_subtract_fusion = f32[512,96,128]{2,1,0:T(8,128)} fusion(f32[512,96,128]{2,1,0:T(8,128)} %bitcast.470, bf16[512,96,128]{2,1,0:T(8,128)(2,1)} %get-tuple-element.314, f32[]{:T(128)} %bitcast.137), kind=kLoop, calls=%fused_computation | loop fusion | flops 18874368 | bytes 62914564 | tf_op jit(solution)/shard_map/sub | solution.py:197
  (901 shorter events, 473.1 us)
Async XLA Ops:
  2.7 15.9 %collective-permute-start = (bf16[32,128]{1,0:T(8,128)(2,1)S(1)}, bf16[32,128]{1,0:T(8,128)(2,1)S(1)}, u32[]{:S(2)}, u32[]{:S(2)}) collective-permute-start(bf16[32,128]{1,0:T(8,128)(2,1)S(1)} %get-tuple-element.363), channel_id=1, source_target_pairs={{0,1},{1,0},{2,3},{3,2},{4,5},{5,4},{6,7},{7,6},{8,9},{9,8},{10,11... | collective-permute-start | bytes 24584 | tf_op jit(solution)/shard_map/ppermute | solution.py:502
  4.1 25.4 %collective-permute-start.13 = (bf16[1,16,64,32]{2,3,1,0:T(8,128)(2,1)S(1)}, bf16[1,16,64,32]{2,3,1,0:T(8,128)(2,1)S(1)}, u32[]{:S(2)}, u32[]{:S(2)}) collective-permute-start(bf16[1,16,64,32]{2,3,1,0:T(8,128)(2,1)S(1)} %convert_bitcast_fusion), channel_id=1, source_target_pairs={{0,1},{1,0},{2,3},{3,2},{4,5},{5,4},{6,7},{7,6},{8,9},{9,8},{10,11... | collective-permute-start | bytes 196616 | tf_op jit(solution)/shard_map/ppermute | solution.py:502
  63.2 21.2 %collective-permute-start.5 = (bf16[512,768]{1,0:T(8,128)(2,1)}, bf16[512,768]{1,0:T(8,128)(2,1)S(1)}, u32[]{:S(2)}, u32[]{:S(2)}) collective-permute-start(bf16[512,768]{1,0:T(8,128)(2,1)} %copy-done.30), channel_id=1, source_target_pairs={{0,4},{4,0},{8,12},{12,8},{1,5},{5,1},{9,13},{13,9},{2,6},{6,2},{1... | collective-permute-start | bytes 2359304 | tf_op jit(solution)/shard_map/ppermute | solution.py:505
  64.8 20.7 %collective-permute-start.6 = (bf16[512,768]{1,0:T(8,128)(2,1)}, bf16[512,768]{1,0:T(8,128)(2,1)S(1)}, u32[]{:S(2)}, u32[]{:S(2)}) collective-permute-start(bf16[512,768]{1,0:T(8,128)(2,1)} %copy-done.29), channel_id=1, source_target_pairs={{0,8},{4,12},{8,0},{12,4},{1,9},{5,13},{9,1},{13,5},{2,10},{6,14},... | collective-permute-start | bytes 2359304 | tf_op jit(solution)/shard_map/ppermute | solution.py:505
  65.2 30.1 %collective-permute-start.7 = (bf16[512,768]{1,0:T(8,128)(2,1)S(1)}, bf16[512,768]{1,0:T(8,128)(2,1)S(1)}, u32[]{:S(2)}, u32[]{:S(2)}) collective-permute-start(bf16[512,768]{1,0:T(8,128)(2,1)S(1)} %copy-done.28), channel_id=1, source_target_pairs={{0,12},{4,8},{8,4},{12,0},{1,13},{5,9},{9,5},{13,1},{2,14},{6,10},... | collective-permute-start | bytes 2359304 | tf_op jit(solution)/shard_map/ppermute | solution.py:505
  118.0 65.1 %collective-permute-start.9 = (bf16[1024,768]{1,0:T(8,128)(2,1)}, bf16[1024,768]{1,0:T(8,128)(2,1)}, u32[]{:S(2)}, u32[]{:S(2)}) collective-permute-start(bf16[1024,768]{1,0:T(8,128)(2,1)} %convolution_convert_fusion.7), channel_id=1, source_target_pairs={{0,16},{16,0},{1,17},{17,1},{2,18},{18,2},{3,19},{19,3},{4,20},{20... | collective-permute-start | bytes 4718600 | tf_op jit(solution)/shard_map/ppermute | solution.py:542
  122.8 62.6 %collective-permute-start.10 = (bf16[512,1280]{1,0:T(8,128)(2,1)}, bf16[512,1280]{1,0:T(8,128)(2,1)}, u32[]{:S(2)}, u32[]{:S(2)}) collective-permute-start(bf16[512,1280]{1,0:T(8,128)(2,1)} %get-tuple-element.202), channel_id=1, source_target_pairs={{0,4},{4,0},{8,12},{12,8},{1,5},{5,1},{9,13},{13,9},{2,6},{6,2},{1... | collective-permute-start | bytes 3932168 | tf_op jit(solution)/shard_map/ppermute | solution.py:505
  124.3 64.7 %collective-permute-start.11 = (bf16[512,1280]{1,0:T(8,128)(2,1)}, bf16[512,1280]{1,0:T(8,128)(2,1)}, u32[]{:S(2)}, u32[]{:S(2)}) collective-permute-start(bf16[512,1280]{1,0:T(8,128)(2,1)} %get-tuple-element.203), channel_id=1, source_target_pairs={{0,8},{4,12},{8,0},{12,4},{1,9},{5,13},{9,1},{13,5},{2,10},{6,14},... | collective-permute-start | bytes 3932168 | tf_op jit(solution)/shard_map/ppermute | solution.py:505
  126.1 82.8 %collective-permute-start.12 = (bf16[512,1280]{1,0:T(8,128)(2,1)}, bf16[512,1280]{1,0:T(8,128)(2,1)}, u32[]{:S(2)}, u32[]{:S(2)}) collective-permute-start(bf16[512,1280]{1,0:T(8,128)(2,1)} %get-tuple-element.204), channel_id=1, source_target_pairs={{0,12},{4,8},{8,4},{12,0},{1,13},{5,9},{9,5},{13,1},{2,14},{6,10},... | collective-permute-start | bytes 3932168 | tf_op jit(solution)/shard_map/ppermute | solution.py:505
  209.8 14.9 %collective-permute-start.16 = (bf16[1024,256]{1,0:T(8,128)(2,1)S(1)}, bf16[1024,256]{1,0:T(8,128)(2,1)S(1)}, u32[]{:S(2)}, u32[]{:S(2)}) collective-permute-start(bf16[1024,256]{1,0:T(8,128)(2,1)S(1)} %get-tuple-element.365), channel_id=1, source_target_pairs={{0,4},{4,0},{1,5},{5,1},{2,6},{6,2},{3,7},{7,3},{8,12},{12,8},{9,1... | collective-permute-start | bytes 1572872 | tf_op jit(solution)/shard_map/ppermute | solution.py:605
  211.3 19.9 %collective-permute-start.15 = (bf16[1024,256]{1,0:T(8,128)(2,1)S(1)}, bf16[1024,256]{1,0:T(8,128)(2,1)S(1)}, u32[]{:S(2)}, u32[]{:S(2)}) collective-permute-start(bf16[1024,256]{1,0:T(8,128)(2,1)S(1)} %get-tuple-element.366), channel_id=1, source_target_pairs={{0,4},{4,0},{1,5},{5,1},{2,6},{6,2},{3,7},{7,3},{8,12},{12,8},{9,1... | collective-permute-start | bytes 1572872 | tf_op jit(solution)/shard_map/ppermute | solution.py:605
  245.2 16.8 %collective-permute-start.23 = (bf16[64,2048]{1,0:T(8,128)(2,1)}, bf16[64,2048]{1,0:T(8,128)(2,1)S(1)}, u32[]{:S(2)}, u32[]{:S(2)}) collective-permute-start(bf16[64,2048]{1,0:T(8,128)(2,1)} %get-tuple-element.225), channel_id=1, source_target_pairs={{0,12},{1,13},{2,14},{3,15},{4,8},{5,9},{6,10},{7,11},{8,4},{9,5},... | collective-permute-start | bytes 786440 | tf_op jit(solution)/shard_map/ppermute | solution.py:502
  249.0 22.7 %collective-permute-start.22 = (bf16[64,2048]{1,0:T(8,128)(2,1)}, bf16[64,2048]{1,0:T(8,128)(2,1)S(1)}, u32[]{:S(2)}, u32[]{:S(2)}) collective-permute-start(bf16[64,2048]{1,0:T(8,128)(2,1)} %get-tuple-element.224), channel_id=1, source_target_pairs={{0,10},{1,11},{2,8},{3,9},{4,14},{5,15},{6,12},{7,13},{8,2},{9,3},... | collective-permute-start | bytes 786440 | tf_op jit(solution)/shard_map/ppermute | solution.py:502
  249.1 26.5 %collective-permute-start.21 = (bf16[64,2048]{1,0:T(8,128)(2,1)}, bf16[64,2048]{1,0:T(8,128)(2,1)S(1)}, u32[]{:S(2)}, u32[]{:S(2)}) collective-permute-start(bf16[64,2048]{1,0:T(8,128)(2,1)} %get-tuple-element.223), channel_id=1, source_target_pairs={{0,8},{1,9},{2,10},{3,11},{4,12},{5,13},{6,14},{7,15},{8,0},{9,1},... | collective-permute-start | bytes 786440 | tf_op jit(solution)/shard_map/ppermute | solution.py:502
  251.0 24.6 %collective-permute-start.20 = (bf16[64,2048]{1,0:T(8,128)(2,1)}, bf16[64,2048]{1,0:T(8,128)(2,1)S(1)}, u32[]{:S(2)}, u32[]{:S(2)}) collective-permute-start(bf16[64,2048]{1,0:T(8,128)(2,1)} %get-tuple-element.222), channel_id=1, source_target_pairs={{0,6},{1,7},{2,4},{3,5},{4,2},{5,3},{6,0},{7,1},{8,14},{9,15},{10,... | collective-permute-start | bytes 786440 | tf_op jit(solution)/shard_map/ppermute | solution.py:502
  256.4 19.7 %collective-permute-start.19 = (bf16[64,2048]{1,0:T(8,128)(2,1)}, bf16[64,2048]{1,0:T(8,128)(2,1)S(1)}, u32[]{:S(2)}, u32[]{:S(2)}) collective-permute-start(bf16[64,2048]{1,0:T(8,128)(2,1)} %get-tuple-element.221), channel_id=1, source_target_pairs={{0,4},{1,5},{2,6},{3,7},{4,0},{5,1},{6,2},{7,3},{8,12},{9,13},{10,... | collective-permute-start | bytes 786440 | tf_op jit(solution)/shard_map/ppermute | solution.py:502
  262.0 15.2 %collective-permute-start.18 = (bf16[64,2048]{1,0:T(8,128)(2,1)}, bf16[64,2048]{1,0:T(8,128)(2,1)S(1)}, u32[]{:S(2)}, u32[]{:S(2)}) collective-permute-start(bf16[64,2048]{1,0:T(8,128)(2,1)} %get-tuple-element.220), channel_id=1, source_target_pairs={{0,2},{1,3},{2,0},{3,1},{4,6},{5,7},{6,4},{7,5},{8,10},{9,11},{10,... | collective-permute-start | bytes 786440 | tf_op jit(solution)/shard_map/ppermute | solution.py:502
  283.8 17.4 %collective-permute-start.26 = (bf16[64,2048]{1,0:T(8,128)(2,1)S(1)}, bf16[64,2048]{1,0:T(8,128)(2,1)S(1)}, u32[]{:S(2)}, u32[]{:S(2)}) collective-permute-start(bf16[64,2048]{1,0:T(8,128)(2,1)S(1)} %multiply_convert_fusion.11.refs_0_), channel_id=1, source_target_pairs={{0,2},{1,3},{2,0},{3,1},{4,6},{5,7},{6,4},{7,5},{8,10},{9,11},{10,... | collective-permute-start | bytes 786440 | tf_op jit(solution)/shard_map/ppermute | solution.py:502
  285.4 16.7 %collective-permute-start.27 = (bf16[64,2048]{1,0:T(8,128)(2,1)S(1)}, bf16[64,2048]{1,0:T(8,128)(2,1)S(1)}, u32[]{:S(2)}, u32[]{:S(2)}) collective-permute-start(bf16[64,2048]{1,0:T(8,128)(2,1)S(1)} %multiply_convert_fusion.11.refs_0_), channel_id=1, source_target_pairs={{0,4},{1,5},{2,6},{3,7},{4,0},{5,1},{6,2},{7,3},{8,12},{9,13},{10,... | collective-permute-start | bytes 786440 | tf_op jit(solution)/shard_map/ppermute | solution.py:502
  286.4 19.7 %collective-permute-start.28 = (bf16[64,2048]{1,0:T(8,128)(2,1)S(1)}, bf16[64,2048]{1,0:T(8,128)(2,1)S(1)}, u32[]{:S(2)}, u32[]{:S(2)}) collective-permute-start(bf16[64,2048]{1,0:T(8,128)(2,1)S(1)} %multiply_convert_fusion.11.refs_0_), channel_id=1, source_target_pairs={{0,6},{1,7},{2,4},{3,5},{4,2},{5,3},{6,0},{7,1},{8,14},{9,15},{10,... | collective-permute-start | bytes 786440 | tf_op jit(solution)/shard_map/ppermute | solution.py:502
  287.4 18.8 %collective-permute-start.29 = (bf16[64,2048]{1,0:T(8,128)(2,1)S(1)}, bf16[64,2048]{1,0:T(8,128)(2,1)S(1)}, u32[]{:S(2)}, u32[]{:S(2)}) collective-permute-start(bf16[64,2048]{1,0:T(8,128)(2,1)S(1)} %multiply_convert_fusion.11.refs_0_), channel_id=1, source_target_pairs={{0,8},{1,9},{2,10},{3,11},{4,12},{5,13},{6,14},{7,15},{8,0},{9,1},... | collective-permute-start | bytes 786440 | tf_op jit(solution)/shard_map/ppermute | solution.py:502
  287.5 18.6 %collective-permute-start.30 = (bf16[64,2048]{1,0:T(8,128)(2,1)S(1)}, bf16[64,2048]{1,0:T(8,128)(2,1)S(1)}, u32[]{:S(2)}, u32[]{:S(2)}) collective-permute-start(bf16[64,2048]{1,0:T(8,128)(2,1)S(1)} %multiply_convert_fusion.11.refs_0_), channel_id=1, source_target_pairs={{0,10},{1,11},{2,8},{3,9},{4,14},{5,15},{6,12},{7,13},{8,2},{9,3},... | collective-permute-start | bytes 786440 | tf_op jit(solution)/shard_map/ppermute | solution.py:502
  327.0 48.8 %collective-permute-start.35 = (bf16[512,1024]{1,0:T(8,128)(2,1)S(1)}, bf16[512,1024]{1,0:T(8,128)(2,1)S(1)}, u32[]{:S(2)}, u32[]{:S(2)}) collective-permute-start(bf16[512,1024]{1,0:T(8,128)(2,1)S(1)} %convolution_convert_fusion.11), channel_id=1, source_target_pairs={{0,16},{16,0},{1,17},{17,1},{2,18},{18,2},{3,19},{19,3},{4,20},{20... | collective-permute-start | bytes 3145736 | tf_op jit(solution)/shard_map/ppermute | solution.py:542
  327.4 48.7 %collective-permute-start.36 = (bf16[512,1024]{1,0:T(8,128)(2,1)S(1)}, bf16[512,1024]{1,0:T(8,128)(2,1)S(1)}, u32[]{:S(2)}, u32[]{:S(2)}) collective-permute-start(bf16[512,1024]{1,0:T(8,128)(2,1)S(1)} %copy-done.26), channel_id=1, source_target_pairs={{0,4},{4,0},{8,12},{12,8},{1,5},{5,1},{9,13},{13,9},{2,6},{6,2},{1... | collective-permute-start | bytes 3145736 | tf_op jit(solution)/shard_map/ppermute | solution.py:505
  328.4 71.3 %collective-permute-start.37 = (bf16[512,1024]{1,0:T(8,128)(2,1)S(1)}, bf16[512,1024]{1,0:T(8,128)(2,1)S(1)}, u32[]{:S(2)}, u32[]{:S(2)}) collective-permute-start(bf16[512,1024]{1,0:T(8,128)(2,1)S(1)} %copy-done.24), channel_id=1, source_target_pairs={{0,8},{4,12},{8,0},{12,4},{1,9},{5,13},{9,1},{13,5},{2,10},{6,14},... | collective-permute-start | bytes 3145736 | tf_op jit(solution)/shard_map/ppermute | solution.py:505
  330.9 91.1 %collective-permute-start.38 = (bf16[512,1024]{1,0:T(8,128)(2,1)S(1)}, bf16[512,1024]{1,0:T(8,128)(2,1)S(1)}, u32[]{:S(2)}, u32[]{:S(2)}) collective-permute-start(bf16[512,1024]{1,0:T(8,128)(2,1)S(1)} %get-tuple-element.236), channel_id=1, source_target_pairs={{0,12},{4,8},{8,4},{12,0},{1,13},{5,9},{9,5},{13,1},{2,14},{6,10},... | collective-permute-start | bytes 3145736 | tf_op jit(solution)/shard_map/ppermute | solution.py:505
  333.6 92.8 %collective-permute-start.34 = (bf16[512,1024]{1,0:T(8,128)(2,1)S(1)}, bf16[512,1024]{1,0:T(8,128)(2,1)S(1)}, u32[]{:S(2)}, u32[]{:S(2)}) collective-permute-start(bf16[512,1024]{1,0:T(8,128)(2,1)S(1)} %convolution_convert_fusion.10), channel_id=1, source_target_pairs={{0,16},{16,0},{1,17},{17,1},{2,18},{18,2},{3,19},{19,3},{4,20},{20... | collective-permute-start | bytes 3145736 | tf_op jit(solution)/shard_map/ppermute | solution.py:542
  440.9 15.1 %collective-permute-start.45 = (bf16[64,2048]{1,0:T(8,128)(2,1)}, bf16[64,2048]{1,0:T(8,128)(2,1)S(1)}, u32[]{:S(2)}, u32[]{:S(2)}) collective-permute-start(bf16[64,2048]{1,0:T(8,128)(2,1)} %get-tuple-element.250), channel_id=1, source_target_pairs={{0,12},{1,13},{2,14},{3,15},{4,8},{5,9},{6,10},{7,11},{8,4},{9,5},... | collective-permute-start | bytes 786440 | tf_op jit(solution)/shard_map/ppermute | solution.py:502
  443.0 23.8 %collective-permute-start.44 = (bf16[64,2048]{1,0:T(8,128)(2,1)}, bf16[64,2048]{1,0:T(8,128)(2,1)S(1)}, u32[]{:S(2)}, u32[]{:S(2)}) collective-permute-start(bf16[64,2048]{1,0:T(8,128)(2,1)} %get-tuple-element.249), channel_id=1, source_target_pairs={{0,10},{1,11},{2,8},{3,9},{4,14},{5,15},{6,12},{7,13},{8,2},{9,3},... | collective-permute-start | bytes 786440 | tf_op jit(solution)/shard_map/ppermute | solution.py:502
  444.3 24.7 %collective-permute-start.43 = (bf16[64,2048]{1,0:T(8,128)(2,1)}, bf16[64,2048]{1,0:T(8,128)(2,1)S(1)}, u32[]{:S(2)}, u32[]{:S(2)}) collective-permute-start(bf16[64,2048]{1,0:T(8,128)(2,1)} %get-tuple-element.248), channel_id=1, source_target_pairs={{0,8},{1,9},{2,10},{3,11},{4,12},{5,13},{6,14},{7,15},{8,0},{9,1},... | collective-permute-start | bytes 786440 | tf_op jit(solution)/shard_map/ppermute | solution.py:502
  446.8 22.2 %collective-permute-start.42 = (bf16[64,2048]{1,0:T(8,128)(2,1)}, bf16[64,2048]{1,0:T(8,128)(2,1)S(1)}, u32[]{:S(2)}, u32[]{:S(2)}) collective-permute-start(bf16[64,2048]{1,0:T(8,128)(2,1)} %get-tuple-element.247), channel_id=1, source_target_pairs={{0,6},{1,7},{2,4},{3,5},{4,2},{5,3},{6,0},{7,1},{8,14},{9,15},{10,... | collective-permute-start | bytes 786440 | tf_op jit(solution)/shard_map/ppermute | solution.py:502
  452.2 18.2 %collective-permute-start.41 = (bf16[64,2048]{1,0:T(8,128)(2,1)}, bf16[64,2048]{1,0:T(8,128)(2,1)S(1)}, u32[]{:S(2)}, u32[]{:S(2)}) collective-permute-start(bf16[64,2048]{1,0:T(8,128)(2,1)} %get-tuple-element.246), channel_id=1, source_target_pairs={{0,4},{1,5},{2,6},{3,7},{4,0},{5,1},{6,2},{7,3},{8,12},{9,13},{10,... | collective-permute-start | bytes 786440 | tf_op jit(solution)/shard_map/ppermute | solution.py:502
  456.0 16.7 %collective-permute-start.40 = (bf16[64,2048]{1,0:T(8,128)(2,1)}, bf16[64,2048]{1,0:T(8,128)(2,1)S(1)}, u32[]{:S(2)}, u32[]{:S(2)}) collective-permute-start(bf16[64,2048]{1,0:T(8,128)(2,1)} %get-tuple-element.245), channel_id=1, source_target_pairs={{0,2},{1,3},{2,0},{3,1},{4,6},{5,7},{6,4},{7,5},{8,10},{9,11},{10,... | collective-permute-start | bytes 786440 | tf_op jit(solution)/shard_map/ppermute | solution.py:502
  560.3 17.7 %collective-permute-start.51 = (bf16[64,2048]{1,0:T(8,128)(2,1)S(1)}, bf16[64,2048]{1,0:T(8,128)(2,1)S(1)}, u32[]{:S(2)}, u32[]{:S(2)}) collective-permute-start(bf16[64,2048]{1,0:T(8,128)(2,1)S(1)} %pad_maximum_fusion.22.refs_0_), channel_id=1, source_target_pairs={{0,6},{1,7},{2,4},{3,5},{4,2},{5,3},{6,0},{7,1},{8,14},{9,15},{10,... | collective-permute-start | bytes 786440 | tf_op jit(solution)/shard_map/ppermute | solution.py:502
  562.7 15.3 %collective-permute-start.52 = (bf16[64,2048]{1,0:T(8,128)(2,1)S(1)}, bf16[64,2048]{1,0:T(8,128)(2,1)S(1)}, u32[]{:S(2)}, u32[]{:S(2)}) collective-permute-start(bf16[64,2048]{1,0:T(8,128)(2,1)S(1)} %pad_maximum_fusion.22.refs_0_), channel_id=1, source_target_pairs={{0,8},{1,9},{2,10},{3,11},{4,12},{5,13},{6,14},{7,15},{8,0},{9,1},... | collective-permute-start | bytes 786440 | tf_op jit(solution)/shard_map/ppermute | solution.py:502
  562.7 16.4 %collective-permute-start.53 = (bf16[64,2048]{1,0:T(8,128)(2,1)S(1)}, bf16[64,2048]{1,0:T(8,128)(2,1)S(1)}, u32[]{:S(2)}, u32[]{:S(2)}) collective-permute-start(bf16[64,2048]{1,0:T(8,128)(2,1)S(1)} %pad_maximum_fusion.22.refs_0_), channel_id=1, source_target_pairs={{0,10},{1,11},{2,8},{3,9},{4,14},{5,15},{6,12},{7,13},{8,2},{9,3},... | collective-permute-start | bytes 786440 | tf_op jit(solution)/shard_map/ppermute | solution.py:502
  567.5 17.9 %collective-permute-start.54 = (bf16[64,2048]{1,0:T(8,128)(2,1)S(1)}, bf16[64,2048]{1,0:T(8,128)(2,1)S(1)}, u32[]{:S(2)}, u32[]{:S(2)}) collective-permute-start(bf16[64,2048]{1,0:T(8,128)(2,1)S(1)} %pad_maximum_fusion.22.refs_0_), channel_id=1, source_target_pairs={{0,12},{1,13},{2,14},{3,15},{4,8},{5,9},{6,10},{7,11},{8,4},{9,5},... | collective-permute-start | bytes 786440 | tf_op jit(solution)/shard_map/ppermute | solution.py:502
  568.4 20.8 %collective-permute-start.55 = (bf16[64,2048]{1,0:T(8,128)(2,1)S(1)}, bf16[64,2048]{1,0:T(8,128)(2,1)}, u32[]{:S(2)}, u32[]{:S(2)}) collective-permute-start(bf16[64,2048]{1,0:T(8,128)(2,1)S(1)} %pad_maximum_fusion.22.refs_0_), channel_id=1, source_target_pairs={{0,14},{1,15},{2,12},{3,13},{4,10},{5,11},{6,8},{7,9},{8,6},{9,7},... | collective-permute-start | bytes 786440 | tf_op jit(solution)/shard_map/ppermute | solution.py:502
  609.9 49.4 %collective-permute-start.58 = (bf16[512,1024]{1,0:T(8,128)(2,1)S(1)}, bf16[512,1024]{1,0:T(8,128)(2,1)S(1)}, u32[]{:S(2)}, u32[]{:S(2)}) collective-permute-start(bf16[512,1024]{1,0:T(8,128)(2,1)S(1)} %convolution_convert_fusion.9), channel_id=1, source_target_pairs={{0,16},{16,0},{1,17},{17,1},{2,18},{18,2},{3,19},{19,3},{4,20},{20... | collective-permute-start | bytes 3145736 | tf_op jit(solution)/shard_map/ppermute | solution.py:542
  614.3 46.7 %collective-permute-start.59 = (bf16[512,1024]{1,0:T(8,128)(2,1)S(1)}, bf16[512,1024]{1,0:T(8,128)(2,1)}, u32[]{:S(2)}, u32[]{:S(2)}) collective-permute-start(bf16[512,1024]{1,0:T(8,128)(2,1)S(1)} %get-tuple-element.492), channel_id=1, source_target_pairs={{0,4},{4,0},{8,12},{12,8},{1,5},{5,1},{9,13},{13,9},{2,6},{6,2},{1... | collective-permute-start | bytes 3145736 | tf_op jit(solution)/shard_map/ppermute | solution.py:505
  618.7 70.5 %collective-permute-start.60 = (bf16[512,1024]{1,0:T(8,128)(2,1)S(1)}, bf16[512,1024]{1,0:T(8,128)(2,1)}, u32[]{:S(2)}, u32[]{:S(2)}) collective-permute-start(bf16[512,1024]{1,0:T(8,128)(2,1)S(1)} %get-tuple-element.494), channel_id=1, source_target_pairs={{0,8},{4,12},{8,0},{12,4},{1,9},{5,13},{9,1},{13,5},{2,10},{6,14},... | collective-permute-start | bytes 3145736 | tf_op jit(solution)/shard_map/ppermute | solution.py:505
  623.2 87.9 %collective-permute-start.61 = (bf16[512,1024]{1,0:T(8,128)(2,1)S(1)}, bf16[512,1024]{1,0:T(8,128)(2,1)}, u32[]{:S(2)}, u32[]{:S(2)}) collective-permute-start(bf16[512,1024]{1,0:T(8,128)(2,1)S(1)} %get-tuple-element.496), channel_id=1, source_target_pairs={{0,12},{4,8},{8,4},{12,0},{1,13},{5,9},{9,5},{13,1},{2,14},{6,10},... | collective-permute-start | bytes 3145736 | tf_op jit(solution)/shard_map/ppermute | solution.py:505
  624.6 95.2 %collective-permute-start.57 = (bf16[512,1024]{1,0:T(8,128)(2,1)}, bf16[512,1024]{1,0:T(8,128)(2,1)}, u32[]{:S(2)}, u32[]{:S(2)}) collective-permute-start(bf16[512,1024]{1,0:T(8,128)(2,1)} %convolution_convert_fusion.8), channel_id=1, source_target_pairs={{0,16},{16,0},{1,17},{17,1},{2,18},{18,2},{3,19},{19,3},{4,20},{20... | collective-permute-start | bytes 3145736 | tf_op jit(solution)/shard_map/ppermute | solution.py:542
  727.8 26.7 %collective-permute-start.62 = (bf16[512,2048]{1,0:T(8,128)(2,1)S(1)}, bf16[512,2048]{1,0:T(8,128)(2,1)S(1)}, u32[]{:S(2)}, u32[]{:S(2)}) collective-permute-start(bf16[512,2048]{1,0:T(8,128)(2,1)S(1)} %convolution_convert_fusion), channel_id=1, source_target_pairs={{0,1},{1,0},{2,3},{3,2},{4,5},{5,4},{6,7},{7,6},{8,9},{9,8},{10,11... | collective-permute-start | bytes 6291464 | tf_op jit(solution)/shard_map/ppermute | solution.py:502
  750.8 17.5 %collective-permute-start.75 = (f32[641,128]{1,0:T(8,128)S(1)}, f32[641,128]{1,0:T(8,128)}, u32[]{:S(2)}, u32[]{:S(2)}) collective-permute-start(f32[641,128]{1,0:T(8,128)S(1)} %fusion.344), channel_id=1, source_target_pairs={{0,16},{16,0},{1,17},{17,1},{2,18},{18,2},{3,19},{19,3},{4,20},{20... | collective-permute-start | bytes 984584 | tf_op jit(solution)/shard_map/ppermute | solution.py:542
  762.8 14.9 %collective-permute-start.68 = (bf16[64,2048]{1,0:T(8,128)(2,1)}, bf16[64,2048]{1,0:T(8,128)(2,1)S(1)}, u32[]{:S(2)}, u32[]{:S(2)}) collective-permute-start(bf16[64,2048]{1,0:T(8,128)(2,1)} %get-tuple-element.266), channel_id=1, source_target_pairs={{0,12},{1,13},{2,14},{3,15},{4,8},{5,9},{6,10},{7,11},{8,4},{9,5},... | collective-permute-start | bytes 786440 | tf_op jit(solution)/shard_map/ppermute | solution.py:502
  765.7 23.4 %collective-permute-start.67 = (bf16[64,2048]{1,0:T(8,128)(2,1)S(1)}, bf16[64,2048]{1,0:T(8,128)(2,1)S(1)}, u32[]{:S(2)}, u32[]{:S(2)}) collective-permute-start(bf16[64,2048]{1,0:T(8,128)(2,1)S(1)} %copy-done.197), channel_id=1, source_target_pairs={{0,10},{1,11},{2,8},{3,9},{4,14},{5,15},{6,12},{7,13},{8,2},{9,3},... | collective-permute-start | bytes 786440 | tf_op jit(solution)/shard_map/ppermute | solution.py:502
  768.0 24.5 %collective-permute-start.66 = (bf16[64,2048]{1,0:T(8,128)(2,1)S(1)}, bf16[64,2048]{1,0:T(8,128)(2,1)S(1)}, u32[]{:S(2)}, u32[]{:S(2)}) collective-permute-start(bf16[64,2048]{1,0:T(8,128)(2,1)S(1)} %copy-done.196), channel_id=1, source_target_pairs={{0,8},{1,9},{2,10},{3,11},{4,12},{5,13},{6,14},{7,15},{8,0},{9,1},... | collective-permute-start | bytes 786440 | tf_op jit(solution)/shard_map/ppermute | solution.py:502
  768.3 24.2 %collective-permute-start.65 = (bf16[64,2048]{1,0:T(8,128)(2,1)S(1)}, bf16[64,2048]{1,0:T(8,128)(2,1)S(1)}, u32[]{:S(2)}, u32[]{:S(2)}) collective-permute-start(bf16[64,2048]{1,0:T(8,128)(2,1)S(1)} %copy-done.195), channel_id=1, source_target_pairs={{0,6},{1,7},{2,4},{3,5},{4,2},{5,3},{6,0},{7,1},{8,14},{9,15},{10,... | collective-permute-start | bytes 786440 | tf_op jit(solution)/shard_map/ppermute | solution.py:502
  773.2 20.1 %collective-permute-start.64 = (bf16[64,2048]{1,0:T(8,128)(2,1)S(1)}, bf16[64,2048]{1,0:T(8,128)(2,1)S(1)}, u32[]{:S(2)}, u32[]{:S(2)}) collective-permute-start(bf16[64,2048]{1,0:T(8,128)(2,1)S(1)} %copy-done.194), channel_id=1, source_target_pairs={{0,4},{1,5},{2,6},{3,7},{4,0},{5,1},{6,2},{7,3},{8,12},{9,13},{10,... | collective-permute-start | bytes 786440 | tf_op jit(solution)/shard_map/ppermute | solution.py:502
  777.8 17.2 %collective-permute-start.63 = (bf16[64,2048]{1,0:T(8,128)(2,1)S(1)}, bf16[64,2048]{1,0:T(8,128)(2,1)S(1)}, u32[]{:S(2)}, u32[]{:S(2)}) collective-permute-start(bf16[64,2048]{1,0:T(8,128)(2,1)S(1)} %copy-done.193), channel_id=1, source_target_pairs={{0,2},{1,3},{2,0},{3,1},{4,6},{5,7},{6,4},{7,5},{8,10},{9,11},{10,... | collective-permute-start | bytes 786440 | tf_op jit(solution)/shard_map/ppermute | solution.py:502
  800.5 18.4 %collective-permute-start.76 = (bf16[64,2048]{1,0:T(8,128)(2,1)S(1)}, bf16[64,2048]{1,0:T(8,128)(2,1)S(1)}, u32[]{:S(2)}, u32[]{:S(2)}) collective-permute-start(bf16[64,2048]{1,0:T(8,128)(2,1)S(1)} %multiply_add_fusion.refs_0_), channel_id=1, source_target_pairs={{0,2},{1,3},{2,0},{3,1},{4,6},{5,7},{6,4},{7,5},{8,10},{9,11},{10,... | collective-permute-start | bytes 786440 | tf_op jit(solution)/shard_map/ppermute | solution.py:502
  801.0 18.0 %collective-permute-start.77 = (bf16[64,2048]{1,0:T(8,128)(2,1)S(1)}, bf16[64,2048]{1,0:T(8,128)(2,1)S(1)}, u32[]{:S(2)}, u32[]{:S(2)}) collective-permute-start(bf16[64,2048]{1,0:T(8,128)(2,1)S(1)} %multiply_add_fusion.refs_0_), channel_id=1, source_target_pairs={{0,4},{1,5},{2,6},{3,7},{4,0},{5,1},{6,2},{7,3},{8,12},{9,13},{10,... | collective-permute-start | bytes 786440 | tf_op jit(solution)/shard_map/ppermute | solution.py:502
  802.0 18.8 %collective-permute-start.78 = (bf16[64,2048]{1,0:T(8,128)(2,1)S(1)}, bf16[64,2048]{1,0:T(8,128)(2,1)S(1)}, u32[]{:S(2)}, u32[]{:S(2)}) collective-permute-start(bf16[64,2048]{1,0:T(8,128)(2,1)S(1)} %multiply_add_fusion.refs_0_), channel_id=1, source_target_pairs={{0,6},{1,7},{2,4},{3,5},{4,2},{5,3},{6,0},{7,1},{8,14},{9,15},{10,... | collective-permute-start | bytes 786440 | tf_op jit(solution)/shard_map/ppermute | solution.py:502
  804.0 16.7 %collective-permute-start.79 = (bf16[64,2048]{1,0:T(8,128)(2,1)S(1)}, bf16[64,2048]{1,0:T(8,128)(2,1)S(1)}, u32[]{:S(2)}, u32[]{:S(2)}) collective-permute-start(bf16[64,2048]{1,0:T(8,128)(2,1)S(1)} %multiply_add_fusion.refs_0_), channel_id=1, source_target_pairs={{0,8},{1,9},{2,10},{3,11},{4,12},{5,13},{6,14},{7,15},{8,0},{9,1},... | collective-permute-start | bytes 786440 | tf_op jit(solution)/shard_map/ppermute | solution.py:502
  804.0 16.7 %collective-permute-start.80 = (bf16[64,2048]{1,0:T(8,128)(2,1)S(1)}, bf16[64,2048]{1,0:T(8,128)(2,1)S(1)}, u32[]{:S(2)}, u32[]{:S(2)}) collective-permute-start(bf16[64,2048]{1,0:T(8,128)(2,1)S(1)} %multiply_add_fusion.refs_0_), channel_id=1, source_target_pairs={{0,10},{1,11},{2,8},{3,9},{4,14},{5,15},{6,12},{7,13},{8,2},{9,3},... | collective-permute-start | bytes 786440 | tf_op jit(solution)/shard_map/ppermute | solution.py:502
  832.0 28.7 %collective-permute-start.83 = (bf16[512,2048]{1,0:T(8,128)(2,1)}, bf16[512,2048]{1,0:T(8,128)(2,1)}, u32[]{:S(2)}, u32[]{:S(2)}) collective-permute-start(bf16[512,2048]{1,0:T(8,128)(2,1)} %shard_map.373), channel_id=1, source_target_pairs={{0,1},{1,0},{2,3},{3,2},{4,5},{5,4},{6,7},{7,6},{8,9},{9,8},{10,11... | collective-permute-start | bytes 6291464 | tf_op jit(solution)/shard_map/ppermute | solution.py:502
  853.3 59.8 %collective-permute-start.85 = (bf16[512,1024]{1,0:T(8,128)(2,1)}, bf16[512,1024]{1,0:T(8,128)(2,1)S(1)}, u32[]{:S(2)}, u32[]{:S(2)}) collective-permute-start(bf16[512,1024]{1,0:T(8,128)(2,1)} %get-tuple-element.276), channel_id=1, source_target_pairs={{0,4},{4,0},{8,12},{12,8},{1,5},{5,1},{9,13},{13,9},{2,6},{6,2},{1... | collective-permute-start | bytes 3145736 | tf_op jit(solution)/shard_map/ppermute | solution.py:505
  854.4 58.7 %collective-permute-start.86 = (bf16[512,1024]{1,0:T(8,128)(2,1)}, bf16[512,1024]{1,0:T(8,128)(2,1)}, u32[]{:S(2)}, u32[]{:S(2)}) collective-permute-start(bf16[512,1024]{1,0:T(8,128)(2,1)} %get-tuple-element.277), channel_id=1, source_target_pairs={{0,8},{4,12},{8,0},{12,4},{1,9},{5,13},{9,1},{13,5},{2,10},{6,14},... | collective-permute-start | bytes 3145736 | tf_op jit(solution)/shard_map/ppermute | solution.py:505
  856.0 57.2 %collective-permute-start.87 = (bf16[512,1024]{1,0:T(8,128)(2,1)}, bf16[512,1024]{1,0:T(8,128)(2,1)}, u32[]{:S(2)}, u32[]{:S(2)}) collective-permute-start(bf16[512,1024]{1,0:T(8,128)(2,1)} %get-tuple-element.278), channel_id=1, source_target_pairs={{0,12},{4,8},{8,4},{12,0},{1,13},{5,9},{9,5},{13,1},{2,14},{6,10},... | collective-permute-start | bytes 3145736 | tf_op jit(solution)/shard_map/ppermute | solution.py:505
  863.2 48.7 %collective-permute-start.84 = (bf16[1024,256]{1,0:T(8,128)(2,1)S(1)}, bf16[1024,256]{1,0:T(8,128)(2,1)}, u32[]{:S(2)}, u32[]{:S(2)}) collective-permute-start(bf16[1024,256]{1,0:T(8,128)(2,1)S(1)} %pad_maximum_fusion.16), channel_id=1, source_target_pairs={{0,16},{16,0},{1,17},{17,1},{2,18},{18,2},{3,19},{19,3},{4,20},{20... | collective-permute-start | bytes 1572872 | tf_op jit(solution)/shard_map/ppermute | solution.py:542
  954.8 41.4 %collective-permute-start.91 = (bf16[512,1024]{1,0:T(8,128)(2,1)}, bf16[512,1024]{1,0:T(8,128)(2,1)S(1)}, u32[]{:S(2)}, u32[]{:S(2)}) collective-permute-start(bf16[512,1024]{1,0:T(8,128)(2,1)} %pad_maximum_fusion.5), channel_id=1, source_target_pairs={{0,4},{4,0},{8,12},{12,8},{1,5},{5,1},{9,13},{13,9},{2,6},{6,2},{1... | collective-permute-start | bytes 3145736 | tf_op jit(solution)/shard_map/ppermute | solution.py:505
  955.8 40.3 %collective-permute-start.92 = (bf16[512,1024]{1,0:T(8,128)(2,1)}, bf16[512,1024]{1,0:T(8,128)(2,1)}, u32[]{:S(2)}, u32[]{:S(2)}) collective-permute-start(bf16[512,1024]{1,0:T(8,128)(2,1)} %pad_maximum_fusion.6), channel_id=1, source_target_pairs={{0,8},{4,12},{8,0},{12,4},{1,9},{5,13},{9,1},{13,5},{2,10},{6,14},... | collective-permute-start | bytes 3145736 | tf_op jit(solution)/shard_map/ppermute | solution.py:505
  955.8 45.3 %collective-permute-start.93 = (bf16[512,1024]{1,0:T(8,128)(2,1)}, bf16[512,1024]{1,0:T(8,128)(2,1)}, u32[]{:S(2)}, u32[]{:S(2)}) collective-permute-start(bf16[512,1024]{1,0:T(8,128)(2,1)} %pad_maximum_fusion.7), channel_id=1, source_target_pairs={{0,12},{4,8},{8,4},{12,0},{1,13},{5,9},{9,5},{13,1},{2,14},{6,10},... | collective-permute-start | bytes 3145736 | tf_op jit(solution)/shard_map/ppermute | solution.py:505
  (242 other events, 2870.1 us)

commit v6 on v5

--- a/solution.py
+++ b/solution.py
@@ -716,9 +716,8 @@
         return [values[0]] + [grid.trade(values[j], j) for j in (1, 2, 3)]
 
     weight_view = native_view(abd_weights) if native else None
-    qkv_pieces, picked_all, side, table = tied(
-        pieces_of(SECTIONS[:1]), picked_all, side, embed_table
-    )
+    qkv_pieces, table = tied(pieces_of(SECTIONS[:1]), embed_table)
+    qkv_pieces, picked_all, side = tied(qkv_pieces, picked_all, side)
     qkv_w = traded(qkv_pieces)
     picked_all, other_pieces = tied(picked_all, pieces_of(SECTIONS[1:3]))
 
@@ -856,8 +855,29 @@
     hidden_grad = [grid.row_sum(g) for g in hidden_grad]
     down_gradient = traded(row_gradients(down_grad, hidden))
 
-    hidden_grad[0], down_gradient, output_part, aba_part, aba_gains_part = tied(
-        hidden_grad[0], down_gradient, output_part, aba_part, aba_gains_part
+    hidden_grad[0], down_gradient = tied(hidden_grad[0], down_gradient)
+
+    before_grad = [gelu_back(before[0], hidden_grad[0]).astype(LOW)]
+    second_grad = [dot(before_grad[0], up_turned).astype(LOW)]
+    hidden_grad[1], before_grad[0], second_grad[0] = tied(
+        hidden_grad[1], before_grad[0], second_grad[0]
+    )
+    before_grad.append(gelu_back(before[1], hidden_grad[1]).astype(LOW))
+    second_grad.append(dot(before_grad[1], up_turned).astype(LOW))
+    second_grad = grid.gathered_sum(*second_grad)
+    gained = second_grad * gains[1]
+    sums = jnp.stack([jnp.sum(gained, axis=1), jnp.sum(gained * hat_two, axis=1)])
+    sums = sum(grid.row_list(sums)) / model_width
+    middle_grad = upstream.astype(WIDE) + scale_two * (
+        gained - sums[0][:, None] - hat_two * sums[1][:, None]
+    )
+    middle_grad, up_gradient = tied(middle_grad, row_gradients(second, before_grad))
+    up_gradient = traded(up_gradient)
+    gain_two = jnp.sum(second_grad * hat_two, axis=0)
+    branch_grad = grid.spread(middle_grad.astype(LOW))
+    attended_grad = jnp.concatenate([dot(a, out_w).astype(LOW) for a in branch_grad], axis=0)
+    attended_grad, attended, table_acts, output_part, aba_part, aba_gains_part = tied(
+        attended_grad, attended, middle_grad.astype(LOW), output_part, aba_part, aba_gains_part
     )
 
     small = jnp.concatenate([aba_part.reshape(-1), aba_gains_part.reshape(-1)])
@@ -874,35 +894,14 @@
     packed = jnp.concatenate([blocks.reshape(-1), small]).reshape(-1, 128)
     for step in (grid.heads, 2 * grid.heads):
         packed = packed + grid.pair(packed, step)
-    packed = grid.row_sum(packed).reshape(-1)
+    packed = grid.row_sum(packed.astype(LOW)).reshape(-1)
     output_grad = packed[: blocks.size].reshape(-1, classes, embed_width)
     aba_grad = packed[blocks.size : blocks.size + aba_weights.size].reshape(aba_weights.shape)
     aba_gains_grad = packed[blocks.size + aba_weights.size :].reshape(aba_gains.shape)
 
-
-    before_grad = [gelu_back(before[0], hidden_grad[0]).astype(LOW)]
-    second_grad = [dot(before_grad[0], up_turned).astype(LOW)]
-    hidden_grad[1], before_grad[0], second_grad[0] = tied(
-        hidden_grad[1], before_grad[0], second_grad[0]
-    )
-    before_grad.append(gelu_back(before[1], hidden_grad[1]).astype(LOW))
-    second_grad.append(dot(before_grad[1], up_turned).astype(LOW))
-    second_grad = grid.gathered_sum(*second_grad)
-    gained = second_grad * gains[1]
-    sums = jnp.stack([jnp.sum(gained, axis=1), jnp.sum(gained * hat_two, axis=1)])
-    sums = sum(grid.row_list(sums)) / model_width
-    middle_grad = upstream.astype(WIDE) + scale_two * (
-        gained - sums[0][:, None] - hat_two * sums[1][:, None]
-    )
-    middle_grad, up_gradient, output_grad, aba_grad, aba_gains_grad = tied(
-        middle_grad, row_gradients(second, before_grad), output_grad, aba_grad, aba_gains_grad
-    )
-    up_gradient = traded(up_gradient)
-    gain_two = jnp.sum(second_grad * hat_two, axis=0)
-    branch_grad = grid.spread(middle_grad.astype(LOW))
-    attended_grad = jnp.concatenate([dot(a, out_w).astype(LOW) for a in branch_grad], axis=0)
-    attended_grad, attended, table_acts = tied(attended_grad, attended, middle_grad.astype(LOW))
-    attended_grad, up_gradient = tied(grid.row_sum(attended_grad).astype(LOW), up_gradient)
+    attended_grad, up_gradient, output_grad, aba_grad, aba_gains_grad = tied(
+        grid.row_sum(attended_grad).astype(LOW), up_gradient, output_grad, aba_grad, aba_gains_grad
+    )
     out_gradient = row_gradients(branch_grad, attended)
     prob_grad = dot(grid.columns(attended_grad), value_rows, 1, 1)
     score_grad = probs * (prob_grad - jnp.sum(probs * prob_grad, axis=1, keepdims=True))

time: 1180 us -> 1160 us (0.983)
    ppermute x66, waiting for transfers between devices: 180 us -> 198 us  [pair(): lax.ppermute(values, ('q', 'p', 'h'), [(i, i ^ step) for i in range(self....]
    ppermute x15, waiting for transfers between devices: 181 us -> 164 us  [facing(): return lax.ppermute(values, 'a', [(0, 1), (1, 0)])]
    ppermute x4, waiting for transfers between devices: 37.1 us -> 23 us  [columns(): got = lax.ppermute(values, 'p', [(i, i ^ d) for i in range(self.parts)])]
    unnamed x417 -> x407, local copies, waits for them, and re-layouts: 39.4 us -> 41.3 us
  transfers between devices with their start and end apart: 104 -> 104, of which waited for: 72 -> 66; matrix products, arithmetic and copies ran while one was open for 13% -> 14% of each run, Pallas kernels for 3% -> 3%
where the time goes in v6:
time: 1160 us; the launch traced here: 1140 us
  waiting for transfers between devices  526 us (45%)
  matrix products  151 us (13%)
  Pallas kernels  126 us (11%)
  starting transfers between devices  116 us (10%)
  other arithmetic  115 us (10%)
  local copies, waits for them, and re-layouts  85.7 us (7%)
  between operations  24.4 us (2%)
    ppermute x66, waiting for transfers between devices, pair(): lax.ppermute(values, ('q', 'p', 'h'), [(i, i ^ step) for i in range(self....  198 us
    ppermute x15, waiting for transfers between devices, facing(): return lax.ppermute(values, 'a', [(0, 1), (1, 0)])  164 us
    ppermute x18, waiting for transfers between devices, trade(): lax.ppermute(values, ('q', 'p'), [(i, i ^ step) for i in range(SHARERS)])  139 us
    dot_general x57, matrix products, dot(): lax.dot_general(left, right, (((left_dim,), (right_dim,)), ((), ())), pre...  118 us
    ppermute x66, starting transfers between devices, pair(): lax.ppermute(values, ('q', 'p', 'h'), [(i, i ^ step) for i in range(self....  71.3 us
    pallas_call x1, Pallas kernels, moments_step(): pl.pallas_call(moments_kernel, out_shape=[shape, shape, jax.ShapeDtypeStr...  53.7 us
    unnamed x407, local copies, waits for them, and re-layouts  41.3 us
    pallas_call x3, Pallas kernels, split_weights(): pl.pallas_call(functools.partial(split_kernel, sections), out_shape=[jax....  33.8 us
  transfers between devices with their start and end apart: 104, of which 66 were waited for; matrix products, arithmetic and copies ran while one was open for 14% of the time, Pallas kernels for 3%

profile of v6, /device:TPU:0, one launch (start us, length us, event | category | flops | bytes accessed | tf_op | source)
XLA Modules:
  0.0 1144.2 jit_solution(18439398943102304552)
XLA Ops:
  5.7 10.8 shard_map.364
  43.5 12.5 %shard_map.365 = (bf16[512,1280]{1,0:T(8,128)(2,1)S(1)}, bf16[512,1280]{1,0:T(8,128)(2,1)}, bf16[512,1280]{1,0:T(8,128)(2,1)}, bf16[512,1280]{1,0:T(8,128)(2,1)}) custom-call(s32[2]{0:T(128)S(1)} %pad_add_fusion.side_ref, f32[512,96,128]{2,1,0:T(8,128)} %bitcast.466, f32[512,96,128]{2,1,0:T(8,128)} %bitcast.467), custom_call_target="tpu_custom_call" | custom-call | flops 1 | bytes 1 | tf_op jit(solution)/shard_map/pallas_call | solution.py:291
  60.6 10.4 shard_map.366
  71.0 3.4 copy-done
  78.2 11.4 collective-permute-done.7
  89.6 3.8 reduce_sum.607
  93.5 4.4 multiply_reduce_fusion.3
  103.1 5.2 multiply_convert_fusion.2
  108.3 4.5 convolution_convert_fusion.7
  122.7 10.6 shard_map.367
  133.4 45.0 %collective-permute-done.9 = bf16[1024,768]{1,0:T(8,128)(2,1)} collective-permute-done((bf16[1024,768]{1,0:T(8,128)(2,1)}, bf16[1024,768]{1,0:T(8,128)(2,1)}, u32[]{:S(2)}, u32[]{:S(2)}) %collective-permute-start.9) | collective-permute-done | bytes 1572896 | tf_op jit(solution)/shard_map/ppermute | solution.py:542
  182.4 21.0 %collective-permute-done.12 = bf16[512,1280]{1,0:T(8,128)(2,1)} collective-permute-done((bf16[512,1280]{1,0:T(8,128)(2,1)}, bf16[512,1280]{1,0:T(8,128)(2,1)}, u32[]{:S(2)}, u32[]{:S(2)}) %collective-permute-start.12) | collective-permute-done | bytes 1310752 | tf_op jit(solution)/shard_map/ppermute | solution.py:505
  209.6 9.7 collective-permute-done.16
  219.3 6.4 collective-permute-done.15
  235.5 4.2 shard_map.368
  246.8 4.3 collective-permute-done.24
  257.2 9.1 collective-permute-done.22
  284.2 13.2 %collective-permute-done.26.refs_1_ = bf16[64,2048]{1,0:T(8,128)(2,1)S(1)} collective-permute-done((bf16[64,2048]{1,0:T(8,128)(2,1)S(1)}, bf16[64,2048]{1,0:T(8,128)(2,1)S(1)}, u32[]{:S(2)}, u32[]{:S(2)}) %collective-permute-start.26) | collective-permute-done | bytes 262176 | tf_op jit(solution)/shard_map/ppermute | solution.py:502
  299.6 5.0 collective-permute-done.31.refs_6_
  306.8 3.9 shard_map.369
  329.6 40.2 %collective-permute-done.35 = bf16[512,1024]{1,0:T(8,128)(2,1)S(1)} collective-permute-done((bf16[512,1024]{1,0:T(8,128)(2,1)S(1)}, bf16[512,1024]{1,0:T(8,128)(2,1)S(1)}, u32[]{:S(2)}, u32[]{:S(2)}) %collective-permute-start.35) | collective-permute-done | bytes 1048608 | tf_op jit(solution)/shard_map/ppermute | solution.py:542
  370.2 23.1 %collective-permute-done.37 = bf16[512,1024]{1,0:T(8,128)(2,1)S(1)} collective-permute-done((bf16[512,1024]{1,0:T(8,128)(2,1)S(1)}, bf16[512,1024]{1,0:T(8,128)(2,1)S(1)}, u32[]{:S(2)}, u32[]{:S(2)}) %collective-permute-start.37) | collective-permute-done | bytes 1048608 | tf_op jit(solution)/shard_map/ppermute | solution.py:505
  393.3 22.5 %collective-permute-done.38 = bf16[512,1024]{1,0:T(8,128)(2,1)S(1)} collective-permute-done((bf16[512,1024]{1,0:T(8,128)(2,1)S(1)}, bf16[512,1024]{1,0:T(8,128)(2,1)S(1)}, u32[]{:S(2)}, u32[]{:S(2)}) %collective-permute-start.38) | collective-permute-done | bytes 1048608 | tf_op jit(solution)/shard_map/ppermute | solution.py:505
  416.5 3.7 convolution_convert_fusion.3.refs_0_.refs_1_.refs_2_.refs_3_.refs_4_.refs_5_.refs_6_.refs_7_
  424.9 4.1 collective-permute-done.39.refs_8_.refs_9_.refs_10_.refs_11_.refs_12_.refs_13_.refs_14_.refs_15_
  430.3 4.4 shard_map.370
  436.3 3.4 collective-permute-start.45
  446.7 5.9 collective-permute-done.45
  452.7 7.6 collective-permute-done.44
  460.3 5.5 collective-permute-done.43
  470.9 12.6 %collective-permute-done.47 = f32[32,2048]{1,0:T(8,128)S(1)} collective-permute-done((f32[32,2048]{1,0:T(8,128)S(1)}, f32[32,2048]{1,0:T(8,128)S(1)}, u32[]{:S(2)}, u32[]{:S(2)}) %collective-permute-start.47) | collective-permute-done | bytes 262176 | tf_op jit(solution)/shard_map/ppermute | solution.py:542
  542.3 8.0 collective-permute-done.48
  562.4 6.9 collective-permute-done.51.refs_3_
  571.2 5.5 collective-permute-done.54.refs_6_
  576.7 3.9 collective-permute-done.55.refs_7_
  581.3 3.7 shard_map.371
  585.1 5.3 convolution_convert_fusion.9
  609.6 32.6 %collective-permute-done.58 = bf16[512,1024]{1,0:T(8,128)(2,1)S(1)} collective-permute-done((bf16[512,1024]{1,0:T(8,128)(2,1)S(1)}, bf16[512,1024]{1,0:T(8,128)(2,1)S(1)}, u32[]{:S(2)}, u32[]{:S(2)}) %collective-permute-start.58) | collective-permute-done | bytes 1048608 | tf_op jit(solution)/shard_map/ppermute | solution.py:542
  642.6 28.3 %collective-permute-done.60.rest_10_ = bf16[512,1024]{1,0:T(8,128)(2,1)S(1)} collective-permute-done((bf16[512,1024]{1,0:T(8,128)(2,1)S(1)}, bf16[512,1024]{1,0:T(8,128)(2,1)S(1)}, u32[]{:S(2)}, u32[]{:S(2)}) %collective-permute-start.60) | collective-permute-done | bytes 1048608 | tf_op jit(solution)/shard_map/ppermute | solution.py:505
  671.0 21.8 %collective-permute-done.61.rest_11_ = bf16[512,1024]{1,0:T(8,128)(2,1)S(1)} collective-permute-done((bf16[512,1024]{1,0:T(8,128)(2,1)S(1)}, bf16[512,1024]{1,0:T(8,128)(2,1)S(1)}, u32[]{:S(2)}, u32[]{:S(2)}) %collective-permute-start.61) | collective-permute-done | bytes 1048608 | tf_op jit(solution)/shard_map/ppermute | solution.py:505
  695.9 3.7 convolution_convert_fusion.1.refs_0_.refs_1_.refs_2_.refs_3_.refs_4_.refs_5_.refs_6_.refs_7_
  713.7 4.2 shard_map.372
  721.2 4.4 multiply_reduce_fusion.9
  737.1 7.4 collective-permute-done.67
  751.1 3.4 multiply_reduce_fusion.8
  770.0 15.1 %collective-permute-done.73.refs_3_ = bf16[64,2048]{1,0:T(8,128)(2,1)S(1)} collective-permute-done((bf16[64,2048]{1,0:T(8,128)(2,1)S(1)}, bf16[64,2048]{1,0:T(8,128)(2,1)S(1)}, u32[]{:S(2)}, u32[]{:S(2)}) %collective-permute-start.73) | collective-permute-done | bytes 262176 | tf_op jit(solution)/shard_map/ppermute | solution.py:502
  786.7 3.9 shard_map.373
  831.6 6.0 collective-permute-done.84
  841.8 27.9 %collective-permute-done.85 = f32[641,128]{1,0:T(8,128)S(1)} collective-permute-done((f32[641,128]{1,0:T(8,128)S(1)}, f32[641,128]{1,0:T(8,128)S(1)}, u32[]{:S(2)}, u32[]{:S(2)}) %collective-permute-start.85) | collective-permute-done | bytes 328224 | tf_op jit(solution)/shard_map/ppermute | solution.py:502
  881.8 6.3 collective-permute-done.87
  890.9 3.5 convolution_convert_fusion.16
  894.4 6.9 collective-permute-done.88
  920.3 7.9 multiply_reduce_fusion.1
  937.2 7.6 multiply_convert_fusion
  970.2 7.1 collective-permute-done.93.rest_3_
  981.2 8.7 collective-permute-done.95
  990.6 7.5 collective-permute-done.96
  999.9 5.6 collective-permute-done.97
  1008.3 10.7 collective-permute-done.98
  1033.1 53.7 %shard_map.374 = (f32[512,96,128]{2,1,0:T(8,128)}, f32[512,96,128]{2,1,0:T(8,128)}, bf16[512,96,128]{2,1,0:T(8,128)(2,1)}, f32[2,8,128]{2,1,0:T(8,128)S(1)}) custom-call(s32[2]{0:T(128)S(1)} %copy-done.19, f32[1]{0:T(128)} %bitcast.123.clip_ref, f32[512,96,128]{2,1,0:T(8,128)} %bitcast.469, f32[512,96,128]{2,1,0:T(8,128)} %bitcast.474, ...), custom_call_target="tpu_custom_call" | custom-call | flops 125829120 | bytes 150994944 | tf_op jit(solution)/shard_map/pallas_call | solution.py:352
  1096.1 4.0 shard_map.375
  1109.9 3.5 collective-permute-done.102
  1113.5 4.4 collective-permute-done.103
  1121.3 20.8 %multiply_subtract_fusion = f32[512,96,128]{2,1,0:T(8,128)} fusion(f32[512,96,128]{2,1,0:T(8,128)} %bitcast.470, bf16[512,96,128]{2,1,0:T(8,128)(2,1)} %get-tuple-element.322, f32[]{:T(128)} %bitcast.137), kind=kLoop, calls=%fused_computation | loop fusion | flops 18874368 | bytes 62914564 | tf_op jit(solution)/shard_map/sub | solution.py:197
  (891 shorter events, 437.8 us)
Async XLA Ops:
  3.3 17.7 %collective-permute-start = (bf16[32,128]{1,0:T(8,128)(2,1)S(1)}, bf16[32,128]{1,0:T(8,128)(2,1)S(1)}, u32[]{:S(2)}, u32[]{:S(2)}) collective-permute-start(bf16[32,128]{1,0:T(8,128)(2,1)S(1)} %get-tuple-element.371), channel_id=1, source_target_pairs={{0,1},{1,0},{2,3},{3,2},{4,5},{5,4},{6,7},{7,6},{8,9},{9,8},{10,11... | collective-permute-start | bytes 24584 | tf_op jit(solution)/shard_map/ppermute | solution.py:502
  5.4 26.5 %collective-permute-start.13 = (bf16[1,16,64,32]{2,3,1,0:T(8,128)(2,1)}, bf16[1,16,64,32]{2,3,1,0:T(8,128)(2,1)}, u32[]{:S(2)}, u32[]{:S(2)}) collective-permute-start(bf16[1,16,64,32]{2,3,1,0:T(8,128)(2,1)} %convert_bitcast_fusion), channel_id=1, source_target_pairs={{0,1},{1,0},{2,3},{3,2},{4,5},{5,4},{6,7},{7,6},{8,9},{9,8},{10,11... | collective-permute-start | bytes 196616 | tf_op jit(solution)/shard_map/ppermute | solution.py:502
  55.9 20.2 %collective-permute-start.5 = (bf16[512,768]{1,0:T(8,128)(2,1)}, bf16[512,768]{1,0:T(8,128)(2,1)}, u32[]{:S(2)}, u32[]{:S(2)}) collective-permute-start(bf16[512,768]{1,0:T(8,128)(2,1)} %get-tuple-element.197), channel_id=1, source_target_pairs={{0,4},{4,0},{8,12},{12,8},{1,5},{5,1},{9,13},{13,9},{2,6},{6,2},{1... | collective-permute-start | bytes 2359304 | tf_op jit(solution)/shard_map/ppermute | solution.py:505
  57.4 20.8 %collective-permute-start.6 = (bf16[512,768]{1,0:T(8,128)(2,1)}, bf16[512,768]{1,0:T(8,128)(2,1)}, u32[]{:S(2)}, u32[]{:S(2)}) collective-permute-start(bf16[512,768]{1,0:T(8,128)(2,1)} %get-tuple-element.198), channel_id=1, source_target_pairs={{0,8},{4,12},{8,0},{12,4},{1,9},{5,13},{9,1},{13,5},{2,10},{6,14},... | collective-permute-start | bytes 2359304 | tf_op jit(solution)/shard_map/ppermute | solution.py:505
  57.7 31.9 %collective-permute-start.7 = (bf16[512,768]{1,0:T(8,128)(2,1)}, bf16[512,768]{1,0:T(8,128)(2,1)}, u32[]{:S(2)}, u32[]{:S(2)}) collective-permute-start(bf16[512,768]{1,0:T(8,128)(2,1)} %get-tuple-element.199), channel_id=1, source_target_pairs={{0,12},{4,8},{8,4},{12,0},{1,13},{5,9},{9,5},{13,1},{2,14},{6,10},... | collective-permute-start | bytes 2359304 | tf_op jit(solution)/shard_map/ppermute | solution.py:505
  112.8 65.5 %collective-permute-start.9 = (bf16[1024,768]{1,0:T(8,128)(2,1)}, bf16[1024,768]{1,0:T(8,128)(2,1)}, u32[]{:S(2)}, u32[]{:S(2)}) collective-permute-start(bf16[1024,768]{1,0:T(8,128)(2,1)} %convolution_convert_fusion.7), channel_id=1, source_target_pairs={{0,16},{16,0},{1,17},{17,1},{2,18},{18,2},{3,19},{19,3},{4,20},{20... | collective-permute-start | bytes 4718600 | tf_op jit(solution)/shard_map/ppermute | solution.py:542
  116.2 64.5 %collective-permute-start.10 = (bf16[512,1280]{1,0:T(8,128)(2,1)}, bf16[512,1280]{1,0:T(8,128)(2,1)}, u32[]{:S(2)}, u32[]{:S(2)}) collective-permute-start(bf16[512,1280]{1,0:T(8,128)(2,1)} %get-tuple-element.210), channel_id=1, source_target_pairs={{0,4},{4,0},{8,12},{12,8},{1,5},{5,1},{9,13},{13,9},{2,6},{6,2},{1... | collective-permute-start | bytes 3932168 | tf_op jit(solution)/shard_map/ppermute | solution.py:505
  117.7 64.7 %collective-permute-start.11 = (bf16[512,1280]{1,0:T(8,128)(2,1)}, bf16[512,1280]{1,0:T(8,128)(2,1)}, u32[]{:S(2)}, u32[]{:S(2)}) collective-permute-start(bf16[512,1280]{1,0:T(8,128)(2,1)} %get-tuple-element.211), channel_id=1, source_target_pairs={{0,8},{4,12},{8,0},{12,4},{1,9},{5,13},{9,1},{13,5},{2,10},{6,14},... | collective-permute-start | bytes 3932168 | tf_op jit(solution)/shard_map/ppermute | solution.py:505
  117.9 85.5 %collective-permute-start.12 = (bf16[512,1280]{1,0:T(8,128)(2,1)}, bf16[512,1280]{1,0:T(8,128)(2,1)}, u32[]{:S(2)}, u32[]{:S(2)}) collective-permute-start(bf16[512,1280]{1,0:T(8,128)(2,1)} %get-tuple-element.212), channel_id=1, source_target_pairs={{0,12},{4,8},{8,4},{12,0},{1,13},{5,9},{9,5},{13,1},{2,14},{6,10},... | collective-permute-start | bytes 3932168 | tf_op jit(solution)/shard_map/ppermute | solution.py:505
  204.4 14.9 %collective-permute-start.16 = (bf16[1024,256]{1,0:T(8,128)(2,1)S(1)}, bf16[1024,256]{1,0:T(8,128)(2,1)S(1)}, u32[]{:S(2)}, u32[]{:S(2)}) collective-permute-start(bf16[1024,256]{1,0:T(8,128)(2,1)S(1)} %get-tuple-element.373), channel_id=1, source_target_pairs={{0,4},{4,0},{1,5},{5,1},{2,6},{6,2},{3,7},{7,3},{8,12},{12,8},{9,1... | collective-permute-start | bytes 1572872 | tf_op jit(solution)/shard_map/ppermute | solution.py:605
  205.9 19.9 %collective-permute-start.15 = (bf16[1024,256]{1,0:T(8,128)(2,1)S(1)}, bf16[1024,256]{1,0:T(8,128)(2,1)S(1)}, u32[]{:S(2)}, u32[]{:S(2)}) collective-permute-start(bf16[1024,256]{1,0:T(8,128)(2,1)S(1)} %get-tuple-element.374), channel_id=1, source_target_pairs={{0,4},{4,0},{1,5},{5,1},{2,6},{6,2},{3,7},{7,3},{8,12},{12,8},{9,1... | collective-permute-start | bytes 1572872 | tf_op jit(solution)/shard_map/ppermute | solution.py:605
  239.8 15.6 %collective-permute-start.23 = (bf16[64,2048]{1,0:T(8,128)(2,1)}, bf16[64,2048]{1,0:T(8,128)(2,1)S(1)}, u32[]{:S(2)}, u32[]{:S(2)}) collective-permute-start(bf16[64,2048]{1,0:T(8,128)(2,1)} %get-tuple-element.233), channel_id=1, source_target_pairs={{0,12},{1,13},{2,14},{3,15},{4,8},{5,9},{6,10},{7,11},{8,4},{9,5},... | collective-permute-start | bytes 786440 | tf_op jit(solution)/shard_map/ppermute | solution.py:502
  242.4 23.9 %collective-permute-start.22 = (bf16[64,2048]{1,0:T(8,128)(2,1)}, bf16[64,2048]{1,0:T(8,128)(2,1)S(1)}, u32[]{:S(2)}, u32[]{:S(2)}) collective-permute-start(bf16[64,2048]{1,0:T(8,128)(2,1)} %get-tuple-element.232), channel_id=1, source_target_pairs={{0,10},{1,11},{2,8},{3,9},{4,14},{5,15},{6,12},{7,13},{8,2},{9,3},... | collective-permute-start | bytes 786440 | tf_op jit(solution)/shard_map/ppermute | solution.py:502
  243.7 25.3 %collective-permute-start.21 = (bf16[64,2048]{1,0:T(8,128)(2,1)}, bf16[64,2048]{1,0:T(8,128)(2,1)S(1)}, u32[]{:S(2)}, u32[]{:S(2)}) collective-permute-start(bf16[64,2048]{1,0:T(8,128)(2,1)} %get-tuple-element.231), channel_id=1, source_target_pairs={{0,8},{1,9},{2,10},{3,11},{4,12},{5,13},{6,14},{7,15},{8,0},{9,1},... | collective-permute-start | bytes 786440 | tf_op jit(solution)/shard_map/ppermute | solution.py:502
  245.7 23.3 %collective-permute-start.20 = (bf16[64,2048]{1,0:T(8,128)(2,1)}, bf16[64,2048]{1,0:T(8,128)(2,1)S(1)}, u32[]{:S(2)}, u32[]{:S(2)}) collective-permute-start(bf16[64,2048]{1,0:T(8,128)(2,1)} %get-tuple-element.230), channel_id=1, source_target_pairs={{0,6},{1,7},{2,4},{3,5},{4,2},{5,3},{6,0},{7,1},{8,14},{9,15},{10,... | collective-permute-start | bytes 786440 | tf_op jit(solution)/shard_map/ppermute | solution.py:502
  251.1 18.4 %collective-permute-start.19 = (bf16[64,2048]{1,0:T(8,128)(2,1)}, bf16[64,2048]{1,0:T(8,128)(2,1)S(1)}, u32[]{:S(2)}, u32[]{:S(2)}) collective-permute-start(bf16[64,2048]{1,0:T(8,128)(2,1)} %get-tuple-element.229), channel_id=1, source_target_pairs={{0,4},{1,5},{2,6},{3,7},{4,0},{5,1},{6,2},{7,3},{8,12},{9,13},{10,... | collective-permute-start | bytes 786440 | tf_op jit(solution)/shard_map/ppermute | solution.py:502
  255.4 16.5 %collective-permute-start.18 = (bf16[64,2048]{1,0:T(8,128)(2,1)}, bf16[64,2048]{1,0:T(8,128)(2,1)S(1)}, u32[]{:S(2)}, u32[]{:S(2)}) collective-permute-start(bf16[64,2048]{1,0:T(8,128)(2,1)} %get-tuple-element.228), channel_id=1, source_target_pairs={{0,2},{1,3},{2,0},{3,1},{4,6},{5,7},{6,4},{7,5},{8,10},{9,11},{10,... | collective-permute-start | bytes 786440 | tf_op jit(solution)/shard_map/ppermute | solution.py:502
  279.0 18.4 %collective-permute-start.26 = (bf16[64,2048]{1,0:T(8,128)(2,1)S(1)}, bf16[64,2048]{1,0:T(8,128)(2,1)S(1)}, u32[]{:S(2)}, u32[]{:S(2)}) collective-permute-start(bf16[64,2048]{1,0:T(8,128)(2,1)S(1)} %multiply_convert_fusion.11.refs_0_), channel_id=1, source_target_pairs={{0,2},{1,3},{2,0},{3,1},{4,6},{5,7},{6,4},{7,5},{8,10},{9,11},{10,... | collective-permute-start | bytes 786440 | tf_op jit(solution)/shard_map/ppermute | solution.py:502
  279.3 18.3 %collective-permute-start.27 = (bf16[64,2048]{1,0:T(8,128)(2,1)S(1)}, bf16[64,2048]{1,0:T(8,128)(2,1)S(1)}, u32[]{:S(2)}, u32[]{:S(2)}) collective-permute-start(bf16[64,2048]{1,0:T(8,128)(2,1)S(1)} %multiply_convert_fusion.11.refs_0_), channel_id=1, source_target_pairs={{0,4},{1,5},{2,6},{3,7},{4,0},{5,1},{6,2},{7,3},{8,12},{9,13},{10,... | collective-permute-start | bytes 786440 | tf_op jit(solution)/shard_map/ppermute | solution.py:502
  280.4 19.2 %collective-permute-start.28 = (bf16[64,2048]{1,0:T(8,128)(2,1)S(1)}, bf16[64,2048]{1,0:T(8,128)(2,1)S(1)}, u32[]{:S(2)}, u32[]{:S(2)}) collective-permute-start(bf16[64,2048]{1,0:T(8,128)(2,1)S(1)} %multiply_convert_fusion.11.refs_0_), channel_id=1, source_target_pairs={{0,6},{1,7},{2,4},{3,5},{4,2},{5,3},{6,0},{7,1},{8,14},{9,15},{10,... | collective-permute-start | bytes 786440 | tf_op jit(solution)/shard_map/ppermute | solution.py:502
  282.5 17.0 %collective-permute-start.29 = (bf16[64,2048]{1,0:T(8,128)(2,1)S(1)}, bf16[64,2048]{1,0:T(8,128)(2,1)S(1)}, u32[]{:S(2)}, u32[]{:S(2)}) collective-permute-start(bf16[64,2048]{1,0:T(8,128)(2,1)S(1)} %multiply_convert_fusion.11.refs_0_), channel_id=1, source_target_pairs={{0,8},{1,9},{2,10},{3,11},{4,12},{5,13},{6,14},{7,15},{8,0},{9,1},... | collective-permute-start | bytes 786440 | tf_op jit(solution)/shard_map/ppermute | solution.py:502
  282.5 17.0 %collective-permute-start.30 = (bf16[64,2048]{1,0:T(8,128)(2,1)S(1)}, bf16[64,2048]{1,0:T(8,128)(2,1)S(1)}, u32[]{:S(2)}, u32[]{:S(2)}) collective-permute-start(bf16[64,2048]{1,0:T(8,128)(2,1)S(1)} %multiply_convert_fusion.11.refs_0_), channel_id=1, source_target_pairs={{0,10},{1,11},{2,8},{3,9},{4,14},{5,15},{6,12},{7,13},{8,2},{9,3},... | collective-permute-start | bytes 786440 | tf_op jit(solution)/shard_map/ppermute | solution.py:502
  320.3 49.5 %collective-permute-start.35 = (bf16[512,1024]{1,0:T(8,128)(2,1)S(1)}, bf16[512,1024]{1,0:T(8,128)(2,1)S(1)}, u32[]{:S(2)}, u32[]{:S(2)}) collective-permute-start(bf16[512,1024]{1,0:T(8,128)(2,1)S(1)} %convolution_convert_fusion.11), channel_id=1, source_target_pairs={{0,16},{16,0},{1,17},{17,1},{2,18},{18,2},{3,19},{19,3},{4,20},{20... | collective-permute-start | bytes 3145736 | tf_op jit(solution)/shard_map/ppermute | solution.py:542
  323.0 47.2 %collective-permute-start.36 = (bf16[512,1024]{1,0:T(8,128)(2,1)S(1)}, bf16[512,1024]{1,0:T(8,128)(2,1)S(1)}, u32[]{:S(2)}, u32[]{:S(2)}) collective-permute-start(bf16[512,1024]{1,0:T(8,128)(2,1)S(1)} %copy-done.29), channel_id=1, source_target_pairs={{0,4},{4,0},{8,12},{12,8},{1,5},{5,1},{9,13},{13,9},{2,6},{6,2},{1... | collective-permute-start | bytes 3145736 | tf_op jit(solution)/shard_map/ppermute | solution.py:505
  324.1 69.2 %collective-permute-start.37 = (bf16[512,1024]{1,0:T(8,128)(2,1)S(1)}, bf16[512,1024]{1,0:T(8,128)(2,1)S(1)}, u32[]{:S(2)}, u32[]{:S(2)}) collective-permute-start(bf16[512,1024]{1,0:T(8,128)(2,1)S(1)} %copy-done.27), channel_id=1, source_target_pairs={{0,8},{4,12},{8,0},{12,4},{1,9},{5,13},{9,1},{13,5},{2,10},{6,14},... | collective-permute-start | bytes 3145736 | tf_op jit(solution)/shard_map/ppermute | solution.py:505
  326.5 89.3 %collective-permute-start.38 = (bf16[512,1024]{1,0:T(8,128)(2,1)S(1)}, bf16[512,1024]{1,0:T(8,128)(2,1)S(1)}, u32[]{:S(2)}, u32[]{:S(2)}) collective-permute-start(bf16[512,1024]{1,0:T(8,128)(2,1)S(1)} %copy-done.25), channel_id=1, source_target_pairs={{0,12},{4,8},{8,4},{12,0},{1,13},{5,9},{9,5},{13,1},{2,14},{6,10},... | collective-permute-start | bytes 3145736 | tf_op jit(solution)/shard_map/ppermute | solution.py:505
  329.4 90.9 %collective-permute-start.34 = (bf16[512,1024]{1,0:T(8,128)(2,1)S(1)}, bf16[512,1024]{1,0:T(8,128)(2,1)S(1)}, u32[]{:S(2)}, u32[]{:S(2)}) collective-permute-start(bf16[512,1024]{1,0:T(8,128)(2,1)S(1)} %convolution_convert_fusion.10), channel_id=1, source_target_pairs={{0,16},{16,0},{1,17},{17,1},{2,18},{18,2},{3,19},{19,3},{4,20},{20... | collective-permute-start | bytes 3145736 | tf_op jit(solution)/shard_map/ppermute | solution.py:542
  436.3 16.4 %collective-permute-start.45 = (bf16[64,2048]{1,0:T(8,128)(2,1)}, bf16[64,2048]{1,0:T(8,128)(2,1)S(1)}, u32[]{:S(2)}, u32[]{:S(2)}) collective-permute-start(bf16[64,2048]{1,0:T(8,128)(2,1)} %get-tuple-element.258), channel_id=1, source_target_pairs={{0,12},{1,13},{2,14},{3,15},{4,8},{5,9},{6,10},{7,11},{8,4},{9,5},... | collective-permute-start | bytes 786440 | tf_op jit(solution)/shard_map/ppermute | solution.py:502
  439.7 20.6 %collective-permute-start.44 = (bf16[64,2048]{1,0:T(8,128)(2,1)}, bf16[64,2048]{1,0:T(8,128)(2,1)S(1)}, u32[]{:S(2)}, u32[]{:S(2)}) collective-permute-start(bf16[64,2048]{1,0:T(8,128)(2,1)} %get-tuple-element.257), channel_id=1, source_target_pairs={{0,10},{1,11},{2,8},{3,9},{4,14},{5,15},{6,12},{7,13},{8,2},{9,3},... | collective-permute-start | bytes 786440 | tf_op jit(solution)/shard_map/ppermute | solution.py:502
  439.7 26.0 %collective-permute-start.43 = (bf16[64,2048]{1,0:T(8,128)(2,1)}, bf16[64,2048]{1,0:T(8,128)(2,1)S(1)}, u32[]{:S(2)}, u32[]{:S(2)}) collective-permute-start(bf16[64,2048]{1,0:T(8,128)(2,1)} %get-tuple-element.256), channel_id=1, source_target_pairs={{0,8},{1,9},{2,10},{3,11},{4,12},{5,13},{6,14},{7,15},{8,0},{9,1},... | collective-permute-start | bytes 786440 | tf_op jit(solution)/shard_map/ppermute | solution.py:502
  440.6 25.1 %collective-permute-start.42 = (bf16[64,2048]{1,0:T(8,128)(2,1)}, bf16[64,2048]{1,0:T(8,128)(2,1)S(1)}, u32[]{:S(2)}, u32[]{:S(2)}) collective-permute-start(bf16[64,2048]{1,0:T(8,128)(2,1)} %get-tuple-element.255), channel_id=1, source_target_pairs={{0,6},{1,7},{2,4},{3,5},{4,2},{5,3},{6,0},{7,1},{8,14},{9,15},{10,... | collective-permute-start | bytes 786440 | tf_op jit(solution)/shard_map/ppermute | solution.py:502
  446.0 21.0 %collective-permute-start.41 = (bf16[64,2048]{1,0:T(8,128)(2,1)}, bf16[64,2048]{1,0:T(8,128)(2,1)S(1)}, u32[]{:S(2)}, u32[]{:S(2)}) collective-permute-start(bf16[64,2048]{1,0:T(8,128)(2,1)} %get-tuple-element.254), channel_id=1, source_target_pairs={{0,4},{1,5},{2,6},{3,7},{4,0},{5,1},{6,2},{7,3},{8,12},{9,13},{10,... | collective-permute-start | bytes 786440 | tf_op jit(solution)/shard_map/ppermute | solution.py:502
  468.7 14.8 %collective-permute-start.47 = (f32[32,2048]{1,0:T(8,128)S(1)}, f32[32,2048]{1,0:T(8,128)S(1)}, u32[]{:S(2)}, u32[]{:S(2)}) collective-permute-start(f32[32,2048]{1,0:T(8,128)S(1)} %slice_select_fusion.1), channel_id=1, source_target_pairs={{0,16},{16,0},{1,17},{17,1},{2,18},{18,2},{3,19},{19,3},{4,20},{20... | collective-permute-start | bytes 786440 | tf_op jit(solution)/shard_map/ppermute | solution.py:542
  552.3 16.9 %collective-permute-start.51 = (bf16[64,2048]{1,0:T(8,128)(2,1)S(1)}, bf16[64,2048]{1,0:T(8,128)(2,1)S(1)}, u32[]{:S(2)}, u32[]{:S(2)}) collective-permute-start(bf16[64,2048]{1,0:T(8,128)(2,1)S(1)} %pad_maximum_fusion.22.refs_0_), channel_id=1, source_target_pairs={{0,6},{1,7},{2,4},{3,5},{4,2},{5,3},{6,0},{7,1},{8,14},{9,15},{10,... | collective-permute-start | bytes 786440 | tf_op jit(solution)/shard_map/ppermute | solution.py:502
  554.0 15.2 %collective-permute-start.52 = (bf16[64,2048]{1,0:T(8,128)(2,1)S(1)}, bf16[64,2048]{1,0:T(8,128)(2,1)S(1)}, u32[]{:S(2)}, u32[]{:S(2)}) collective-permute-start(bf16[64,2048]{1,0:T(8,128)(2,1)S(1)} %pad_maximum_fusion.22.refs_0_), channel_id=1, source_target_pairs={{0,8},{1,9},{2,10},{3,11},{4,12},{5,13},{6,14},{7,15},{8,0},{9,1},... | collective-permute-start | bytes 786440 | tf_op jit(solution)/shard_map/ppermute | solution.py:502
  554.0 17.1 %collective-permute-start.53 = (bf16[64,2048]{1,0:T(8,128)(2,1)S(1)}, bf16[64,2048]{1,0:T(8,128)(2,1)S(1)}, u32[]{:S(2)}, u32[]{:S(2)}) collective-permute-start(bf16[64,2048]{1,0:T(8,128)(2,1)S(1)} %pad_maximum_fusion.22.refs_0_), channel_id=1, source_target_pairs={{0,10},{1,11},{2,8},{3,9},{4,14},{5,15},{6,12},{7,13},{8,2},{9,3},... | collective-permute-start | bytes 786440 | tf_op jit(solution)/shard_map/ppermute | solution.py:502
  558.9 17.8 %collective-permute-start.54 = (bf16[64,2048]{1,0:T(8,128)(2,1)S(1)}, bf16[64,2048]{1,0:T(8,128)(2,1)S(1)}, u32[]{:S(2)}, u32[]{:S(2)}) collective-permute-start(bf16[64,2048]{1,0:T(8,128)(2,1)S(1)} %pad_maximum_fusion.22.refs_0_), channel_id=1, source_target_pairs={{0,12},{1,13},{2,14},{3,15},{4,8},{5,9},{6,10},{7,11},{8,4},{9,5},... | collective-permute-start | bytes 786440 | tf_op jit(solution)/shard_map/ppermute | solution.py:502
  560.9 19.6 %collective-permute-start.55 = (bf16[64,2048]{1,0:T(8,128)(2,1)S(1)}, bf16[64,2048]{1,0:T(8,128)(2,1)S(1)}, u32[]{:S(2)}, u32[]{:S(2)}) collective-permute-start(bf16[64,2048]{1,0:T(8,128)(2,1)S(1)} %pad_maximum_fusion.22.refs_0_), channel_id=1, source_target_pairs={{0,14},{1,15},{2,12},{3,13},{4,10},{5,11},{6,8},{7,9},{8,6},{9,7},... | collective-permute-start | bytes 786440 | tf_op jit(solution)/shard_map/ppermute | solution.py:502
  592.9 49.3 %collective-permute-start.58 = (bf16[512,1024]{1,0:T(8,128)(2,1)S(1)}, bf16[512,1024]{1,0:T(8,128)(2,1)S(1)}, u32[]{:S(2)}, u32[]{:S(2)}) collective-permute-start(bf16[512,1024]{1,0:T(8,128)(2,1)S(1)} %convolution_convert_fusion.9), channel_id=1, source_target_pairs={{0,16},{16,0},{1,17},{17,1},{2,18},{18,2},{3,19},{19,3},{4,20},{20... | collective-permute-start | bytes 3145736 | tf_op jit(solution)/shard_map/ppermute | solution.py:542
  597.0 45.6 %collective-permute-start.59 = (bf16[512,1024]{1,0:T(8,128)(2,1)S(1)}, bf16[512,1024]{1,0:T(8,128)(2,1)S(1)}, u32[]{:S(2)}, u32[]{:S(2)}) collective-permute-start(bf16[512,1024]{1,0:T(8,128)(2,1)S(1)} %get-tuple-element.500), channel_id=1, source_target_pairs={{0,4},{4,0},{8,12},{12,8},{1,5},{5,1},{9,13},{13,9},{2,6},{6,2},{1... | collective-permute-start | bytes 3145736 | tf_op jit(solution)/shard_map/ppermute | solution.py:505
  600.4 70.6 %collective-permute-start.60 = (bf16[512,1024]{1,0:T(8,128)(2,1)S(1)}, bf16[512,1024]{1,0:T(8,128)(2,1)S(1)}, u32[]{:S(2)}, u32[]{:S(2)}) collective-permute-start(bf16[512,1024]{1,0:T(8,128)(2,1)S(1)} %get-tuple-element.502), channel_id=1, source_target_pairs={{0,8},{4,12},{8,0},{12,4},{1,9},{5,13},{9,1},{13,5},{2,10},{6,14},... | collective-permute-start | bytes 3145736 | tf_op jit(solution)/shard_map/ppermute | solution.py:505
  604.0 88.7 %collective-permute-start.61 = (bf16[512,1024]{1,0:T(8,128)(2,1)S(1)}, bf16[512,1024]{1,0:T(8,128)(2,1)S(1)}, u32[]{:S(2)}, u32[]{:S(2)}) collective-permute-start(bf16[512,1024]{1,0:T(8,128)(2,1)S(1)} %get-tuple-element.504), channel_id=1, source_target_pairs={{0,12},{4,8},{8,4},{12,0},{1,13},{5,9},{9,5},{13,1},{2,14},{6,10},... | collective-permute-start | bytes 3145736 | tf_op jit(solution)/shard_map/ppermute | solution.py:505
  605.3 94.3 %collective-permute-start.57 = (bf16[512,1024]{1,0:T(8,128)(2,1)S(1)}, bf16[512,1024]{1,0:T(8,128)(2,1)S(1)}, u32[]{:S(2)}, u32[]{:S(2)}) collective-permute-start(bf16[512,1024]{1,0:T(8,128)(2,1)S(1)} %convolution_convert_fusion.8), channel_id=1, source_target_pairs={{0,16},{16,0},{1,17},{17,1},{2,18},{18,2},{3,19},{19,3},{4,20},{20... | collective-permute-start | bytes 3145736 | tf_op jit(solution)/shard_map/ppermute | solution.py:542
  718.0 16.0 %collective-permute-start.68 = (bf16[64,2048]{1,0:T(8,128)(2,1)}, bf16[64,2048]{1,0:T(8,128)(2,1)S(1)}, u32[]{:S(2)}, u32[]{:S(2)}) collective-permute-start(bf16[64,2048]{1,0:T(8,128)(2,1)} %get-tuple-element.274), channel_id=1, source_target_pairs={{0,12},{1,13},{2,14},{3,15},{4,8},{5,9},{6,10},{7,11},{8,4},{9,5},... | collective-permute-start | bytes 786440 | tf_op jit(solution)/shard_map/ppermute | solution.py:502
  725.7 18.9 %collective-permute-start.67 = (bf16[64,2048]{1,0:T(8,128)(2,1)S(1)}, bf16[64,2048]{1,0:T(8,128)(2,1)S(1)}, u32[]{:S(2)}, u32[]{:S(2)}) collective-permute-start(bf16[64,2048]{1,0:T(8,128)(2,1)S(1)} %copy-done.192), channel_id=1, source_target_pairs={{0,10},{1,11},{2,8},{3,9},{4,14},{5,15},{6,12},{7,13},{8,2},{9,3},... | collective-permute-start | bytes 786440 | tf_op jit(solution)/shard_map/ppermute | solution.py:502
  726.0 22.4 %collective-permute-start.66 = (bf16[64,2048]{1,0:T(8,128)(2,1)S(1)}, bf16[64,2048]{1,0:T(8,128)(2,1)S(1)}, u32[]{:S(2)}, u32[]{:S(2)}) collective-permute-start(bf16[64,2048]{1,0:T(8,128)(2,1)S(1)} %copy-done.191), channel_id=1, source_target_pairs={{0,8},{1,9},{2,10},{3,11},{4,12},{5,13},{6,14},{7,15},{8,0},{9,1},... | collective-permute-start | bytes 786440 | tf_op jit(solution)/shard_map/ppermute | solution.py:502
  728.4 20.0 %collective-permute-start.65 = (bf16[64,2048]{1,0:T(8,128)(2,1)S(1)}, bf16[64,2048]{1,0:T(8,128)(2,1)S(1)}, u32[]{:S(2)}, u32[]{:S(2)}) collective-permute-start(bf16[64,2048]{1,0:T(8,128)(2,1)S(1)} %copy-done.190), channel_id=1, source_target_pairs={{0,6},{1,7},{2,4},{3,5},{4,2},{5,3},{6,0},{7,1},{8,14},{9,15},{10,... | collective-permute-start | bytes 786440 | tf_op jit(solution)/shard_map/ppermute | solution.py:502
  729.9 19.4 %collective-permute-start.64 = (bf16[64,2048]{1,0:T(8,128)(2,1)S(1)}, bf16[64,2048]{1,0:T(8,128)(2,1)S(1)}, u32[]{:S(2)}, u32[]{:S(2)}) collective-permute-start(bf16[64,2048]{1,0:T(8,128)(2,1)S(1)} %copy-done.189), channel_id=1, source_target_pairs={{0,4},{1,5},{2,6},{3,7},{4,0},{5,1},{6,2},{7,3},{8,12},{9,13},{10,... | collective-permute-start | bytes 786440 | tf_op jit(solution)/shard_map/ppermute | solution.py:502
  734.1 16.4 %collective-permute-start.63 = (bf16[64,2048]{1,0:T(8,128)(2,1)S(1)}, bf16[64,2048]{1,0:T(8,128)(2,1)S(1)}, u32[]{:S(2)}, u32[]{:S(2)}) collective-permute-start(bf16[64,2048]{1,0:T(8,128)(2,1)S(1)} %copy-done.188), channel_id=1, source_target_pairs={{0,2},{1,3},{2,0},{3,1},{4,6},{5,7},{6,4},{7,5},{8,10},{9,11},{10,... | collective-permute-start | bytes 786440 | tf_op jit(solution)/shard_map/ppermute | solution.py:502
  744.5 16.2 %collective-permute-start.89 = (bf16[1024,256]{1,0:T(8,128)(2,1)}, bf16[1024,256]{1,0:T(8,128)(2,1)S(1)}, u32[]{:S(2)}, u32[]{:S(2)}) collective-permute-start(bf16[1024,256]{1,0:T(8,128)(2,1)} %get-tuple-element.372), channel_id=1, source_target_pairs={{0,4},{4,0},{1,5},{5,1},{2,6},{6,2},{3,7},{7,3},{8,12},{12,8},{9,1... | collective-permute-start | bytes 1572872 | tf_op jit(solution)/shard_map/ppermute | solution.py:605
  757.9 27.2 %collective-permute-start.73 = (bf16[64,2048]{1,0:T(8,128)(2,1)S(1)}, bf16[64,2048]{1,0:T(8,128)(2,1)S(1)}, u32[]{:S(2)}, u32[]{:S(2)}) collective-permute-start(bf16[64,2048]{1,0:T(8,128)(2,1)S(1)} %multiply_add_fusion.refs_0_), channel_id=1, source_target_pairs={{0,6},{1,7},{2,4},{3,5},{4,2},{5,3},{6,0},{7,1},{8,14},{9,15},{10,... | collective-permute-start | bytes 786440 | tf_op jit(solution)/shard_map/ppermute | solution.py:502
  759.5 25.6 %collective-permute-start.74 = (bf16[64,2048]{1,0:T(8,128)(2,1)S(1)}, bf16[64,2048]{1,0:T(8,128)(2,1)S(1)}, u32[]{:S(2)}, u32[]{:S(2)}) collective-permute-start(bf16[64,2048]{1,0:T(8,128)(2,1)S(1)} %multiply_add_fusion.refs_0_), channel_id=1, source_target_pairs={{0,8},{1,9},{2,10},{3,11},{4,12},{5,13},{6,14},{7,15},{8,0},{9,1},... | collective-permute-start | bytes 786440 | tf_op jit(solution)/shard_map/ppermute | solution.py:502
  760.8 24.4 %collective-permute-start.75 = (bf16[64,2048]{1,0:T(8,128)(2,1)S(1)}, bf16[64,2048]{1,0:T(8,128)(2,1)S(1)}, u32[]{:S(2)}, u32[]{:S(2)}) collective-permute-start(bf16[64,2048]{1,0:T(8,128)(2,1)S(1)} %multiply_add_fusion.refs_0_), channel_id=1, source_target_pairs={{0,10},{1,11},{2,8},{3,9},{4,14},{5,15},{6,12},{7,13},{8,2},{9,3},... | collective-permute-start | bytes 786440 | tf_op jit(solution)/shard_map/ppermute | solution.py:502
  763.2 21.9 %collective-permute-start.76 = (bf16[64,2048]{1,0:T(8,128)(2,1)S(1)}, bf16[64,2048]{1,0:T(8,128)(2,1)S(1)}, u32[]{:S(2)}, u32[]{:S(2)}) collective-permute-start(bf16[64,2048]{1,0:T(8,128)(2,1)S(1)} %multiply_add_fusion.refs_0_), channel_id=1, source_target_pairs={{0,12},{1,13},{2,14},{3,15},{4,8},{5,9},{6,10},{7,11},{8,4},{9,5},... | collective-permute-start | bytes 786440 | tf_op jit(solution)/shard_map/ppermute | solution.py:502
  766.1 20.6 %collective-permute-start.77 = (bf16[64,2048]{1,0:T(8,128)(2,1)S(1)}, bf16[64,2048]{1,0:T(8,128)(2,1)}, u32[]{:S(2)}, u32[]{:S(2)}) collective-permute-start(bf16[64,2048]{1,0:T(8,128)(2,1)S(1)} %multiply_add_fusion.refs_0_), channel_id=1, source_target_pairs={{0,14},{1,15},{2,12},{3,13},{4,10},{5,11},{6,8},{7,9},{8,6},{9,7},... | collective-permute-start | bytes 786440 | tf_op jit(solution)/shard_map/ppermute | solution.py:502
  790.7 20.2 %collective-permute-start.78 = (bf16[512,2048]{1,0:T(8,128)(2,1)}, bf16[512,2048]{1,0:T(8,128)(2,1)}, u32[]{:S(2)}, u32[]{:S(2)}) collective-permute-start(bf16[512,2048]{1,0:T(8,128)(2,1)} %shard_map.373), channel_id=1, source_target_pairs={{0,1},{1,0},{2,3},{3,2},{4,5},{5,4},{6,7},{7,6},{8,9},{9,8},{10,11... | collective-permute-start | bytes 6291464 | tf_op jit(solution)/shard_map/ppermute | solution.py:502
  805.0 83.5 %collective-permute-start.80 = (bf16[512,1024]{1,0:T(8,128)(2,1)}, bf16[512,1024]{1,0:T(8,128)(2,1)}, u32[]{:S(2)}, u32[]{:S(2)}) collective-permute-start(bf16[512,1024]{1,0:T(8,128)(2,1)} %get-tuple-element.281), channel_id=1, source_target_pairs={{0,4},{4,0},{8,12},{12,8},{1,5},{5,1},{9,13},{13,9},{2,6},{6,2},{1... | collective-permute-start | bytes 3145736 | tf_op jit(solution)/shard_map/ppermute | solution.py:505
  806.0 82.5 %collective-permute-start.81 = (bf16[512,1024]{1,0:T(8,128)(2,1)}, bf16[512,1024]{1,0:T(8,128)(2,1)}, u32[]{:S(2)}, u32[]{:S(2)}) collective-permute-start(bf16[512,1024]{1,0:T(8,128)(2,1)} %get-tuple-element.282), channel_id=1, source_target_pairs={{0,8},{4,12},{8,0},{12,4},{1,9},{5,13},{9,1},{13,5},{2,10},{6,14},... | collective-permute-start | bytes 3145736 | tf_op jit(solution)/shard_map/ppermute | solution.py:505
  806.4 82.1 %collective-permute-start.82 = (bf16[512,1024]{1,0:T(8,128)(2,1)}, bf16[512,1024]{1,0:T(8,128)(2,1)}, u32[]{:S(2)}, u32[]{:S(2)}) collective-permute-start(bf16[512,1024]{1,0:T(8,128)(2,1)} %get-tuple-element.283), channel_id=1, source_target_pairs={{0,12},{4,8},{8,4},{12,0},{1,13},{5,9},{9,5},{13,1},{2,14},{6,10},... | collective-permute-start | bytes 3145736 | tf_op jit(solution)/shard_map/ppermute | solution.py:505
  813.2 67.4 %collective-permute-start.79 = (bf16[1024,256]{1,0:T(8,128)(2,1)S(1)}, bf16[1024,256]{1,0:T(8,128)(2,1)}, u32[]{:S(2)}, u32[]{:S(2)}) collective-permute-start(bf16[1024,256]{1,0:T(8,128)(2,1)S(1)} %pad_maximum_fusion.16), channel_id=1, source_target_pairs={{0,16},{16,0},{1,17},{17,1},{2,18},{18,2},{3,19},{19,3},{4,20},{20... | collective-permute-start | bytes 1572872 | tf_op jit(solution)/shard_map/ppermute | solution.py:542
  837.7 32.0 %collective-permute-start.85 = (f32[641,128]{1,0:T(8,128)S(1)}, f32[641,128]{1,0:T(8,128)S(1)}, u32[]{:S(2)}, u32[]{:S(2)}) collective-permute-start(f32[641,128]{1,0:T(8,128)S(1)} %maximum_bitcast_fusion.2), channel_id=1, source_target_pairs={{0,4},{1,5},{2,6},{3,7},{4,0},{5,1},{6,2},{7,3},{8,12},{9,13},{10,... | collective-permute-start | bytes 984584 | tf_op jit(solution)/shard_map/ppermute | solution.py:502
  928.9 41.3 %collective-permute-start.91 = (bf16[512,1024]{1,0:T(8,128)(2,1)}, bf16[512,1024]{1,0:T(8,128)(2,1)S(1)}, u32[]{:S(2)}, u32[]{:S(2)}) collective-permute-start(bf16[512,1024]{1,0:T(8,128)(2,1)} %pad_maximum_fusion.5), channel_id=1, source_target_pairs={{0,4},{4,0},{8,12},{12,8},{1,5},{5,1},{9,13},{13,9},{2,6},{6,2},{1... | collective-permute-start | bytes 3145736 | tf_op jit(solution)/shard_map/ppermute | solution.py:505
  930.0 40.2 %collective-permute-start.92 = (bf16[512,1024]{1,0:T(8,128)(2,1)}, bf16[512,1024]{1,0:T(8,128)(2,1)}, u32[]{:S(2)}, u32[]{:S(2)}) collective-permute-start(bf16[512,1024]{1,0:T(8,128)(2,1)} %pad_maximum_fusion.6), channel_id=1, source_target_pairs={{0,8},{4,12},{8,0},{12,4},{1,9},{5,13},{9,1},{13,5},{2,10},{6,14},... | collective-permute-start | bytes 3145736 | tf_op jit(solution)/shard_map/ppermute | solution.py:505
  932.6 44.6 %collective-permute-start.93 = (bf16[512,1024]{1,0:T(8,128)(2,1)}, bf16[512,1024]{1,0:T(8,128)(2,1)}, u32[]{:S(2)}, u32[]{:S(2)}) collective-permute-start(bf16[512,1024]{1,0:T(8,128)(2,1)} %pad_maximum_fusion.7), channel_id=1, source_target_pairs={{0,12},{4,8},{8,4},{12,0},{1,13},{5,9},{9,5},{13,1},{2,14},{6,10},... | collective-permute-start | bytes 3145736 | tf_op jit(solution)/shard_map/ppermute | solution.py:505
  (237 other events, 2759.3 us)

commit v7 on v6

--- a/solution.py
+++ b/solution.py
@@ -894,7 +894,7 @@
     packed = jnp.concatenate([blocks.reshape(-1), small]).reshape(-1, 128)
     for step in (grid.heads, 2 * grid.heads):
         packed = packed + grid.pair(packed, step)
-    packed = grid.row_sum(packed.astype(LOW)).reshape(-1)
+    packed = grid.row_sum(lax.reduce_precision(packed, 8, 7).astype(LOW)).reshape(-1)
     output_grad = packed[: blocks.size].reshape(-1, classes, embed_width)
     aba_grad = packed[blocks.size : blocks.size + aba_weights.size].reshape(aba_weights.shape)
     aba_gains_grad = packed[blocks.size + aba_weights.size :].reshape(aba_gains.shape)
@@ -940,11 +940,11 @@
     scalars = sum(jnp.where(lane == i, scalars[i], 0.0) for i in range(3))
     packed, qkv_gradient = tied(packed, traded(qkv_gradient))
     gradients = qkv_gradient + up_gradient + down_gradient
-    packed = jnp.stack(
-        grid.row_gather(grid.group_total(jnp.concatenate([scalars, packed], axis=0)))
-    )
-    summed = jnp.sum(packed[:, 0, :3], axis=0)
-    packed = packed[:, 8:].reshape(grid.rows * SHARERS, -1)
+    packed = grid.group_total(jnp.concatenate([scalars, packed], axis=0))
+    summed = grid.row_sum(packed[:8])[0, :3]
+    packed = lax.reduce_precision(packed[8:], 8, 7).astype(LOW)
+    packed = jnp.stack(grid.row_gather(packed)).astype(WIDE)
+    packed = packed.reshape(grid.rows * SHARERS, -1)
     embed_grad = packed[:, :table_size].reshape(embed_table.shape).transpose(1, 0, 2)
     abd_gains_grad = packed[:, table_size:].reshape(-1, 2, width).transpose(1, 0, 2)
     abd_gains_grad = abd_gains_grad.reshape(2, model_width)

time: 1160 us -> 1150 us (level)
    ppermute x15 -> x16, waiting for transfers between devices: 164 us -> 157 us  [facing(): return lax.ppermute(values, 'a', [(0, 1), (1, 0)])]
  transfers between devices with their start and end apart: 104 -> 105, of which waited for: 66 -> 67; matrix products, arithmetic and copies ran while one was open for 14% -> 14% of each run, Pallas kernels for 3% -> 3%
where the time goes in v7:
time: 1150 us; the launch traced here: 1140 us
  waiting for transfers between devices  516 us (45%)
  matrix products  151 us (13%)
  Pallas kernels  126 us (11%)
  starting transfers between devices  119 us (10%)
  other arithmetic  115 us (10%)
  local copies, waits for them, and re-layouts  85.7 us (7%)
  between operations  24.6 us (2%)
    ppermute x66, waiting for transfers between devices, pair(): lax.ppermute(values, ('q', 'p', 'h'), [(i, i ^ step) for i in range(self....  195 us
    ppermute x16, waiting for transfers between devices, facing(): return lax.ppermute(values, 'a', [(0, 1), (1, 0)])  157 us
    ppermute x18, waiting for transfers between devices, trade(): lax.ppermute(values, ('q', 'p'), [(i, i ^ step) for i in range(SHARERS)])  139 us
    dot_general x57, matrix products, dot(): lax.dot_general(left, right, (((left_dim,), (right_dim,)), ((), ())), pre...  118 us
    ppermute x66, starting transfers between devices, pair(): lax.ppermute(values, ('q', 'p', 'h'), [(i, i ^ step) for i in range(self....  72.3 us
    pallas_call x1, Pallas kernels, moments_step(): pl.pallas_call(moments_kernel, out_shape=[shape, shape, jax.ShapeDtypeStr...  53.8 us
    unnamed x407, local copies, waits for them, and re-layouts  41.2 us
    pallas_call x3, Pallas kernels, split_weights(): pl.pallas_call(functools.partial(split_kernel, sections), out_shape=[jax....  33.8 us
  transfers between devices with their start and end apart: 105, of which 67 were waited for; matrix products, arithmetic and copies ran while one was open for 14% of the time, Pallas kernels for 3%

profile of v7, /device:TPU:0, one launch (start us, length us, event | category | flops | bytes accessed | tf_op | source)
XLA Modules:
  0.0 1138.5 jit_solution(939474971537425738)
XLA Ops:
  5.7 10.8 shard_map.364
  43.5 12.5 %shard_map.365 = (bf16[512,1280]{1,0:T(8,128)(2,1)S(1)}, bf16[512,1280]{1,0:T(8,128)(2,1)}, bf16[512,1280]{1,0:T(8,128)(2,1)}, bf16[512,1280]{1,0:T(8,128)(2,1)}) custom-call(s32[2]{0:T(128)S(1)} %pad_add_fusion.side_ref, f32[512,96,128]{2,1,0:T(8,128)} %bitcast.466, f32[512,96,128]{2,1,0:T(8,128)} %bitcast.467), custom_call_target="tpu_custom_call" | custom-call | flops 1 | bytes 1 | tf_op jit(solution)/shard_map/pallas_call | solution.py:291
  60.6 10.4 shard_map.366
  71.0 3.4 copy-done
  78.2 11.4 %collective-permute-done.7 = bf16[512,768]{1,0:T(8,128)(2,1)} collective-permute-done((bf16[512,768]{1,0:T(8,128)(2,1)}, bf16[512,768]{1,0:T(8,128)(2,1)}, u32[]{:S(2)}, u32[]{:S(2)}) %collective-permute-start.7) | collective-permute-done | bytes 786464 | tf_op jit(solution)/shard_map/ppermute | solution.py:505
  89.6 3.8 reduce_sum.598
  93.5 4.4 multiply_reduce_fusion.3
  103.1 5.2 multiply_convert_fusion.2
  108.3 4.5 convolution_convert_fusion.7
  122.7 10.6 shard_map.367
  133.3 45.0 %collective-permute-done.9 = bf16[1024,768]{1,0:T(8,128)(2,1)} collective-permute-done((bf16[1024,768]{1,0:T(8,128)(2,1)}, bf16[1024,768]{1,0:T(8,128)(2,1)}, u32[]{:S(2)}, u32[]{:S(2)}) %collective-permute-start.9) | collective-permute-done | bytes 1572896 | tf_op jit(solution)/shard_map/ppermute | solution.py:542
  182.4 21.0 %collective-permute-done.12 = bf16[512,1280]{1,0:T(8,128)(2,1)} collective-permute-done((bf16[512,1280]{1,0:T(8,128)(2,1)}, bf16[512,1280]{1,0:T(8,128)(2,1)}, u32[]{:S(2)}, u32[]{:S(2)}) %collective-permute-start.12) | collective-permute-done | bytes 1310752 | tf_op jit(solution)/shard_map/ppermute | solution.py:505
  209.6 9.7 collective-permute-done.16
  219.3 6.4 collective-permute-done.15
  235.5 4.2 shard_map.368
  246.8 4.3 collective-permute-done.24
  257.2 9.1 collective-permute-done.22
  284.2 13.1 %collective-permute-done.26.refs_1_ = bf16[64,2048]{1,0:T(8,128)(2,1)S(1)} collective-permute-done((bf16[64,2048]{1,0:T(8,128)(2,1)S(1)}, bf16[64,2048]{1,0:T(8,128)(2,1)S(1)}, u32[]{:S(2)}, u32[]{:S(2)}) %collective-permute-start.26) | collective-permute-done | bytes 262176 | tf_op jit(solution)/shard_map/ppermute | solution.py:502
  299.6 5.0 collective-permute-done.31.refs_6_
  306.8 3.8 shard_map.369
  329.6 40.2 %collective-permute-done.35 = bf16[512,1024]{1,0:T(8,128)(2,1)S(1)} collective-permute-done((bf16[512,1024]{1,0:T(8,128)(2,1)S(1)}, bf16[512,1024]{1,0:T(8,128)(2,1)S(1)}, u32[]{:S(2)}, u32[]{:S(2)}) %collective-permute-start.35) | collective-permute-done | bytes 1048608 | tf_op jit(solution)/shard_map/ppermute | solution.py:542
  370.2 23.1 %collective-permute-done.37 = bf16[512,1024]{1,0:T(8,128)(2,1)S(1)} collective-permute-done((bf16[512,1024]{1,0:T(8,128)(2,1)S(1)}, bf16[512,1024]{1,0:T(8,128)(2,1)S(1)}, u32[]{:S(2)}, u32[]{:S(2)}) %collective-permute-start.37) | collective-permute-done | bytes 1048608 | tf_op jit(solution)/shard_map/ppermute | solution.py:505
  393.3 22.5 %collective-permute-done.38 = bf16[512,1024]{1,0:T(8,128)(2,1)S(1)} collective-permute-done((bf16[512,1024]{1,0:T(8,128)(2,1)S(1)}, bf16[512,1024]{1,0:T(8,128)(2,1)S(1)}, u32[]{:S(2)}, u32[]{:S(2)}) %collective-permute-start.38) | collective-permute-done | bytes 1048608 | tf_op jit(solution)/shard_map/ppermute | solution.py:505
  416.5 3.7 convolution_convert_fusion.3.refs_0_.refs_1_.refs_2_.refs_3_.refs_4_.refs_5_.refs_6_.refs_7_
  424.8 4.1 collective-permute-done.39.refs_8_.refs_9_.refs_10_.refs_11_.refs_12_.refs_13_.refs_14_.refs_15_
  430.3 4.4 shard_map.370
  436.3 3.4 collective-permute-start.45
  446.7 5.9 collective-permute-done.45
  452.7 7.6 collective-permute-done.44
  460.3 5.5 collective-permute-done.43
  470.9 12.6 %collective-permute-done.47 = f32[32,2048]{1,0:T(8,128)S(1)} collective-permute-done((f32[32,2048]{1,0:T(8,128)S(1)}, f32[32,2048]{1,0:T(8,128)S(1)}, u32[]{:S(2)}, u32[]{:S(2)}) %collective-permute-start.47) | collective-permute-done | bytes 262176 | tf_op jit(solution)/shard_map/ppermute | solution.py:542
  542.3 8.0 collective-permute-done.48
  562.4 6.9 collective-permute-done.51.refs_3_
  571.2 5.5 collective-permute-done.54.refs_6_
  576.7 3.9 collective-permute-done.55.refs_7_
  581.3 3.7 shard_map.371
  585.1 5.3 convolution_convert_fusion.9
  609.6 32.6 %collective-permute-done.58 = bf16[512,1024]{1,0:T(8,128)(2,1)S(1)} collective-permute-done((bf16[512,1024]{1,0:T(8,128)(2,1)S(1)}, bf16[512,1024]{1,0:T(8,128)(2,1)S(1)}, u32[]{:S(2)}, u32[]{:S(2)}) %collective-permute-start.58) | collective-permute-done | bytes 1048608 | tf_op jit(solution)/shard_map/ppermute | solution.py:542
  642.6 28.4 %collective-permute-done.60.rest_10_ = bf16[512,1024]{1,0:T(8,128)(2,1)S(1)} collective-permute-done((bf16[512,1024]{1,0:T(8,128)(2,1)S(1)}, bf16[512,1024]{1,0:T(8,128)(2,1)S(1)}, u32[]{:S(2)}, u32[]{:S(2)}) %collective-permute-start.60) | collective-permute-done | bytes 1048608 | tf_op jit(solution)/shard_map/ppermute | solution.py:505
  670.9 21.8 %collective-permute-done.61.rest_11_ = bf16[512,1024]{1,0:T(8,128)(2,1)S(1)} collective-permute-done((bf16[512,1024]{1,0:T(8,128)(2,1)S(1)}, bf16[512,1024]{1,0:T(8,128)(2,1)S(1)}, u32[]{:S(2)}, u32[]{:S(2)}) %collective-permute-start.61) | collective-permute-done | bytes 1048608 | tf_op jit(solution)/shard_map/ppermute | solution.py:505
  695.9 3.7 convolution_convert_fusion.1.refs_0_.refs_1_.refs_2_.refs_3_.refs_4_.refs_5_.refs_6_.refs_7_
  713.7 4.2 shard_map.372
  721.2 4.4 multiply_reduce_fusion.9
  730.7 3.4 collective-permute-done.68
  737.1 7.4 collective-permute-done.67
  751.1 3.5 multiply_reduce_fusion.8
  770.0 15.1 %collective-permute-done.73.refs_3_ = bf16[64,2048]{1,0:T(8,128)(2,1)S(1)} collective-permute-done((bf16[64,2048]{1,0:T(8,128)(2,1)S(1)}, bf16[64,2048]{1,0:T(8,128)(2,1)S(1)}, u32[]{:S(2)}, u32[]{:S(2)}) %collective-permute-start.73) | collective-permute-done | bytes 262176 | tf_op jit(solution)/shard_map/ppermute | solution.py:502
  786.8 3.9 shard_map.373
  831.7 6.0 collective-permute-done.84
  841.9 27.9 %collective-permute-done.85 = f32[641,128]{1,0:T(8,128)S(1)} collective-permute-done((f32[641,128]{1,0:T(8,128)S(1)}, f32[641,128]{1,0:T(8,128)S(1)}, u32[]{:S(2)}, u32[]{:S(2)}) %collective-permute-start.85) | collective-permute-done | bytes 328224 | tf_op jit(solution)/shard_map/ppermute | solution.py:502
  881.9 6.4 collective-permute-done.87
  891.1 3.5 convolution_convert_fusion.16
  894.6 7.0 collective-permute-done.88
  920.5 7.9 multiply_reduce_fusion.1
  937.3 7.6 multiply_convert_fusion
  970.3 7.1 collective-permute-done.93.rest_3_
  981.4 8.6 collective-permute-done.95
  990.8 7.4 collective-permute-done.96
  1001.2 4.3 collective-permute-done.97
  1027.1 53.8 %shard_map.374 = (f32[512,96,128]{2,1,0:T(8,128)}, f32[512,96,128]{2,1,0:T(8,128)}, bf16[512,96,128]{2,1,0:T(8,128)(2,1)}, f32[2,8,128]{2,1,0:T(8,128)S(1)}) custom-call(s32[2]{0:T(128)S(1)} %copy-done.19, f32[1]{0:T(128)} %bitcast.123.clip_ref, f32[512,96,128]{2,1,0:T(8,128)} %bitcast.469, f32[512,96,128]{2,1,0:T(8,128)} %bitcast.474, ...), custom_call_target="tpu_custom_call" | custom-call | flops 125829120 | bytes 150994944 | tf_op jit(solution)/shard_map/pallas_call | solution.py:352
  1090.2 4.0 shard_map.375
  1104.1 3.5 collective-permute-done.103
  1108.4 3.6 collective-permute-done.104
  1115.6 20.8 %multiply_subtract_fusion = f32[512,96,128]{2,1,0:T(8,128)} fusion(f32[512,96,128]{2,1,0:T(8,128)} %bitcast.470, bf16[512,96,128]{2,1,0:T(8,128)(2,1)} %get-tuple-element.322, f32[]{:T(128)} %bitcast.137), kind=kLoop, calls=%fused_computation | loop fusion | flops 18874368 | bytes 62914564 | tf_op jit(solution)/shard_map/sub | solution.py:197
  (895 shorter events, 441.0 us)
Async XLA Ops:
  3.3 17.7 %collective-permute-start = (bf16[32,128]{1,0:T(8,128)(2,1)S(1)}, bf16[32,128]{1,0:T(8,128)(2,1)S(1)}, u32[]{:S(2)}, u32[]{:S(2)}) collective-permute-start(bf16[32,128]{1,0:T(8,128)(2,1)S(1)} %get-tuple-element.371), channel_id=1, source_target_pairs={{0,1},{1,0},{2,3},{3,2},{4,5},{5,4},{6,7},{7,6},{8,9},{9,8},{10,11... | collective-permute-start | bytes 24584 | tf_op jit(solution)/shard_map/ppermute | solution.py:502
  5.4 26.5 %collective-permute-start.13 = (bf16[1,16,64,32]{2,3,1,0:T(8,128)(2,1)}, bf16[1,16,64,32]{2,3,1,0:T(8,128)(2,1)}, u32[]{:S(2)}, u32[]{:S(2)}) collective-permute-start(bf16[1,16,64,32]{2,3,1,0:T(8,128)(2,1)} %convert_bitcast_fusion), channel_id=1, source_target_pairs={{0,1},{1,0},{2,3},{3,2},{4,5},{5,4},{6,7},{7,6},{8,9},{9,8},{10,11... | collective-permute-start | bytes 196616 | tf_op jit(solution)/shard_map/ppermute | solution.py:502
  55.9 20.2 %collective-permute-start.5 = (bf16[512,768]{1,0:T(8,128)(2,1)}, bf16[512,768]{1,0:T(8,128)(2,1)}, u32[]{:S(2)}, u32[]{:S(2)}) collective-permute-start(bf16[512,768]{1,0:T(8,128)(2,1)} %get-tuple-element.197), channel_id=1, source_target_pairs={{0,4},{4,0},{8,12},{12,8},{1,5},{5,1},{9,13},{13,9},{2,6},{6,2},{1... | collective-permute-start | bytes 2359304 | tf_op jit(solution)/shard_map/ppermute | solution.py:505
  57.4 20.8 %collective-permute-start.6 = (bf16[512,768]{1,0:T(8,128)(2,1)}, bf16[512,768]{1,0:T(8,128)(2,1)}, u32[]{:S(2)}, u32[]{:S(2)}) collective-permute-start(bf16[512,768]{1,0:T(8,128)(2,1)} %get-tuple-element.198), channel_id=1, source_target_pairs={{0,8},{4,12},{8,0},{12,4},{1,9},{5,13},{9,1},{13,5},{2,10},{6,14},... | collective-permute-start | bytes 2359304 | tf_op jit(solution)/shard_map/ppermute | solution.py:505
  57.7 31.9 %collective-permute-start.7 = (bf16[512,768]{1,0:T(8,128)(2,1)}, bf16[512,768]{1,0:T(8,128)(2,1)}, u32[]{:S(2)}, u32[]{:S(2)}) collective-permute-start(bf16[512,768]{1,0:T(8,128)(2,1)} %get-tuple-element.199), channel_id=1, source_target_pairs={{0,12},{4,8},{8,4},{12,0},{1,13},{5,9},{9,5},{13,1},{2,14},{6,10},... | collective-permute-start | bytes 2359304 | tf_op jit(solution)/shard_map/ppermute | solution.py:505
  112.8 65.5 %collective-permute-start.9 = (bf16[1024,768]{1,0:T(8,128)(2,1)}, bf16[1024,768]{1,0:T(8,128)(2,1)}, u32[]{:S(2)}, u32[]{:S(2)}) collective-permute-start(bf16[1024,768]{1,0:T(8,128)(2,1)} %convolution_convert_fusion.7), channel_id=1, source_target_pairs={{0,16},{16,0},{1,17},{17,1},{2,18},{18,2},{3,19},{19,3},{4,20},{20... | collective-permute-start | bytes 4718600 | tf_op jit(solution)/shard_map/ppermute | solution.py:542
  116.2 64.5 %collective-permute-start.10 = (bf16[512,1280]{1,0:T(8,128)(2,1)}, bf16[512,1280]{1,0:T(8,128)(2,1)}, u32[]{:S(2)}, u32[]{:S(2)}) collective-permute-start(bf16[512,1280]{1,0:T(8,128)(2,1)} %get-tuple-element.210), channel_id=1, source_target_pairs={{0,4},{4,0},{8,12},{12,8},{1,5},{5,1},{9,13},{13,9},{2,6},{6,2},{1... | collective-permute-start | bytes 3932168 | tf_op jit(solution)/shard_map/ppermute | solution.py:505
  117.7 64.7 %collective-permute-start.11 = (bf16[512,1280]{1,0:T(8,128)(2,1)}, bf16[512,1280]{1,0:T(8,128)(2,1)}, u32[]{:S(2)}, u32[]{:S(2)}) collective-permute-start(bf16[512,1280]{1,0:T(8,128)(2,1)} %get-tuple-element.211), channel_id=1, source_target_pairs={{0,8},{4,12},{8,0},{12,4},{1,9},{5,13},{9,1},{13,5},{2,10},{6,14},... | collective-permute-start | bytes 3932168 | tf_op jit(solution)/shard_map/ppermute | solution.py:505
  117.9 85.5 %collective-permute-start.12 = (bf16[512,1280]{1,0:T(8,128)(2,1)}, bf16[512,1280]{1,0:T(8,128)(2,1)}, u32[]{:S(2)}, u32[]{:S(2)}) collective-permute-start(bf16[512,1280]{1,0:T(8,128)(2,1)} %get-tuple-element.212), channel_id=1, source_target_pairs={{0,12},{4,8},{8,4},{12,0},{1,13},{5,9},{9,5},{13,1},{2,14},{6,10},... | collective-permute-start | bytes 3932168 | tf_op jit(solution)/shard_map/ppermute | solution.py:505
  204.4 14.9 %collective-permute-start.16 = (bf16[1024,256]{1,0:T(8,128)(2,1)S(1)}, bf16[1024,256]{1,0:T(8,128)(2,1)S(1)}, u32[]{:S(2)}, u32[]{:S(2)}) collective-permute-start(bf16[1024,256]{1,0:T(8,128)(2,1)S(1)} %get-tuple-element.373), channel_id=1, source_target_pairs={{0,4},{4,0},{1,5},{5,1},{2,6},{6,2},{3,7},{7,3},{8,12},{12,8},{9,1... | collective-permute-start | bytes 1572872 | tf_op jit(solution)/shard_map/ppermute | solution.py:605
  205.9 19.8 %collective-permute-start.15 = (bf16[1024,256]{1,0:T(8,128)(2,1)S(1)}, bf16[1024,256]{1,0:T(8,128)(2,1)S(1)}, u32[]{:S(2)}, u32[]{:S(2)}) collective-permute-start(bf16[1024,256]{1,0:T(8,128)(2,1)S(1)} %get-tuple-element.374), channel_id=1, source_target_pairs={{0,4},{4,0},{1,5},{5,1},{2,6},{6,2},{3,7},{7,3},{8,12},{12,8},{9,1... | collective-permute-start | bytes 1572872 | tf_op jit(solution)/shard_map/ppermute | solution.py:605
  239.8 15.5 %collective-permute-start.23 = (bf16[64,2048]{1,0:T(8,128)(2,1)}, bf16[64,2048]{1,0:T(8,128)(2,1)S(1)}, u32[]{:S(2)}, u32[]{:S(2)}) collective-permute-start(bf16[64,2048]{1,0:T(8,128)(2,1)} %get-tuple-element.233), channel_id=1, source_target_pairs={{0,12},{1,13},{2,14},{3,15},{4,8},{5,9},{6,10},{7,11},{8,4},{9,5},... | collective-permute-start | bytes 786440 | tf_op jit(solution)/shard_map/ppermute | solution.py:502
  242.4 24.0 %collective-permute-start.22 = (bf16[64,2048]{1,0:T(8,128)(2,1)}, bf16[64,2048]{1,0:T(8,128)(2,1)S(1)}, u32[]{:S(2)}, u32[]{:S(2)}) collective-permute-start(bf16[64,2048]{1,0:T(8,128)(2,1)} %get-tuple-element.232), channel_id=1, source_target_pairs={{0,10},{1,11},{2,8},{3,9},{4,14},{5,15},{6,12},{7,13},{8,2},{9,3},... | collective-permute-start | bytes 786440 | tf_op jit(solution)/shard_map/ppermute | solution.py:502
  243.7 25.3 %collective-permute-start.21 = (bf16[64,2048]{1,0:T(8,128)(2,1)}, bf16[64,2048]{1,0:T(8,128)(2,1)S(1)}, u32[]{:S(2)}, u32[]{:S(2)}) collective-permute-start(bf16[64,2048]{1,0:T(8,128)(2,1)} %get-tuple-element.231), channel_id=1, source_target_pairs={{0,8},{1,9},{2,10},{3,11},{4,12},{5,13},{6,14},{7,15},{8,0},{9,1},... | collective-permute-start | bytes 786440 | tf_op jit(solution)/shard_map/ppermute | solution.py:502
  245.7 23.3 %collective-permute-start.20 = (bf16[64,2048]{1,0:T(8,128)(2,1)}, bf16[64,2048]{1,0:T(8,128)(2,1)S(1)}, u32[]{:S(2)}, u32[]{:S(2)}) collective-permute-start(bf16[64,2048]{1,0:T(8,128)(2,1)} %get-tuple-element.230), channel_id=1, source_target_pairs={{0,6},{1,7},{2,4},{3,5},{4,2},{5,3},{6,0},{7,1},{8,14},{9,15},{10,... | collective-permute-start | bytes 786440 | tf_op jit(solution)/shard_map/ppermute | solution.py:502
  251.1 18.4 %collective-permute-start.19 = (bf16[64,2048]{1,0:T(8,128)(2,1)}, bf16[64,2048]{1,0:T(8,128)(2,1)S(1)}, u32[]{:S(2)}, u32[]{:S(2)}) collective-permute-start(bf16[64,2048]{1,0:T(8,128)(2,1)} %get-tuple-element.229), channel_id=1, source_target_pairs={{0,4},{1,5},{2,6},{3,7},{4,0},{5,1},{6,2},{7,3},{8,12},{9,13},{10,... | collective-permute-start | bytes 786440 | tf_op jit(solution)/shard_map/ppermute | solution.py:502
  255.4 16.5 %collective-permute-start.18 = (bf16[64,2048]{1,0:T(8,128)(2,1)}, bf16[64,2048]{1,0:T(8,128)(2,1)S(1)}, u32[]{:S(2)}, u32[]{:S(2)}) collective-permute-start(bf16[64,2048]{1,0:T(8,128)(2,1)} %get-tuple-element.228), channel_id=1, source_target_pairs={{0,2},{1,3},{2,0},{3,1},{4,6},{5,7},{6,4},{7,5},{8,10},{9,11},{10,... | collective-permute-start | bytes 786440 | tf_op jit(solution)/shard_map/ppermute | solution.py:502
  279.0 18.4 %collective-permute-start.26 = (bf16[64,2048]{1,0:T(8,128)(2,1)S(1)}, bf16[64,2048]{1,0:T(8,128)(2,1)S(1)}, u32[]{:S(2)}, u32[]{:S(2)}) collective-permute-start(bf16[64,2048]{1,0:T(8,128)(2,1)S(1)} %multiply_convert_fusion.11.refs_0_), channel_id=1, source_target_pairs={{0,2},{1,3},{2,0},{3,1},{4,6},{5,7},{6,4},{7,5},{8,10},{9,11},{10,... | collective-permute-start | bytes 786440 | tf_op jit(solution)/shard_map/ppermute | solution.py:502
  279.3 18.3 %collective-permute-start.27 = (bf16[64,2048]{1,0:T(8,128)(2,1)S(1)}, bf16[64,2048]{1,0:T(8,128)(2,1)S(1)}, u32[]{:S(2)}, u32[]{:S(2)}) collective-permute-start(bf16[64,2048]{1,0:T(8,128)(2,1)S(1)} %multiply_convert_fusion.11.refs_0_), channel_id=1, source_target_pairs={{0,4},{1,5},{2,6},{3,7},{4,0},{5,1},{6,2},{7,3},{8,12},{9,13},{10,... | collective-permute-start | bytes 786440 | tf_op jit(solution)/shard_map/ppermute | solution.py:502
  280.4 19.2 %collective-permute-start.28 = (bf16[64,2048]{1,0:T(8,128)(2,1)S(1)}, bf16[64,2048]{1,0:T(8,128)(2,1)S(1)}, u32[]{:S(2)}, u32[]{:S(2)}) collective-permute-start(bf16[64,2048]{1,0:T(8,128)(2,1)S(1)} %multiply_convert_fusion.11.refs_0_), channel_id=1, source_target_pairs={{0,6},{1,7},{2,4},{3,5},{4,2},{5,3},{6,0},{7,1},{8,14},{9,15},{10,... | collective-permute-start | bytes 786440 | tf_op jit(solution)/shard_map/ppermute | solution.py:502
  282.5 17.0 %collective-permute-start.29 = (bf16[64,2048]{1,0:T(8,128)(2,1)S(1)}, bf16[64,2048]{1,0:T(8,128)(2,1)S(1)}, u32[]{:S(2)}, u32[]{:S(2)}) collective-permute-start(bf16[64,2048]{1,0:T(8,128)(2,1)S(1)} %multiply_convert_fusion.11.refs_0_), channel_id=1, source_target_pairs={{0,8},{1,9},{2,10},{3,11},{4,12},{5,13},{6,14},{7,15},{8,0},{9,1},... | collective-permute-start | bytes 786440 | tf_op jit(solution)/shard_map/ppermute | solution.py:502
  282.5 17.0 %collective-permute-start.30 = (bf16[64,2048]{1,0:T(8,128)(2,1)S(1)}, bf16[64,2048]{1,0:T(8,128)(2,1)S(1)}, u32[]{:S(2)}, u32[]{:S(2)}) collective-permute-start(bf16[64,2048]{1,0:T(8,128)(2,1)S(1)} %multiply_convert_fusion.11.refs_0_), channel_id=1, source_target_pairs={{0,10},{1,11},{2,8},{3,9},{4,14},{5,15},{6,12},{7,13},{8,2},{9,3},... | collective-permute-start | bytes 786440 | tf_op jit(solution)/shard_map/ppermute | solution.py:502
  320.3 49.5 %collective-permute-start.35 = (bf16[512,1024]{1,0:T(8,128)(2,1)S(1)}, bf16[512,1024]{1,0:T(8,128)(2,1)S(1)}, u32[]{:S(2)}, u32[]{:S(2)}) collective-permute-start(bf16[512,1024]{1,0:T(8,128)(2,1)S(1)} %convolution_convert_fusion.11), channel_id=1, source_target_pairs={{0,16},{16,0},{1,17},{17,1},{2,18},{18,2},{3,19},{19,3},{4,20},{20... | collective-permute-start | bytes 3145736 | tf_op jit(solution)/shard_map/ppermute | solution.py:542
  323.0 47.2 %collective-permute-start.36 = (bf16[512,1024]{1,0:T(8,128)(2,1)S(1)}, bf16[512,1024]{1,0:T(8,128)(2,1)S(1)}, u32[]{:S(2)}, u32[]{:S(2)}) collective-permute-start(bf16[512,1024]{1,0:T(8,128)(2,1)S(1)} %copy-done.29), channel_id=1, source_target_pairs={{0,4},{4,0},{8,12},{12,8},{1,5},{5,1},{9,13},{13,9},{2,6},{6,2},{1... | collective-permute-start | bytes 3145736 | tf_op jit(solution)/shard_map/ppermute | solution.py:505
  324.1 69.2 %collective-permute-start.37 = (bf16[512,1024]{1,0:T(8,128)(2,1)S(1)}, bf16[512,1024]{1,0:T(8,128)(2,1)S(1)}, u32[]{:S(2)}, u32[]{:S(2)}) collective-permute-start(bf16[512,1024]{1,0:T(8,128)(2,1)S(1)} %copy-done.27), channel_id=1, source_target_pairs={{0,8},{4,12},{8,0},{12,4},{1,9},{5,13},{9,1},{13,5},{2,10},{6,14},... | collective-permute-start | bytes 3145736 | tf_op jit(solution)/shard_map/ppermute | solution.py:505
  326.5 89.3 %collective-permute-start.38 = (bf16[512,1024]{1,0:T(8,128)(2,1)S(1)}, bf16[512,1024]{1,0:T(8,128)(2,1)S(1)}, u32[]{:S(2)}, u32[]{:S(2)}) collective-permute-start(bf16[512,1024]{1,0:T(8,128)(2,1)S(1)} %copy-done.25), channel_id=1, source_target_pairs={{0,12},{4,8},{8,4},{12,0},{1,13},{5,9},{9,5},{13,1},{2,14},{6,10},... | collective-permute-start | bytes 3145736 | tf_op jit(solution)/shard_map/ppermute | solution.py:505
  329.4 90.9 %collective-permute-start.34 = (bf16[512,1024]{1,0:T(8,128)(2,1)S(1)}, bf16[512,1024]{1,0:T(8,128)(2,1)S(1)}, u32[]{:S(2)}, u32[]{:S(2)}) collective-permute-start(bf16[512,1024]{1,0:T(8,128)(2,1)S(1)} %convolution_convert_fusion.10), channel_id=1, source_target_pairs={{0,16},{16,0},{1,17},{17,1},{2,18},{18,2},{3,19},{19,3},{4,20},{20... | collective-permute-start | bytes 3145736 | tf_op jit(solution)/shard_map/ppermute | solution.py:542
  436.3 16.4 %collective-permute-start.45 = (bf16[64,2048]{1,0:T(8,128)(2,1)}, bf16[64,2048]{1,0:T(8,128)(2,1)S(1)}, u32[]{:S(2)}, u32[]{:S(2)}) collective-permute-start(bf16[64,2048]{1,0:T(8,128)(2,1)} %get-tuple-element.258), channel_id=1, source_target_pairs={{0,12},{1,13},{2,14},{3,15},{4,8},{5,9},{6,10},{7,11},{8,4},{9,5},... | collective-permute-start | bytes 786440 | tf_op jit(solution)/shard_map/ppermute | solution.py:502
  439.7 20.6 %collective-permute-start.44 = (bf16[64,2048]{1,0:T(8,128)(2,1)}, bf16[64,2048]{1,0:T(8,128)(2,1)S(1)}, u32[]{:S(2)}, u32[]{:S(2)}) collective-permute-start(bf16[64,2048]{1,0:T(8,128)(2,1)} %get-tuple-element.257), channel_id=1, source_target_pairs={{0,10},{1,11},{2,8},{3,9},{4,14},{5,15},{6,12},{7,13},{8,2},{9,3},... | collective-permute-start | bytes 786440 | tf_op jit(solution)/shard_map/ppermute | solution.py:502
  439.7 26.1 %collective-permute-start.43 = (bf16[64,2048]{1,0:T(8,128)(2,1)}, bf16[64,2048]{1,0:T(8,128)(2,1)S(1)}, u32[]{:S(2)}, u32[]{:S(2)}) collective-permute-start(bf16[64,2048]{1,0:T(8,128)(2,1)} %get-tuple-element.256), channel_id=1, source_target_pairs={{0,8},{1,9},{2,10},{3,11},{4,12},{5,13},{6,14},{7,15},{8,0},{9,1},... | collective-permute-start | bytes 786440 | tf_op jit(solution)/shard_map/ppermute | solution.py:502
  440.6 25.1 %collective-permute-start.42 = (bf16[64,2048]{1,0:T(8,128)(2,1)}, bf16[64,2048]{1,0:T(8,128)(2,1)S(1)}, u32[]{:S(2)}, u32[]{:S(2)}) collective-permute-start(bf16[64,2048]{1,0:T(8,128)(2,1)} %get-tuple-element.255), channel_id=1, source_target_pairs={{0,6},{1,7},{2,4},{3,5},{4,2},{5,3},{6,0},{7,1},{8,14},{9,15},{10,... | collective-permute-start | bytes 786440 | tf_op jit(solution)/shard_map/ppermute | solution.py:502
  446.0 21.0 %collective-permute-start.41 = (bf16[64,2048]{1,0:T(8,128)(2,1)}, bf16[64,2048]{1,0:T(8,128)(2,1)S(1)}, u32[]{:S(2)}, u32[]{:S(2)}) collective-permute-start(bf16[64,2048]{1,0:T(8,128)(2,1)} %get-tuple-element.254), channel_id=1, source_target_pairs={{0,4},{1,5},{2,6},{3,7},{4,0},{5,1},{6,2},{7,3},{8,12},{9,13},{10,... | collective-permute-start | bytes 786440 | tf_op jit(solution)/shard_map/ppermute | solution.py:502
  468.7 14.8 %collective-permute-start.47 = (f32[32,2048]{1,0:T(8,128)S(1)}, f32[32,2048]{1,0:T(8,128)S(1)}, u32[]{:S(2)}, u32[]{:S(2)}) collective-permute-start(f32[32,2048]{1,0:T(8,128)S(1)} %slice_select_fusion.1), channel_id=1, source_target_pairs={{0,16},{16,0},{1,17},{17,1},{2,18},{18,2},{3,19},{19,3},{4,20},{20... | collective-permute-start | bytes 786440 | tf_op jit(solution)/shard_map/ppermute | solution.py:542
  552.3 17.0 %collective-permute-start.51 = (bf16[64,2048]{1,0:T(8,128)(2,1)S(1)}, bf16[64,2048]{1,0:T(8,128)(2,1)S(1)}, u32[]{:S(2)}, u32[]{:S(2)}) collective-permute-start(bf16[64,2048]{1,0:T(8,128)(2,1)S(1)} %pad_maximum_fusion.21.refs_0_), channel_id=1, source_target_pairs={{0,6},{1,7},{2,4},{3,5},{4,2},{5,3},{6,0},{7,1},{8,14},{9,15},{10,... | collective-permute-start | bytes 786440 | tf_op jit(solution)/shard_map/ppermute | solution.py:502
  554.0 15.2 %collective-permute-start.52 = (bf16[64,2048]{1,0:T(8,128)(2,1)S(1)}, bf16[64,2048]{1,0:T(8,128)(2,1)S(1)}, u32[]{:S(2)}, u32[]{:S(2)}) collective-permute-start(bf16[64,2048]{1,0:T(8,128)(2,1)S(1)} %pad_maximum_fusion.21.refs_0_), channel_id=1, source_target_pairs={{0,8},{1,9},{2,10},{3,11},{4,12},{5,13},{6,14},{7,15},{8,0},{9,1},... | collective-permute-start | bytes 786440 | tf_op jit(solution)/shard_map/ppermute | solution.py:502
  554.1 17.1 %collective-permute-start.53 = (bf16[64,2048]{1,0:T(8,128)(2,1)S(1)}, bf16[64,2048]{1,0:T(8,128)(2,1)S(1)}, u32[]{:S(2)}, u32[]{:S(2)}) collective-permute-start(bf16[64,2048]{1,0:T(8,128)(2,1)S(1)} %pad_maximum_fusion.21.refs_0_), channel_id=1, source_target_pairs={{0,10},{1,11},{2,8},{3,9},{4,14},{5,15},{6,12},{7,13},{8,2},{9,3},... | collective-permute-start | bytes 786440 | tf_op jit(solution)/shard_map/ppermute | solution.py:502
  558.9 17.8 %collective-permute-start.54 = (bf16[64,2048]{1,0:T(8,128)(2,1)S(1)}, bf16[64,2048]{1,0:T(8,128)(2,1)S(1)}, u32[]{:S(2)}, u32[]{:S(2)}) collective-permute-start(bf16[64,2048]{1,0:T(8,128)(2,1)S(1)} %pad_maximum_fusion.21.refs_0_), channel_id=1, source_target_pairs={{0,12},{1,13},{2,14},{3,15},{4,8},{5,9},{6,10},{7,11},{8,4},{9,5},... | collective-permute-start | bytes 786440 | tf_op jit(solution)/shard_map/ppermute | solution.py:502
  560.9 19.6 %collective-permute-start.55 = (bf16[64,2048]{1,0:T(8,128)(2,1)S(1)}, bf16[64,2048]{1,0:T(8,128)(2,1)S(1)}, u32[]{:S(2)}, u32[]{:S(2)}) collective-permute-start(bf16[64,2048]{1,0:T(8,128)(2,1)S(1)} %pad_maximum_fusion.21.refs_0_), channel_id=1, source_target_pairs={{0,14},{1,15},{2,12},{3,13},{4,10},{5,11},{6,8},{7,9},{8,6},{9,7},... | collective-permute-start | bytes 786440 | tf_op jit(solution)/shard_map/ppermute | solution.py:502
  592.8 49.3 %collective-permute-start.58 = (bf16[512,1024]{1,0:T(8,128)(2,1)S(1)}, bf16[512,1024]{1,0:T(8,128)(2,1)S(1)}, u32[]{:S(2)}, u32[]{:S(2)}) collective-permute-start(bf16[512,1024]{1,0:T(8,128)(2,1)S(1)} %convolution_convert_fusion.9), channel_id=1, source_target_pairs={{0,16},{16,0},{1,17},{17,1},{2,18},{18,2},{3,19},{19,3},{4,20},{20... | collective-permute-start | bytes 3145736 | tf_op jit(solution)/shard_map/ppermute | solution.py:542
  597.0 45.5 %collective-permute-start.59 = (bf16[512,1024]{1,0:T(8,128)(2,1)S(1)}, bf16[512,1024]{1,0:T(8,128)(2,1)S(1)}, u32[]{:S(2)}, u32[]{:S(2)}) collective-permute-start(bf16[512,1024]{1,0:T(8,128)(2,1)S(1)} %get-tuple-element.500), channel_id=1, source_target_pairs={{0,4},{4,0},{8,12},{12,8},{1,5},{5,1},{9,13},{13,9},{2,6},{6,2},{1... | collective-permute-start | bytes 3145736 | tf_op jit(solution)/shard_map/ppermute | solution.py:505
  600.4 70.5 %collective-permute-start.60 = (bf16[512,1024]{1,0:T(8,128)(2,1)S(1)}, bf16[512,1024]{1,0:T(8,128)(2,1)S(1)}, u32[]{:S(2)}, u32[]{:S(2)}) collective-permute-start(bf16[512,1024]{1,0:T(8,128)(2,1)S(1)} %get-tuple-element.502), channel_id=1, source_target_pairs={{0,8},{4,12},{8,0},{12,4},{1,9},{5,13},{9,1},{13,5},{2,10},{6,14},... | collective-permute-start | bytes 3145736 | tf_op jit(solution)/shard_map/ppermute | solution.py:505
  604.0 88.7 %collective-permute-start.61 = (bf16[512,1024]{1,0:T(8,128)(2,1)S(1)}, bf16[512,1024]{1,0:T(8,128)(2,1)S(1)}, u32[]{:S(2)}, u32[]{:S(2)}) collective-permute-start(bf16[512,1024]{1,0:T(8,128)(2,1)S(1)} %get-tuple-element.504), channel_id=1, source_target_pairs={{0,12},{4,8},{8,4},{12,0},{1,13},{5,9},{9,5},{13,1},{2,14},{6,10},... | collective-permute-start | bytes 3145736 | tf_op jit(solution)/shard_map/ppermute | solution.py:505
  605.3 94.3 %collective-permute-start.57 = (bf16[512,1024]{1,0:T(8,128)(2,1)S(1)}, bf16[512,1024]{1,0:T(8,128)(2,1)S(1)}, u32[]{:S(2)}, u32[]{:S(2)}) collective-permute-start(bf16[512,1024]{1,0:T(8,128)(2,1)S(1)} %convolution_convert_fusion.8), channel_id=1, source_target_pairs={{0,16},{16,0},{1,17},{17,1},{2,18},{18,2},{3,19},{19,3},{4,20},{20... | collective-permute-start | bytes 3145736 | tf_op jit(solution)/shard_map/ppermute | solution.py:542
  718.0 16.0 %collective-permute-start.68 = (bf16[64,2048]{1,0:T(8,128)(2,1)}, bf16[64,2048]{1,0:T(8,128)(2,1)S(1)}, u32[]{:S(2)}, u32[]{:S(2)}) collective-permute-start(bf16[64,2048]{1,0:T(8,128)(2,1)} %get-tuple-element.274), channel_id=1, source_target_pairs={{0,12},{1,13},{2,14},{3,15},{4,8},{5,9},{6,10},{7,11},{8,4},{9,5},... | collective-permute-start | bytes 786440 | tf_op jit(solution)/shard_map/ppermute | solution.py:502
  725.6 18.9 %collective-permute-start.67 = (bf16[64,2048]{1,0:T(8,128)(2,1)S(1)}, bf16[64,2048]{1,0:T(8,128)(2,1)S(1)}, u32[]{:S(2)}, u32[]{:S(2)}) collective-permute-start(bf16[64,2048]{1,0:T(8,128)(2,1)S(1)} %copy-done.192), channel_id=1, source_target_pairs={{0,10},{1,11},{2,8},{3,9},{4,14},{5,15},{6,12},{7,13},{8,2},{9,3},... | collective-permute-start | bytes 786440 | tf_op jit(solution)/shard_map/ppermute | solution.py:502
  726.0 22.5 %collective-permute-start.66 = (bf16[64,2048]{1,0:T(8,128)(2,1)S(1)}, bf16[64,2048]{1,0:T(8,128)(2,1)S(1)}, u32[]{:S(2)}, u32[]{:S(2)}) collective-permute-start(bf16[64,2048]{1,0:T(8,128)(2,1)S(1)} %copy-done.191), channel_id=1, source_target_pairs={{0,8},{1,9},{2,10},{3,11},{4,12},{5,13},{6,14},{7,15},{8,0},{9,1},... | collective-permute-start | bytes 786440 | tf_op jit(solution)/shard_map/ppermute | solution.py:502
  728.4 20.1 %collective-permute-start.65 = (bf16[64,2048]{1,0:T(8,128)(2,1)S(1)}, bf16[64,2048]{1,0:T(8,128)(2,1)S(1)}, u32[]{:S(2)}, u32[]{:S(2)}) collective-permute-start(bf16[64,2048]{1,0:T(8,128)(2,1)S(1)} %copy-done.190), channel_id=1, source_target_pairs={{0,6},{1,7},{2,4},{3,5},{4,2},{5,3},{6,0},{7,1},{8,14},{9,15},{10,... | collective-permute-start | bytes 786440 | tf_op jit(solution)/shard_map/ppermute | solution.py:502
  729.9 19.4 %collective-permute-start.64 = (bf16[64,2048]{1,0:T(8,128)(2,1)S(1)}, bf16[64,2048]{1,0:T(8,128)(2,1)S(1)}, u32[]{:S(2)}, u32[]{:S(2)}) collective-permute-start(bf16[64,2048]{1,0:T(8,128)(2,1)S(1)} %copy-done.189), channel_id=1, source_target_pairs={{0,4},{1,5},{2,6},{3,7},{4,0},{5,1},{6,2},{7,3},{8,12},{9,13},{10,... | collective-permute-start | bytes 786440 | tf_op jit(solution)/shard_map/ppermute | solution.py:502
  734.1 16.4 %collective-permute-start.63 = (bf16[64,2048]{1,0:T(8,128)(2,1)S(1)}, bf16[64,2048]{1,0:T(8,128)(2,1)S(1)}, u32[]{:S(2)}, u32[]{:S(2)}) collective-permute-start(bf16[64,2048]{1,0:T(8,128)(2,1)S(1)} %copy-done.188), channel_id=1, source_target_pairs={{0,2},{1,3},{2,0},{3,1},{4,6},{5,7},{6,4},{7,5},{8,10},{9,11},{10,... | collective-permute-start | bytes 786440 | tf_op jit(solution)/shard_map/ppermute | solution.py:502
  744.5 16.3 %collective-permute-start.89 = (bf16[1024,256]{1,0:T(8,128)(2,1)}, bf16[1024,256]{1,0:T(8,128)(2,1)S(1)}, u32[]{:S(2)}, u32[]{:S(2)}) collective-permute-start(bf16[1024,256]{1,0:T(8,128)(2,1)} %get-tuple-element.372), channel_id=1, source_target_pairs={{0,4},{4,0},{1,5},{5,1},{2,6},{6,2},{3,7},{7,3},{8,12},{12,8},{9,1... | collective-permute-start | bytes 1572872 | tf_op jit(solution)/shard_map/ppermute | solution.py:605
  757.9 27.2 %collective-permute-start.73 = (bf16[64,2048]{1,0:T(8,128)(2,1)S(1)}, bf16[64,2048]{1,0:T(8,128)(2,1)S(1)}, u32[]{:S(2)}, u32[]{:S(2)}) collective-permute-start(bf16[64,2048]{1,0:T(8,128)(2,1)S(1)} %multiply_add_fusion.refs_0_), channel_id=1, source_target_pairs={{0,6},{1,7},{2,4},{3,5},{4,2},{5,3},{6,0},{7,1},{8,14},{9,15},{10,... | collective-permute-start | bytes 786440 | tf_op jit(solution)/shard_map/ppermute | solution.py:502
  759.5 25.7 %collective-permute-start.74 = (bf16[64,2048]{1,0:T(8,128)(2,1)S(1)}, bf16[64,2048]{1,0:T(8,128)(2,1)S(1)}, u32[]{:S(2)}, u32[]{:S(2)}) collective-permute-start(bf16[64,2048]{1,0:T(8,128)(2,1)S(1)} %multiply_add_fusion.refs_0_), channel_id=1, source_target_pairs={{0,8},{1,9},{2,10},{3,11},{4,12},{5,13},{6,14},{7,15},{8,0},{9,1},... | collective-permute-start | bytes 786440 | tf_op jit(solution)/shard_map/ppermute | solution.py:502
  760.8 24.4 %collective-permute-start.75 = (bf16[64,2048]{1,0:T(8,128)(2,1)S(1)}, bf16[64,2048]{1,0:T(8,128)(2,1)S(1)}, u32[]{:S(2)}, u32[]{:S(2)}) collective-permute-start(bf16[64,2048]{1,0:T(8,128)(2,1)S(1)} %multiply_add_fusion.refs_0_), channel_id=1, source_target_pairs={{0,10},{1,11},{2,8},{3,9},{4,14},{5,15},{6,12},{7,13},{8,2},{9,3},... | collective-permute-start | bytes 786440 | tf_op jit(solution)/shard_map/ppermute | solution.py:502
  763.3 21.9 %collective-permute-start.76 = (bf16[64,2048]{1,0:T(8,128)(2,1)S(1)}, bf16[64,2048]{1,0:T(8,128)(2,1)S(1)}, u32[]{:S(2)}, u32[]{:S(2)}) collective-permute-start(bf16[64,2048]{1,0:T(8,128)(2,1)S(1)} %multiply_add_fusion.refs_0_), channel_id=1, source_target_pairs={{0,12},{1,13},{2,14},{3,15},{4,8},{5,9},{6,10},{7,11},{8,4},{9,5},... | collective-permute-start | bytes 786440 | tf_op jit(solution)/shard_map/ppermute | solution.py:502
  766.2 20.6 %collective-permute-start.77 = (bf16[64,2048]{1,0:T(8,128)(2,1)S(1)}, bf16[64,2048]{1,0:T(8,128)(2,1)}, u32[]{:S(2)}, u32[]{:S(2)}) collective-permute-start(bf16[64,2048]{1,0:T(8,128)(2,1)S(1)} %multiply_add_fusion.refs_0_), channel_id=1, source_target_pairs={{0,14},{1,15},{2,12},{3,13},{4,10},{5,11},{6,8},{7,9},{8,6},{9,7},... | collective-permute-start | bytes 786440 | tf_op jit(solution)/shard_map/ppermute | solution.py:502
  790.7 20.2 %collective-permute-start.78 = (bf16[512,2048]{1,0:T(8,128)(2,1)}, bf16[512,2048]{1,0:T(8,128)(2,1)}, u32[]{:S(2)}, u32[]{:S(2)}) collective-permute-start(bf16[512,2048]{1,0:T(8,128)(2,1)} %shard_map.373), channel_id=1, source_target_pairs={{0,1},{1,0},{2,3},{3,2},{4,5},{5,4},{6,7},{7,6},{8,9},{9,8},{10,11... | collective-permute-start | bytes 6291464 | tf_op jit(solution)/shard_map/ppermute | solution.py:502
  805.1 83.5 %collective-permute-start.80 = (bf16[512,1024]{1,0:T(8,128)(2,1)}, bf16[512,1024]{1,0:T(8,128)(2,1)}, u32[]{:S(2)}, u32[]{:S(2)}) collective-permute-start(bf16[512,1024]{1,0:T(8,128)(2,1)} %get-tuple-element.281), channel_id=1, source_target_pairs={{0,4},{4,0},{8,12},{12,8},{1,5},{5,1},{9,13},{13,9},{2,6},{6,2},{1... | collective-permute-start | bytes 3145736 | tf_op jit(solution)/shard_map/ppermute | solution.py:505
  805.1 83.5 %collective-permute-start.81 = (bf16[512,1024]{1,0:T(8,128)(2,1)}, bf16[512,1024]{1,0:T(8,128)(2,1)}, u32[]{:S(2)}, u32[]{:S(2)}) collective-permute-start(bf16[512,1024]{1,0:T(8,128)(2,1)} %get-tuple-element.282), channel_id=1, source_target_pairs={{0,8},{4,12},{8,0},{12,4},{1,9},{5,13},{9,1},{13,5},{2,10},{6,14},... | collective-permute-start | bytes 3145736 | tf_op jit(solution)/shard_map/ppermute | solution.py:505
  806.5 82.1 %collective-permute-start.82 = (bf16[512,1024]{1,0:T(8,128)(2,1)}, bf16[512,1024]{1,0:T(8,128)(2,1)}, u32[]{:S(2)}, u32[]{:S(2)}) collective-permute-start(bf16[512,1024]{1,0:T(8,128)(2,1)} %get-tuple-element.283), channel_id=1, source_target_pairs={{0,12},{4,8},{8,4},{12,0},{1,13},{5,9},{9,5},{13,1},{2,14},{6,10},... | collective-permute-start | bytes 3145736 | tf_op jit(solution)/shard_map/ppermute | solution.py:505
  813.4 67.3 %collective-permute-start.79 = (bf16[1024,256]{1,0:T(8,128)(2,1)S(1)}, bf16[1024,256]{1,0:T(8,128)(2,1)}, u32[]{:S(2)}, u32[]{:S(2)}) collective-permute-start(bf16[1024,256]{1,0:T(8,128)(2,1)S(1)} %pad_maximum_fusion.15), channel_id=1, source_target_pairs={{0,16},{16,0},{1,17},{17,1},{2,18},{18,2},{3,19},{19,3},{4,20},{20... | collective-permute-start | bytes 1572872 | tf_op jit(solution)/shard_map/ppermute | solution.py:542
  837.8 32.1 %collective-permute-start.85 = (f32[641,128]{1,0:T(8,128)S(1)}, f32[641,128]{1,0:T(8,128)S(1)}, u32[]{:S(2)}, u32[]{:S(2)}) collective-permute-start(f32[641,128]{1,0:T(8,128)S(1)} %maximum_bitcast_fusion.2), channel_id=1, source_target_pairs={{0,4},{1,5},{2,6},{3,7},{4,0},{5,1},{6,2},{7,3},{8,12},{9,13},{10,... | collective-permute-start | bytes 984584 | tf_op jit(solution)/shard_map/ppermute | solution.py:502
  929.1 41.2 %collective-permute-start.91 = (bf16[512,1024]{1,0:T(8,128)(2,1)}, bf16[512,1024]{1,0:T(8,128)(2,1)S(1)}, u32[]{:S(2)}, u32[]{:S(2)}) collective-permute-start(bf16[512,1024]{1,0:T(8,128)(2,1)} %pad_maximum_fusion.5), channel_id=1, source_target_pairs={{0,4},{4,0},{8,12},{12,8},{1,5},{5,1},{9,13},{13,9},{2,6},{6,2},{1... | collective-permute-start | bytes 3145736 | tf_op jit(solution)/shard_map/ppermute | solution.py:505
  930.2 40.1 %collective-permute-start.92 = (bf16[512,1024]{1,0:T(8,128)(2,1)}, bf16[512,1024]{1,0:T(8,128)(2,1)}, u32[]{:S(2)}, u32[]{:S(2)}) collective-permute-start(bf16[512,1024]{1,0:T(8,128)(2,1)} %pad_maximum_fusion.6), channel_id=1, source_target_pairs={{0,8},{4,12},{8,0},{12,4},{1,9},{5,13},{9,1},{13,5},{2,10},{6,14},... | collective-permute-start | bytes 3145736 | tf_op jit(solution)/shard_map/ppermute | solution.py:505
  932.8 44.5 %collective-permute-start.93 = (bf16[512,1024]{1,0:T(8,128)(2,1)}, bf16[512,1024]{1,0:T(8,128)(2,1)}, u32[]{:S(2)}, u32[]{:S(2)}) collective-permute-start(bf16[512,1024]{1,0:T(8,128)(2,1)} %pad_maximum_fusion.7), channel_id=1, source_target_pairs={{0,12},{4,8},{8,4},{12,0},{1,13},{5,9},{9,5},{13,1},{2,14},{6,10},... | collective-permute-start | bytes 3145736 | tf_op jit(solution)/shard_map/ppermute | solution.py:505
  (238 other events, 2755.0 us)
